TPU v7x, 32 devices: a whole 2x2x4 slice. The times are simulated.
32 devices in a mesh: batch: 16 (over z, y, core), heads: 2 (over x).
Axes of the slice: x: 2, y: 2, z: 4, core: 2. Of those that a mesh axis runs over, the one named last changes fastest.
Arguments:
- residual_in: bfloat16 [16, 1024, 768], P('batch', 'heads'), may hold values from -6 to 6
- norm_gain: bfloat16 [768], replicated, may hold values from 0.5 to 1.5
- gate_proj: bfloat16 [768, 1536], P(None, 'heads'), may hold values from -0.21875 to 0.21875
- value_proj: bfloat16 [768, 1536], P(None, 'heads'), may hold values from -0.21875 to 0.21875
- state_proj: bfloat16 [768, 256], replicated, may hold values from -0.21875 to 0.21875
- step_proj: bfloat16 [768, 24], P(None, 'heads'), may hold values from -0.21875 to 0.21875
- value_conv: bfloat16 [4, 1536], P(None, 'heads'), may hold values from -3 to 3
- value_shift: bfloat16 [1536], P('heads'), may hold values from -0.5 to 0.5
- state_conv: bfloat16 [4, 256], replicated, may hold values from -3 to 3
- state_shift: bfloat16 [256], replicated, may hold values from -0.5 to 0.5
- step_bias: float32 [24], P('heads'), may hold values from -4 to 1
- log_rate: float32 [24], P('heads'), may hold values from -2 to 1.5
- skip_gain: float32 [24], P('heads'), may hold values from 0.5 to 1.5
- gated_gain: bfloat16 [1536], P('heads'), may hold values from 0.5 to 1.5
- out_proj: bfloat16 [1536, 768], P('heads'), may hold values from -0.15625 to 0.15625
- grad_out: bfloat16 [16, 1024, 768], P('batch', 'heads'), may hold values from -6 to 6
Outputs:
- mixed: float32 [16, 1024, 768], P('batch', 'heads')
- grad_input: float32 [16, 1024, 768], P('batch', 'heads')
- grad_norm_gain: float32 [768], replicated
- grad_gate_proj: float32 [768, 1536], P(None, 'heads')
- grad_value_proj: float32 [768, 1536], P(None, 'heads')
- grad_state_proj: float32 [768, 256], replicated
- grad_step_proj: float32 [768, 24], P(None, 'heads')
- grad_value_conv: float32 [4, 1536], P(None, 'heads')
- grad_value_shift: float32 [1536], P('heads')
- grad_state_conv: float32 [4, 256], replicated
- grad_state_shift: float32 [256], replicated
- grad_step_bias: float32 [24], P('heads')
- grad_log_rate: float32 [24], P('heads')
- grad_skip_gain: float32 [24], P('heads')
- grad_gated_gain: float32 [1536], P('heads')
- grad_out_proj: float32 [1536, 768], P('heads')
All inputs are finite; a program needn't handle non-finite values.
Results may differ from a plain program's by a relative error of at most 0.0083.
Values may be sent and summed in bfloat16 or wider, within the bound.
No kernel may reach another device: no remote copies, remote signals or barrier semaphores. Data moves between devices by JAX's collectives and lax.ppermute only.
A program may use at most 128 MiB of HBM per device.

v0:
```python
import jax
import jax.numpy as jnp
from jax import lax
from jax.sharding import PartitionSpec as P

GROUP = 256


EPSILON = 1e-05
HIGHEST = lax.Precision.HIGHEST


def causal_conv(signal, kernel, offset):
    taps = kernel.shape[0]
    length = signal.shape[0]
    padded = jnp.pad(signal, ((taps - 1, 0), (0, 0)))
    summed = jnp.zeros_like(signal) + offset[None, :]
    for lag_index in range(taps):
        summed = summed + kernel[lag_index][None, :] * padded[lag_index : lag_index + length]
    return summed


def scan_heads(values, step_sizes, decays, b_rows, c_rows, skip_gain, span_rows):
    length, head_count, head_width = values.shape
    number = length // span_rows
    state_width = b_rows.shape[1]

    def advance(carry_state, pieces):
        value_blk, step_blk, decay_blk, b_blk, c_blk = pieces
        running = jnp.cumsum(decay_blk, axis=0)
        scores = jnp.dot(c_blk, b_blk.T, precision=HIGHEST)
        causal = lax.broadcasted_iota(jnp.int32, (span_rows, span_rows), 0) >= lax.broadcasted_iota(
            jnp.int32, (span_rows, span_rows), 1
        )
        spread = running[:, None, :] - running[None, :, :]
        factor = jnp.where(
            causal[:, :, None], jnp.exp(jnp.where(causal[:, :, None], spread, 0.0)), 0.0
        )
        mixing = scores[:, :, None] * factor * step_blk[None, :, :]
        output = jnp.einsum("tsh,shp->thp", mixing, value_blk, precision=HIGHEST)
        carried = jnp.einsum("tn,nhp->thp", c_blk, carry_state, precision=HIGHEST)
        output = (
            output + jnp.exp(running)[:, :, None] * carried + skip_gain[None, :, None] * value_blk
        )
        tail_weight = jnp.exp(running[-1][None, :] - running) * step_blk
        update = jnp.einsum(
            "sn,shp->nhp", b_blk, value_blk * tail_weight[:, :, None], precision=HIGHEST
        )
        carry_state = jnp.exp(running[-1])[None, :, None] * carry_state + update
        return (carry_state, output)

    pieces = (
        values.reshape(number, span_rows, head_count, head_width),
        step_sizes.reshape(number, span_rows, head_count),
        decays.reshape(number, span_rows, head_count),
        b_rows.reshape(number, span_rows, state_width),
        c_rows.reshape(number, span_rows, state_width),
    )
    initial = jnp.zeros((state_width, head_count, head_width), jnp.float32)
    final_state, outputs = lax.scan(jax.checkpoint(advance), initial, pieces)
    return outputs.reshape(length, head_count * head_width)


def mixer_core(
    projected,
    value_conv,
    value_shift,
    state_conv,
    state_shift,
    step_bias,
    log_rate,
    skip_gain,
    span_rows,
):
    inner_width = value_conv.shape[1]
    state_width = state_conv.shape[1] // 2
    head_count = step_bias.shape[0]
    length = projected.shape[0]
    gate_part = projected[:, :inner_width]
    value_pre = projected[:, inner_width : 2 * inner_width]
    state_pre = projected[:, 2 * inner_width : 2 * inner_width + 2 * state_width]
    step_raw = projected[:, 2 * inner_width + 2 * state_width :]
    values = jax.nn.silu(causal_conv(value_pre, value_conv, value_shift))
    states = jax.nn.silu(causal_conv(state_pre, state_conv, state_shift))
    step_sizes = jax.nn.softplus(step_raw + step_bias[None, :])
    decays = -jnp.exp(log_rate)[None, :] * step_sizes
    scanned = scan_heads(
        values.reshape(length, head_count, inner_width // head_count),
        step_sizes,
        decays,
        states[:, :state_width],
        states[:, state_width:],
        skip_gain,
        span_rows,
    )
    return scanned * jax.nn.silu(gate_part)


def local_core(
    projected, value_conv, value_shift, state_conv, state_shift, step_bias, log_rate, skip_gain
):
    return mixer_core(
        projected,
        value_conv,
        value_shift,
        state_conv,
        state_shift,
        step_bias,
        log_rate,
        skip_gain,
        GROUP,
    )


def per_device(
    residual_in,
    norm_gain,
    gate_proj,
    value_proj,
    state_proj,
    step_proj,
    value_conv,
    value_shift,
    state_conv,
    state_shift,
    step_bias,
    log_rate,
    skip_gain,
    gated_gain,
    out_proj,
    grad_out,
):
    rows_here = residual_in.shape[1]
    model_width = residual_in.shape[2]
    inner_local = value_conv.shape[1]
    inner_all = inner_local * lax.axis_size("heads")
    state_begin = 2 * inner_local
    state_end = state_begin + state_proj.shape[1]
    residual_rows = residual_in[0].astype(jnp.float32)
    scale_in = lax.rsqrt(jnp.mean(residual_rows * residual_rows, axis=-1, keepdims=True) + EPSILON)
    gain_in = norm_gain.astype(jnp.float32)[None, :]
    normed_rows = (residual_rows * scale_in * gain_in).astype(jnp.bfloat16)
    weights = jnp.concatenate([gate_proj, value_proj, state_proj, step_proj], axis=1)
    normed_all = lax.all_gather(normed_rows, "heads", axis=0, tiled=True)
    projected = jnp.dot(normed_all, weights, preferred_element_type=jnp.float32)
    gated, pull_core = jax.vjp(
        local_core,
        projected,
        value_conv.astype(jnp.float32),
        value_shift.astype(jnp.float32),
        state_conv.astype(jnp.float32),
        state_shift.astype(jnp.float32),
        step_bias,
        log_rate,
        skip_gain,
    )
    squares = lax.psum(jnp.sum(gated * gated, axis=1), "heads")
    scale_out = lax.rsqrt(squares / inner_all + EPSILON)[:, None]
    gain_out = gated_gain.astype(jnp.float32)[None, :]
    normed_out = (gated * scale_out * gain_out).astype(jnp.bfloat16)
    picked = normed_out
    branch = lax.psum_scatter(
        jnp.dot(picked, out_proj, preferred_element_type=jnp.float32),
        "heads",
        scatter_dimension=0,
        tiled=True,
    )
    mixed = residual_rows + branch
    cot_rows = grad_out[0]
    piece = lax.all_gather(cot_rows, "heads", axis=0, tiled=True)
    picked = normed_out
    weight_grad = lax.dot_general(
        picked, piece, (((0,), (0,)), ((), ())), preferred_element_type=jnp.float32
    )
    block_grad = lax.dot_general(
        piece, out_proj, (((1,), (1,)), ((), ())), preferred_element_type=jnp.float32
    )
    grad_out_proj = weight_grad
    grad_gated_gain = jnp.sum(block_grad * gated * scale_out, axis=0)
    row_dots_sum = lax.psum(jnp.sum(block_grad * gain_out * gated, axis=1), "heads")
    gated_grad = (
        gain_out * scale_out * block_grad
        - gated * (scale_out * scale_out * scale_out) * row_dots_sum[:, None] / inner_all
    )
    (
        proj_grad,
        grad_vconv,
        grad_vshift,
        grad_sconv,
        grad_sshift,
        grad_sbias,
        grad_rate,
        grad_skip,
    ) = pull_core(gated_grad)
    state_grad, grad_sconv, grad_sshift = lax.psum(
        (proj_grad[:, state_begin:state_end], grad_sconv, grad_sshift), "heads"
    )
    proj_low = jnp.concatenate(
        [proj_grad[:, :state_begin], state_grad, proj_grad[:, state_end:]], axis=1
    ).astype(jnp.bfloat16)
    grad_weights = lax.dot_general(
        normed_all, proj_low, (((0,), (0,)), ((), ())), preferred_element_type=jnp.float32
    )
    picked = proj_low
    front = lax.dot_general(
        picked[:, :state_begin],
        weights[:, :state_begin],
        (((1,), (1,)), ((), ())),
        preferred_element_type=jnp.float32,
    )
    back_part = lax.dot_general(
        picked[:, state_end:],
        weights[:, state_end:],
        (((1,), (1,)), ((), ())),
        preferred_element_type=jnp.float32,
    )
    normed_grad = lax.psum_scatter(front + back_part, "heads", scatter_dimension=0, tiled=True)
    own_start = lax.axis_index("heads") * rows_here
    own_state = lax.dynamic_slice_in_dim(
        proj_low[:, state_begin:state_end], own_start, rows_here, 0
    )
    normed_grad = normed_grad + lax.dot_general(
        own_state, state_proj, (((1,), (1,)), ((), ())), preferred_element_type=jnp.float32
    )
    grad_norm_part = jnp.sum(normed_grad * residual_rows * scale_in, axis=0)
    inner_dot = jnp.sum(normed_grad * gain_in * residual_rows, axis=1, keepdims=True)
    grad_input = (
        cot_rows.astype(jnp.float32)
        + gain_in * scale_in * normed_grad
        - residual_rows * (scale_in * scale_in * scale_in) * inner_dot / model_width
    )
    (
        grad_weights,
        grad_vconv,
        grad_vshift,
        grad_sconv,
        grad_sshift,
        grad_sbias,
        grad_rate,
        grad_skip,
        grad_gated_gain,
        grad_out_proj,
    ) = lax.psum(
        (
            grad_weights,
            grad_vconv,
            grad_vshift,
            grad_sconv,
            grad_sshift,
            grad_sbias,
            grad_rate,
            grad_skip,
            grad_gated_gain,
            grad_out_proj,
        ),
        "batch",
    )
    grad_norm_gain = lax.psum(grad_norm_part, ("batch", "heads"))
    return (
        mixed[None],
        grad_input[None],
        grad_norm_gain,
        grad_weights[:, :inner_local],
        grad_weights[:, inner_local:state_begin],
        grad_weights[:, state_begin:state_end],
        grad_weights[:, state_end:],
        grad_vconv,
        grad_vshift,
        grad_sconv,
        grad_sshift,
        grad_sbias,
        grad_rate,
        grad_skip,
        grad_gated_gain,
        grad_out_proj,
    )


def solution(mesh):
    return jax.shard_map(
        per_device,
        mesh=mesh,
        in_specs=(
            P("batch", "heads", None),
            P(),
            P(None, "heads"),
            P(None, "heads"),
            P(),
            P(None, "heads"),
            P(None, "heads"),
            P("heads"),
            P(),
            P(),
            P("heads"),
            P("heads"),
            P("heads"),
            P("heads"),
            P("heads", None),
            P("batch", "heads", None),
        ),
        out_specs=(
            P("batch", "heads", None),
            P("batch", "heads", None),
            P(),
            P(None, "heads"),
            P(None, "heads"),
            P(),
            P(None, "heads"),
            P(None, "heads"),
            P("heads"),
            P(),
            P(),
            P("heads"),
            P("heads"),
            P("heads"),
            P("heads"),
            P("heads", None),
        ),
        check_vma=False,
    )
```

profile of v0, /device:TPU:0, one launch (start us, length us, event | category | flops | bytes accessed | tf_op | source)
XLA Modules:
  0.0 831.4 jit_solution(84336020585082975)
XLA Ops:
  14.4 28.1 %all-gather.4.cloned.1.call-done = bf16[1024,768]{1,0:T(8,128)(2,1)} async-done(((bf16[512,768]{1,0:T(8,128)(2,1)}), bf16[1024,768]{1,0:T(8,128)(2,1)}) %all-gather.4.cloned.1.call-update) | async-done | bytes 1572880 | tf_op jit(solution)/shard_map/all_gather | solution.py:144
  56.3 10.9 %fusion.91 = (f32[1024,768]{0,1:T(8,128)}, f32[1024,768]{0,1:T(8,128)}) fusion(f32[1024,768]{0,1:T(8,128)} %slice.209, f32[768]{0:T(1024)S(1)} %get-tuple-element.760, f32[768]{0:T(1024)S(1)} %get-tuple-element.761, f32[768]{0:T(1024)S(1)} %get-tuple-element.762, f32[768]{0:T(1024)S(1)} %get-tuple-element.759, f32[768]{0:T(1024)S(1)} %convert_element_type.44), kind=kLoop, calls=%fused_computation.150 | loop fusion | flops 9437184 | bytes 9452544 | tf_op jit(solution)/shard_map/jvp(jit(silu))/mul | solution.py:83
  80.7 120.0 %while.46 = (s32[]{:T(128)}, f32[128,12,64]{0,2,1:T(8,128)S(1)}, f32[4,256,12,64]{1,0,3,2:T(4,128)}, f32[4,128,12,64]{1,3,2,0:T(8,128)}, f32[4,256,12]{1,2,0:T(8...) while((s32[]{:T(128)}, f32[128,12,64]{0,2,1:T(8,128)S(1)}, ...), condition=%wide.region_4.5_spmd.clone.clone, body=%wide.region_1.4_spmd.clone.clone.sunk | while | flops 1314232320 | bytes 14049443 | solution.py:60
  90.6 17.9 %dynamic_update_slice.86 = f32[4,256,12,64]{1,0,3,2:T(4,128)} dynamic-update-slice(f32[4,256,12,64]{1,0,3,2:T(4,128)} %get-tuple-element.1137, f32[1,256,12,64]{1,0,3,2:T(1,128)S(1)} %copy.214, s32[]{:T(128)} %get-tuple-element.1135, s32[]{:T(128)} %constant.133.clone.1..sunk.1, s32[]{:T(128)} %constant.133.clone.1..sunk.1, s32[]{:T(128)} %constant.133.clone.1..sunk.1) | dynamic-update-slice | bytes 1572868 | tf_op jit(solution)/shard_map/jvp()/while/body/jit(dynamic_update_index_in_dim)/dynamic_update_slice | solution.py:60
  120.7 17.9 %dynamic_update_slice.86 = f32[4,256,12,64]{1,0,3,2:T(4,128)} dynamic-update-slice(f32[4,256,12,64]{1,0,3,2:T(4,128)} %get-tuple-element.1137, f32[1,256,12,64]{1,0,3,2:T(1,128)S(1)} %copy.214, s32[]{:T(128)} %get-tuple-element.1135, s32[]{:T(128)} %constant.133.clone.1..sunk.1, s32[]{:T(128)} %constant.133.clone.1..sunk.1, s32[]{:T(128)} %constant.133.clone.1..sunk.1) | dynamic-update-slice | bytes 1572868 | tf_op jit(solution)/shard_map/jvp()/while/body/jit(dynamic_update_index_in_dim)/dynamic_update_slice | solution.py:60
  150.7 17.9 %dynamic_update_slice.86 = f32[4,256,12,64]{1,0,3,2:T(4,128)} dynamic-update-slice(f32[4,256,12,64]{1,0,3,2:T(4,128)} %get-tuple-element.1137, f32[1,256,12,64]{1,0,3,2:T(1,128)S(1)} %copy.214, s32[]{:T(128)} %get-tuple-element.1135, s32[]{:T(128)} %constant.133.clone.1..sunk.1, s32[]{:T(128)} %constant.133.clone.1..sunk.1, s32[]{:T(128)} %constant.133.clone.1..sunk.1) | dynamic-update-slice | bytes 1572868 | tf_op jit(solution)/shard_map/jvp()/while/body/jit(dynamic_update_index_in_dim)/dynamic_update_slice | solution.py:60
  180.7 17.9 %dynamic_update_slice.86 = f32[4,256,12,64]{1,0,3,2:T(4,128)} dynamic-update-slice(f32[4,256,12,64]{1,0,3,2:T(4,128)} %get-tuple-element.1137, f32[1,256,12,64]{1,0,3,2:T(1,128)S(1)} %copy.214, s32[]{:T(128)} %get-tuple-element.1135, s32[]{:T(128)} %constant.133.clone.1..sunk.1, s32[]{:T(128)} %constant.133.clone.1..sunk.1, s32[]{:T(128)} %constant.133.clone.1..sunk.1) | dynamic-update-slice | bytes 1572868 | tf_op jit(solution)/shard_map/jvp()/while/body/jit(dynamic_update_index_in_dim)/dynamic_update_slice | solution.py:60
  203.3 6.0 multiply_reduce_fusion.11
  214.2 6.2 multiply_reduce_fusion.5
  225.3 7.6 fusion.119
  243.3 247.7 %while.45 = (s32[]{:T(128)}, f32[12]{0:T(128)}, f32[128,12,64]{0,2,1:T(8,128)}, f32[4,256,12,64]{1,0,3,2:T(4,128)}, f32[4,256,12]{1,0,2:T(4,128)}, /*index=5*/f3...) while((s32[]{:T(128)}, f32[12]{0:T(128)}, ...), condition=%wide.region_24.25_spmd.clone, body=%wide.region_10.24_spmd.clone.sunk | while | flops 3039361024 | bytes 43319236 | solution.py:60
  261.7 5.7 fusion.238
  284.6 17.9 %dynamic_update_slice.82 = f32[4,256,12,64]{1,0,3,2:T(4,128)} dynamic-update-slice(f32[4,256,12,64]{1,0,3,2:T(4,128)} %get-tuple-element.1186, f32[1,256,12,64]{1,0,3,2:T(1,128)S(1)} %copy.203, s32[]{:T(128)S(6)} %sub.299, s32[]{:T(128)} %constant.133.clone.1..sunk, s32[]{:T(128)} %constant.133.clone.1..sunk, s32[]{:T(128)} %constant.133.clone.1..sunk) | dynamic-update-slice | bytes 1572868 | tf_op jit(solution)/shard_map/transpose(jvp())/while/body/jit(dynamic_update_index_in_dim)/dynamic_update_slice | solution.py:60
  323.7 5.7 fusion.238
  346.7 17.9 %dynamic_update_slice.82 = f32[4,256,12,64]{1,0,3,2:T(4,128)} dynamic-update-slice(f32[4,256,12,64]{1,0,3,2:T(4,128)} %get-tuple-element.1186, f32[1,256,12,64]{1,0,3,2:T(1,128)S(1)} %copy.203, s32[]{:T(128)S(6)} %sub.299, s32[]{:T(128)} %constant.133.clone.1..sunk, s32[]{:T(128)} %constant.133.clone.1..sunk, s32[]{:T(128)} %constant.133.clone.1..sunk) | dynamic-update-slice | bytes 1572868 | tf_op jit(solution)/shard_map/transpose(jvp())/while/body/jit(dynamic_update_index_in_dim)/dynamic_update_slice | solution.py:60
  408.7 17.9 %dynamic_update_slice.82 = f32[4,256,12,64]{1,0,3,2:T(4,128)} dynamic-update-slice(f32[4,256,12,64]{1,0,3,2:T(4,128)} %get-tuple-element.1186, f32[1,256,12,64]{1,0,3,2:T(1,128)S(1)} %copy.203, s32[]{:T(128)S(6)} %sub.299, s32[]{:T(128)} %constant.133.clone.1..sunk, s32[]{:T(128)} %constant.133.clone.1..sunk, s32[]{:T(128)} %constant.133.clone.1..sunk) | dynamic-update-slice | bytes 1572868 | tf_op jit(solution)/shard_map/transpose(jvp())/while/body/jit(dynamic_update_index_in_dim)/dynamic_update_slice | solution.py:60
  447.8 5.7 fusion.238
  470.8 17.9 %dynamic_update_slice.82 = f32[4,256,12,64]{1,0,3,2:T(4,128)} dynamic-update-slice(f32[4,256,12,64]{1,0,3,2:T(4,128)} %get-tuple-element.1186, f32[1,256,12,64]{1,0,3,2:T(1,128)S(1)} %copy.203, s32[]{:T(128)S(6)} %sub.299, s32[]{:T(128)} %constant.133.clone.1..sunk, s32[]{:T(128)} %constant.133.clone.1..sunk, s32[]{:T(128)} %constant.133.clone.1..sunk) | dynamic-update-slice | bytes 1572868 | tf_op jit(solution)/shard_map/transpose(jvp())/while/body/jit(dynamic_update_index_in_dim)/dynamic_update_slice | solution.py:60
  523.9 25.7 %all-reduce.33 = (bf16[1024,256]{0,1:T(8,128)(2,1)S(1)}, f32[4,256]{1,0:T(4,128)S(1)}, f32[256]{0:T(256)S(1)}) all-reduce(f32[1024,256]{0,1:T(8,128)S(1)} %slice.217, f32[4,256]{1,0:T(4,128)S(1)} %pad_add_fusion.8, f32[256]{0:T(256)S(1)} %get-tuple-element.757), channel_id=1, replica_groups=mesh['batch'=16,'heads'=2] {'heads'}, use_global_device_ids=true, to_apply=%region_26.27 | all-reduce | flops 263424 | bytes 1583104 | tf_op jit(solution)/shard_map/psum | solution.py:195
  555.1 7.5 fusion.80
  577.7 61.3 %all-reduce.26 = (f32[4,768]{1,0:T(4,128)}, f32[768]{0:T(1024)}, f32[4,256]{1,0:T(4,128)}, f32[256]{0:T(256)}, f32[12]{0:T(128)}, /*index=5*/f32[12]{0:T(128)}, f32[12]{0:T(128)}, f32[768]{0:T(1024)}) all-reduce(f32[4,768]{1,0:T(4,128)S(1)} %pad_add_fusion.7, ...), channel_id=1, replica_groups=mesh['batch'=16,'heads'=2] {'batch'}, use_global_device_ids=true, to_apply=%region_35.36 | all-reduce | flops 5924 | bytes 47392 | tf_op jit(solution)/shard_map/psum | solution.py:243
  639.1 88.1 %all-reduce.32.cloned.1.call-done = (f32[768,1804]{0,1:T(8,128)}, f32[768,768]{1,0:T(8,128)}) async-done(((f32[768,1804]{0,1:T(8,128)}, f32[768,768]{1,0:T(8,128)}), (f32[768,1804]{0,1:T(8,128)}, f32[768,768]{1,0:T(8,128)})) %all-reduce.32.cloned.1.call-update) | async-done | bytes 7901200 | tf_op jit(solution)/shard_map/psum | solution.py:243
  741.0 31.5 %reduce-scatter.5.cloned.1.call-done = f32[512,768]{1,0:T(8,128)} async-done(((f32[1024,768]{1,0:T(8,128)}), f32[512,768]{1,0:T(8,128)}) %reduce-scatter.5.cloned.1.call-update) | async-done | bytes 1572880 | tf_op jit(solution)/shard_map/reduce_scatter | solution.py:217
  774.8 39.9 %psum.115 = f32[768]{0:T(1024)} all-reduce(f32[768]{0:T(1024)S(1)} %get-tuple-element.752), channel_id=1, replica_groups=mesh['batch'=16,'heads'=2] {'batch','heads'}, use_global_device_ids=true, to_apply=%region_29.30 | all-reduce | flops 768 | bytes 6144 | tf_op jit(solution)/shard_map/psum | solution.py:258
  (659 shorter events, 341.5 us)
Async XLA Ops:
  7.2 207.0 %copy-start = (bf16[768,768]{1,0:T(8,128)(2,1)S(1)}, bf16[768,768]{1,0:T(8,128)(2,1)}, u32[]{:S(2)}) copy-start(bf16[768,768]{1,0:T(8,128)(2,1)} %param.34) | copy-start | bytes 3538948
  7.3 35.2 %copy-start.32 = (bf16[768,256]{1,0:T(8,128)(2,1)S(1)}, bf16[768,256]{1,0:T(8,128)(2,1)}, u32[]{:S(2)}) copy-start(bf16[768,256]{1,0:T(8,128)(2,1)} %param.24) | copy-start | bytes 1179652
  7.3 35.2 %all-gather.4.cloned.1.call-start = ((), (), s32[]{:S(2)}) async-start(), calls=%async_computation.2 | async-start | bytes 2359296 | tf_op jit(solution)/shard_map/all_gather | solution.py:144
  12.4 201.8 %all-gather.6.cloned.1.call-start = ((), (), s32[]{:S(2)}) async-start(), calls=%async_computation.5 | async-start | bytes 2359296 | tf_op jit(solution)/shard_map/all_gather | solution.py:170
  13.2 713.9 %all-reduce.32.cloned.1.call-start = ((), (), s32[]{:S(2)}) async-start(), calls=%async_computation.6 | async-start | bytes 15826944 | tf_op jit(solution)/shard_map/psum | solution.py:243
  14.2 37.6 %copy-start.59 = (f32[1,256]{1,0:T(1,128)}, f32[1,256]{1,0:T(1,128)S(1)}, u32[]{:S(2)}) copy-start(f32[1,256]{1,0:T(1,128)S(1)} %get-tuple-element.883) | copy-start | bytes 3076
  14.2 37.6 %copy-start.61 = (f32[1,256]{1,0:T(1,128)}, f32[1,256]{1,0:T(1,128)S(1)}, u32[]{:S(2)}) copy-start(f32[1,256]{1,0:T(1,128)S(1)} %get-tuple-element.884) | copy-start | bytes 3076
  14.2 37.6 %copy-start.63 = (f32[1,256]{1,0:T(1,128)}, f32[1,256]{1,0:T(1,128)S(1)}, u32[]{:S(2)}) copy-start(f32[1,256]{1,0:T(1,128)S(1)} %get-tuple-element.885) | copy-start | bytes 3076
  14.2 37.6 %copy-start.65 = (f32[1,256]{1,0:T(1,128)}, f32[1,256]{1,0:T(1,128)S(1)}, u32[]{:S(2)}) copy-start(f32[1,256]{1,0:T(1,128)S(1)} %get-tuple-element.886) | copy-start | bytes 3076
  14.3 42.0 %copy-start.42 = (f32[768]{0:T(1024)}, f32[768]{0:T(1024)S(1)}, u32[]{:S(2)}) copy-start(f32[768]{0:T(1024)S(1)} %get-tuple-element.759) | copy-start | bytes 9220
  14.3 42.0 %copy-start.44 = (f32[768]{0:T(1024)}, f32[768]{0:T(1024)S(1)}, u32[]{:S(2)}) copy-start(f32[768]{0:T(1024)S(1)} %get-tuple-element.760) | copy-start | bytes 9220
  14.3 42.0 %copy-start.46 = (f32[768]{0:T(1024)}, f32[768]{0:T(1024)S(1)}, u32[]{:S(2)}) copy-start(f32[768]{0:T(1024)S(1)} %get-tuple-element.761) | copy-start | bytes 9220
  14.3 42.0 %copy-start.48 = (f32[768]{0:T(1024)}, f32[768]{0:T(1024)S(1)}, u32[]{:S(2)}) copy-start(f32[768]{0:T(1024)S(1)} %get-tuple-element.762) | copy-start | bytes 9220
  14.4 62.2 %copy-start.72 = (f32[12]{0:T(128)}, f32[12]{0:T(128)S(1)}, u32[]{:S(2)}) copy-start(f32[12]{0:T(128)S(1)} %exponential_negate_fusion) | copy-start | bytes 148
  14.4 210.9 %copy-start.57 = (f32[768]{0:T(1024)}, f32[768]{0:T(1024)S(1)}, u32[]{:S(2)}) copy-start(f32[768]{0:T(1024)S(1)} %convert_element_type.46) | copy-start | bytes 9220
  345.8 20.7 %copy-start.13 = (f32[4,256,128]{2,1,0:T(8,128)S(1)}, f32[4,256,128]{2,1,0:T(8,128)}, u32[]{:S(2)}) copy-start(f32[4,256,128]{2,1,0:T(8,128)} %copy-done.12) | copy-start | bytes 1572868 | tf_op jit(solution)/shard_map/transpose(jvp())/while
  407.9 20.7 %copy-start.13 = (f32[4,256,128]{2,1,0:T(8,128)S(1)}, f32[4,256,128]{2,1,0:T(8,128)}, u32[]{:S(2)}) copy-start(f32[4,256,128]{2,1,0:T(8,128)} %copy-done.12) | copy-start | bytes 1572868 | tf_op jit(solution)/shard_map/transpose(jvp())/while
  523.8 25.8 %copy-start.56 = (f32[1024]{0:T(1024)S(1)}, f32[1024]{0:T(1024)}, u32[]{:S(2)}) copy-start(f32[1024]{0:T(1024)} %copy-done.55) | copy-start | bytes 12292
  523.8 25.8 %copy-start.58 = (f32[768]{0:T(1024)S(1)}, f32[768]{0:T(1024)}, u32[]{:S(2)}) copy-start(f32[768]{0:T(1024)} %copy-done.57) | copy-start | bytes 9220
  562.7 209.8 %reduce-scatter.5.cloned.1.call-start = ((), (), s32[]{:S(2)}) async-start(), calls=%async_computation.4 | async-start | bytes 4718592 | tf_op jit(solution)/shard_map/reduce_scatter | solution.py:217
  571.9 247.3 %reduce-scatter.3.cloned.1.call-start = ((), (), s32[]{:S(2)}) async-start(), calls=%async_computation.3 | async-start | bytes 4718592 | tf_op jit(solution)/shard_map/reduce_scatter | solution.py:162
  736.6 35.8 %copy-start.9 = (bf16[1,512,768]{2,1,0:T(8,128)(2,1)S(1)}, bf16[1,512,768]{2,1,0:T(8,128)(2,1)}, u32[]{:S(2)}) copy-start(bf16[1,512,768]{2,1,0:T(8,128)(2,1)} %param.20) | copy-start | bytes 2359300
  736.6 35.8 %copy-start.39 = (f32[768]{0:T(1024)S(1)}, f32[768]{0:T(1024)}, u32[]{:S(2)}) copy-start(f32[768]{0:T(1024)} %copy-done.38) | copy-start | bytes 9220
  736.6 35.8 %copy-start.51 = (f32[512]{0:T(512)S(1)}, f32[512]{0:T(512)}, u32[]{:S(2)}) copy-start(f32[512]{0:T(512)} %copy-done.50) | copy-start | bytes 6148
  (116 other events, 771.6 us)
Sparse Core Ops, SparseCore 0:
  12.6 29.8 all-gather.3
  44.0 27.2 all-gather.5
  562.8 164.2 all-reduce.31
  729.2 43.1 reduce-scatter.4
  774.6 44.5 reduce-scatter.2
where the time goes:
time: 843 us; the launch traced here: 831 us
  local copies, waits for them, and re-layouts  273 us (32%)
  waiting for transfers between devices  153 us (18%)
  matrix products  141 us (17%)
  blocking collectives  137 us (16%)
  other arithmetic  110 us (13%)
  between operations  14.9 us (2%)
    dynamic_update_slice x32, local copies, waits for them, and re-layouts, scan_heads(): final_state, outputs = lax.scan(jax.checkpoint(advance), initial, pieces)  161 us
    psum x1, waiting for transfers between devices, per_device(): lax.psum((grad_weights, grad_vconv, grad_vshift, grad_sconv, grad_sshift,...  88.1 us
    dot_general x12, matrix products, advance(): output = jnp.einsum('tsh,shp->thp', mixing, value_blk, precision=HIGHEST)  62.3 us
    psum x1, blocking collectives, per_device(): lax.psum((grad_weights, grad_vconv, grad_vshift, grad_sconv, grad_sshift,...  61.3 us
    psum x1, blocking collectives, per_device(): grad_norm_gain = lax.psum(grad_norm_part, ('batch', 'heads'))  39.9 us
    reduce_scatter x1, waiting for transfers between devices, per_device(): lax.psum_scatter(front + back_part, 'heads', scatter_dimension=0, tiled=T...  31.5 us
    all_gather x1, waiting for transfers between devices, per_device(): normed_all = lax.all_gather(normed_rows, 'heads', axis=0, tiled=True)  28.1 us
    unnamed x142, local copies, waits for them, and re-layouts  27.3 us
  transfers between devices with their start and end apart: 5, of which 4 were waited for; matrix products, arithmetic and copies ran while one was open for 23% of the time, Pallas kernels for 0%

commit v1 on v0

v1 whole, which is shorter than its diff:
```python
import functools

import jax
import jax.numpy as jnp
from jax import lax
from jax.experimental import pallas as pl
from jax.experimental.pallas import tpu as pltpu
from jax.sharding import PartitionSpec as P

EPSILON = 1e-05
HIGHEST = lax.Precision.HIGHEST
BLOCK = 256
CHUNK = 128
LANES = 128
LOG2E = 1.4426950408889634
f32 = jnp.float32
bf16 = jnp.bfloat16


def dot(left, right, over=((1,), (0,)), precision=None):
    return lax.dot_general(
        left, right, (over, ((), ())), preferred_element_type=f32, precision=precision
    )


TN = ((0,), (0,))
NT = ((1,), (1,))


def sigmoid(v):
    return 0.5 * jnp.tanh(0.5 * v) + 0.5


def split(v):
    high = v.astype(bf16)
    return jnp.concatenate([high, (v - high.astype(f32)).astype(bf16)], axis=1)


def lower_mask(rows):
    return lax.broadcasted_iota(jnp.int32, (rows, rows), 0) >= lax.broadcasted_iota(
        jnp.int32, (rows, rows), 1
    )


def chunk_scalars(z, log_rate):
    step = jnp.maximum(z, 0.0) + jnp.log1p(jnp.exp(-jnp.abs(z)))
    rate = -jnp.exp(log_rate)
    decay = step * (rate * LOG2E)
    ones = lower_mask(CHUNK).astype(f32)
    running = dot(ones, decay, precision=HIGHEST)
    grown = jnp.exp2(running)
    tail = jnp.exp2(running[CHUNK - 1 : CHUNK, :] - running)
    return step, rate, running, grown, tail


def pair_decay(running, running_t, pair, mask):
    out = []
    for head in (2 * pair, 2 * pair + 1):
        spread = running[:, head : head + 1] - running_t[head : head + 1, :]
        out.append(jnp.exp2(jnp.where(mask, spread, -1e30)))
    return out


def half_masks():
    lane = lax.broadcasted_iota(jnp.int32, (1, LANES), 1)
    first = (lane < LANES // 2).astype(bf16)
    return first, 1 - first


def stacked(rows, masks):
    return jnp.concatenate([rows * masks[0], rows * masks[1]], axis=0)


def forward_kernel(
    half_blocks,
    at_ref,
    own_ref,
    other_ref,
    gain_ref,
    gate_w,
    value_w,
    state_w,
    step_w,
    vconv_ref,
    vshift_ref,
    sconv_ref,
    sshift_ref,
    sbias_ref,
    rate_ref,
    skip_ref,
    ggain_ref,
    out_w,
    spread_ref,
    normed_ref,
    g_ref,
    y_ref,
    gg_ref,
    av_ref,
    vp_ref,
    as_ref,
    sp_ref,
    z_ref,
    sin_ref,
    sq_ref,
    branch_ref,
    gbuf,
    vbuf,
    sbuf,
    state,
    stepx,
    grownx,
    tailx,
    carried,
    vtail,
):
    step_at = pl.program_id(0)
    pairs = vbuf.shape[1] // LANES
    nstate = state.shape[0]

    @pl.when(step_at == 0)
    def _():
        state[...] = jnp.zeros_like(state)
        vbuf[0:8, :] = jnp.zeros((8, vbuf.shape[1]), f32)
        sbuf[0:8, :] = jnp.zeros((8, sbuf.shape[1]), f32)

    mine = (step_at // half_blocks) == at_ref[0]
    rows = jnp.where(mine, own_ref[...].astype(f32), other_ref[...].astype(f32))
    scale = lax.rsqrt(jnp.mean(rows * rows, axis=1, keepdims=True) + EPSILON)
    normed = (rows * scale * gain_ref[...]).astype(bf16)
    normed_ref[...] = normed
    gbuf[...] = dot(normed, gate_w[...])
    g_ref[...] = gbuf[...]
    vbuf[8:, :] = dot(normed, value_w[...])
    vp_ref[...] = vbuf[8:, :]
    sbuf[8:, :] = dot(normed, state_w[...])
    sp_ref[...] = sbuf[8:, :]
    z_ref[...] = dot(normed, step_w[...]) + sbias_ref[...]

    mask = lower_mask(CHUNK)
    masks = half_masks()
    for chunk in range(BLOCK // CHUNK):
        r0 = chunk * CHUNK
        here = pl.ds(r0, CHUNK)
        step, _, running, grown, tail = chunk_scalars(z_ref[here, :], rate_ref[...])
        running_t = running.T
        stepx[...] = dot(split(step), spread_ref[...])
        grownx[...] = dot(split(grown), spread_ref[...])
        tailx[...] = dot(split(tail), spread_ref[...])
        conv = sshift_ref[...]
        for tap in range(4):
            conv = conv + sconv_ref[tap : tap + 1, :] * sbuf[pl.ds(r0 + 5 + tap, CHUNK), :]
        as_ref[here, :] = conv
        states_f = conv * sigmoid(conv)
        states = states_f.astype(bf16)
        b_rows, c_rows = states[:, :nstate], states[:, nstate:]
        bb, cc = split(states_f[:, :nstate]), split(states_f[:, nstate:])
        scores = dot(jnp.concatenate([cc, cc[:, :nstate]], axis=1), jnp.concatenate([bb[:, :nstate], bb[:, :nstate], bb[:, nstate:]], axis=1), NT)
        before = state[...].astype(bf16)
        sin_ref[chunk, :, :] = before
        carried[...] = dot(c_rows, before)
        squares = jnp.zeros((CHUNK, LANES), f32)
        for pair in range(pairs):
            lanes = slice(pair * LANES, (pair + 1) * LANES)
            conv = vshift_ref[:, lanes]
            for tap in range(4):
                conv = conv + vconv_ref[tap : tap + 1, lanes] * vbuf[pl.ds(r0 + 5 + tap, CHUNK), lanes]
            av_ref[here, lanes] = conv
            values = conv * sigmoid(conv)
            stepped = values * stepx[:, lanes]
            vtail[:, lanes] = (stepped * tailx[:, lanes]).astype(bf16)
            first, second = pair_decay(running, running_t, pair, mask)
            mixing = jnp.concatenate(
                [(scores * first).astype(bf16), (scores * second).astype(bf16)], axis=1
            )
            scanned = dot(mixing, stacked(stepped.astype(bf16), masks))
            scanned = scanned + grownx[:, lanes] * carried[:, lanes] + skip_ref[:, lanes] * values
            y_ref[here, lanes] = scanned
            g = gbuf[here, lanes]
            gated = scanned * (g * sigmoid(g))
            gg_ref[here, lanes] = (gated * ggain_ref[:, lanes]).astype(bf16)
            squares = squares + gated * gated
        sq_ref[:, here] = dot(jnp.ones((8, LANES), f32), squares, NT, HIGHEST)
        state[...] = grownx[CHUNK - 1 : CHUNK, :] * state[...] + dot(b_rows, vtail[...], TN)
    branch_ref[...] = dot(gg_ref[...], out_w[...]).astype(bf16)
    vbuf[0:8, :] = vbuf[BLOCK : BLOCK + 8, :]
    sbuf[0:8, :] = sbuf[BLOCK : BLOCK + 8, :]


def stats_kernel(half_blocks, at_ref, own_ref, other_ref, gg_ref, sq_ref, out_w, og_ref, stats_ref):
    mine = (pl.program_id(0) // half_blocks) == at_ref[0]
    cot = jnp.where(mine, own_ref[...], other_ref[...])
    og = dot(cot, out_w[...], NT)
    og_ref[...] = og
    prod = (og * gg_ref[...].astype(f32)).astype(bf16)
    dots = dot(jnp.ones((8, prod.shape[1]), bf16), prod, NT)
    row = lax.broadcasted_iota(jnp.int32, dots.shape, 0)
    stats_ref[...] = jnp.where(row == 0, sq_ref[...], dots)


def gate_kernel(
    half_blocks,
    inner_all,
    at_ref,
    own_ref,
    other_ref,
    here_ref,
    there_ref,
    normed_ref,
    og_ref,
    y_ref,
    g_ref,
    gg_ref,
    ggain_ref,
    dg_ref,
    dy_ref,
    grad_out_ref,
    grad_gate_ref,
    grad_gain_ref,
):
    step_at = pl.program_id(0)
    pairs = og_ref.shape[1] // LANES

    @pl.when(step_at == 0)
    def _():
        grad_out_ref[...] = jnp.zeros_like(grad_out_ref)
        grad_gate_ref[...] = jnp.zeros_like(grad_gate_ref)
        grad_gain_ref[...] = jnp.zeros_like(grad_gain_ref)

    sums = here_ref[...] + there_ref[...]
    scale_row = lax.rsqrt(sums[0:1, :] / inner_all + EPSILON)
    pull_row = scale_row * scale_row * scale_row * sums[1:2, :] / inner_all
    columns = jnp.concatenate(
        [scale_row, pull_row, jnp.zeros((LANES - 2, BLOCK), f32)], axis=0
    ).T
    scale, pull = columns[:, 0:1], columns[:, 1:2]
    mine = (step_at // half_blocks) == at_ref[0]
    cot = jnp.where(mine, own_ref[...], other_ref[...]).astype(f32)
    scaled = (cot * scale).astype(bf16)
    for pair in range(pairs):
        lanes = slice(pair * LANES, (pair + 1) * LANES)
        og = og_ref[:, lanes].astype(f32) * scale
        y = y_ref[:, lanes].astype(f32)
        g = g_ref[:, lanes].astype(f32)
        sig = sigmoid(g)
        silu = g * sig
        gated = y * silu
        grad_gain_ref[0:1, lanes] += jnp.sum(og * gated, axis=0, keepdims=True)
        gated_grad = ggain_ref[:, lanes] * og - gated * pull
        dy_ref[:, lanes] = (gated_grad * silu).astype(bf16)
        dg_ref[:, lanes] = (gated_grad * y * (sig + silu * (1.0 - sig))).astype(bf16)
    grad_out_ref[...] += dot(gg_ref[...], scaled, TN)
    grad_gate_ref[...] += dot(normed_ref[...], dg_ref[...], TN)


def backward_kernel(
    at_ref,
    normed_ref,
    dg_ref,
    dy_ref,
    av_ref,
    vp_ref,
    as_ref,
    sp_ref,
    z_ref,
    sin_ref,
    gate_w,
    value_w,
    state_w,
    step_w,
    vconv_ref,
    sconv_ref,
    rate_ref,
    skip_ref,
    spread_ref,
    gather_ref,
    ng_ref,
    grad_value_ref,
    grad_state_ref,
    grad_step_ref,
    grad_vconv_ref,
    grad_sconv_ref,
    grad_head_ref,
    dabuf,
    dsbuf,
    dstate,
    stepx,
    grownx,
    tailx,
    carried,
    pulled,
    ubuf,
    vtail,
    dvalue,
    dstates,
    dstep,
):
    step_at = pl.program_id(0)
    width = dabuf.shape[1]
    pairs = width // LANES
    nstate = dstate.shape[0]

    @pl.when(step_at == 0)
    def _():
        dstate[...] = jnp.zeros_like(dstate)
        dabuf[BLOCK:, :] = jnp.zeros((8, width), f32)
        dsbuf[BLOCK:, :] = jnp.zeros((8, dsbuf.shape[1]), f32)
        for ref in (
            grad_value_ref,
            grad_state_ref,
            grad_step_ref,
            grad_vconv_ref,
            grad_sconv_ref,
            grad_head_ref,
        ):
            ref[...] = jnp.zeros_like(ref)

    @pl.when(step_at > 0)
    def _():
        dabuf[BLOCK:, :] = dabuf[0:8, :]
        dsbuf[BLOCK:, :] = dsbuf[0:8, :]

    mask = lower_mask(CHUNK)
    later = jnp.logical_not(mask).astype(f32)
    masks = half_masks()
    for chunk in reversed(range(BLOCK // CHUNK)):
        r0 = chunk * CHUNK
        here = pl.ds(r0, CHUNK)
        z = z_ref[here, :]
        step, rate, running, grown, tail = chunk_scalars(z, rate_ref[...])
        running_t = running.T
        stepx[...] = dot(split(step), spread_ref[...])
        grownx[...] = dot(split(grown), spread_ref[...])
        tailx[...] = dot(split(tail), spread_ref[...])
        conv_s = as_ref[here, :]
        sig_s = sigmoid(conv_s)
        states_f = conv_s * sig_s
        states = states_f.astype(bf16)
        b_rows, c_rows = states[:, :nstate], states[:, nstate:]
        bb, cc = split(states_f[:, :nstate]), split(states_f[:, nstate:])
        scores = dot(jnp.concatenate([cc, cc[:, :nstate]], axis=1), jnp.concatenate([bb[:, :nstate], bb[:, :nstate], bb[:, nstate:]], axis=1), NT)
        before = sin_ref[chunk, :, :]
        after = dstate[...].astype(bf16)
        carried[...] = dot(c_rows, before)
        pulled[...] = dot(b_rows, after)
        dscores = jnp.zeros((CHUNK, CHUNK), f32)
        inner = jnp.zeros((CHUNK, LANES), f32)
        outer = jnp.zeros((CHUNK, LANES), f32)
        sides = jnp.zeros((CHUNK, LANES), f32)
        for pair in range(pairs):
            lanes = slice(pair * LANES, (pair + 1) * LANES)
            conv = av_ref[here, lanes].astype(f32)
            sig = sigmoid(conv)
            values = conv * sig
            steps = stepx[:, lanes]
            stepped = values * steps
            low = stepped.astype(bf16)
            dy_low = dy_ref[here, lanes]
            dy = dy_low.astype(f32)
            first, second = pair_decay(running, running_t, pair, mask)
            mixing = jnp.concatenate(
                [(scores * first).astype(bf16), (scores * second).astype(bf16)], axis=1
            )
            dy_two = stacked(dy_low, masks)
            scanned = dot(mixing, stacked(low, masks))
            both = jnp.concatenate([mixing[:, :CHUNK], mixing[:, CHUNK:]], axis=0)
            dstepped = dot(both, dy_two, TN)
            dmixing = dot(dy_two, low, NT)
            dscores = dscores + dmixing[:CHUNK] * first + dmixing[CHUNK:] * second
            inside = dy * scanned - low.astype(f32) * dstepped
            u = (dy * grownx[:, lanes]).astype(bf16)
            ubuf[:, lanes] = u
            tails = tailx[:, lanes]
            v = (stepped * tails).astype(bf16)
            vtail[:, lanes] = v
            pull = pulled[:, lanes]
            dstepped = dstepped + tails * pull
            sums = gather_ref[pair * 2 * LANES : (pair + 1) * 2 * LANES, :]
            inner = inner + dot(split(inside), sums[:, :LANES])
            outer = outer + dot(
                jnp.concatenate(
                    [
                        (u.astype(f32) * carried[:, lanes]).astype(bf16),
                        (v.astype(f32) * pull).astype(bf16),
                    ],
                    axis=1,
                ),
                sums[:, LANES:],
            )
            sides = sides + dot(
                jnp.concatenate(
                    [(values * dstepped).astype(bf16), (values * dy).astype(bf16)], axis=1
                ),
                sums[:, LANES:],
            )
            dvalues = steps * dstepped + skip_ref[:, lanes] * dy
            da = dvalues * (sig + values * (1.0 - sig))
            dabuf[here, lanes] = da
            vp = vp_ref[here, lanes].astype(f32)
            dv = jnp.zeros((CHUNK, LANES), f32)
            rows = []
            for tap in range(4):
                moved = da if tap == 3 else dabuf[pl.ds(r0 + 3 - tap, CHUNK), lanes]
                dv = dv + vconv_ref[tap : tap + 1, lanes] * moved
                rows.append(jnp.sum(vp * moved, axis=0, keepdims=True))
            rows.append(jnp.sum(da, axis=0, keepdims=True))
            rows.append(jnp.zeros((3, LANES), f32))
            grad_vconv_ref[:, lanes] += jnp.concatenate(rows, axis=0)
            dvalue[here, lanes] = dv.astype(bf16)
        dlow = dscores.astype(bf16)
        drest = (dscores - dlow.astype(f32)).astype(bf16)
        db = dot(dlow, cc[:, :nstate], TN) + dot(dlow, cc[:, nstate:], TN)+ dot(drest, c_rows, TN) + dot(vtail[...], after, NT)
        dc = dot(dlow, b_rows) + dot(drest, b_rows) + dot(dlow, bb[:, nstate:]) + dot(ubuf[...], before, NT)
        ds = jnp.concatenate([db, dc], axis=1) * (sig_s + conv_s * sig_s * (1.0 - sig_s))
        dsbuf[here, :] = ds
        sp = sp_ref[here, :]
        dpre = jnp.zeros(ds.shape, f32)
        rows = []
        for tap in range(4):
            moved = ds if tap == 3 else dsbuf[pl.ds(r0 + 3 - tap, CHUNK), :]
            dpre = dpre + sconv_ref[tap : tap + 1, :] * moved
            rows.append(jnp.sum(sp * moved, axis=0, keepdims=True))
        rows.append(jnp.sum(ds, axis=0, keepdims=True))
        rows.append(jnp.zeros((3, ds.shape[1]), f32))
        grad_sconv_ref[...] += jnp.concatenate(rows, axis=0)
        dstates[here, :] = dpre.astype(bf16)

        overlap = jnp.sum(before.astype(f32) * dstate[...], axis=0, keepdims=True)
        overlap = jnp.broadcast_to(overlap * grownx[CHUNK - 1 : CHUNK, :], (8, width))
        held = jnp.zeros((8, LANES), f32)
        for pair in range(pairs):
            lanes = slice(pair * LANES, (pair + 1) * LANES)
            sums = gather_ref[pair * 2 * LANES : (pair + 1) * 2 * LANES, :]
            held = held + dot(split(overlap[:, lanes]), sums[:, :LANES])
        half = LANES // 2
        spare = jnp.zeros((CHUNK, half), f32)
        ddecay = (
            dot(mask.astype(f32), inner + jnp.concatenate([outer[:, :half], spare], axis=1), TN, HIGHEST)
            + dot(1.0 - mask.astype(f32).T, jnp.concatenate([outer[:, half:], spare], axis=1), precision=HIGHEST)
            + held[0:1, :]
        )
        dstep_all = jnp.concatenate([sides[:, :half], spare], axis=1) + ddecay * rate
        dz = dstep_all * sigmoid(z)
        dstep[here, :] = dz.astype(bf16)
        skips = jnp.concatenate([sides[:, half:], spare], axis=1)
        grad_head_ref[...] += jnp.concatenate(
            [
                jnp.sum(dz, axis=0, keepdims=True),
                jnp.sum(ddecay * step, axis=0, keepdims=True) * rate,
                jnp.sum(skips, axis=0, keepdims=True),
                jnp.zeros((5, LANES), f32),
            ],
            axis=0,
        )
        dstate[...] = grownx[CHUNK - 1 : CHUNK, :] * dstate[...] + dot(c_rows, ubuf[...], TN)

    normed = normed_ref[...]
    grad_value_ref[...] += dot(normed, dvalue[...], TN)
    grad_state_ref[...] += dot(normed, dstates[...], TN)
    grad_step_ref[...] += dot(normed, dstep[...], TN)
    ng_ref[...] = (
        dot(dg_ref[...], gate_w[...], NT)
        + dot(dvalue[...], value_w[...], NT)
        + dot(dstates[...], state_w[...], NT)
        + dot(dstep[...], step_w[...], NT)
    ).astype(ng_ref.dtype)


def whole(array):
    return pl.BlockSpec(array.shape, lambda i, at: (0,) * array.ndim)


def call(kernel, blocks, at, ins, outs, scratch):
    return pl.pallas_call(
        kernel,
        grid_spec=pltpu.PrefetchScalarGridSpec(
            num_scalar_prefetch=1,
            grid=(blocks,),
            in_specs=[whole(a) if s is None else s for a, s in ins],
            out_specs=[s for _, _, s in outs],
            scratch_shapes=scratch,
        ),
        out_shape=[jax.ShapeDtypeStruct(shape, dtype) for shape, dtype, _ in outs],
        compiler_params=pltpu.CompilerParams(
            dimension_semantics=("arbitrary",), vmem_limit_bytes=56 * 2**20
        ),
    )(at, *[a for a, _ in ins])


def per_device(
    residual_in,
    norm_gain,
    gate_proj,
    value_proj,
    state_proj,
    step_proj,
    value_conv,
    value_shift,
    state_conv,
    state_shift,
    step_bias,
    log_rate,
    skip_gain,
    gated_gain,
    out_proj,
    grad_out,
):
    parts = lax.axis_size("heads")
    two = parts == 2
    rows_here, model = residual_in.shape[1:]
    length = rows_here * parts
    inner = value_conv.shape[1]
    inner_all = inner * parts
    heads = step_bias.shape[0]
    head_width = inner // heads
    pad_heads = heads % 2
    nheads = heads + pad_heads
    width = nheads * head_width
    nstate2 = state_conv.shape[1]
    blocks = length // BLOCK
    chunks = BLOCK // CHUNK
    half_blocks = rows_here // BLOCK if two else blocks

    def wide(a, axis):
        pads = [(0, 0)] * a.ndim
        pads[axis] = (0, width - inner)
        return jnp.pad(a, pads) if width > inner else a

    def lanes_of(a):
        return jnp.pad(a, [(0, 0)] * (a.ndim - 1) + [(0, LANES - a.shape[-1])])

    residual = residual_in[0]
    cot = grad_out[0]
    if two:
        swap = [(0, 1), (1, 0)]
        at = lax.axis_index("heads").astype(jnp.int32).reshape(1)
        pair_of = lambda a: (a, lax.ppermute(a, "heads", swap))
        add_other = lambda a: lax.ppermute(a, "heads", swap)
    else:
        at = jnp.zeros((1,), jnp.int32)

        def pair_of(a):
            full = lax.all_gather(a, "heads", axis=0, tiled=True)
            return (full, full)

        add_other = lambda a: lax.psum(a, "heads") - a

    own_rows, other_rows = pair_of(residual)
    own_cot, other_cot = pair_of(cot)

    gate_w, value_w = wide(gate_proj, 1), wide(value_proj, 1)
    out_w = wide(out_proj, 0)
    step_w = lanes_of(step_proj)
    gain_in = norm_gain.astype(f32)[None, :]
    vconv = wide(value_conv.astype(f32), 1)
    vshift = wide(value_shift.astype(f32)[None, :], 1)
    sconv = state_conv.astype(f32)
    sshift = state_shift.astype(f32)[None, :]
    sbias, rate = lanes_of(step_bias[None, :]), lanes_of(log_rate[None, :])
    skipx = wide(jnp.repeat(skip_gain, head_width)[None, :], 1)
    ggain = wide(gated_gain.astype(f32)[None, :], 1)
    head_of = jnp.arange(width) // head_width
    spread = (jnp.arange(LANES)[:, None] == head_of[None, :]).astype(bf16)
    spread = jnp.concatenate([spread, spread], axis=0)
    half = LANES // 2
    first = head_of.reshape(-1, 1, LANES, 1)
    column = jnp.arange(2 * LANES)
    top = (column == first) | (column == first + LANES)
    bottom = (column == first) | (column == first + LANES + half)
    gather = jnp.concatenate([top, bottom], axis=1).reshape(-1, 2 * LANES).astype(bf16)

    if two:

        def own_block(i, a):
            return (jnp.clip(i - a[0] * half_blocks, 0, half_blocks - 1), 0)

        def other_block(i, a):
            return (jnp.clip(i - (1 - a[0]) * half_blocks, 0, half_blocks - 1), 0)

        def turned(i, a):
            return (lax.rem(i + a[0] * half_blocks, blocks), 0)

    else:
        own_block = other_block = turned = lambda i, a: (i, 0)

    def rows(n, index=lambda i, a: (i, 0)):
        return pl.BlockSpec((BLOCK, n), index)

    def back(index):
        return lambda i, a: index(blocks - 1 - i, a)

    along = pl.BlockSpec((8, BLOCK), lambda i, a: (0, i))
    fixed = lambda *shape: pl.BlockSpec(shape, lambda i, a: (0,) * len(shape))
    states_spec = lambda index: pl.BlockSpec((chunks, nstate2 // 2, width), index)
    big = lambda *shape: pltpu.VMEM(shape, f32)
    low = lambda *shape: pltpu.VMEM(shape, bf16)

    normed, g, y, gg, av, vp, conv_s, sp, z, sin, sq, branch = call(
        functools.partial(forward_kernel, half_blocks),
        blocks,
        at,
        [
            (own_rows, rows(model, own_block)),
            (other_rows, rows(model, other_block)),
            (gain_in, None),
            (gate_w, None),
            (value_w, None),
            (state_proj, None),
            (step_w, None),
            (vconv, None),
            (vshift, None),
            (sconv, None),
            (sshift, None),
            (sbias, None),
            (rate, None),
            (skipx, None),
            (ggain, None),
            (out_w, None),
            (spread, None),
        ],
        [
            ((length, model), bf16, rows(model)),
            ((length, width), f32, rows(width)),
            ((length, width), f32, rows(width)),
            ((length, width), bf16, rows(width)),
            ((length, width), f32, rows(width)),
            ((length, width), f32, rows(width)),
            ((length, nstate2), f32, rows(nstate2)),
            ((length, nstate2), f32, rows(nstate2)),
            ((length, LANES), f32, rows(LANES)),
            ((blocks * chunks, nstate2 // 2, width), bf16, states_spec(lambda i, a: (i, 0, 0))),
            ((8, length), f32, along),
            ((length, model), bf16, rows(model, turned)),
        ],
        [
            big(BLOCK, width),
            big(BLOCK + 8, width),
            big(BLOCK + 8, nstate2),
            big(nstate2 // 2, width),
            big(CHUNK, width),
            big(CHUNK, width),
            big(CHUNK, width),
            big(CHUNK, width),
            low(CHUNK, width),
        ],
    )
    og, stats = call(
        functools.partial(stats_kernel, half_blocks),
        blocks,
        at,
        [
            (own_cot, rows(model, own_block)),
            (other_cot, rows(model, other_block)),
            (gg, rows(width)),
            (sq, along),
            (out_w, None),
        ],
        [((length, width), f32, rows(width)), ((8, length), f32, along)],
        [],
    )
    other_stats = add_other(stats)
    dg, dy, grad_out_proj, grad_gate, grad_gain = call(
        functools.partial(gate_kernel, half_blocks, inner_all),
        blocks,
        at,
        [
            (own_cot, rows(model, own_block)),
            (other_cot, rows(model, other_block)),
            (stats, along),
            (other_stats, along),
            (normed, rows(model)),
            (og, rows(width)),
            (y, rows(width)),
            (g, rows(width)),
            (gg, rows(width)),
            (ggain, None),
        ],
        [
            ((length, width), bf16, rows(width)),
            ((length, width), bf16, rows(width)),
            ((width, model), f32, fixed(width, model)),
            ((model, width), f32, fixed(model, width)),
            ((8, width), f32, fixed(8, width)),
        ],
        [],
    )
    plain = lambda i, a: (i, 0)
    ng, grad_value, grad_state, grad_step, grad_vconv, grad_sconv, grad_head = call(
        backward_kernel,
        blocks,
        at,
        [
            (normed, rows(model, back(plain))),
            (dg, rows(width, back(plain))),
            (dy, rows(width, back(plain))),
            (av, rows(width, back(plain))),
            (vp, rows(width, back(plain))),
            (conv_s, rows(nstate2, back(plain))),
            (sp, rows(nstate2, back(plain))),
            (z, rows(LANES, back(plain))),
            (sin, states_spec(lambda i, a: (blocks - 1 - i, 0, 0))),
            (gate_w, None),
            (value_w, None),
            (state_proj, None),
            (step_w, None),
            (vconv, None),
            (sconv, None),
            (rate, None),
            (skipx, None),
            (spread, None),
            (gather, None),
        ],
        [
            ((length, model), bf16, rows(model, back(turned))),
            ((model, width), f32, fixed(model, width)),
            ((model, nstate2), f32, fixed(model, nstate2)),
            ((model, LANES), f32, fixed(model, LANES)),
            ((8, width), f32, fixed(8, width)),
            ((8, nstate2), f32, fixed(8, nstate2)),
            ((8, LANES), f32, fixed(8, LANES)),
        ],
        [
            big(BLOCK + 8, width),
            big(BLOCK + 8, nstate2),
            big(nstate2 // 2, width),
            big(CHUNK, width),
            big(CHUNK, width),
            big(CHUNK, width),
            big(CHUNK, width),
            big(CHUNK, width),
            low(CHUNK, width),
            low(CHUNK, width),
            low(BLOCK, width),
            low(BLOCK, nstate2),
            low(BLOCK, LANES),
        ],
    )

    def scattered(a):
        if two:
            return a[:rows_here].astype(f32) + lax.ppermute(a[rows_here:], "heads", swap).astype(f32)
        return lax.psum_scatter(a.astype(f32), "heads", scatter_dimension=0, tiled=True)

    sums = stats[0] + other_stats[0]
    own_sums = lax.dynamic_slice_in_dim(sums, lax.axis_index("heads") * rows_here, rows_here, 0)
    scale_out = lax.rsqrt(own_sums / inner_all + EPSILON)[:, None]
    residual_rows = residual.astype(f32)
    mixed = residual_rows + scale_out * scattered(branch)

    normed_grad = scattered(ng)
    scale_in = lax.rsqrt(jnp.mean(residual_rows * residual_rows, axis=-1, keepdims=True) + EPSILON)
    inner_dot = jnp.sum(normed_grad * gain_in * residual_rows, axis=1, keepdims=True)
    grad_input = (
        cot.astype(f32)
        + gain_in * scale_in * normed_grad
        - residual_rows * (scale_in * scale_in * scale_in) * inner_dot / model
    )

    grad_norm = (
        jnp.sum(grad_gate * gate_w.astype(f32), axis=1)
        + jnp.sum(grad_value * value_w.astype(f32), axis=1)
        + jnp.sum(grad_state * state_proj.astype(f32), axis=1)
        + jnp.sum(grad_step * step_w.astype(f32), axis=1)
    ) / gain_in[0]

    big_sums = lax.psum(
        tuple(a.astype(bf16) for a in (grad_gate, grad_value, grad_out_proj, grad_step)), "batch"
    )
    grad_gate, grad_value, grad_out_proj, grad_step = (a.astype(f32) for a in big_sums)
    grad_state = lax.psum(grad_state.astype(bf16), ("batch", "heads")).astype(f32)
    grad_vconv, grad_head, grad_gain = lax.psum((grad_vconv, grad_head, grad_gain), "batch")
    grad_sconv, grad_norm = lax.psum((grad_sconv, grad_norm), ("batch", "heads"))
    return (
        mixed[None],
        grad_input[None],
        grad_norm,
        grad_gate[:, :inner],
        grad_value[:, :inner],
        grad_state,
        grad_step[:, :heads],
        grad_vconv[:4, :inner],
        grad_vconv[4, :inner],
        grad_sconv[:4],
        grad_sconv[4],
        grad_head[0, :heads],
        grad_head[1, :heads],
        grad_head[2, :heads],
        grad_gain[0, :inner],
        grad_out_proj[:inner],
    )


def solution(mesh):
    return jax.shard_map(
        per_device,
        mesh=mesh,
        in_specs=(
            P("batch", "heads", None),
            P(),
            P(None, "heads"),
            P(None, "heads"),
            P(),
            P(None, "heads"),
            P(None, "heads"),
            P("heads"),
            P(),
            P(),
            P("heads"),
            P("heads"),
            P("heads"),
            P("heads"),
            P("heads", None),
            P("batch", "heads", None),
        ),
        out_specs=(
            P("batch", "heads", None),
            P("batch", "heads", None),
            P(),
            P(None, "heads"),
            P(None, "heads"),
            P(),
            P(None, "heads"),
            P(None, "heads"),
            P("heads"),
            P(),
            P(),
            P("heads"),
            P("heads"),
            P("heads"),
            P("heads"),
            P("heads", None),
        ),
        check_vma=False,
    )
```

time: 843 us -> 374 us (0.44); the launches traced: 831 us -> 373 us
  local copies, waits for them, and re-layouts: 273 us -> 20.6 us
  matrix products: 141 us -> 0 us
  other arithmetic: 110 us -> 28.5 us
  Pallas kernels: 0 us -> 72.3 us
  waiting for transfers between devices: 153 us -> 104 us
  blocking collectives: 137 us -> 125 us
    dynamic_update_slice x32 -> x0, local copies, waits for them, and re-layouts: 161 us -> none  [scan_heads(): final_state, outputs = lax.scan(jax.checkpoint(advance), initial, pieces)]
    dot_general x44 -> x0, matrix products: 126 us -> none  [the longest x12 62.3 us: advance(): output = jnp.einsum('tsh,shp->thp', mixing, value_blk, precision=HIGHEST)]
    pallas_call x0 -> x4, Pallas kernels: none -> 72.3 us  [call(): pl.pallas_call(kernel, grid_spec=pltpu.PrefetchScalarGridSpec(num_scalar_...]
    reduce_scatter x2 -> x0, waiting for transfers between devices: 36 us -> none  [the longest x1 31.5 us: per_device(): lax.psum_scatter(front + back_part, 'heads', scatter_dimension=0, tiled=T...]
    mul x21 -> x0, other arithmetic: 33 us -> none  [the longest x1 10.9 us: mixer_core(): values = jax.nn.silu(causal_conv(value_pre, value_conv, value_shift))]
    another operation x44 -> x0, other arithmetic: 30 us -> none
    all_gather x2 -> x0, waiting for transfers between devices: 28.1 us -> none  [the longest x1 28.1 us: per_device(): normed_all = lax.all_gather(normed_rows, 'heads', axis=0, tiled=True)]
    reduce_sum x16 -> x0, other arithmetic: 26.2 us -> none  [the longest x2 8.22 us: causal_conv(): kernel[lag_index][None, :] * padded[lag_index:lag_index + length]]
  transfers between devices with their start and end apart: 5 -> 7, of which waited for: 4 -> 3; matrix products, arithmetic and copies ran while one was open for 23% -> 8% of each run, Pallas kernels for 0% -> 6%
where the time goes in v1:
time: 374 us; the launch traced here: 373 us
  blocking collectives  125 us (33%)
  waiting for transfers between devices  104 us (28%)
  Pallas kernels  72.3 us (19%)
  other arithmetic  28.5 us (8%)
  local copies, waits for them, and re-layouts  20.6 us (6%)
  between operations  14.3 us (4%)
  starting transfers between devices  7.52 us (2%)
    psum x1, waiting for transfers between devices, per_device(): lax.psum(tuple((a.astype(bf16) for a in (grad_gate, grad_value, grad_out_...  99 us
    pallas_call x4, Pallas kernels, call(): pl.pallas_call(kernel, grid_spec=pltpu.PrefetchScalarGridSpec(num_scalar_...  72.3 us
    psum x1, blocking collectives, per_device(): lax.psum((grad_sconv, grad_norm), ('batch', 'heads'))  66.4 us
    psum x1, blocking collectives, per_device(): lax.psum((grad_vconv, grad_head, grad_gain), 'batch')  59 us
  transfers between devices with their start and end apart: 7, of which 3 were waited for; matrix products, arithmetic and copies ran while one was open for 8% of the time, Pallas kernels for 6%

profile of v1, /device:TPU:0, one launch (start us, length us, event | category | flops | bytes accessed | tf_op | source)
XLA Modules:
  0.0 372.8 jit_solution(7032013286557210980)
XLA Ops:
  7.2 3.0 collective-permute-start.1
  11.2 1.3 convert_element_type.83.vconv_ref
  13.9 1.3 convert_element_type.84.sconv_ref
  15.2 1.3 reshape.182.ggain_ref
  16.5 1.3 broadcast_in_dim.42.gain_ref
  17.7 1.3 reshape.180.vshift_ref
  24.6 4.2 %collective-permute-done.1.other_ref = bf16[512,768]{1,0:T(8,128)(2,1)S(1)} collective-permute-done((bf16[512,768]{1,0:T(8,128)(2,1)}, bf16[512,768]{1,0:T(8,128)(2,1)S(1)}, u32[]{:S(2)}, u32[]{:S(2)}) %collective-permute-start.1) | collective-permute-done | bytes 786464 | tf_op jit(solution)/shard_map/ppermute | solution.py:536
  29.7 21.3 %shard_map.279 = (bf16[1024,768]{1,0:T(8,128)(2,1)}, f32[1024,768]{1,0:T(8,128)}, f32[1024,768]{1,0:T(8,128)}, bf16[1024,768]{1,0:T(8,128)(2,1)}, f32[1024,768]{...) custom-call(s32[1]{0:T(128)} %bitcast.1.at_ref, ...), custom_call_target="tpu_custom_call" | custom-call | tf_op jit(solution)/shard_map/pallas_call | solution.py:473
  51.9 5.9 %shard_map.280 = (f32[1024,768]{1,0:T(8,128)}, f32[8,1024]{1,0:T(8,128)}) custom-call(s32[1]{0:T(128)} %bitcast.1.at_ref, bf16[512,768]{1,0:T(8,128)(2,1)} %bitcast.25, bf16[512,768]{1,0:T(8,128)(2,1)} %copy-done.6, bf16[1024,768]{1,0:T(8,128)(2,1)} %get-tuple-element.42.gg_ref, f32[8,1024]{1,0:T(8,128)} %get-tuple-element.43.sq_ref, bf16[768,768]{1,0:T(8,128)(2,1)} %out_w.3), custom_call_target="tpu_custom_call" | custom-call | tf_op jit(solution)/shard_map/pallas_call | solution.py:473
  57.8 2.2 collective-permute-start.2
  62.7 11.3 %shard_map.281 = (bf16[1024,768]{1,0:T(8,128)(2,1)}, bf16[1024,768]{1,0:T(8,128)(2,1)}, f32[768,768]{1,0:T(8,128)}, f32[768,768]{1,0:T(8,128)}, f32[8,768]{1,0:T(8,128)}) custom-call(s32[1]{0:T(128)} %bitcast.1.at_ref, bf16[512,768]{1,0:T(8,128)(2,1)} %bitcast.26, bf16[512,768]{1,0:T(8,128)(2,1)} %copy-done.6, f32[8,1024]{1,0:T(8,128)} %get-tuple-element.44.here_ref, ...), custom_call_target="tpu_custom_call" | custom-call | tf_op jit(solution)/shard_map/pallas_call | solution.py:473
  74.1 33.8 %shard_map.282 = (bf16[1024,768]{1,0:T(8,128)(2,1)}, f32[768,768]{1,0:T(8,128)}, f32[768,256]{1,0:T(8,128)}, f32[768,128]{1,0:T(8,128)}, f32[8,768]{1,0:T(8,128)}, /*index=5*/f32[8,256]{1,0:T(8,128)}, f32[8,128]{1,0:T(8,128)}) custom-call(s32[1]{0:T(128)} %bitcast.1.at_ref, bf16[1024,768]{1,0:T(8,128)(2,1)} %get-tuple-element.46.normed_ref, ...), custom_call_target="tpu_custom_call" | custom-call | tf_op jit(solution)/shard_map/pallas_call | solution.py:473
  107.8 3.9 %fusion.16 = (bf16[768,768]{1,0:T(8,128)(2,1)}, f32[768]{0:T(1024)S(1)}) fusion(f32[768,768]{1,0:T(8,128)} %get-tuple-element.60, bf16[768,768]{1,0:T(8,128)(2,1)S(1)} %copy-done), kind=kLoop, calls=%fused_computation.54 | loop fusion | flops 2358528 | bytes 4721664 | tf_op jit(solution)/shard_map/convert_element_type | solution.py:766
  111.8 1.4 fusion.17
  119.9 2.1 collective-permute-start.3
  123.0 66.4 %all-reduce.3 = (f32[768]{0:T(1024)}, f32[8,256]{1,0:T(8,128)S(1)}) all-reduce(f32[768]{0:T(1024)S(1)} %add_divide_fusion, f32[8,256]{1,0:T(8,128)S(1)} %copy-done.21), channel_id=1, replica_groups=mesh['batch'=16,'heads'=2] {'batch','heads'}, use_global_device_ids=true, to_apply=%region_6.7 | all-reduce | flops 2816 | bytes 22528 | tf_op jit(solution)/shard_map/psum | solution.py:771
  190.6 59.0 %all-reduce.4 = (f32[8,768]{1,0:T(8,128)S(1)}, f32[8,128]{1,0:T(8,128)S(1)}, f32[8,768]{1,0:T(8,128)S(1)}) all-reduce(f32[8,768]{1,0:T(8,128)S(1)} %copy-done.19, f32[8,128]{1,0:T(8,128)S(1)} %copy-done.22, f32[8,768]{1,0:T(8,128)S(1)} %copy-done.18), channel_id=1, replica_groups=mesh['batch'=16,'heads'=2] {'batch'}, use_global_device_ids=true, to_apply=%region_11.12 | all-reduce | flops 13312 | bytes 106496 | tf_op jit(solution)/shard_map/psum | solution.py:770
  252.0 2.1 convert_element_type.101
  254.0 1.7 fusion.1
  255.8 4.2 %fusion.5 = (f32[1,512,768]{2,1,0:T(8,128)}, f32[1,512,768]{2,1,0:T(8,128)}) fusion(bf16[512,768]{1,0:T(8,128)(2,1)} %collective-permute-done.4, f32[512]{0:T(512)S(1)} %get-tuple-element.85, f32[512]{0:T(512)S(1)} %get-tuple-element.111, f32[512]{0:T(512)S(1)} %get-tuple-element.110, f32[768]{0:T(1024)S(1)} %convert_element_type.82, ...), kind=kLoop, calls=%fused_computation.11 | loop fusion | flops 6684672 | bytes 7875584 | tf_op jit(solution)/shard_map/broadcast_in_dim | solution.py:774
  260.0 99.0 %all-reduce.11.cloned.1.call-done = (bf16[768,768]{1,0:T(8,128)(2,1)}, bf16[768,768]{1,0:T(8,128)(2,1)}, bf16[768,128]{1,0:T(8,128)(2,1)}, bf16[768,768]{1,0:T(8,128)(2,1)}) async-done(((bf16[768,768]{1,0:T(8,128)(2,1)}, bf16[768,768]{1,0:T(8,128)(2,1)}, bf16[768,128]{1,0:T(8,128)(2,1)}, bf16[768,768]{1,0:T(8,128)(2,1)}), (bf16[768,768]{1,0:T(8,128)(2,1)}, bf16[768,768]{1,0:T(8,128)(2,1)}, ...) | async-done | bytes 3735568 | tf_op jit(solution)/shard_map/psum | solution.py:765
  359.0 2.9 convert_element_type.104
  361.9 1.6 convert_element_type.97
  363.6 1.6 convert_element_type.99
  (91 shorter events, 24.6 us)
Async XLA Ops:
  7.2 244.8 %all-reduce.9.cloned.1.call-start = ((), (), s32[]{:S(2)}) async-start(), calls=%async_computation | async-start | bytes 786432 | tf_op jit(solution)/shard_map/psum | solution.py:769
  7.2 21.6 %collective-permute-start.1 = (bf16[512,768]{1,0:T(8,128)(2,1)}, bf16[512,768]{1,0:T(8,128)(2,1)S(1)}, u32[]{:S(2)}, u32[]{:S(2)}) collective-permute-start(bf16[512,768]{1,0:T(8,128)(2,1)} %bitcast.27), channel_id=1, source_target_pairs={{0,1},{1,0},{2,3},{3,2},{4,5},{5,4},{6,7},{7,6},{8,9},{9,8},{10,11... | collective-permute-start | bytes 2359304 | tf_op jit(solution)/shard_map/ppermute | solution.py:536
  10.2 40.8 %collective-permute-start = (bf16[512,768]{1,0:T(8,128)(2,1)}, bf16[512,768]{1,0:T(8,128)(2,1)S(1)}, u32[]{:S(2)}, u32[]{:S(2)}) collective-permute-start(bf16[512,768]{1,0:T(8,128)(2,1)} %bitcast.24), channel_id=1, source_target_pairs={{0,1},{1,0},{2,3},{3,2},{4,5},{5,4},{6,7},{7,6},{8,9},{9,8},{10,11... | collective-permute-start | bytes 2359304 | tf_op jit(solution)/shard_map/ppermute | solution.py:536
  57.8 4.3 %collective-permute-start.2 = (f32[8,1024]{1,0:T(8,128)}, f32[8,1024]{1,0:T(8,128)S(1)}, u32[]{:S(2)}, u32[]{:S(2)}) collective-permute-start(f32[8,1024]{1,0:T(8,128)} %get-tuple-element.44.here_ref), channel_id=1, source_target_pairs={{0,1},{1,0},{2,3},{3,2},{4,5},{5,4},{6,7},{7,6},{8,9},{9,8},{10,11... | collective-permute-start | bytes 98312 | tf_op jit(solution)/shard_map/ppermute | solution.py:537
  74.1 33.8 %copy-start = (bf16[768,768]{1,0:T(8,128)(2,1)S(1)}, bf16[768,768]{1,0:T(8,128)(2,1)}, u32[]{:S(2)}) copy-start(bf16[768,768]{1,0:T(8,128)(2,1)} %value_w.3) | copy-start | bytes 3538948
  107.8 4.0 %copy-start.1 = (bf16[768,768]{1,0:T(8,128)(2,1)S(1)}, bf16[768,768]{1,0:T(8,128)(2,1)}, u32[]{:S(2)}) copy-start(bf16[768,768]{1,0:T(8,128)(2,1)} %gate_w.3) | copy-start | bytes 3538948
  107.8 3.9 %copy-start.8 = (f32[768,768]{1,0:T(8,128)S(1)}, f32[768,768]{1,0:T(8,128)}, u32[]{:S(2)}) copy-start(f32[768,768]{1,0:T(8,128)} %get-tuple-element.59) | copy-start | bytes 7077892
  111.8 2.1 copy-start.7
  113.9 1.7 copy-start.14
  116.5 242.5 %all-reduce.11.cloned.1.call-start = ((), (), s32[]{:S(2)}) async-start(), calls=%async_computation.1 | async-start | bytes 7471104 | tf_op jit(solution)/shard_map/psum | solution.py:765
  118.0 4.0 %copy-start.4 = (bf16[1024,768]{1,0:T(8,128)(2,1)S(1)}, bf16[1024,768]{1,0:T(8,128)(2,1)}, u32[]{:S(2)}) copy-start(bf16[1024,768]{1,0:T(8,128)(2,1)} %get-tuple-element.58) | copy-start | bytes 4718596
  118.9 4.1 %copy-start.21 = (f32[8,256]{1,0:T(8,128)S(1)}, f32[8,256]{1,0:T(8,128)}, u32[]{:S(2)}) copy-start(f32[8,256]{1,0:T(8,128)} %get-tuple-element.64) | copy-start | bytes 24580
  118.9 71.7 %copy-start.18 = (f32[8,768]{1,0:T(8,128)S(1)}, f32[8,768]{1,0:T(8,128)}, u32[]{:S(2)}) copy-start(f32[8,768]{1,0:T(8,128)} %get-tuple-element.66) | copy-start | bytes 73732
  118.9 71.6 %copy-start.19 = (f32[8,768]{1,0:T(8,128)S(1)}, f32[8,768]{1,0:T(8,128)}, u32[]{:S(2)}) copy-start(f32[8,768]{1,0:T(8,128)} %get-tuple-element.63) | copy-start | bytes 73732
  118.9 71.6 %copy-start.22 = (f32[8,128]{1,0:T(8,128)S(1)}, f32[8,128]{1,0:T(8,128)}, u32[]{:S(2)}) copy-start(f32[8,128]{1,0:T(8,128)} %get-tuple-element.65) | copy-start | bytes 12292
  119.0 132.5 %slice-start = ((f32[8,1024]{1,0:T(8,128)}), f32[1,1024]{1,0:T(1,128)S(1)}, s32[]{:S(2)}) async-start(f32[8,1024]{1,0:T(8,128)} %copy-done.17), calls=%async_computation.2 | async-start | bytes 8192 | tf_op jit(solution)/shard_map/slice | solution.py:743
  119.9 134.1 %copy-start.3 = (bf16[1,512,768]{2,1,0:T(8,128)(2,1)S(1)}, bf16[1,512,768]{2,1,0:T(8,128)(2,1)}, u32[]{:S(2)}) copy-start(bf16[1,512,768]{2,1,0:T(8,128)(2,1)} %param.16) | copy-start | bytes 2359300
  119.9 135.8 %collective-permute-start.3 = (bf16[512,768]{1,0:T(8,128)(2,1)}, bf16[512,768]{1,0:T(8,128)(2,1)}, u32[]{:S(2)}, u32[]{:S(2)}) collective-permute-start(bf16[512,768]{1,0:T(8,128)(2,1)} %slice.51), channel_id=1, source_target_pairs={{0,1},{1,0},{2,3},{3,2},{4,5},{5,4},{6,7},{7,6},{8,9},{9,8},{10,11... | collective-permute-start | bytes 2359304 | tf_op jit(solution)/shard_map/ppermute | solution.py:740
  123.0 131.1 %collective-permute-start.4 = (bf16[512,768]{1,0:T(8,128)(2,1)}, bf16[512,768]{1,0:T(8,128)(2,1)}, u32[]{:S(2)}, u32[]{:S(2)}) collective-permute-start(bf16[512,768]{1,0:T(8,128)(2,1)} %slice.53), channel_id=1, source_target_pairs={{0,1},{1,0},{2,3},{3,2},{4,5},{5,4},{6,7},{7,6},{8,9},{9,8},{10,11... | collective-permute-start | bytes 2359304 | tf_op jit(solution)/shard_map/ppermute | solution.py:740
  251.9 3.8 %copy-start.2 = (bf16[1,512,768]{2,1,0:T(8,128)(2,1)S(1)}, bf16[1,512,768]{2,1,0:T(8,128)(2,1)}, u32[]{:S(2)}) copy-start(bf16[1,512,768]{2,1,0:T(8,128)(2,1)} %param.31) | copy-start | bytes 2359300
  252.0 3.8 %copy-start.10 = (bf16[1024,768]{1,0:T(8,128)(2,1)S(1)}, bf16[1024,768]{1,0:T(8,128)(2,1)}, u32[]{:S(2)}) copy-start(bf16[1024,768]{1,0:T(8,128)(2,1)} %get-tuple-element.45) | copy-start | bytes 4718596
  359.0 2.9 copy-start.12
  361.9 1.7 copy-start.11
  363.6 1.6 copy-start.16
  (7 other events, 7.3 us)
Sparse Core Ops, SparseCore 0:
  116.6 129.4 all-reduce.8
  251.8 107.0 all-reduce.10

commit v2 on v1

v2 whole, which is shorter than its diff:
```python
import functools

import jax
import jax.numpy as jnp
from jax import lax
from jax.experimental import pallas as pl
from jax.experimental.pallas import tpu as pltpu
from jax.sharding import PartitionSpec as P

EPSILON = 1e-05
HIGHEST = lax.Precision.HIGHEST
BLOCK = 256
CHUNK = 128
LANES = 128
LOG2E = 1.4426950408889634
f32 = jnp.float32
bf16 = jnp.bfloat16


def dot(left, right, over=((1,), (0,)), precision=None):
    return lax.dot_general(
        left, right, (over, ((), ())), preferred_element_type=f32, precision=precision
    )


TN = ((0,), (0,))
NT = ((1,), (1,))


def sigmoid(v):
    return 0.5 * jnp.tanh(0.5 * v) + 0.5


def split(v):
    high = v.astype(bf16)
    return jnp.concatenate([high, (v - high.astype(f32)).astype(bf16)], axis=1)


def lower_mask(rows):
    return lax.broadcasted_iota(jnp.int32, (rows, rows), 0) >= lax.broadcasted_iota(
        jnp.int32, (rows, rows), 1
    )


def chunk_scalars(z, log_rate):
    step = jnp.maximum(z, 0.0) + jnp.log1p(jnp.exp(-jnp.abs(z)))
    rate = -jnp.exp(log_rate)
    decay = step * (rate * LOG2E)
    ones = lower_mask(CHUNK).astype(f32)
    running = dot(ones, decay, precision=HIGHEST)
    grown = jnp.exp2(running)
    tail = jnp.exp2(running[CHUNK - 1 : CHUNK, :] - running)
    return step, rate, running, grown, tail


def chunk_scores(states):
    n = states.shape[1] // 2
    b, c = split(states[:, :n]), split(states[:, n:])
    left = jnp.concatenate([c, c[:, :n]], axis=1)
    right = jnp.concatenate([b[:, :n], b[:, :n], b[:, n:]], axis=1)
    return b, c, dot(left, right, NT)


def pair_decay(running, running_t, pair, mask):
    out = []
    for head in (2 * pair, 2 * pair + 1):
        spread = running[:, head : head + 1] - running_t[head : head + 1, :]
        out.append(jnp.exp2(jnp.where(mask, spread, -1e30)))
    return out


def half_masks():
    lane = lax.broadcasted_iota(jnp.int32, (1, LANES), 1)
    first = (lane < LANES // 2).astype(bf16)
    return first, 1 - first


def stacked(rows, masks):
    return jnp.concatenate([rows * masks[0], rows * masks[1]], axis=0)


def forward_kernel(
    half_blocks,
    at_ref,
    own_ref,
    other_ref,
    gain_ref,
    gate_w,
    value_w,
    state_w,
    step_w,
    vconv_ref,
    vshift_ref,
    sconv_ref,
    sshift_ref,
    sbias_ref,
    rate_ref,
    skip_ref,
    ggain_ref,
    spread_ref,
    normed_ref,
    g_ref,
    y_ref,
    gg_ref,
    av_ref,
    vp_ref,
    as_ref,
    sp_ref,
    z_ref,
    sin_ref,
    sq_ref,
    gbuf,
    vbuf,
    sbuf,
    state,
    stepx,
    grownx,
    tailx,
    carried,
    vtail,
):
    step_at = pl.program_id(0)
    pairs = vbuf.shape[1] // LANES
    nstate = state.shape[0]

    @pl.when(step_at == 0)
    def _():
        state[...] = jnp.zeros_like(state)
        vbuf[0:8, :] = jnp.zeros((8, vbuf.shape[1]), f32)
        sbuf[0:8, :] = jnp.zeros((8, sbuf.shape[1]), f32)

    mine = (step_at // half_blocks) == at_ref[0]
    rows = jnp.where(mine, own_ref[...].astype(f32), other_ref[...].astype(f32))
    scale = lax.rsqrt(jnp.mean(rows * rows, axis=1, keepdims=True) + EPSILON)
    normed = (rows * scale * gain_ref[...].astype(f32)).astype(bf16)
    normed_ref[...] = normed
    gbuf[...] = dot(normed, gate_w[...])
    g_ref[...] = gbuf[...]
    vbuf[8:, :] = dot(normed, value_w[...])
    vp_ref[...] = vbuf[8:, :]
    sbuf[8:, :] = dot(normed, state_w[...])
    sp_ref[...] = sbuf[8:, :]
    z_ref[...] = dot(normed, step_w[...]) + sbias_ref[...]

    mask = lower_mask(CHUNK)
    masks = half_masks()
    for chunk in range(BLOCK // CHUNK):
        r0 = chunk * CHUNK
        here = pl.ds(r0, CHUNK)
        step, _, running, grown, tail = chunk_scalars(z_ref[here, :], rate_ref[...])
        running_t = running.T
        stepx[...] = dot(split(step), spread_ref[...])
        grownx[...] = dot(split(grown), spread_ref[...])
        tailx[...] = dot(split(tail), spread_ref[...])
        conv = sshift_ref[...].astype(f32)
        for tap in range(4):
            conv = conv + sconv_ref[tap : tap + 1, :].astype(f32) * sbuf[pl.ds(r0 + 5 + tap, CHUNK), :]
        as_ref[here, :] = conv
        b_two, c_two, scores = chunk_scores(conv * sigmoid(conv))
        b_rows, c_rows = b_two[:, :nstate], c_two[:, :nstate]
        before = state[...].astype(bf16)
        sin_ref[chunk, :, :] = before
        carried[...] = dot(c_rows, before)
        squares = jnp.zeros((CHUNK, LANES), f32)
        for pair in range(pairs):
            lanes = slice(pair * LANES, (pair + 1) * LANES)
            conv = vshift_ref[:, lanes].astype(f32)
            for tap in range(4):
                moved = vbuf[pl.ds(r0 + 5 + tap, CHUNK), lanes]
                conv = conv + vconv_ref[tap : tap + 1, lanes].astype(f32) * moved
            av_ref[here, lanes] = conv
            values = conv * sigmoid(conv)
            stepped = values * stepx[:, lanes]
            vtail[:, lanes] = (stepped * tailx[:, lanes]).astype(bf16)
            first, second = pair_decay(running, running_t, pair, mask)
            mixing = jnp.concatenate(
                [(scores * first).astype(bf16), (scores * second).astype(bf16)], axis=1
            )
            scanned = dot(mixing, stacked(stepped.astype(bf16), masks))
            scanned = scanned + grownx[:, lanes] * carried[:, lanes] + skip_ref[:, lanes] * values
            y_ref[here, lanes] = scanned
            g = gbuf[here, lanes]
            gated = scanned * (g * sigmoid(g))
            gg_ref[here, lanes] = (gated * ggain_ref[:, lanes].astype(f32)).astype(bf16)
            squares = squares + gated * gated
        sq_ref[:, here] = dot(jnp.ones((8, LANES), f32), squares, NT, HIGHEST)
        state[...] = grownx[CHUNK - 1 : CHUNK, :] * state[...] + dot(b_rows, vtail[...], TN)
    vbuf[0:8, :] = vbuf[BLOCK : BLOCK + 8, :]
    sbuf[0:8, :] = sbuf[BLOCK : BLOCK + 8, :]


def stats_kernel(half_blocks, at_ref, own_ref, other_ref, gg_ref, sq_ref, out_w, og_ref, stats_ref):
    mine = (pl.program_id(0) // half_blocks) == at_ref[0]
    cot = jnp.where(mine, own_ref[...], other_ref[...])
    og = dot(cot, out_w[...], NT)
    og_ref[...] = og
    prod = (og * gg_ref[...].astype(f32)).astype(bf16)
    dots = dot(jnp.ones((8, prod.shape[1]), bf16), prod, NT)
    row = lax.broadcasted_iota(jnp.int32, dots.shape, 0)
    stats_ref[...] = jnp.where(row == 0, sq_ref[...], dots)


def branch_kernel(half_blocks, at_ref, gg_ref, out_w, own_ref, other_ref):
    mine = (pl.program_id(0) // half_blocks) == at_ref[0]
    rows = dot(gg_ref[...], out_w[...]).astype(bf16)

    @pl.when(mine)
    def _():
        own_ref[...] = rows

    @pl.when(jnp.logical_not(mine))
    def _():
        other_ref[...] = rows


def picked(cut, early, late):
    return jnp.where(pl.program_id(0) < cut, early[...], late[...])


def normed_grad_kernel(half_blocks, cut, at_ref, dg_ref, *refs):
    lows, (gate_w, value_w, state_w, step_w, own_ref, other_ref) = refs[:6], refs[6:]
    dv, ds, dz = (picked(cut, a, b) for a, b in zip(lows[:3], lows[3:]))
    mine = (pl.program_id(0) // half_blocks) == at_ref[0]
    rows = (
        dot(dg_ref[...], gate_w[...], NT)
        + dot(dv, value_w[...], NT)
        + dot(ds, state_w[...], NT)
        + dot(dz, step_w[...], NT)
    ).astype(bf16)

    @pl.when(mine)
    def _():
        own_ref[...] = rows

    @pl.when(jnp.logical_not(mine))
    def _():
        other_ref[...] = rows


def row_sums(grads, weights):
    prod = (grads * weights.astype(f32)).astype(bf16)
    return dot(jnp.ones((8, prod.shape[1]), bf16), prod, NT)


def emit(at_ref, parts, outs):
    half = outs[0].shape[0]
    for j, out in enumerate(outs):
        rows = pl.ds(pl.multiple_of((at_ref[1] ^ j) * half, LANES), half)
        left = 0
        for part in parts:
            out[:, left : left + part.shape[1]] = part[rows, :].astype(out.dtype)
            left += part.shape[1]


def row_column(rows):
    return jnp.concatenate([rows, jnp.zeros((LANES - rows.shape[0], BLOCK), f32)], axis=0).T


def mixed_kernel(inner_all, at_ref, rows_ref, own_ref, other_ref, here_ref, there_ref, out_ref, token_ref):
    token_ref[...] = jnp.zeros_like(token_ref)
    sums = here_ref[...] + there_ref[...]
    scale = row_column(lax.rsqrt(sums / inner_all + EPSILON))[:, 0:1]
    branch = own_ref[...].astype(f32) + other_ref[...].astype(f32)
    out_ref[...] = rows_ref[...].astype(f32) + scale * branch


def input_kernel(at_ref, rows_ref, cot_ref, own_ref, other_ref, gain_ref, out_ref, token_ref):
    token_ref[...] = jnp.zeros_like(token_ref)
    rows = rows_ref[...].astype(f32)
    scale = lax.rsqrt(jnp.mean(rows * rows, axis=1, keepdims=True) + EPSILON)
    pulled = (own_ref[...].astype(f32) + other_ref[...].astype(f32)) * gain_ref[...].astype(f32)
    inner = jnp.mean(pulled * rows, axis=1, keepdims=True) * (scale * scale * scale)
    out_ref[...] = cot_ref[...].astype(f32) + scale * pulled - rows * inner


def gate_kernel(
    half_blocks,
    inner_all,
    fast,
    at_ref,
    own_ref,
    other_ref,
    here_ref,
    there_ref,
    normed_ref,
    og_ref,
    y_ref,
    g_ref,
    gg_ref,
    ggain_ref,
    gate_w,
    _,
    dg_ref,
    dy_ref,
    first_ref,
    second_ref,
    grad_gain_ref,
    norm_ref,
    *scratch,
):
    step_at = pl.program_id(0)
    pairs = og_ref.shape[1] // LANES
    grad_gate, grad_out = scratch if fast else (first_ref, second_ref)

    @pl.when(step_at == 0)
    def _():
        grad_out[...] = jnp.zeros_like(grad_out)
        grad_gate[...] = jnp.zeros_like(grad_gate)
        grad_gain_ref[...] = jnp.zeros_like(grad_gain_ref)

    sums = here_ref[...] + there_ref[...]
    scale_row = lax.rsqrt(sums[0:1, :] / inner_all + EPSILON)
    pull_row = scale_row * scale_row * scale_row * sums[1:2, :] / inner_all
    columns = row_column(jnp.concatenate([scale_row, pull_row], axis=0))
    scale, pull = columns[:, 0:1], columns[:, 1:2]
    mine = (step_at // half_blocks) == at_ref[0]
    cot = jnp.where(mine, own_ref[...], other_ref[...]).astype(f32)
    scaled = (cot * scale).astype(bf16)
    for pair in range(pairs):
        lanes = slice(pair * LANES, (pair + 1) * LANES)
        og = og_ref[:, lanes] * scale
        y = y_ref[:, lanes]
        g = g_ref[:, lanes]
        sig = sigmoid(g)
        silu = g * sig
        gated = y * silu
        grad_gain_ref[0:1, lanes] += jnp.sum(og * gated, axis=0, keepdims=True)
        gated_grad = ggain_ref[:, lanes].astype(f32) * og - gated * pull
        dy_ref[:, lanes] = (gated_grad * silu).astype(bf16)
        dg_ref[:, lanes] = (gated_grad * y * (sig + silu * (1.0 - sig))).astype(bf16)
    grad_out[...] += dot(gg_ref[...], scaled, TN)
    grad_gate[...] += dot(normed_ref[...], dg_ref[...], TN)

    @pl.when(step_at == pl.num_programs(0) - 1)
    def _():
        norm_ref[...] = row_sums(grad_gate[...], gate_w[...])
        if fast:
            emit(at_ref, (grad_gate, grad_out), (first_ref, second_ref))


def weights_kernel(fast, extra, cut, at_ref, normed_ref, *refs):
    step_at = pl.program_id(0)
    lows, refs = refs[:6], refs[6:]
    value_w, state_w, step_w, gain_ref, vec_ref, svec_ref, head_ref, ggain_ref, norm_ref = refs[:9]
    outs, acc = refs[9 + extra : -3], refs[-3:]

    @pl.when(step_at == 0)
    def _():
        for a in acc:
            a[...] = jnp.zeros_like(a)

    normed = normed_ref[...]
    for a, early, late in zip(acc, lows[:3], lows[3:]):
        a[...] += dot(normed, picked(cut, early, late), TN)

    @pl.when(step_at == pl.num_programs(0) - 1)
    def _():
        norm = norm_ref[...]
        for a, w in zip(acc, (value_w, state_w, step_w)):
            norm = norm + row_sums(a[...], w[...])
        norm = norm / gain_ref[...].astype(f32)
        if not fast:
            for o, a in zip(outs, acc):
                o[...] = a[...]
            outs[3][...] = norm
            return
        pack_vectors(acc[2], vec_ref, svec_ref, head_ref, ggain_ref, norm)
        emit(at_ref, acc, outs)


VEC_AT = 16
SVEC_AT = 24
HEAD_AT = 32
HALF = LANES // 2


def pack_vectors(block, vec_ref, svec_ref, head_ref, ggain_ref, norm):
    model = block.shape[0]
    row = lax.broadcasted_iota(jnp.int32, (8, model), 0)
    vec = jnp.where(row == 5, ggain_ref[0:1, :], jnp.where(row == 6, norm[0:1, :], vec_ref[...]))

    def tall(v):
        return jnp.concatenate([v, jnp.zeros((8, model - v.shape[1]), f32)], axis=1)

    rows = jnp.concatenate(
        [
            jnp.zeros((VEC_AT, model), f32),
            vec,
            tall(svec_ref[...]),
            tall(head_ref[...]),
            jnp.zeros((LANES - HEAD_AT - 8, model), f32),
        ],
        axis=0,
    )
    lane = lax.broadcasted_iota(jnp.int32, (1, LANES), 1)
    full = jnp.where(lane < VEC_AT, block[...], rows.T)
    block[...] = carry_rest(jnp.where(lane < HALF, full, 0.0))


def carry_rest(full):
    high = full.astype(bf16).astype(f32)
    return high + pltpu.roll(full - high, HALF, 1)


def join_rest(block):
    lane = lax.broadcasted_iota(jnp.int32, (1, LANES), 1)
    return jnp.where(lane < HALF, block + pltpu.roll(block, HALF, 1), 0.0)


def fold_step(me, ins, outs, buf, vectors):
    width = buf.shape[1] - (LANES if vectors else 0)
    total = ins[0][:, :width].astype(f32)
    for r in ins[1:]:
        total = total + r[:, :width].astype(f32)
    buf[:, :width] = total.astype(bf16)
    if vectors:
        last = ins[0][:, width:].astype(f32)
        for r in ins[1:]:
            last = last + r[:, width:].astype(f32)
        buf[:, width:] = carry_rest(join_rest(last)).astype(bf16)
    rows = outs[0].shape[0]
    if len(outs) == 1:
        outs[0][...] = buf[...]
        return
    for j, o in enumerate(outs):
        o[...] = buf[pl.ds(pl.multiple_of((me ^ j) * rows, 16), rows), :]


def join_step(me, ins, out):
    rows = ins[0].shape[0]
    for j, r in enumerate(ins):
        out[pl.ds(pl.multiple_of((me ^ j) * rows, 16), rows), :] = r[...]


def stage_kernel(plan, extra, at_ref, *refs):
    n_in = sum(count for _, _, count, _, _ in plan)
    ins, refs = refs[:n_in], refs[n_in + extra :]
    n_out = sum(count for _, _, _, count, _ in plan)
    outs, bufs = refs[:n_out], list(refs[n_out:])
    for kind, axis, take, give, vectors in plan:
        if kind == "fold":
            fold_step(at_ref[axis], ins[:take], outs[:give], bufs.pop(0), vectors)
        else:
            join_step(at_ref[axis], ins[:take], outs[0])
        ins, outs = ins[take:], outs[give:]


def stage(at, steps, after=()):
    plan, arrays, shapes, scratch = [], [], [], []
    for kind, axis, ins, *rest in steps:
        rows, width = ins[0].shape
        count, vectors = rest if rest else (1, False)
        if kind == "fold":
            shapes += [(rows // count, width)] * count
            scratch.append(pltpu.VMEM((rows, width), bf16))
        else:
            shapes.append((rows * len(ins), width))
        plan.append((kind, axis, len(ins), count, vectors))
        arrays += ins
    out = call(
        functools.partial(stage_kernel, tuple(plan), len(after)),
        1,
        at,
        [(a, None) for a in arrays] + [(a, pl.BlockSpec(memory_space=pl.ANY)) for a in after],
        [(shape, bf16, pl.BlockSpec(shape, lambda i, a: (0, 0))) for shape in shapes],
        scratch,
        24,
    )
    out, results = list(out), []
    for _, _, _, give, _ in plan:
        results.append(out[:give])
        out = out[give:]
    return results


def heads_kernel(at_ref, own_ref, other_ref, out_ref):
    split_at = out_ref.shape[1] - other_ref.shape[1]
    state = other_ref.shape[1] - LANES
    out_ref[:, :split_at] = own_ref[:, :split_at]
    out_ref[:, split_at : split_at + state] = (
        own_ref[:, split_at : split_at + state].astype(f32) + other_ref[:, :state].astype(f32)
    ).astype(bf16)
    lane = lax.broadcasted_iota(jnp.int32, (1, LANES), 1)
    shared = (lane == VEC_AT + 6) | ((lane >= SVEC_AT) & (lane < HEAD_AT))
    mine = join_rest(own_ref[:, split_at + state :].astype(f32))
    theirs = join_rest(other_ref[:, state:].astype(f32))
    out_ref[:, split_at + state :] = carry_rest(
        mine + jnp.where(shared, theirs, 0.0)
    ).astype(bf16)


def halves_of(at_ref, own_ref, other_ref, left, right):
    rows = own_ref.shape[0]
    for j, ref in enumerate((own_ref, other_ref)):
        yield pl.ds(pl.multiple_of((at_ref[1] ^ j) * rows, LANES), rows), ref[:, left:right].astype(f32)


def early_kernel(at_ref, own_ref, other_ref, *outs):
    outs[-1][...] = jnp.zeros_like(outs[-1])
    left = 0
    for o in outs[:-1]:
        right = left + o.shape[1]
        for at, v in halves_of(at_ref, own_ref, other_ref, left, right):
            o[at, :] = v
        left = right


def late_kernel(at_ref, own_ref, other_ref, *refs):
    outs, block = refs[:-1], refs[-1]
    left = 0
    for o in (outs[0], outs[1], block):
        right = left + o.shape[1]
        for at, v in halves_of(at_ref, own_ref, other_ref, left, right):
            o[at, :] = v
        left = right
    full = join_rest(block[...])
    heads = outs[2].shape[1]
    outs[2][...] = full[:, :heads]
    rows = full.T
    vec, svec = rows[VEC_AT : VEC_AT + 8], rows[SVEC_AT : SVEC_AT + 8]
    head = rows[HEAD_AT : HEAD_AT + 8]
    vconv, vshift, ggain, norm, sconv, sshift, bias, rate, skip = outs[3:]
    vconv[...] = vec[:4]
    for o, row in ((vshift, vec[4:5]), (ggain, vec[5:6]), (norm, vec[6:7]), (sshift, svec[4:5])):
        o[...] = row[:, : o.shape[0]].reshape(o.shape)
    sconv[...] = svec[:4, : sconv.shape[1]]
    for j, o in enumerate((bias, rate, skip)):
        o[...] = head[j : j + 1, : o.shape[0]].reshape(o.shape)


def backward_kernel(
    carried_in,
    extra,
    at_ref,
    dy_ref,
    av_ref,
    vp_ref,
    as_ref,
    sp_ref,
    z_ref,
    sin_ref,
    vconv_ref,
    sconv_ref,
    rate_ref,
    skip_ref,
    spread_ref,
    gather_ref,
    *refs,
):
    carries, refs = (refs[:6], refs[6:]) if carried_in else ((), refs)
    refs = refs[extra:]
    dvalue, dstates, dstep, dstate_out, dahalo, dshalo, grad_vconv_ref, grad_sconv_ref, grad_head_ref = refs[:9]
    dabuf, dsbuf, dstate, stepx, grownx, tailx, carried, pulled, ubuf, vtail = refs[9:]
    step_at = pl.program_id(0)
    width = dabuf.shape[1]
    pairs = width // LANES
    nstate = dstate.shape[0]

    @pl.when(step_at == 0)
    def _():
        if carried_in:
            dstate[...] = carries[0][...]
            dabuf[BLOCK:, :] = carries[1][...]
            dsbuf[BLOCK:, :] = carries[2][...]
            grad_vconv_ref[...] = carries[3][...]
            grad_sconv_ref[...] = carries[4][...]
            grad_head_ref[...] = carries[5][...]
        else:
            dstate[...] = jnp.zeros_like(dstate)
            dabuf[BLOCK:, :] = jnp.zeros((8, width), f32)
            dsbuf[BLOCK:, :] = jnp.zeros((8, dsbuf.shape[1]), f32)
            for ref in (grad_vconv_ref, grad_sconv_ref, grad_head_ref):
                ref[...] = jnp.zeros_like(ref)

    @pl.when(step_at > 0)
    def _():
        dabuf[BLOCK:, :] = dabuf[0:8, :]
        dsbuf[BLOCK:, :] = dsbuf[0:8, :]

    mask = lower_mask(CHUNK)
    masks = half_masks()
    for chunk in reversed(range(BLOCK // CHUNK)):
        r0 = chunk * CHUNK
        here = pl.ds(r0, CHUNK)
        z = z_ref[here, :]
        step, rate, running, grown, tail = chunk_scalars(z, rate_ref[...])
        running_t = running.T
        stepx[...] = dot(split(step), spread_ref[...])
        grownx[...] = dot(split(grown), spread_ref[...])
        tailx[...] = dot(split(tail), spread_ref[...])
        conv_s = as_ref[here, :]
        sig_s = sigmoid(conv_s)
        b_two, c_two, scores = chunk_scores(conv_s * sig_s)
        b_rows, c_rows = b_two[:, :nstate], c_two[:, :nstate]
        before = sin_ref[chunk, :, :]
        after = dstate[...].astype(bf16)
        carried[...] = dot(c_rows, before)
        pulled[...] = dot(b_rows, after)
        dscores = jnp.zeros((CHUNK, CHUNK), f32)
        inner = jnp.zeros((CHUNK, LANES), f32)
        outer = jnp.zeros((CHUNK, LANES), f32)
        sides = jnp.zeros((CHUNK, LANES), f32)
        for pair in range(pairs):
            lanes = slice(pair * LANES, (pair + 1) * LANES)
            conv = av_ref[here, lanes]
            sig = sigmoid(conv)
            values = conv * sig
            steps = stepx[:, lanes]
            stepped = values * steps
            low = stepped.astype(bf16)
            dy_low = dy_ref[here, lanes]
            dy = dy_low.astype(f32)
            first, second = pair_decay(running, running_t, pair, mask)
            mixing = jnp.concatenate(
                [(scores * first).astype(bf16), (scores * second).astype(bf16)], axis=1
            )
            dy_two = stacked(dy_low, masks)
            scanned = dot(mixing, stacked(low, masks))
            both = jnp.concatenate([mixing[:, :CHUNK], mixing[:, CHUNK:]], axis=0)
            dstepped = dot(both, dy_two, TN)
            dmixing = dot(dy_two, low, NT)
            dscores = dscores + dmixing[:CHUNK] * first + dmixing[CHUNK:] * second
            inside = dy * scanned - low.astype(f32) * dstepped
            u = (dy * grownx[:, lanes]).astype(bf16)
            ubuf[:, lanes] = u
            tails = tailx[:, lanes]
            v = (stepped * tails).astype(bf16)
            vtail[:, lanes] = v
            pull = pulled[:, lanes]
            dstepped = dstepped + tails * pull
            sums = gather_ref[pair * 2 * LANES : (pair + 1) * 2 * LANES, :]
            inner = inner + dot(split(inside), sums[:, :LANES])
            outer = outer + dot(
                jnp.concatenate(
                    [
                        (u.astype(f32) * carried[:, lanes]).astype(bf16),
                        (v.astype(f32) * pull).astype(bf16),
                    ],
                    axis=1,
                ),
                sums[:, LANES:],
            )
            sides = sides + dot(
                jnp.concatenate(
                    [(values * dstepped).astype(bf16), (values * dy).astype(bf16)], axis=1
                ),
                sums[:, LANES:],
            )
            dvalues = steps * dstepped + skip_ref[:, lanes] * dy
            da = dvalues * (sig + values * (1.0 - sig))
            dabuf[here, lanes] = da
            vp = vp_ref[here, lanes]
            dv = jnp.zeros((CHUNK, LANES), f32)
            rows = []
            for tap in range(4):
                moved = da if tap == 3 else dabuf[pl.ds(r0 + 3 - tap, CHUNK), lanes]
                dv = dv + vconv_ref[tap : tap + 1, lanes].astype(f32) * moved
                rows.append(jnp.sum(vp * moved, axis=0, keepdims=True))
            rows.append(jnp.sum(da, axis=0, keepdims=True))
            rows.append(jnp.zeros((3, LANES), f32))
            grad_vconv_ref[:, lanes] += jnp.concatenate(rows, axis=0)
            dvalue[here, lanes] = dv.astype(bf16)
        dlow = dscores.astype(bf16)
        drest = (dscores - dlow.astype(f32)).astype(bf16)
        db = (
            dot(jnp.concatenate([dlow, dlow, drest], axis=0), jnp.concatenate([c_rows, c_two[:, nstate:], c_rows], axis=0), TN)
            + dot(vtail[...], after, NT)
        )
        dc = (
            dot(jnp.concatenate([dlow, dlow, drest], axis=1), jnp.concatenate([b_rows, b_two[:, nstate:], b_rows], axis=0))
            + dot(ubuf[...], before, NT)
        )
        ds = jnp.concatenate([db, dc], axis=1) * (sig_s + conv_s * sig_s * (1.0 - sig_s))
        dsbuf[here, :] = ds
        sp = sp_ref[here, :]
        dpre = jnp.zeros(ds.shape, f32)
        rows = []
        for tap in range(4):
            moved = ds if tap == 3 else dsbuf[pl.ds(r0 + 3 - tap, CHUNK), :]
            dpre = dpre + sconv_ref[tap : tap + 1, :].astype(f32) * moved
            rows.append(jnp.sum(sp * moved, axis=0, keepdims=True))
        rows.append(jnp.sum(ds, axis=0, keepdims=True))
        rows.append(jnp.zeros((3, ds.shape[1]), f32))
        grad_sconv_ref[...] += jnp.concatenate(rows, axis=0)
        dstates[here, :] = dpre.astype(bf16)

        overlap = jnp.sum(before.astype(f32) * dstate[...], axis=0, keepdims=True)
        overlap = jnp.broadcast_to(overlap * grownx[CHUNK - 1 : CHUNK, :], (8, width))
        held = jnp.zeros((8, LANES), f32)
        for pair in range(pairs):
            lanes = slice(pair * LANES, (pair + 1) * LANES)
            sums = gather_ref[pair * 2 * LANES : (pair + 1) * 2 * LANES, :]
            held = held + dot(split(overlap[:, lanes]), sums[:, :LANES])
        spare = jnp.zeros((CHUNK, HALF), f32)
        lower = mask.astype(f32)
        ddecay = (
            dot(lower, inner + jnp.concatenate([outer[:, :HALF], spare], axis=1), TN, HIGHEST)
            + dot(1.0 - lower.T, jnp.concatenate([outer[:, HALF:], spare], axis=1), precision=HIGHEST)
            + held[0:1, :]
        )
        dstep_all = jnp.concatenate([sides[:, :HALF], spare], axis=1) + ddecay * rate
        dz = dstep_all * sigmoid(z)
        dstep[here, :] = dz.astype(bf16)
        skips = jnp.concatenate([sides[:, HALF:], spare], axis=1)
        grad_head_ref[...] += jnp.concatenate(
            [
                jnp.sum(dz, axis=0, keepdims=True),
                jnp.sum(ddecay * step, axis=0, keepdims=True) * rate,
                jnp.sum(skips, axis=0, keepdims=True),
                jnp.zeros((5, LANES), f32),
            ],
            axis=0,
        )
        dstate[...] = grownx[CHUNK - 1 : CHUNK, :] * dstate[...] + dot(c_rows, ubuf[...], TN)

    @pl.when(step_at == pl.num_programs(0) - 1)
    def _():
        dstate_out[...] = dstate[...]
        dahalo[...] = dabuf[0:8, :]
        dshalo[...] = dsbuf[0:8, :]


COST = dict(forward_kernel=4.5, backward_kernel=7, stats_kernel=1, branch_kernel=.6, gate_kernel=2.4, weights_kernel=1.2, normed_grad_kernel=1.2, mixed_kernel=1, input_kernel=1, early_kernel=3, late_kernel=3)


def whole(array):
    return pl.BlockSpec(array.shape, lambda i, at: (0,) * array.ndim)


def call(kernel, blocks, at, ins, outs, scratch, mib=40):
    return pl.pallas_call(
        kernel,
        name=getattr(kernel, "func", kernel).__name__,
        grid_spec=pltpu.PrefetchScalarGridSpec(
            num_scalar_prefetch=1,
            grid=(blocks,),
            in_specs=[whole(a) if s is None else s for a, s in ins],
            out_specs=[s for _, _, s in outs],
            scratch_shapes=scratch,
        ),
        out_shape=[jax.ShapeDtypeStruct(shape, dtype) for shape, dtype, _ in outs],
        cost_estimate=pl.CostEstimate(flops=int(COST.get(getattr(kernel, "func", kernel).__name__, 1)*blocks * 10**9), bytes_accessed=0, transcendentals=0),
        compiler_params=pltpu.CompilerParams(
            dimension_semantics=("arbitrary",), vmem_limit_bytes=mib * 2**20
        ),
    )(at, *[a for a, _ in ins])


def per_device(
    residual_in,
    norm_gain,
    gate_proj,
    value_proj,
    state_proj,
    step_proj,
    value_conv,
    value_shift,
    state_conv,
    state_shift,
    step_bias,
    log_rate,
    skip_gain,
    gated_gain,
    out_proj,
    grad_out,
):
    parts = lax.axis_size("heads")
    two = parts == 2
    rows_here, model = residual_in.shape[1:]
    length = rows_here * parts
    inner = value_conv.shape[1]
    inner_all = inner * parts
    heads = step_bias.shape[0]
    head_width = inner // heads
    pad_heads = heads % 2
    nheads = heads + pad_heads
    width = nheads * head_width
    nstate2 = state_conv.shape[1]
    blocks = length // BLOCK
    chunks = BLOCK // CHUNK
    half_blocks = rows_here // BLOCK if two else blocks

    def wide(a, axis):
        pads = [(0, 0)] * a.ndim
        pads[axis] = (0, width - inner)
        return jnp.pad(a, pads) if width > inner else a

    def lanes_of(a):
        return jnp.pad(a, [(0, 0)] * (a.ndim - 1) + [(0, LANES - a.shape[-1])])

    residual = residual_in[0]
    cot = grad_out[0]
    batch = lax.axis_size("batch")
    fast = two and batch == 16 and width == model and model % BLOCK == 0
    nstate = nstate2 // 2
    place = lax.axis_index("batch").astype(jnp.int32)
    across = lax.axis_index("heads").astype(jnp.int32) if two else jnp.int32(0)
    own_from = lax.axis_index("heads").astype(jnp.int32) * rows_here
    at = jnp.stack([across, place & 1, (place >> 1) & 1, place >> 2, own_from])
    if two:
        swap = [(0, 1), (1, 0)]
        pair_of = lambda a: (a, lax.ppermute(a, "heads", swap))
        add_other = lambda a: lax.ppermute(a, "heads", swap)
    else:

        def pair_of(a):
            full = lax.all_gather(a, "heads", axis=0, tiled=True)
            return (full, full)

        add_other = lambda a: lax.psum(a, "heads") - a

    def hop(a, way):
        mask = {"core": 1, "line": 2}.get(way) or 4 * way
        return lax.ppermute(a, "batch", [(i, i ^ mask) for i in range(batch)])

    own_rows, other_rows = pair_of(residual)
    own_cot, other_cot = pair_of(cot)

    gate_w, value_w = wide(gate_proj, 1), wide(value_proj, 1)
    out_w = wide(out_proj, 0)
    step_w = lanes_of(step_proj)
    gain_in = norm_gain[None, :]
    vconv, vshift = wide(value_conv, 1), wide(value_shift[None, :], 1)
    sshift = state_shift[None, :]
    sbias, rate = lanes_of(step_bias[None, :]), lanes_of(log_rate[None, :])
    skipx = wide(jnp.repeat(skip_gain, head_width)[None, :], 1)
    ggain = wide(gated_gain[None, :], 1)
    head_of = jnp.arange(width) // head_width
    spread = (jnp.arange(LANES)[:, None] == head_of[None, :]).astype(bf16)
    spread = jnp.concatenate([spread, spread], axis=0)
    first = head_of.reshape(-1, 1, LANES, 1)
    column = jnp.arange(2 * LANES)
    top = (column == first) | (column == first + LANES)
    bottom = (column == first) | (column == first + LANES + HALF)
    gather = jnp.concatenate([top, bottom], axis=1).reshape(-1, 2 * LANES).astype(bf16)

    def own_block(i, a):
        return (jnp.clip(i - a[0] * half_blocks, 0, half_blocks - 1), 0)

    def other_block(i, a):
        return (jnp.clip(i - (1 - a[0]) * half_blocks, 0, half_blocks - 1), 0) if two else (0, 0)

    other_read = other_block if two else own_block

    def rows(n, index=lambda i, a: (i, 0)):
        return pl.BlockSpec((BLOCK, n), index)

    along = pl.BlockSpec((8, BLOCK), lambda i, a: (0, i))
    fixed = lambda *shape: pl.BlockSpec(shape, lambda i, a: (0,) * len(shape))
    states_spec = lambda index: pl.BlockSpec((chunks, nstate, width), index)
    big = lambda *shape: pltpu.VMEM(shape, f32)
    low = lambda *shape: pltpu.VMEM(shape, bf16)
    halves = [
        ((rows_here if two else length, model), bf16, rows(model, own_block)),
        ((rows_here if two else BLOCK, model), bf16, rows(model, other_block)),
    ]

    normed, g, y, gg, av, vp, conv_s, sp, z, sin, sq = call(
        functools.partial(forward_kernel, half_blocks),
        blocks,
        at,
        [
            (own_rows, rows(model, own_block)),
            (other_rows, rows(model, other_read)),
            (gain_in, None),
            (gate_w, None),
            (value_w, None),
            (state_proj, None),
            (step_w, None),
            (vconv, None),
            (vshift, None),
            (state_conv, None),
            (sshift, None),
            (sbias, None),
            (rate, None),
            (skipx, None),
            (ggain, None),
            (spread, None),
        ],
        [
            ((length, model), bf16, rows(model)),
            ((length, width), f32, rows(width)),
            ((length, width), f32, rows(width)),
            ((length, width), bf16, rows(width)),
            ((length, width), f32, rows(width)),
            ((length, width), f32, rows(width)),
            ((length, nstate2), f32, rows(nstate2)),
            ((length, nstate2), f32, rows(nstate2)),
            ((length, LANES), f32, rows(LANES)),
            ((blocks * chunks, nstate, width), bf16, states_spec(lambda i, a: (i, 0, 0))),
            ((8, length), f32, along),
        ],
        [
            big(BLOCK, width),
            big(BLOCK + 8, width),
            big(BLOCK + 8, nstate2),
            big(nstate, width),
            big(CHUNK, width),
            big(CHUNK, width),
            big(CHUNK, width),
            big(CHUNK, width),
            low(CHUNK, width),
        ],
    )
    og, stats = call(
        functools.partial(stats_kernel, half_blocks),
        blocks,
        at,
        [
            (own_cot, rows(model, own_block)),
            (other_cot, rows(model, other_read)),
            (gg, rows(width)),
            (sq, along),
            (out_w, None),
        ],
        [((length, width), f32, rows(width)), ((8, length), f32, along)],
        [],
    )
    other_stats = add_other(stats)
    own_along = pl.BlockSpec((8, BLOCK), lambda i, a: (0, i + a[4] // BLOCK))
    branch, branch_sent = call(
        functools.partial(branch_kernel, half_blocks),
        blocks,
        at,
        [(gg, rows(width)), (out_w, None)],
        halves,
        [],
    )

    def other_half(own, sent):
        if two:
            return lax.ppermute(sent, "heads", swap)
        total = lax.psum_scatter(own.astype(f32), "heads", scatter_dimension=0, tiled=True)
        mine = lax.dynamic_slice_in_dim(own, own_from, rows_here, 0).astype(f32)
        return total - mine

    branch_got = other_half(branch, branch_sent)
    if not two:
        branch = lax.dynamic_slice_in_dim(branch, own_from, rows_here, 0)
    if fast:
        pieces = [((model // 2, 2 * model), bf16, fixed(model // 2, 2 * model))] * 2
    else:
        pieces = [
            ((model, width), f32, fixed(model, width)),
            ((width, model), f32, fixed(width, model)),
        ]
    dg, dy, early_a, early_b, grad_gain, norm = call(
        functools.partial(gate_kernel, half_blocks, inner_all, fast),
        blocks,
        at,
        [
            (own_cot, rows(model, own_block)),
            (other_cot, rows(model, other_read)),
            (stats, along),
            (other_stats, along),
            (normed, rows(model)),
            (og, rows(width)),
            (y, rows(width)),
            (g, rows(width)),
            (gg, rows(width)),
            (ggain, None),
            (gate_w, None),
            (branch, pl.BlockSpec(memory_space=pl.ANY)),
        ],
        [
            ((length, width), bf16, rows(width)),
            ((length, width), bf16, rows(width)),
            *pieces,
            ((8, width), f32, fixed(8, width)),
            ((8, model), f32, fixed(8, model)),
        ],
        [big(model, width), big(width, model)] if fast else [],
    )

    def backward(start, count, carry, after=()):
        def behind(n):
            return rows(n, lambda i, a: (start + count - 1 - i, 0))

        def local(n):
            return rows(n, lambda i, a: (count - 1 - i, 0))

        states = states_spec(lambda i, a: (start + count - 1 - i, 0, 0))
        vectors = [(nstate, width), (8, width), (8, nstate2), (8, width), (8, nstate2), (8, LANES)]
        out = call(
            functools.partial(backward_kernel, bool(carry), len(after)),
            count,
            at,
            [
                (dy, behind(width)),
                (av, behind(width)),
                (vp, behind(width)),
                (conv_s, behind(nstate2)),
                (sp, behind(nstate2)),
                (z, behind(LANES)),
                (sin, states),
                (vconv, None),
                (state_conv, None),
                (rate, None),
                (skipx, None),
                (spread, None),
                (gather, None),
                *[(c, None) for c in carry],
                *[(a, pl.BlockSpec(memory_space=pl.ANY)) for a in after],
            ],
            [
                ((count * BLOCK, width), bf16, local(width)),
                ((count * BLOCK, nstate2), bf16, local(nstate2)),
                ((count * BLOCK, LANES), bf16, local(LANES)),
                *[(shape, f32, fixed(*shape)) for shape in vectors],
            ],
            [
                big(BLOCK + 8, width),
                big(BLOCK + 8, nstate2),
                big(nstate, width),
                big(CHUNK, width),
                big(CHUNK, width),
                big(CHUNK, width),
                big(CHUNK, width),
                big(CHUNK, width),
                low(CHUNK, width),
                low(CHUNK, width),
            ],
        )
        return out[:3], out[3:]

    cut = blocks // 2
    behind = ()
    if fast:
        ((kept, sent),) = stage(at, [("fold", 2, [early_a, hop(early_b, "core")], 2, False)])
        early = [kept, hop(sent, "line")]
        behind = (kept,)
    low_b, carry = backward(cut, blocks - cut, (), behind)
    if fast:
        ((kept, *sent),) = stage(at, [("fold", 3, early, 4, False)])
        early = [kept] + [hop(a, k + 1) for k, a in enumerate(sent)]
        behind = (kept, branch_got)
    low_a, carry = backward(0, cut, carry, behind)
    vec, svec, head = carry[3:]
    lows = [(a, rows(a.shape[1], lambda i, at: (jnp.minimum(i, cut - 1), 0))) for a in low_a]
    lows += [(a, rows(a.shape[1], lambda i, at: (jnp.maximum(i - cut, 0), 0))) for a in low_b]
    behind = early[1:] if fast else ()

    if fast:
        shape = (model // 2, width + nstate2 + LANES)
        pieces = [(shape, bf16, fixed(*shape))] * 2
    else:
        shapes = [(model, width), (model, nstate2), (model, LANES), (8, model)]
        pieces = [(shape, f32, fixed(*shape)) for shape in shapes]
    late = call(
        functools.partial(weights_kernel, fast, len(behind), cut),
        blocks,
        at,
        [
            (normed, rows(model)),
            *lows,
            (value_w, None),
            (state_proj, None),
            (step_w, None),
            (gain_in, None),
            (vec, None),
            (svec, None),
            (head, None),
            (grad_gain, None),
            (norm, None),
            *[(a, pl.BlockSpec(memory_space=pl.ANY)) for a in behind],
        ],
        pieces,
        [big(model, width), big(model, nstate2), big(model, LANES)],
    )
    ng, ng_sent = call(
        functools.partial(normed_grad_kernel, half_blocks, cut),
        blocks,
        at,
        [
            (dg, rows(width)),
            *lows,
            (gate_w, None),
            (value_w, None),
            (state_proj, None),
            (step_w, None),
        ],
        halves,
        [],
    )

    mixed, token = call(
        functools.partial(mixed_kernel, inner_all),
        rows_here // BLOCK,
        at,
        [
            (residual, rows(model)),
            (branch, rows(model)),
            (branch_got, rows(model)),
            (stats, own_along),
            (other_stats, own_along),
        ],
        [((rows_here, model), f32, rows(model)), ((8, LANES), f32, fixed(8, LANES))],
        [],
    )
    ng_got = other_half(ng, ng_sent)
    if not two:
        ng = lax.dynamic_slice_in_dim(ng, own_from, rows_here, 0)
    grad_input, token_b = call(
        input_kernel,
        rows_here // BLOCK,
        at,
        [
            (residual, rows(model)),
            (cot, rows(model)),
            (ng, rows(model)),
            (ng_got, rows(model)),
            (gain_in, None),
        ],
        [((rows_here, model), f32, rows(model)), ((8, LANES), f32, fixed(8, LANES))],
        [],
    )

    if fast:
        kept, sent = late
        steps = [("fold", 2, [kept, hop(sent, "core")], 2, True), ("fold", 3, early, 1, False)]
        (kept, sent), (early,) = stage(at, steps)
        got = hop(sent, "line")
        early = [early] + [hop(early, k) for k in (1, 2, 3)]
        steps = [("fold", 3, [kept, got], 4, True), ("join", 3, early)]
        (kept, *sent), (early,) = stage(at, steps, (ng, token))
        got = [hop(a, k + 1) for k, a in enumerate(sent)]
        early = [early, hop(early, "line")]
        steps = [("fold", 3, [kept, *got], 1, True), ("join", 2, early)]
        (done,), (early,) = stage(at, steps, (ng_got,))
        theirs = lax.ppermute(done[:, width:], "heads", swap)
        done = call(
            heads_kernel,
            1,
            at,
            [(done, None), (theirs, None)],
            [(done.shape, bf16, fixed(*done.shape))],
            [],
            16,
        )[0]
        grad_gate, grad_out_proj, token_c = call(
            early_kernel,
            1,
            at,
            [(early, None), (hop(early, "core"), None)],
            [((model, model), f32, fixed(model, model))] * 2
            + [((8, LANES), f32, fixed(8, LANES))],
            [],
        )
        ((done,),) = stage(at, [("join", 3, [done] + [hop(done, k) for k in (1, 2, 3)])])
        steps = [("join", 2, [done, hop(done, "line")])]
        ((done,),) = stage(at, steps, (token_b, token_c))
        shapes = [
            (model, width),
            (model, nstate2),
            (model, heads),
            (4, width),
            (width,),
            (width,),
            (model,),
            (4, nstate2),
            (nstate2,),
            (heads,),
            (heads,),
            (heads,),
        ]
        (
            grad_value,
            grad_state,
            grad_step,
            grad_vconv,
            grad_vshift,
            grad_ggain,
            grad_norm,
            grad_sconv,
            grad_sshift,
            grad_bias,
            grad_rate,
            grad_skip,
        ) = call(
            late_kernel,
            1,
            at,
            [(done, None), (hop(done, "core"), None)],
            [(shape, f32, fixed(*shape)) for shape in shapes],
            [big(model, LANES)],
        )
        return (
            mixed[None],
            grad_input[None],
            grad_norm,
            grad_gate,
            grad_value,
            grad_state,
            grad_step,
            grad_vconv,
            grad_vshift,
            grad_sconv,
            grad_sshift,
            grad_bias,
            grad_rate,
            grad_skip,
            grad_ggain,
            grad_out_proj,
        )
    grad_value, grad_state, grad_step, norm = late
    grad_gate, grad_value, grad_out_proj, grad_step, vec, head, grad_gain = lax.psum(
        (early_a, grad_value, early_b, grad_step, vec, head, grad_gain), "batch"
    )
    grad_state, svec, norm = lax.psum((grad_state, svec, norm), ("batch", "heads"))
    norm, ggrad = norm[0], grad_gain[0]
    return (
        mixed[None],
        grad_input[None],
        norm,
        grad_gate[:, :inner],
        grad_value[:, :inner],
        grad_state,
        grad_step[:, :heads],
        vec[:4, :inner],
        vec[4, :inner],
        svec[:4],
        svec[4],
        head[0, :heads],
        head[1, :heads],
        head[2, :heads],
        ggrad[:inner],
        grad_out_proj[:inner],
    )


def solution(mesh):
    return jax.shard_map(
        per_device,
        mesh=mesh,
        in_specs=(
            P("batch", "heads", None),
            P(),
            P(None, "heads"),
            P(None, "heads"),
            P(),
            P(None, "heads"),
            P(None, "heads"),
            P("heads"),
            P(),
            P(),
            P("heads"),
            P("heads"),
            P("heads"),
            P("heads"),
            P("heads", None),
            P("batch", "heads", None),
        ),
        out_specs=(
            P("batch", "heads", None),
            P("batch", "heads", None),
            P(),
            P(None, "heads"),
            P(None, "heads"),
            P(),
            P(None, "heads"),
            P(None, "heads"),
            P("heads"),
            P(),
            P(),
            P("heads"),
            P("heads"),
            P("heads"),
            P("heads"),
            P("heads", None),
        ),
        check_vma=False,
    )
```

time: 374 us -> 191 us (0.51)
  blocking collectives: 125 us -> 0 us
  waiting for transfers between devices: 104 us -> 48.1 us
  other arithmetic: 28.5 us -> 0.78 us
  starting transfers between devices: 7.52 us -> 32.6 us
  Pallas kernels: 72.3 us -> 87.5 us
  between operations: 14.3 us -> 1.12 us
    psum x2 -> x0, blocking collectives: 125 us -> none  [the longest x1 66.4 us: per_device(): lax.psum((grad_sconv, grad_norm), ('batch', 'heads'))]
    psum x2 -> x0, waiting for transfers between devices: 99 us -> none  [the longest x1 99 us: per_device(): lax.psum(tuple((a.astype(bf16) for a in (grad_gate, grad_value, grad_out_...]
    ppermute x2 -> x23, waiting for transfers between devices: 0.01 us -> 35.6 us  [the longest x20 32.5 us: hop(): return lax.ppermute(a, 'batch', [(i, i ^ mask) for i in range(batch)])]
    ppermute x2 -> x23, starting transfers between devices: 2.15 us -> 27.5 us  [the longest x20 24.1 us: hop(): return lax.ppermute(a, 'batch', [(i, i ^ mask) for i in range(batch)])]
    convert_element_type x12 -> x0, other arithmetic: 18.9 us -> none  [the longest x4 7.28 us: per_device(): a.astype(bf16)]
    pallas_call x4 -> x20, Pallas kernels: 72.3 us -> 87.5 us  [call(): pl.pallas_call(kernel, name=getattr(kernel, 'func', kernel).__name__, gri...]
    ppermute x2, waiting for transfers between devices: 4.17 us -> 12.5 us  [per_device(): pair_of = lambda a: (a, lax.ppermute(a, 'heads', swap))]
    unnamed x48 -> x66, local copies, waits for them, and re-layouts: 6.1 us -> 13.5 us
  transfers between devices with their start and end apart: 7 -> 26, of which waited for: 3 -> 12; matrix products, arithmetic and copies ran while one was open for 8% -> 4% of each run, Pallas kernels for 6% -> 34%
where the time goes in v2:
time: 191 us; the launch traced here: 189 us
  Pallas kernels  87.5 us (46%)
  waiting for transfers between devices  48.1 us (25%)
  starting transfers between devices  32.6 us (17%)
  local copies, waits for them, and re-layouts  18.4 us (10%)
    pallas_call x20, Pallas kernels, call(): pl.pallas_call(kernel, name=getattr(kernel, 'func', kernel).__name__, gri...  87.5 us
    ppermute x20, waiting for transfers between devices, hop(): return lax.ppermute(a, 'batch', [(i, i ^ mask) for i in range(batch)])  32.5 us
    ppermute x20, starting transfers between devices, hop(): return lax.ppermute(a, 'batch', [(i, i ^ mask) for i in range(batch)])  24.1 us
    unnamed x66, local copies, waits for them, and re-layouts  13.5 us
    ppermute x2, waiting for transfers between devices, per_device(): pair_of = lambda a: (a, lax.ppermute(a, 'heads', swap))  12.5 us
  transfers between devices with their start and end apart: 26, of which 12 were waited for; matrix products, arithmetic and copies ran while one was open for 4% of the time, Pallas kernels for 34%

profile of v2, /device:TPU:0, one launch (start us, length us, event | category | flops | bytes accessed | tf_op | source)
XLA Modules:
  0.0 188.6 jit_solution(17930274808336467130)
XLA Ops:
  0.6 3.0 %collective-permute-start = (bf16[512,768]{1,0:T(8,128)(2,1)}, bf16[512,768]{1,0:T(8,128)(2,1)S(1)}, u32[]{:S(2)}, u32[]{:S(2)}) collective-permute-start(bf16[512,768]{1,0:T(8,128)(2,1)} %bitcast.14), channel_id=1, source_target_pairs={{0,1},{1,0},{2,3},{3,2},{4,5},{5,4},{6,7},{7,6},{8,9},{9,8},{10,11... | collective-permute-start | bytes 2359304 | tf_op jit(solution)/shard_map/ppermute | solution.py:802
  9.7 12.5 %collective-permute-done.other_ref = bf16[512,768]{1,0:T(8,128)(2,1)S(1)} collective-permute-done((bf16[512,768]{1,0:T(8,128)(2,1)}, bf16[512,768]{1,0:T(8,128)(2,1)S(1)}, u32[]{:S(2)}, u32[]{:S(2)}) %collective-permute-start) | collective-permute-done | bytes 786464 | tf_op jit(solution)/shard_map/ppermute | solution.py:802
  28.3 17.7 %forward_kernel.1 = (bf16[1024,768]{1,0:T(8,128)(2,1)S(1)}, f32[1024,768]{1,0:T(8,128)}, f32[1024,768]{1,0:T(8,128)}, bf16[1024,768]{1,0:T(8,128)(2,1)S(1)}, f32...) custom-call(s32[5]{0:T(128)S(1)} %stack.23.at_ref, ...), custom_call_target="tpu_custom_call" | custom-call | flops 17999998976 | tf_op jit(solution)/shard_map/forward_kernel/pallas_call | solution.py:731
  46.0 3.5 %stats_kernel.1 = (f32[1024,768]{1,0:T(8,128)S(1)}, f32[8,1024]{1,0:T(8,128)S(1)}) custom-call(s32[5]{0:T(128)S(1)} %stack.23.at_ref, bf16[512,768]{1,0:T(8,128)(2,1)S(1)} %bitcast.19, bf16[512,768]{1,0:T(8,128)(2,1)S(1)} %collective-permute-done.2.other_ref, bf16[1024,768]{1,0:T(8,128)(2,1)S(1)} %get-tuple-element.91.gg_ref, ...), custom_call_target="tpu_custom_call" | custom-call | flops 4000000000 | tf_op jit(solution)/shard_map/stats_kernel/pallas_call | solution.py:731
  53.2 2.6 %branch_kernel.1 = (bf16[512,768]{1,0:T(8,128)(2,1)S(1)}, bf16[512,768]{1,0:T(8,128)(2,1)S(1)}) custom-call(s32[5]{0:T(128)S(1)} %stack.23.at_ref, bf16[1024,768]{1,0:T(8,128)(2,1)S(1)} %get-tuple-element.91.gg_ref, bf16[768,768]{1,0:T(8,128)(2,1)S(1)} %copy-done), custom_call_target="tpu_custom_call" | custom-call | flops 2400000000 | tf_op jit(solution)/shard_map/branch_kernel/pallas_call | solution.py:731
  55.9 9.4 %gate_kernel.1 = (bf16[1024,768]{1,0:T(8,128)(2,1)S(1)}, bf16[1024,768]{1,0:T(8,128)(2,1)S(1)}, bf16[384,1536]{1,0:T(8,128)(2,1)S(1)}, bf16[384,1536]{1,0:T(8,12...) custom-call(s32[5]{0:T(128)S(1)} %stack.23.at_ref, bf16[512,768]{1,0:T(8,128)(2,1)S(1)} %bitcast.20, ...), custom_call_target="tpu_custom_call" | custom-call | flops 9600000000 | tf_op jit(solution)/shard_map/gate_kernel/pallas_call | solution.py:731
  72.3 13.7 %backward_kernel.2 = (bf16[512,768]{1,0:T(8,128)(2,1)S(1)}, bf16[512,256]{1,0:T(8,128)(2,1)S(1)}, bf16[512,128]{1,0:T(8,128)(2,1)S(1)}, f32[128,768]{1,0:T(8,128...) custom-call(s32[5]{0:T(128)S(1)} %stack.23.at_ref, ...), custom_call_target="tpu_custom_call" | custom-call | flops 14000000000 | tf_op jit(solution)/shard_map/backward_kernel/pallas_call | solution.py:731
  88.6 2.6 %collective-permute-start.8 = (bf16[48,1536]{1,0:T(8,128)(2,1)S(1)}, bf16[48,1536]{1,0:T(8,128)(2,1)S(1)}, u32[]{:S(2)}, u32[]{:S(2)}) collective-permute-start(bf16[48,1536]{1,0:T(8,128)(2,1)S(1)} %get-tuple-element.135), channel_id=1, source_target_pairs={{0,16},{2,18},{4,20},{6,22},{8,24},{10,26},{12,28},{14,30},{16,0},... | collective-permute-start | bytes 442376 | tf_op jit(solution)/shard_map/ppermute | solution.py:814
  92.9 14.3 %backward_kernel.3 = (bf16[512,768]{1,0:T(8,128)(2,1)S(1)}, bf16[512,256]{1,0:T(8,128)(2,1)S(1)}, bf16[512,128]{1,0:T(8,128)(2,1)S(1)}, f32[128,768]{1,0:T(8,128...) custom-call(s32[5]{0:T(128)S(1)} %stack.23.at_ref, ...), custom_call_target="tpu_custom_call" | custom-call | flops 14000000000 | tf_op jit(solution)/shard_map/backward_kernel/pallas_call | solution.py:731
  108.7 4.8 %weights_kernel.1 = (bf16[384,1152]{1,0:T(8,128)(2,1)S(1)}, bf16[384,1152]{1,0:T(8,128)(2,1)S(1)}) custom-call(s32[5]{0:T(128)S(1)} %stack.23.at_ref, bf16[1024,768]{1,0:T(8,128)(2,1)S(1)} %copy-done.16, bf16[512,768]{1,0:T(8,128)(2,1)S(1)} %get-tuple-element.120.refs_0_, bf16[512,256]{1,0:T(8,128)(2,1)S(1)} %get-tuple-element.121.refs_1_, ...), custom_call_target="tpu_custom_call" | custom-call | flops 4800000000 | tf_op jit(solution)/shard_map/weights_kernel/pallas_call | solution.py:731
  113.5 2.4 %collective-permute-done.10.refs_1_ = bf16[384,1152]{1,0:T(8,128)(2,1)S(1)} collective-permute-done((bf16[384,1152]{1,0:T(8,128)(2,1)S(1)}, bf16[384,1152]{1,0:T(8,128)(2,1)S(1)}, u32[]{:S(2)}, u32[]{:S(2)}) %collective-permute-start.10) | collective-permute-done | bytes 884768 | tf_op jit(solution)/shard_map/ppermute | solution.py:814
  117.8 4.9 %normed_grad_kernel.1 = (bf16[512,768]{1,0:T(8,128)(2,1)S(1)}, bf16[512,768]{1,0:T(8,128)(2,1)S(1)}) custom-call(s32[5]{0:T(128)S(1)} %stack.23.at_ref, bf16[1024,768]{1,0:T(8,128)(2,1)S(1)} %get-tuple-element.101.dg_ref, bf16[512,768]{1,0:T(8,128)(2,1)S(1)} %get-tuple-element.120.refs_0_, bf16[512,256]{1,0:T(8,128)(2,1)S(1)} %get-tuple-element.121.refs_1_, ...), custom_call_target="tpu_custom_call" | custom-call | flops 4800000000 | tf_op jit(solution)/shard_map/normed_grad_kernel/pallas_call | solution.py:731
  124.6 3.5 %collective-permute-start.13 = (bf16[48,1536]{1,0:T(8,128)(2,1)S(1)}, bf16[48,1536]{1,0:T(8,128)(2,1)S(1)}, u32[]{:S(2)}, u32[]{:S(2)}) collective-permute-start(bf16[48,1536]{1,0:T(8,128)(2,1)S(1)} %get-tuple-element.141.refs_2_), channel_id=1, source_target_pairs={{0,16},{2,18},{4,20},{6,22},{8,24},{10,26},{12,28},{14,30},{16,0},... | collective-permute-start | bytes 442376 | tf_op jit(solution)/shard_map/ppermute | solution.py:814
  128.3 2.1 %mixed_kernel.1 = (f32[512,768]{1,0:T(8,128)}, f32[8,128]{1,0:T(8,128)S(1)}) custom-call(s32[5]{0:T(128)S(1)} %stack.23.at_ref, bf16[512,768]{1,0:T(8,128)(2,1)S(1)} %bitcast.16, bf16[512,768]{1,0:T(8,128)(2,1)S(1)} %get-tuple-element.92.own_ref._, bf16[512,768]{1,0:T(8,128)(2,1)S(1)} %collective-permute-done.1.other_ref.refs_7_, ...), custom_call_target="tpu_custom_call" | custom-call | flops 2000000000 | tf_op jit(solution)/shard_map/mixed_kernel/pallas_call | solution.py:731
  131.4 7.8 %collective-permute-done.13.refs_4_ = bf16[48,1536]{1,0:T(8,128)(2,1)S(1)} collective-permute-done((bf16[48,1536]{1,0:T(8,128)(2,1)S(1)}, bf16[48,1536]{1,0:T(8,128)(2,1)S(1)}, u32[]{:S(2)}, u32[]{:S(2)}) %collective-permute-start.13) | collective-permute-done | bytes 147488 | tf_op jit(solution)/shard_map/ppermute | solution.py:814
  141.6 2.3 %collective-permute-start.15 = (bf16[48,1152]{1,0:T(8,128)(2,1)S(1)}, bf16[48,1152]{1,0:T(8,128)(2,1)S(1)}, u32[]{:S(2)}, u32[]{:S(2)}) collective-permute-start(bf16[48,1152]{1,0:T(8,128)(2,1)S(1)} %get-tuple-element.144), channel_id=1, source_target_pairs={{0,8},{2,10},{4,12},{6,14},{8,0},{10,2},{12,4},{14,6},{16,24},{18,... | collective-permute-start | bytes 331784 | tf_op jit(solution)/shard_map/ppermute | solution.py:814
  147.7 6.2 %collective-permute-done.16.refs_2_ = bf16[48,1152]{1,0:T(8,128)(2,1)S(1)} collective-permute-done((bf16[48,1152]{1,0:T(8,128)(2,1)S(1)}, bf16[48,1152]{1,0:T(8,128)(2,1)S(1)}, u32[]{:S(2)}, u32[]{:S(2)}) %collective-permute-start.16) | collective-permute-done | bytes 110624 | tf_op jit(solution)/shard_map/ppermute | solution.py:814
  155.6 3.2 %collective-permute-done.19.other_ref = bf16[48,384]{1,0:T(8,128)(2,1)S(1)} collective-permute-done((bf16[48,384]{1,0:T(8,128)(2,1)S(1)}, bf16[48,384]{1,0:T(8,128)(2,1)S(1)}, u32[]{:S(2)}, u32[]{:S(2)}) %collective-permute-start.19) | collective-permute-done | bytes 36896 | tf_op jit(solution)/shard_map/ppermute | solution.py:1130
  159.5 2.5 %collective-permute-start.20 = (bf16[48,1152]{1,0:T(8,128)(2,1)S(1)}, bf16[48,1152]{1,0:T(8,128)(2,1)S(1)}, u32[]{:S(2)}, u32[]{:S(2)}) collective-permute-start(bf16[48,1152]{1,0:T(8,128)(2,1)S(1)} %heads_kernel.1.refs_0_), channel_id=1, source_target_pairs={{0,8},{2,10},{4,12},{6,14},{8,0},{10,2},{12,4},{14,6},{16,24},{18,... | collective-permute-start | bytes 331784 | tf_op jit(solution)/shard_map/ppermute | solution.py:814
  165.8 7.0 %collective-permute-done.21.refs_2_ = bf16[48,1152]{1,0:T(8,128)(2,1)S(1)} collective-permute-done((bf16[48,1152]{1,0:T(8,128)(2,1)S(1)}, bf16[48,1152]{1,0:T(8,128)(2,1)S(1)}, u32[]{:S(2)}, u32[]{:S(2)}) %collective-permute-start.21) | collective-permute-done | bytes 110624 | tf_op jit(solution)/shard_map/ppermute | solution.py:814
  174.9 2.3 %input_kernel.1 = (f32[512,768]{1,0:T(8,128)}, f32[8,128]{1,0:T(8,128)S(1)}) custom-call(s32[5]{0:T(128)S(1)} %stack.23.at_ref, bf16[512,768]{1,0:T(8,128)(2,1)S(1)} %bitcast.17, bf16[512,768]{1,0:T(8,128)(2,1)S(1)} %bitcast.21, bf16[512,768]{1,0:T(8,128)(2,1)S(1)} %get-tuple-element.126.own_ref.refs_6_, ...), custom_call_target="tpu_custom_call" | custom-call | flops 2000000000 | tf_op jit(solution)/shard_map/input_kernel/pallas_call | solution.py:731
  177.2 3.0 %early_kernel.1 = (f32[768,768]{1,0:T(8,128)}, f32[768,768]{1,0:T(8,128)}, f32[8,128]{1,0:T(8,128)S(1)}) custom-call(s32[5]{0:T(128)S(1)} %stack.23.at_ref, bf16[384,1536]{1,0:T(8,128)(2,1)S(1)} %get-tuple-element.150.own_ref, bf16[384,1536]{1,0:T(8,128)(2,1)S(1)} %collective-permute-done.24.other_ref), custom_call_target="tpu_custom_call" | custom-call | flops 3000000000 | tf_op jit(solution)/shard_map/early_kernel/pallas_call | solution.py:731
  182.9 2.4 %collective-permute-done.25.other_ref = bf16[384,1152]{1,0:T(8,128)(2,1)S(1)} collective-permute-done((bf16[384,1152]{1,0:T(8,128)(2,1)S(1)}, bf16[384,1152]{1,0:T(8,128)(2,1)S(1)}, u32[]{:S(2)}, u32[]{:S(2)}) %collective-permute-start.25) | collective-permute-done | bytes 884768 | tf_op jit(solution)/shard_map/ppermute | solution.py:814
  185.3 2.5 %late_kernel.1 = (f32[768,768]{1,0:T(8,128)}, f32[768,256]{1,0:T(8,128)}, f32[768,12]{1,0:T(8,128)S(1)}, f32[4,768]{1,0:T(4,128)}, f32[768]{0:T(1024)}, /*index=...) custom-call(s32[5]{0:T(128)S(1)} %stack.23.at_ref, ...), custom_call_target="tpu_custom_call" | custom-call | flops 3000000000 | tf_op jit(solution)/shard_map/late_kernel/pallas_call | solution.py:731
  (132 shorter events, 51.3 us)
Async XLA Ops:
  0.6 21.6 %collective-permute-start = (bf16[512,768]{1,0:T(8,128)(2,1)}, bf16[512,768]{1,0:T(8,128)(2,1)S(1)}, u32[]{:S(2)}, u32[]{:S(2)}) collective-permute-start(bf16[512,768]{1,0:T(8,128)(2,1)} %bitcast.14), channel_id=1, source_target_pairs={{0,1},{1,0},{2,3},{3,2},{4,5},{5,4},{6,7},{7,6},{8,9},{9,8},{10,11... | collective-permute-start | bytes 2359304 | tf_op jit(solution)/shard_map/ppermute | solution.py:802
  3.6 42.3 %collective-permute-start.2 = (bf16[512,768]{1,0:T(8,128)(2,1)}, bf16[512,768]{1,0:T(8,128)(2,1)S(1)}, u32[]{:S(2)}, u32[]{:S(2)}) collective-permute-start(bf16[512,768]{1,0:T(8,128)(2,1)} %bitcast.18), channel_id=1, source_target_pairs={{0,1},{1,0},{2,3},{3,2},{4,5},{5,4},{6,7},{7,6},{8,9},{9,8},{10,11... | collective-permute-start | bytes 2359304 | tf_op jit(solution)/shard_map/ppermute | solution.py:802
  51.2 4.7 %collective-permute-start.3 = (f32[8,1024]{1,0:T(8,128)S(1)}, f32[8,1024]{1,0:T(8,128)S(1)}, u32[]{:S(2)}, u32[]{:S(2)}) collective-permute-start(f32[8,1024]{1,0:T(8,128)S(1)} %get-tuple-element.95.here_ref), channel_id=1, source_target_pairs={{0,1},{1,0},{2,3},{3,2},{4,5},{5,4},{6,7},{7,6},{8,9},{9,8},{10,11... | collective-permute-start | bytes 98312 | tf_op jit(solution)/shard_map/ppermute | solution.py:803
  65.3 2.9 %collective-permute-start.4 = (bf16[384,1536]{1,0:T(8,128)(2,1)S(1)}, bf16[384,1536]{1,0:T(8,128)(2,1)S(1)}, u32[]{:S(2)}, u32[]{:S(2)}) collective-permute-start(bf16[384,1536]{1,0:T(8,128)(2,1)S(1)} %get-tuple-element.110), channel_id=1, source_target_pairs={{0,2},{2,0},{4,6},{6,4},{8,10},{10,8},{12,14},{14,12},{16,18},{18,... | collective-permute-start | bytes 3538952 | tf_op jit(solution)/shard_map/ppermute | solution.py:814
  66.1 25.3 %collective-permute-start.1 = (bf16[512,768]{1,0:T(8,128)(2,1)S(1)}, bf16[512,768]{1,0:T(8,128)(2,1)S(1)}, u32[]{:S(2)}, u32[]{:S(2)}) collective-permute-start(bf16[512,768]{1,0:T(8,128)(2,1)S(1)} %get-tuple-element.93), channel_id=1, source_target_pairs={{0,1},{1,0},{2,3},{3,2},{4,5},{5,4},{6,7},{7,6},{8,9},{9,8},{10,11... | collective-permute-start | bytes 2359304 | tf_op jit(solution)/shard_map/ppermute | solution.py:932
  69.5 16.6 %collective-permute-start.5 = (bf16[192,1536]{1,0:T(8,128)(2,1)S(1)}, bf16[192,1536]{1,0:T(8,128)(2,1)S(1)}, u32[]{:S(2)}, u32[]{:S(2)}) collective-permute-start(bf16[192,1536]{1,0:T(8,128)(2,1)S(1)} %get-tuple-element.118), channel_id=1, source_target_pairs={{0,4},{2,6},{4,0},{6,2},{8,12},{10,14},{12,8},{14,10},{16,20},{18,... | collective-permute-start | bytes 1769480 | tf_op jit(solution)/shard_map/ppermute | solution.py:814
  87.0 20.2 %collective-permute-start.7 = (bf16[48,1536]{1,0:T(8,128)(2,1)S(1)}, bf16[48,1536]{1,0:T(8,128)(2,1)S(1)}, u32[]{:S(2)}, u32[]{:S(2)}) collective-permute-start(bf16[48,1536]{1,0:T(8,128)(2,1)S(1)} %get-tuple-element.134), channel_id=1, source_target_pairs={{0,8},{2,10},{4,12},{6,14},{8,0},{10,2},{12,4},{14,6},{16,24},{18,... | collective-permute-start | bytes 442376 | tf_op jit(solution)/shard_map/ppermute | solution.py:814
  88.6 18.6 %collective-permute-start.8 = (bf16[48,1536]{1,0:T(8,128)(2,1)S(1)}, bf16[48,1536]{1,0:T(8,128)(2,1)S(1)}, u32[]{:S(2)}, u32[]{:S(2)}) collective-permute-start(bf16[48,1536]{1,0:T(8,128)(2,1)S(1)} %get-tuple-element.135), channel_id=1, source_target_pairs={{0,16},{2,18},{4,20},{6,22},{8,24},{10,26},{12,28},{14,30},{16,0},... | collective-permute-start | bytes 442376 | tf_op jit(solution)/shard_map/ppermute | solution.py:814
  91.2 16.0 %collective-permute-start.9 = (bf16[48,1536]{1,0:T(8,128)(2,1)S(1)}, bf16[48,1536]{1,0:T(8,128)(2,1)S(1)}, u32[]{:S(2)}, u32[]{:S(2)}) collective-permute-start(bf16[48,1536]{1,0:T(8,128)(2,1)S(1)} %get-tuple-element.136), channel_id=1, source_target_pairs={{0,24},{2,26},{4,28},{6,30},{8,16},{10,18},{12,20},{14,22},{16,8},... | collective-permute-start | bytes 442376 | tf_op jit(solution)/shard_map/ppermute | solution.py:814
  117.2 22.0 %collective-permute-start.11 = (bf16[192,1152]{1,0:T(8,128)(2,1)S(1)}, bf16[192,1152]{1,0:T(8,128)(2,1)S(1)}, u32[]{:S(2)}, u32[]{:S(2)}) collective-permute-start(bf16[192,1152]{1,0:T(8,128)(2,1)S(1)} %get-tuple-element.140), channel_id=1, source_target_pairs={{0,4},{2,6},{4,0},{6,2},{8,12},{10,14},{12,8},{14,10},{16,20},{18,... | collective-permute-start | bytes 1327112 | tf_op jit(solution)/shard_map/ppermute | solution.py:814
  122.7 23.6 %collective-permute-start.6 = (bf16[512,768]{1,0:T(8,128)(2,1)S(1)}, bf16[512,768]{1,0:T(8,128)(2,1)S(1)}, u32[]{:S(2)}, u32[]{:S(2)}) collective-permute-start(bf16[512,768]{1,0:T(8,128)(2,1)S(1)} %get-tuple-element.127), channel_id=1, source_target_pairs={{0,1},{1,0},{2,3},{3,2},{4,5},{5,4},{6,7},{7,6},{8,9},{9,8},{10,11... | collective-permute-start | bytes 2359304 | tf_op jit(solution)/shard_map/ppermute | solution.py:932
  124.0 7.4 %collective-permute-start.12 = (bf16[48,1536]{1,0:T(8,128)(2,1)S(1)}, bf16[48,1536]{1,0:T(8,128)(2,1)S(1)}, u32[]{:S(2)}, u32[]{:S(2)}) collective-permute-start(bf16[48,1536]{1,0:T(8,128)(2,1)S(1)} %get-tuple-element.141.refs_2_), channel_id=1, source_target_pairs={{0,8},{2,10},{4,12},{6,14},{8,0},{10,2},{12,4},{14,6},{16,24},{18,... | collective-permute-start | bytes 442376 | tf_op jit(solution)/shard_map/ppermute | solution.py:814
  124.6 14.6 %collective-permute-start.13 = (bf16[48,1536]{1,0:T(8,128)(2,1)S(1)}, bf16[48,1536]{1,0:T(8,128)(2,1)S(1)}, u32[]{:S(2)}, u32[]{:S(2)}) collective-permute-start(bf16[48,1536]{1,0:T(8,128)(2,1)S(1)} %get-tuple-element.141.refs_2_), channel_id=1, source_target_pairs={{0,16},{2,18},{4,20},{6,22},{8,24},{10,26},{12,28},{14,30},{16,0},... | collective-permute-start | bytes 442376 | tf_op jit(solution)/shard_map/ppermute | solution.py:814
  128.1 11.1 %collective-permute-start.14 = (bf16[48,1536]{1,0:T(8,128)(2,1)S(1)}, bf16[48,1536]{1,0:T(8,128)(2,1)S(1)}, u32[]{:S(2)}, u32[]{:S(2)}) collective-permute-start(bf16[48,1536]{1,0:T(8,128)(2,1)S(1)} %get-tuple-element.141.refs_2_), channel_id=1, source_target_pairs={{0,24},{2,26},{4,28},{6,30},{8,16},{10,18},{12,20},{14,22},{16,8},... | collective-permute-start | bytes 442376 | tf_op jit(solution)/shard_map/ppermute | solution.py:814
  140.1 13.9 %collective-permute-start.18 = (bf16[192,1536]{1,0:T(8,128)(2,1)S(1)}, bf16[192,1536]{1,0:T(8,128)(2,1)S(1)}, u32[]{:S(2)}, u32[]{:S(2)}) collective-permute-start(bf16[192,1536]{1,0:T(8,128)(2,1)S(1)} %get-tuple-element.147.refs_4_), channel_id=1, source_target_pairs={{0,4},{2,6},{4,0},{6,2},{8,12},{10,14},{12,8},{14,10},{16,20},{18,... | collective-permute-start | bytes 1769480 | tf_op jit(solution)/shard_map/ppermute | solution.py:814
  141.6 6.1 %collective-permute-start.15 = (bf16[48,1152]{1,0:T(8,128)(2,1)S(1)}, bf16[48,1152]{1,0:T(8,128)(2,1)S(1)}, u32[]{:S(2)}, u32[]{:S(2)}) collective-permute-start(bf16[48,1152]{1,0:T(8,128)(2,1)S(1)} %get-tuple-element.144), channel_id=1, source_target_pairs={{0,8},{2,10},{4,12},{6,14},{8,0},{10,2},{12,4},{14,6},{16,24},{18,... | collective-permute-start | bytes 331784 | tf_op jit(solution)/shard_map/ppermute | solution.py:814
  143.9 10.0 %collective-permute-start.16 = (bf16[48,1152]{1,0:T(8,128)(2,1)S(1)}, bf16[48,1152]{1,0:T(8,128)(2,1)S(1)}, u32[]{:S(2)}, u32[]{:S(2)}) collective-permute-start(bf16[48,1152]{1,0:T(8,128)(2,1)S(1)} %get-tuple-element.145), channel_id=1, source_target_pairs={{0,16},{2,18},{4,20},{6,22},{8,24},{10,26},{12,28},{14,30},{16,0},... | collective-permute-start | bytes 331784 | tf_op jit(solution)/shard_map/ppermute | solution.py:814
  144.8 9.1 %collective-permute-start.17 = (bf16[48,1152]{1,0:T(8,128)(2,1)S(1)}, bf16[48,1152]{1,0:T(8,128)(2,1)S(1)}, u32[]{:S(2)}, u32[]{:S(2)}) collective-permute-start(bf16[48,1152]{1,0:T(8,128)(2,1)S(1)} %get-tuple-element.146), channel_id=1, source_target_pairs={{0,24},{2,26},{4,28},{6,30},{8,16},{10,18},{12,20},{14,22},{16,8},... | collective-permute-start | bytes 331784 | tf_op jit(solution)/shard_map/ppermute | solution.py:814
  154.7 22.5 %collective-permute-start.24 = (bf16[384,1536]{1,0:T(8,128)(2,1)S(1)}, bf16[384,1536]{1,0:T(8,128)(2,1)S(1)}, u32[]{:S(2)}, u32[]{:S(2)}) collective-permute-start(bf16[384,1536]{1,0:T(8,128)(2,1)S(1)} %get-tuple-element.150.own_ref), channel_id=1, source_target_pairs={{0,2},{2,0},{4,6},{6,4},{8,10},{10,8},{12,14},{14,12},{16,18},{18,... | collective-permute-start | bytes 3538952 | tf_op jit(solution)/shard_map/ppermute | solution.py:814
  154.8 4.0 %collective-permute-start.19 = (bf16[48,384]{1,0:T(8,128)(2,1)S(1)}, bf16[48,384]{1,0:T(8,128)(2,1)S(1)}, u32[]{:S(2)}, u32[]{:S(2)}) collective-permute-start(bf16[48,384]{1,0:T(8,128)(2,1)S(1)} %slice.3), channel_id=1, source_target_pairs={{0,1},{1,0},{2,3},{3,2},{4,5},{5,4},{6,7},{7,6},{8,9},{9,8},{10,11... | collective-permute-start | bytes 110600 | tf_op jit(solution)/shard_map/ppermute | solution.py:1130
  159.5 6.3 %collective-permute-start.20 = (bf16[48,1152]{1,0:T(8,128)(2,1)S(1)}, bf16[48,1152]{1,0:T(8,128)(2,1)S(1)}, u32[]{:S(2)}, u32[]{:S(2)}) collective-permute-start(bf16[48,1152]{1,0:T(8,128)(2,1)S(1)} %heads_kernel.1.refs_0_), channel_id=1, source_target_pairs={{0,8},{2,10},{4,12},{6,14},{8,0},{10,2},{12,4},{14,6},{16,24},{18,... | collective-permute-start | bytes 331784 | tf_op jit(solution)/shard_map/ppermute | solution.py:814
  162.0 10.8 %collective-permute-start.21 = (bf16[48,1152]{1,0:T(8,128)(2,1)S(1)}, bf16[48,1152]{1,0:T(8,128)(2,1)S(1)}, u32[]{:S(2)}, u32[]{:S(2)}) collective-permute-start(bf16[48,1152]{1,0:T(8,128)(2,1)S(1)} %heads_kernel.1.refs_0_), channel_id=1, source_target_pairs={{0,16},{2,18},{4,20},{6,22},{8,24},{10,26},{12,28},{14,30},{16,0},... | collective-permute-start | bytes 331784 | tf_op jit(solution)/shard_map/ppermute | solution.py:814
  163.1 9.8 %collective-permute-start.22 = (bf16[48,1152]{1,0:T(8,128)(2,1)S(1)}, bf16[48,1152]{1,0:T(8,128)(2,1)S(1)}, u32[]{:S(2)}, u32[]{:S(2)}) collective-permute-start(bf16[48,1152]{1,0:T(8,128)(2,1)S(1)} %heads_kernel.1.refs_0_), channel_id=1, source_target_pairs={{0,24},{2,26},{4,28},{6,30},{8,16},{10,18},{12,20},{14,22},{16,8},... | collective-permute-start | bytes 331784 | tf_op jit(solution)/shard_map/ppermute | solution.py:814
  173.4 8.8 %collective-permute-start.23 = (bf16[192,1152]{1,0:T(8,128)(2,1)S(1)}, bf16[192,1152]{1,0:T(8,128)(2,1)S(1)}, u32[]{:S(2)}, u32[]{:S(2)}) collective-permute-start(bf16[192,1152]{1,0:T(8,128)(2,1)S(1)} %stage_kernel.12.refs_0_), channel_id=1, source_target_pairs={{0,4},{2,6},{4,0},{6,2},{8,12},{10,14},{12,8},{14,10},{16,20},{18,... | collective-permute-start | bytes 1327112 | tf_op jit(solution)/shard_map/ppermute | solution.py:814
  (34 other events, 240.3 us)

commit v3 on v2

--- a/solution.py
+++ b/solution.py
@@ -12,6 +12,8 @@
 BLOCK = 256
 CHUNK = 128
 LANES = 128
+HALF = LANES // 2
+QUAD = 2 * LANES
 LOG2E = 1.4426950408889634
 f32 = jnp.float32
 bf16 = jnp.bfloat16
@@ -31,6 +33,32 @@
     return 0.5 * jnp.tanh(0.5 * v) + 0.5
 
 
+def silu(v):
+    half = 0.5 * v
+    return half + half * jnp.tanh(half)
+
+
+def silu_slope(v):
+    half = 0.5 * v
+    t = jnp.tanh(half)
+    out = half + half * t
+    sig = 0.5 + 0.5 * t
+    return out, sig + out * (1.0 - sig)
+
+
+def causal_back(buf, slab, r0, grad, pre, taps, extra):
+    buf[slab, pl.ds(r0, CHUNK), :] = grad
+    lanes = slice(slab * LANES, (slab + 1) * LANES)
+    out, rows = 0.0, []
+    for tap in range(4):
+        moved = grad if tap == 3 else buf[slab, pl.ds(r0 + 3 - tap, CHUNK), :]
+        out = out + taps[tap : tap + 1, lanes].astype(f32) * moved
+        rows.append(jnp.sum(pre * moved, axis=0, keepdims=True))
+    rows.append(jnp.sum(grad, axis=0, keepdims=True))
+    rows += [extra, jnp.zeros((2, LANES), f32)]
+    return out, jnp.concatenate(rows, axis=0)
+
+
 def split(v):
     high = v.astype(bf16)
     return jnp.concatenate([high, (v - high.astype(f32)).astype(bf16)], axis=1)
@@ -42,41 +70,61 @@
     )
 
 
-def chunk_scalars(z, log_rate):
+def chunk_mask(strict=False):
+    row = lax.broadcasted_iota(jnp.int32, (BLOCK, BLOCK), 0)
+    column = lax.broadcasted_iota(jnp.int32, (BLOCK, BLOCK), 1)
+    ordered = row > column if strict else row >= column
+    return (ordered & (row // CHUNK == column // CHUNK)).astype(bf16)
+
+
+def block_scalars(z, log_rate, spread):
     step = jnp.maximum(z, 0.0) + jnp.log1p(jnp.exp(-jnp.abs(z)))
     rate = -jnp.exp(log_rate)
-    decay = step * (rate * LOG2E)
-    ones = lower_mask(CHUNK).astype(f32)
-    running = dot(ones, decay, precision=HIGHEST)
-    grown = jnp.exp2(running)
-    tail = jnp.exp2(running[CHUNK - 1 : CHUNK, :] - running)
-    return step, rate, running, grown, tail
-
-
-def chunk_scores(states):
-    n = states.shape[1] // 2
-    b, c = split(states[:, :n]), split(states[:, n:])
+    decay = jnp.where(lax.broadcasted_iota(jnp.int32, (1, LANES), 1) < 32, step * (rate * LOG2E), 0.0)
+    high = decay.astype(bf16).astype(f32)
+    middle = (decay - high).astype(bf16).astype(f32)
+    packed = high + pltpu.roll(middle, 32, 1) + pltpu.roll(decay - high - middle, 64, 1)
+    sums = dot(chunk_mask(), packed.astype(bf16))
+    running = sums + pltpu.roll(sums, LANES - 32, 1) + pltpu.roll(sums, LANES - 64, 1)
+    last = [running[r + CHUNK - 1 : r + CHUNK, :] for r in range(0, BLOCK, CHUNK)]
+    tail = [jnp.exp2(v - running[k * CHUNK : (k + 1) * CHUNK, :]) for k, v in enumerate(last)]
+    tail = step * jnp.concatenate(tail, axis=0)
+    wide = dot(jnp.concatenate([split(jnp.exp2(running)), split(tail)], axis=0), spread)
+    return step, running, running - jnp.log2(step), wide[:BLOCK], wide[BLOCK:]
+
+
+def causal(buf, slab, taps, shift):
+    lanes = slice(slab * LANES, (slab + 1) * LANES)
+    conv = shift[:, lanes].astype(f32)
+    for tap in range(4):
+        conv = conv + taps[tap : tap + 1, lanes].astype(f32) * buf[slab, pl.ds(5 + tap, BLOCK), :]
+    return conv
+
+
+def chunk_scores(b_rows, c_rows):
+    n = b_rows.shape[1]
+    b, c = split(b_rows), split(c_rows)
     left = jnp.concatenate([c, c[:, :n]], axis=1)
     right = jnp.concatenate([b[:, :n], b[:, :n], b[:, n:]], axis=1)
     return b, c, dot(left, right, NT)
 
 
-def pair_decay(running, running_t, pair, mask):
-    out = []
-    for head in (2 * pair, 2 * pair + 1):
-        spread = running[:, head : head + 1] - running_t[head : head + 1, :]
-        out.append(jnp.exp2(jnp.where(mask, spread, -1e30)))
-    return out
-
-
-def half_masks():
+def quad_mixing(scores, running, shifted_t, quad, mask):
+    factors, mixes = [], []
+    for head in range(4 * quad, 4 * quad + 4):
+        spread = running[:, head : head + 1] - shifted_t[head : head + 1, :]
+        factors.append(jnp.exp2(jnp.where(mask, spread, -1e30)))
+        mixes.append((scores * factors[-1]).astype(bf16))
+    return factors, mixes
+
+
+def heads_apart(left, right):
     lane = lax.broadcasted_iota(jnp.int32, (1, LANES), 1)
-    first = (lane < LANES // 2).astype(bf16)
-    return first, 1 - first
-
-
-def stacked(rows, masks):
-    return jnp.concatenate([rows * masks[0], rows * masks[1]], axis=0)
+    first = (lane < HALF).astype(bf16)
+    zero = jnp.zeros(left.shape, bf16)
+    rows = [jnp.concatenate([left * m, zero], axis=1) for m in (first, 1 - first)]
+    rows += [jnp.concatenate([zero, right * m], axis=1) for m in (first, 1 - first)]
+    return jnp.concatenate(rows, axis=0)
 
 
 def forward_kernel(
@@ -109,84 +157,94 @@
     z_ref,
     sin_ref,
     sq_ref,
-    gbuf,
+    step_ref,
+    running_ref,
+    shifted_ref,
+    grownx,
+    tailx,
     vbuf,
     sbuf,
     state,
-    stepx,
-    grownx,
-    tailx,
     carried,
+    values,
+    low,
     vtail,
 ):
     step_at = pl.program_id(0)
-    pairs = vbuf.shape[1] // LANES
+    pairs = vbuf.shape[0]
     nstate = state.shape[0]
 
     @pl.when(step_at == 0)
     def _():
         state[...] = jnp.zeros_like(state)
-        vbuf[0:8, :] = jnp.zeros((8, vbuf.shape[1]), f32)
-        sbuf[0:8, :] = jnp.zeros((8, sbuf.shape[1]), f32)
+        for buf in (vbuf, sbuf):
+            buf[:, 0:8, :] = jnp.zeros((buf.shape[0], 8, LANES), f32)
 
     mine = (step_at // half_blocks) == at_ref[0]
-    rows = jnp.where(mine, own_ref[...].astype(f32), other_ref[...].astype(f32))
+    rows = jnp.where(mine, own_ref[...], other_ref[...]).astype(f32)
     scale = lax.rsqrt(jnp.mean(rows * rows, axis=1, keepdims=True) + EPSILON)
     normed = (rows * scale * gain_ref[...].astype(f32)).astype(bf16)
     normed_ref[...] = normed
-    gbuf[...] = dot(normed, gate_w[...])
-    g_ref[...] = gbuf[...]
-    vbuf[8:, :] = dot(normed, value_w[...])
-    vp_ref[...] = vbuf[8:, :]
-    sbuf[8:, :] = dot(normed, state_w[...])
-    sp_ref[...] = sbuf[8:, :]
-    z_ref[...] = dot(normed, step_w[...]) + sbias_ref[...]
-
-    mask = lower_mask(CHUNK)
-    masks = half_masks()
-    for chunk in range(BLOCK // CHUNK):
-        r0 = chunk * CHUNK
-        here = pl.ds(r0, CHUNK)
-        step, _, running, grown, tail = chunk_scalars(z_ref[here, :], rate_ref[...])
-        running_t = running.T
-        stepx[...] = dot(split(step), spread_ref[...])
-        grownx[...] = dot(split(grown), spread_ref[...])
-        tailx[...] = dot(split(tail), spread_ref[...])
-        conv = sshift_ref[...].astype(f32)
-        for tap in range(4):
-            conv = conv + sconv_ref[tap : tap + 1, :].astype(f32) * sbuf[pl.ds(r0 + 5 + tap, CHUNK), :]
-        as_ref[here, :] = conv
-        b_two, c_two, scores = chunk_scores(conv * sigmoid(conv))
-        b_rows, c_rows = b_two[:, :nstate], c_two[:, :nstate]
+    z = dot(normed, step_w[...]) + sbias_ref[...]
+    z_ref[...] = z
+    for out, buf, w in ((sp_ref, sbuf, state_w), (vp_ref, vbuf, value_w)):
+        pre = dot(normed, w[...])
+        out[...] = pre
+        for slab in range(buf.shape[0]):
+            buf[slab, 8:, :] = pre[:, slab * LANES : (slab + 1) * LANES]
+    g_ref[...] = dot(normed, gate_w[...])
+
+    step, running, shifted, grownx[...], tailx[...] = block_scalars(z, rate_ref[...], spread_ref[...])
+    step_ref[...] = step
+    running_ref[...] = running
+    shifted_ref[...] = shifted
+    chunks = range(BLOCK // CHUNK)
+    states = []
+    for slab in range(sbuf.shape[0]):
+        conv = causal(sbuf, slab, sconv_ref, sshift_ref)
+        as_ref[:, slab * LANES : (slab + 1) * LANES] = conv
+        states.append(silu(conv))
+    for pair in range(pairs):
+        lanes = slice(pair * LANES, (pair + 1) * LANES)
+        conv = causal(vbuf, pair, vconv_ref, vshift_ref)
+        av_ref[:, lanes] = conv
+        out = silu(conv)
+        values[:, lanes] = out
+        low[:, lanes] = out.astype(bf16)
+        vtail[:, lanes] = (out * tailx[:, lanes]).astype(bf16)
+    parts = []
+    for chunk in chunks:
+        here = slice(chunk * CHUNK, (chunk + 1) * CHUNK)
+        b_two, c_two, scores = chunk_scores(*(v[here] for v in states))
+        parts.append(scores)
         before = state[...].astype(bf16)
         sin_ref[chunk, :, :] = before
-        carried[...] = dot(c_rows, before)
+        carried[here, :] = dot(c_two[:, :nstate], before)
+        last = grownx[(chunk + 1) * CHUNK - 1 : (chunk + 1) * CHUNK, :]
+        state[...] = last * state[...] + dot(b_two[:, :nstate], vtail[here, :], TN)
+    mask = lower_mask(CHUNK)
+    for chunk in chunks:
+        here = slice(chunk * CHUNK, (chunk + 1) * CHUNK)
+        run = running[here]
+        run_t = shifted[here].T
         squares = jnp.zeros((CHUNK, LANES), f32)
-        for pair in range(pairs):
-            lanes = slice(pair * LANES, (pair + 1) * LANES)
-            conv = vshift_ref[:, lanes].astype(f32)
-            for tap in range(4):
-                moved = vbuf[pl.ds(r0 + 5 + tap, CHUNK), lanes]
-                conv = conv + vconv_ref[tap : tap + 1, lanes].astype(f32) * moved
-            av_ref[here, lanes] = conv
-            values = conv * sigmoid(conv)
-            stepped = values * stepx[:, lanes]
-            vtail[:, lanes] = (stepped * tailx[:, lanes]).astype(bf16)
-            first, second = pair_decay(running, running_t, pair, mask)
-            mixing = jnp.concatenate(
-                [(scores * first).astype(bf16), (scores * second).astype(bf16)], axis=1
+        for quad in range(pairs // 2):
+            _, mixes = quad_mixing(parts[chunk], run, run_t, quad, mask)
+            sides = [slice((2 * quad + k) * LANES, (2 * quad + k + 1) * LANES) for k in range(2)]
+            both = dot(
+                jnp.concatenate(mixes, axis=1), heads_apart(*(low[here, lanes] for lanes in sides))
             )
-            scanned = dot(mixing, stacked(stepped.astype(bf16), masks))
-            scanned = scanned + grownx[:, lanes] * carried[:, lanes] + skip_ref[:, lanes] * values
-            y_ref[here, lanes] = scanned
-            g = gbuf[here, lanes]
-            gated = scanned * (g * sigmoid(g))
-            gg_ref[here, lanes] = (gated * ggain_ref[:, lanes].astype(f32)).astype(bf16)
-            squares = squares + gated * gated
+            for k, lanes in enumerate(sides):
+                scanned = both[:, k * LANES : (k + 1) * LANES]
+                scanned = scanned + grownx[here, lanes] * carried[here, lanes]
+                scanned = scanned + skip_ref[:, lanes] * values[here, lanes]
+                y_ref[here, lanes] = scanned
+                gated = scanned * silu(g_ref[here, lanes])
+                gg_ref[here, lanes] = (gated * ggain_ref[:, lanes].astype(f32)).astype(bf16)
+                squares = squares + gated * gated
         sq_ref[:, here] = dot(jnp.ones((8, LANES), f32), squares, NT, HIGHEST)
-        state[...] = grownx[CHUNK - 1 : CHUNK, :] * state[...] + dot(b_rows, vtail[...], TN)
-    vbuf[0:8, :] = vbuf[BLOCK : BLOCK + 8, :]
-    sbuf[0:8, :] = sbuf[BLOCK : BLOCK + 8, :]
+    for buf in (vbuf, sbuf):
+        buf[:, 0:8, :] = buf[:, BLOCK : BLOCK + 8, :]
 
 
 def stats_kernel(half_blocks, at_ref, own_ref, other_ref, gg_ref, sq_ref, out_w, og_ref, stats_ref):
@@ -198,6 +256,12 @@
     dots = dot(jnp.ones((8, prod.shape[1]), bf16), prod, NT)
     row = lax.broadcasted_iota(jnp.int32, dots.shape, 0)
     stats_ref[...] = jnp.where(row == 0, sq_ref[...], dots)
+
+
+def bring_kernel(at_ref, *refs):
+    count = len(refs) // 2
+    for src, dst in zip(refs[:count], refs[count:]):
+        dst[...] = src[...]
 
 
 def branch_kernel(half_blocks, at_ref, gg_ref, out_w, own_ref, other_ref):
@@ -296,16 +360,16 @@
     second_ref,
     grad_gain_ref,
     norm_ref,
+    scaled_ref,
     *scratch,
 ):
     step_at = pl.program_id(0)
+    here = pl.ds(pl.multiple_of(step_at * BLOCK, BLOCK), BLOCK)
     pairs = og_ref.shape[1] // LANES
     grad_gate, grad_out = scratch if fast else (first_ref, second_ref)
 
     @pl.when(step_at == 0)
     def _():
-        grad_out[...] = jnp.zeros_like(grad_out)
-        grad_gate[...] = jnp.zeros_like(grad_gate)
         grad_gain_ref[...] = jnp.zeros_like(grad_gain_ref)
 
     sums = here_ref[...] + there_ref[...]
@@ -315,63 +379,50 @@
     scale, pull = columns[:, 0:1], columns[:, 1:2]
     mine = (step_at // half_blocks) == at_ref[0]
     cot = jnp.where(mine, own_ref[...], other_ref[...]).astype(f32)
-    scaled = (cot * scale).astype(bf16)
+    scaled_ref[here, :] = (cot * scale).astype(bf16)
     for pair in range(pairs):
         lanes = slice(pair * LANES, (pair + 1) * LANES)
         og = og_ref[:, lanes] * scale
         y = y_ref[:, lanes]
         g = g_ref[:, lanes]
-        sig = sigmoid(g)
-        silu = g * sig
-        gated = y * silu
+        gate, slope = silu_slope(g)
+        gated = y * gate
         grad_gain_ref[0:1, lanes] += jnp.sum(og * gated, axis=0, keepdims=True)
         gated_grad = ggain_ref[:, lanes].astype(f32) * og - gated * pull
-        dy_ref[:, lanes] = (gated_grad * silu).astype(bf16)
-        dg_ref[:, lanes] = (gated_grad * y * (sig + silu * (1.0 - sig))).astype(bf16)
-    grad_out[...] += dot(gg_ref[...], scaled, TN)
-    grad_gate[...] += dot(normed_ref[...], dg_ref[...], TN)
+        dy_ref[:, lanes] = (gated_grad * gate).astype(bf16)
+        dg_ref[here, lanes] = (gated_grad * y * slope).astype(bf16)
 
     @pl.when(step_at == pl.num_programs(0) - 1)
     def _():
+        grad_out[...] = dot(gg_ref[...], scaled_ref[...], TN)
+        grad_gate[...] = dot(normed_ref[...], dg_ref[...], TN)
         norm_ref[...] = row_sums(grad_gate[...], gate_w[...])
         if fast:
             emit(at_ref, (grad_gate, grad_out), (first_ref, second_ref))
 
 
-def weights_kernel(fast, extra, cut, at_ref, normed_ref, *refs):
-    step_at = pl.program_id(0)
+def weights_kernel(fast, extra, at_ref, normed_ref, *refs):
     lows, refs = refs[:6], refs[6:]
     value_w, state_w, step_w, gain_ref, vec_ref, svec_ref, head_ref, ggain_ref, norm_ref = refs[:9]
     outs, acc = refs[9 + extra : -3], refs[-3:]
-
-    @pl.when(step_at == 0)
-    def _():
-        for a in acc:
-            a[...] = jnp.zeros_like(a)
-
-    normed = normed_ref[...]
     for a, early, late in zip(acc, lows[:3], lows[3:]):
-        a[...] += dot(normed, picked(cut, early, late), TN)
-
-    @pl.when(step_at == pl.num_programs(0) - 1)
-    def _():
-        norm = norm_ref[...]
-        for a, w in zip(acc, (value_w, state_w, step_w)):
-            norm = norm + row_sums(a[...], w[...])
-        norm = norm / gain_ref[...].astype(f32)
-        if not fast:
-            for o, a in zip(outs, acc):
-                o[...] = a[...]
-            outs[3][...] = norm
-            return
+        a[...] = dot(normed_ref[...], jnp.concatenate([early[...], late[...]], axis=0), TN)
+    norm = norm_ref[...]
+    for a, w in zip(acc, (value_w, state_w, step_w)):
+        norm = norm + row_sums(a[...], w[...])
+    norm = norm / gain_ref[...].astype(f32)
+    if fast:
         pack_vectors(acc[2], vec_ref, svec_ref, head_ref, ggain_ref, norm)
         emit(at_ref, acc, outs)
+        return
+    for o, a in zip(outs, acc):
+        o[...] = a[...]
+    outs[3][...] = norm
 
 
 VEC_AT = 16
 SVEC_AT = 24
 HEAD_AT = 32
-HALF = LANES // 2
 
 
 def pack_vectors(block, vec_ref, svec_ref, head_ref, ggain_ref, norm):
@@ -464,7 +515,6 @@
         [(a, None) for a in arrays] + [(a, pl.BlockSpec(memory_space=pl.ANY)) for a in after],
         [(shape, bf16, pl.BlockSpec(shape, lambda i, a: (0, 0))) for shape in shapes],
         scratch,
-        24,
     )
     out, results = list(out), []
     for _, _, _, give, _ in plan:
@@ -538,188 +588,185 @@
     as_ref,
     sp_ref,
     z_ref,
+    step_ref,
+    running_ref,
+    shifted_ref,
+    grownx,
+    tailx,
     sin_ref,
     vconv_ref,
     sconv_ref,
     rate_ref,
     skip_ref,
-    spread_ref,
     gather_ref,
     *refs,
 ):
     carries, refs = (refs[:6], refs[6:]) if carried_in else ((), refs)
     refs = refs[extra:]
     dvalue, dstates, dstep, dstate_out, dahalo, dshalo, grad_vconv_ref, grad_sconv_ref, grad_head_ref = refs[:9]
-    dabuf, dsbuf, dstate, stepx, grownx, tailx, carried, pulled, ubuf, vtail = refs[9:]
+    dabuf, dsbuf, dstate, carried, pulled, ubuf, vtail, inner, outer = refs[9:]
     step_at = pl.program_id(0)
-    width = dabuf.shape[1]
+    nstate, width = dstate.shape
+    size = dy_ref.shape[0]
     pairs = width // LANES
-    nstate = dstate.shape[0]
 
     @pl.when(step_at == 0)
     def _():
         if carried_in:
             dstate[...] = carries[0][...]
-            dabuf[BLOCK:, :] = carries[1][...]
-            dsbuf[BLOCK:, :] = carries[2][...]
+            dabuf[:, size:, :] = carries[1][...]
+            dsbuf[:, size:, :] = carries[2][...]
             grad_vconv_ref[...] = carries[3][...]
             grad_sconv_ref[...] = carries[4][...]
             grad_head_ref[...] = carries[5][...]
         else:
             dstate[...] = jnp.zeros_like(dstate)
-            dabuf[BLOCK:, :] = jnp.zeros((8, width), f32)
-            dsbuf[BLOCK:, :] = jnp.zeros((8, dsbuf.shape[1]), f32)
+            for buf in (dabuf, dsbuf):
+                buf[:, size:, :] = jnp.zeros((buf.shape[0], 8, LANES), f32)
             for ref in (grad_vconv_ref, grad_sconv_ref, grad_head_ref):
                 ref[...] = jnp.zeros_like(ref)
 
     @pl.when(step_at > 0)
     def _():
-        dabuf[BLOCK:, :] = dabuf[0:8, :]
-        dsbuf[BLOCK:, :] = dsbuf[0:8, :]
+        for buf in (dabuf, dsbuf):
+            buf[:, size:, :] = buf[:, 0:8, :]
+
+    chunks = [slice(r, r + CHUNK) for r in range(0, size, CHUNK)]
+    zero_row = jnp.zeros((1, LANES), f32)
+    rate = -jnp.exp(rate_ref[...])
+    states, slopes = [], []
+    for slab in range(2):
+        out, slope = silu_slope(as_ref[:, slab * LANES : (slab + 1) * LANES])
+        states.append(out)
+        slopes.append(slope)
+    for pair in range(pairs):
+        lanes = slice(pair * LANES, (pair + 1) * LANES)
+        ubuf[:, lanes] = (dy_ref[:, lanes].astype(f32) * grownx[:, lanes]).astype(bf16)
+    two = [chunk_scores(*(v[here] for v in states)) for here in chunks]
+    helds, afters = [None] * len(chunks), [None] * len(chunks)
+    for chunk in reversed(range(len(chunks))):
+        here = chunks[chunk]
+        b_two, c_two, _ = two[chunk]
+        before = sin_ref[chunk, :, :]
+        last = grownx[here.stop - 1 : here.stop, :]
+        grad = dstate[...]
+        afters[chunk] = grad.astype(bf16)
+        carried[here, :] = dot(c_two[:, :nstate], before)
+        pulled[here, :] = dot(b_two[:, :nstate], afters[chunk])
+        overlap = jnp.sum(before.astype(f32) * grad, axis=0, keepdims=True) * last
+        overlap = jnp.broadcast_to(overlap, (8, width))
+        tall = [split(overlap[:, p * LANES : (p + 1) * LANES]) for p in range(pairs)]
+        held = dot(jnp.concatenate(tall, axis=1), gather_ref[...])[0:1]
+        helds[chunk] = held[:, :LANES] + held[:, LANES:]
+        dstate[...] = last * grad + dot(c_two[:, :nstate], ubuf[here, :], TN)
 
     mask = lower_mask(CHUNK)
-    masks = half_masks()
-    for chunk in reversed(range(BLOCK // CHUNK)):
-        r0 = chunk * CHUNK
-        here = pl.ds(r0, CHUNK)
-        z = z_ref[here, :]
-        step, rate, running, grown, tail = chunk_scalars(z, rate_ref[...])
-        running_t = running.T
-        stepx[...] = dot(split(step), spread_ref[...])
-        grownx[...] = dot(split(grown), spread_ref[...])
-        tailx[...] = dot(split(tail), spread_ref[...])
-        conv_s = as_ref[here, :]
-        sig_s = sigmoid(conv_s)
-        b_two, c_two, scores = chunk_scores(conv_s * sig_s)
-        b_rows, c_rows = b_two[:, :nstate], c_two[:, :nstate]
-        before = sin_ref[chunk, :, :]
-        after = dstate[...].astype(bf16)
-        carried[...] = dot(c_rows, before)
-        pulled[...] = dot(b_rows, after)
+    for chunk in reversed(range(len(chunks))):
+        here = chunks[chunk]
+        b_two, c_two, scores = two[chunk]
+        run = running_ref[here, :]
+        run_t = shifted_ref[here, :].T
         dscores = jnp.zeros((CHUNK, CHUNK), f32)
-        inner = jnp.zeros((CHUNK, LANES), f32)
-        outer = jnp.zeros((CHUNK, LANES), f32)
-        sides = jnp.zeros((CHUNK, LANES), f32)
-        for pair in range(pairs):
-            lanes = slice(pair * LANES, (pair + 1) * LANES)
-            conv = av_ref[here, lanes]
-            sig = sigmoid(conv)
-            values = conv * sig
-            steps = stepx[:, lanes]
-            stepped = values * steps
-            low = stepped.astype(bf16)
-            dy_low = dy_ref[here, lanes]
-            dy = dy_low.astype(f32)
-            first, second = pair_decay(running, running_t, pair, mask)
-            mixing = jnp.concatenate(
-                [(scores * first).astype(bf16), (scores * second).astype(bf16)], axis=1
-            )
-            dy_two = stacked(dy_low, masks)
-            scanned = dot(mixing, stacked(low, masks))
-            both = jnp.concatenate([mixing[:, :CHUNK], mixing[:, CHUNK:]], axis=0)
-            dstepped = dot(both, dy_two, TN)
-            dmixing = dot(dy_two, low, NT)
-            dscores = dscores + dmixing[:CHUNK] * first + dmixing[CHUNK:] * second
-            inside = dy * scanned - low.astype(f32) * dstepped
-            u = (dy * grownx[:, lanes]).astype(bf16)
-            ubuf[:, lanes] = u
-            tails = tailx[:, lanes]
-            v = (stepped * tails).astype(bf16)
-            vtail[:, lanes] = v
-            pull = pulled[:, lanes]
-            dstepped = dstepped + tails * pull
-            sums = gather_ref[pair * 2 * LANES : (pair + 1) * 2 * LANES, :]
-            inner = inner + dot(split(inside), sums[:, :LANES])
-            outer = outer + dot(
-                jnp.concatenate(
-                    [
-                        (u.astype(f32) * carried[:, lanes]).astype(bf16),
-                        (v.astype(f32) * pull).astype(bf16),
-                    ],
-                    axis=1,
-                ),
-                sums[:, LANES:],
-            )
-            sides = sides + dot(
-                jnp.concatenate(
-                    [(values * dstepped).astype(bf16), (values * dy).astype(bf16)], axis=1
-                ),
-                sums[:, LANES:],
-            )
-            dvalues = steps * dstepped + skip_ref[:, lanes] * dy
-            da = dvalues * (sig + values * (1.0 - sig))
-            dabuf[here, lanes] = da
-            vp = vp_ref[here, lanes]
-            dv = jnp.zeros((CHUNK, LANES), f32)
-            rows = []
-            for tap in range(4):
-                moved = da if tap == 3 else dabuf[pl.ds(r0 + 3 - tap, CHUNK), lanes]
-                dv = dv + vconv_ref[tap : tap + 1, lanes].astype(f32) * moved
-                rows.append(jnp.sum(vp * moved, axis=0, keepdims=True))
-            rows.append(jnp.sum(da, axis=0, keepdims=True))
-            rows.append(jnp.zeros((3, LANES), f32))
-            grad_vconv_ref[:, lanes] += jnp.concatenate(rows, axis=0)
-            dvalue[here, lanes] = dv.astype(bf16)
+        for quad in range(pairs // 2):
+            factors, mixes = quad_mixing(scores, run, run_t, quad, mask)
+            both = [slice((2 * quad + k) * LANES, (2 * quad + k + 1) * LANES) for k in range(2)]
+            values, slope = zip(*(silu_slope(av_ref[here, lanes]) for lanes in both))
+            low = [v.astype(bf16) for v in values]
+            dy_low = [dy_ref[here, lanes] for lanes in both]
+            apart = heads_apart(*low)
+            scanned = dot(jnp.concatenate(mixes, axis=1), apart)
+            dsteps = dot(jnp.concatenate(mixes, axis=0), heads_apart(*dy_low), TN)
+            for k, lanes in enumerate(both):
+                pair = 2 * quad + k
+                own = slice(k * LANES, (k + 1) * LANES)
+                dmixing = dot(dy_low[k], apart[2 * k * CHUNK : 2 * (k + 1) * CHUNK, own], NT)
+                dscores = dscores + dmixing[:, :CHUNK] * factors[2 * k]
+                dscores = dscores + dmixing[:, CHUNK:] * factors[2 * k + 1]
+                wide = slice(2 * pair * LANES, (2 * pair + 1) * LANES)
+                wide_b = slice((2 * pair + 1) * LANES, (2 * pair + 2) * LANES)
+                dy = dy_low[k].astype(f32)
+                dvalues = dsteps[:, own]
+                pulls = low[k].astype(f32) * dvalues
+                inside = dy * scanned[:, own] - pulls + ubuf[here, lanes].astype(f32) * carried[here, lanes]
+                high = inside.astype(bf16)
+                inner[here, wide] = high
+                inner[here, wide_b] = (inside - high.astype(f32)).astype(bf16)
+                tails, pull = tailx[here, lanes], pulled[here, lanes]
+                v = (values[k] * tails).astype(bf16)
+                vtail[here, lanes] = v
+                outer[here, wide] = pulls.astype(bf16)
+                outer[here, wide_b] = (v.astype(f32) * pull).astype(bf16)
+                da = (dvalues + tails * pull + skip_ref[:, lanes] * dy) * slope[k]
+                skips = jnp.sum(values[k] * dy, axis=0, keepdims=True)
+                dv, rows = causal_back(dabuf, pair, here.start, da, vp_ref[here, lanes], vconv_ref, skips)
+                grad_vconv_ref[:, lanes] += rows
+                dvalue[here, lanes] = dv.astype(bf16)
         dlow = dscores.astype(bf16)
         drest = (dscores - dlow.astype(f32)).astype(bf16)
-        db = (
-            dot(jnp.concatenate([dlow, dlow, drest], axis=0), jnp.concatenate([c_rows, c_two[:, nstate:], c_rows], axis=0), TN)
-            + dot(vtail[...], after, NT)
+        b_rows, c_rows = b_two[:, :nstate], c_two[:, :nstate]
+        cross = dot(
+            jnp.concatenate([vtail[here, :], ubuf[here, :]], axis=0),
+            jnp.concatenate([afters[chunk], sin_ref[chunk, :, :]], axis=0),
+            NT,
         )
-        dc = (
-            dot(jnp.concatenate([dlow, dlow, drest], axis=1), jnp.concatenate([b_rows, b_two[:, nstate:], b_rows], axis=0))
-            + dot(ubuf[...], before, NT)
+        db = cross[:CHUNK, :nstate] + dot(
+            jnp.concatenate([dlow, dlow, drest], axis=0),
+            jnp.concatenate([c_rows, c_two[:, nstate:], c_rows], axis=0),
+            TN,
         )
-        ds = jnp.concatenate([db, dc], axis=1) * (sig_s + conv_s * sig_s * (1.0 - sig_s))
-        dsbuf[here, :] = ds
-        sp = sp_ref[here, :]
-        dpre = jnp.zeros(ds.shape, f32)
-        rows = []
-        for tap in range(4):
-            moved = ds if tap == 3 else dsbuf[pl.ds(r0 + 3 - tap, CHUNK), :]
-            dpre = dpre + sconv_ref[tap : tap + 1, :].astype(f32) * moved
-            rows.append(jnp.sum(sp * moved, axis=0, keepdims=True))
-        rows.append(jnp.sum(ds, axis=0, keepdims=True))
-        rows.append(jnp.zeros((3, ds.shape[1]), f32))
-        grad_sconv_ref[...] += jnp.concatenate(rows, axis=0)
-        dstates[here, :] = dpre.astype(bf16)
-
-        overlap = jnp.sum(before.astype(f32) * dstate[...], axis=0, keepdims=True)
-        overlap = jnp.broadcast_to(overlap * grownx[CHUNK - 1 : CHUNK, :], (8, width))
-        held = jnp.zeros((8, LANES), f32)
-        for pair in range(pairs):
-            lanes = slice(pair * LANES, (pair + 1) * LANES)
-            sums = gather_ref[pair * 2 * LANES : (pair + 1) * 2 * LANES, :]
-            held = held + dot(split(overlap[:, lanes]), sums[:, :LANES])
-        spare = jnp.zeros((CHUNK, HALF), f32)
-        lower = mask.astype(f32)
-        ddecay = (
-            dot(lower, inner + jnp.concatenate([outer[:, :HALF], spare], axis=1), TN, HIGHEST)
-            + dot(1.0 - lower.T, jnp.concatenate([outer[:, HALF:], spare], axis=1), precision=HIGHEST)
-            + held[0:1, :]
+        dc = cross[CHUNK:, nstate:] + dot(
+            jnp.concatenate([dlow, dlow, drest], axis=1),
+            jnp.concatenate([b_rows, b_two[:, nstate:], b_rows], axis=0),
         )
-        dstep_all = jnp.concatenate([sides[:, :HALF], spare], axis=1) + ddecay * rate
-        dz = dstep_all * sigmoid(z)
+        for slab, d in enumerate((db, dc)):
+            lanes = slice(slab * LANES, (slab + 1) * LANES)
+            d = d * slopes[slab][here]
+            dpre, rows = causal_back(dsbuf, slab, here.start, d, sp_ref[here, lanes], sconv_ref, zero_row)
+            grad_sconv_ref[:, lanes] += rows
+            dstates[here, lanes] = dpre.astype(bf16)
+
+    gathered = dot(jnp.concatenate([inner[...], outer[...]], axis=0), gather_ref[...])
+    heads = [jnp.zeros((1, LANES), f32)] * 2
+    for r in range(0, size, BLOCK):
+        here = slice(r, r + BLOCK)
+        sums, outs = gathered[here], gathered[size + r : size + r + BLOCK]
+        ddecay = dot(chunk_mask(), split(sums[:, :LANES] + sums[:, LANES:]), TN)
+        ddecay = ddecay[:, :LANES] + ddecay[:, LANES:]
+        ddecay = ddecay + dot(chunk_mask(True), outs[:, LANES:].astype(bf16))
+        held = [jnp.broadcast_to(helds[k // CHUNK], (CHUNK, LANES)) for k in range(r, r + BLOCK, CHUNK)]
+        ddecay = ddecay + jnp.concatenate(held, axis=0)
+        step = step_ref[here, :]
+        direct = (outs[:, :LANES] + outs[:, LANES:]) / jnp.maximum(step, 1e-37)
+        dz = (direct + ddecay * rate) * sigmoid(z_ref[here, :])
         dstep[here, :] = dz.astype(bf16)
-        skips = jnp.concatenate([sides[:, HALF:], spare], axis=1)
-        grad_head_ref[...] += jnp.concatenate(
-            [
-                jnp.sum(dz, axis=0, keepdims=True),
-                jnp.sum(ddecay * step, axis=0, keepdims=True) * rate,
-                jnp.sum(skips, axis=0, keepdims=True),
-                jnp.zeros((5, LANES), f32),
-            ],
-            axis=0,
-        )
-        dstate[...] = grownx[CHUNK - 1 : CHUNK, :] * dstate[...] + dot(c_rows, ubuf[...], TN)
+        heads[0] = heads[0] + jnp.sum(dz, axis=0, keepdims=True)
+        heads[1] = heads[1] + jnp.sum(ddecay * step, axis=0, keepdims=True) * rate
+    grad_head_ref[...] += jnp.concatenate([*heads, jnp.zeros((6, LANES), f32)], axis=0)
 
     @pl.when(step_at == pl.num_programs(0) - 1)
     def _():
         dstate_out[...] = dstate[...]
-        dahalo[...] = dabuf[0:8, :]
-        dshalo[...] = dsbuf[0:8, :]
-
-
+        vectors = grad_vconv_ref[...]
+        tall = [split(vectors[:, p * LANES : (p + 1) * LANES]) for p in range(pairs)]
+        skips = dot(jnp.concatenate(tall, axis=1), gather_ref[...])
+        grad_head_ref[2:3, :] = skips[5:6, :LANES] + skips[5:6, LANES:]
+        dahalo[...] = dabuf[:, 0:8, :]
+        dshalo[...] = dsbuf[:, 0:8, :]
+
+
+MIB = dict(
+    forward_kernel=14,
+    stats_kernel=8,
+    branch_kernel=8,
+    gate_kernel=16,
+    backward_kernel=22,
+    weights_kernel=14,
+    normed_grad_kernel=12,
+    mixed_kernel=8,
+    input_kernel=8,
+    early_kernel=10,
+    late_kernel=10,
+)
 COST = dict(forward_kernel=4.5, backward_kernel=7, stats_kernel=1, branch_kernel=.6, gate_kernel=2.4, weights_kernel=1.2, normed_grad_kernel=1.2, mixed_kernel=1, input_kernel=1, early_kernel=3, late_kernel=3)
 
 
@@ -727,21 +774,25 @@
     return pl.BlockSpec(array.shape, lambda i, at: (0,) * array.ndim)
 
 
-def call(kernel, blocks, at, ins, outs, scratch, mib=40):
+def call(kernel, blocks, at, ins, outs, scratch, small=True):
+    title = getattr(kernel, "func", kernel).__name__
     return pl.pallas_call(
         kernel,
-        name=getattr(kernel, "func", kernel).__name__,
+        name=title,
         grid_spec=pltpu.PrefetchScalarGridSpec(
             num_scalar_prefetch=1,
             grid=(blocks,),
             in_specs=[whole(a) if s is None else s for a, s in ins],
-            out_specs=[s for _, _, s in outs],
+            out_specs=[out[2] for out in outs],
             scratch_shapes=scratch,
         ),
-        out_shape=[jax.ShapeDtypeStruct(shape, dtype) for shape, dtype, _ in outs],
-        cost_estimate=pl.CostEstimate(flops=int(COST.get(getattr(kernel, "func", kernel).__name__, 1)*blocks * 10**9), bytes_accessed=0, transcendentals=0),
+        out_shape=[
+            pltpu.VMEM(shape, dtype) if rest and rest[0] else jax.ShapeDtypeStruct(shape, dtype)
+            for shape, dtype, _, *rest in outs
+        ],
+        cost_estimate=pl.CostEstimate(flops=int(COST.get(title, 1)*blocks * 10**9), bytes_accessed=0, transcendentals=0),
         compiler_params=pltpu.CompilerParams(
-            dimension_semantics=("arbitrary",), vmem_limit_bytes=mib * 2**20
+            dimension_semantics=("arbitrary",), vmem_limit_bytes=(MIB.get(title, 16) if small else 48) * 2**20
         ),
     )(at, *[a for a, _ in ins])
 
@@ -772,7 +823,7 @@
     inner_all = inner * parts
     heads = step_bias.shape[0]
     head_width = inner // heads
-    pad_heads = heads % 2
+    pad_heads = -heads % 4
     nheads = heads + pad_heads
     width = nheads * head_width
     nstate2 = state_conv.shape[1]
@@ -793,6 +844,7 @@
     batch = lax.axis_size("batch")
     fast = two and batch == 16 and width == model and model % BLOCK == 0
     nstate = nstate2 // 2
+    run = functools.partial(call, small=fast)
     place = lax.axis_index("batch").astype(jnp.int32)
     across = lax.axis_index("heads").astype(jnp.int32) if two else jnp.int32(0)
     own_from = lax.axis_index("heads").astype(jnp.int32) * rows_here
@@ -812,6 +864,18 @@
     def hop(a, way):
         mask = {"core": 1, "line": 2}.get(way) or 4 * way
         return lax.ppermute(a, "batch", [(i, i ^ mask) for i in range(batch)])
+
+    def bring(*arrays):
+        if not fast:
+            return arrays
+        return run(
+            bring_kernel,
+            1,
+            at,
+            [(a, None) for a in arrays],
+            [(a.shape, a.dtype, pl.BlockSpec(a.shape, lambda i, at: (0, 0)), True) for a in arrays],
+            [],
+        )
 
     own_rows, other_rows = pair_of(residual)
     own_cot, other_cot = pair_of(cot)
@@ -828,11 +892,15 @@
     head_of = jnp.arange(width) // head_width
     spread = (jnp.arange(LANES)[:, None] == head_of[None, :]).astype(bf16)
     spread = jnp.concatenate([spread, spread], axis=0)
-    first = head_of.reshape(-1, 1, LANES, 1)
-    column = jnp.arange(2 * LANES)
-    top = (column == first) | (column == first + LANES)
-    bottom = (column == first) | (column == first + LANES + HALF)
-    gather = jnp.concatenate([top, bottom], axis=1).reshape(-1, 2 * LANES).astype(bf16)
+    first = head_of.reshape(-1, 1, LANES, 1) + jnp.arange(2).reshape(1, 2, 1, 1) * LANES
+    gather = (jnp.arange(2 * LANES) == first).reshape(-1, 2 * LANES).astype(bf16)
+
+    gate_w, value_w, state_proj, step_w, out_w, spread, gather = bring(
+        gate_w, value_w, state_proj, step_w, out_w, spread, gather
+    )
+    gain_in, vconv, vshift, state_conv, sshift, sbias, rate, skipx, ggain = bring(
+        gain_in, vconv, vshift, state_conv, sshift, sbias, rate, skipx, ggain
+    )
 
     def own_block(i, a):
         return (jnp.clip(i - a[0] * half_blocks, 0, half_blocks - 1), 0)
@@ -855,7 +923,7 @@
         ((rows_here if two else BLOCK, model), bf16, rows(model, other_block)),
     ]
 
-    normed, g, y, gg, av, vp, conv_s, sp, z, sin, sq = call(
+    normed, g, y, gg, av, vp, conv_s, sp, z, sin, sq, step, running, shifted, grownx, tailx = run(
         functools.partial(forward_kernel, half_blocks),
         blocks,
         at,
@@ -878,31 +946,39 @@
             (spread, None),
         ],
         [
-            ((length, model), bf16, rows(model)),
-            ((length, width), f32, rows(width)),
-            ((length, width), f32, rows(width)),
-            ((length, width), bf16, rows(width)),
-            ((length, width), f32, rows(width)),
-            ((length, width), f32, rows(width)),
-            ((length, nstate2), f32, rows(nstate2)),
-            ((length, nstate2), f32, rows(nstate2)),
-            ((length, LANES), f32, rows(LANES)),
-            ((blocks * chunks, nstate, width), bf16, states_spec(lambda i, a: (i, 0, 0))),
-            ((8, length), f32, along),
+            *[
+                (shape, dtype, spec, fast)
+                for shape, dtype, spec in (
+                    ((length, model), bf16, rows(model)),
+                    ((length, width), f32, rows(width)),
+                    ((length, width), f32, rows(width)),
+                    ((length, width), bf16, rows(width)),
+                    ((length, width), f32, rows(width)),
+                    ((length, width), f32, rows(width)),
+                    ((length, nstate2), f32, rows(nstate2)),
+                    ((length, nstate2), f32, rows(nstate2)),
+                    ((length, LANES), f32, rows(LANES)),
+                    ((blocks * chunks, nstate, width), bf16, states_spec(lambda i, a: (i, 0, 0))),
+                    ((8, length), f32, along),
+                    ((length, LANES), f32, rows(LANES)),
+                    ((length, LANES), f32, rows(LANES)),
+                    ((length, LANES), f32, rows(LANES)),
+                    ((length, width), f32, rows(width)),
+                    ((length, width), f32, rows(width)),
+                )
+            ]
         ],
         [
+            big(width // LANES, BLOCK + 8, LANES),
+            big(nstate2 // LANES, BLOCK + 8, LANES),
+            big(nstate, width),
             big(BLOCK, width),
-            big(BLOCK + 8, width),
-            big(BLOCK + 8, nstate2),
-            big(nstate, width),
-            big(CHUNK, width),
-            big(CHUNK, width),
-            big(CHUNK, width),
-            big(CHUNK, width),
-            low(CHUNK, width),
+            big(BLOCK, width),
+            low(BLOCK, width),
+            low(BLOCK, width),
         ],
     )
-    og, stats = call(
+    og, stats = run(
         functools.partial(stats_kernel, half_blocks),
         blocks,
         at,
@@ -913,12 +989,12 @@
             (sq, along),
             (out_w, None),
         ],
-        [((length, width), f32, rows(width)), ((8, length), f32, along)],
+        [((length, width), f32, rows(width), fast), ((8, length), f32, along)],
         [],
     )
     other_stats = add_other(stats)
     own_along = pl.BlockSpec((8, BLOCK), lambda i, a: (0, i + a[4] // BLOCK))
-    branch, branch_sent = call(
+    branch, branch_sent = run(
         functools.partial(branch_kernel, half_blocks),
         blocks,
         at,
@@ -944,7 +1020,7 @@
             ((model, width), f32, fixed(model, width)),
             ((width, model), f32, fixed(width, model)),
         ]
-    dg, dy, early_a, early_b, grad_gain, norm = call(
+    dg, dy, early_a, early_b, grad_gain, norm = run(
         functools.partial(gate_kernel, half_blocks, inner_all, fast),
         blocks,
         at,
@@ -953,37 +1029,43 @@
             (other_cot, rows(model, other_read)),
             (stats, along),
             (other_stats, along),
-            (normed, rows(model)),
+            (normed, None),
             (og, rows(width)),
             (y, rows(width)),
             (g, rows(width)),
-            (gg, rows(width)),
+            (gg, None),
             (ggain, None),
             (gate_w, None),
             (branch, pl.BlockSpec(memory_space=pl.ANY)),
         ],
         [
-            ((length, width), bf16, rows(width)),
-            ((length, width), bf16, rows(width)),
+            ((length, width), bf16, fixed(length, width), fast),
+            ((length, width), bf16, rows(width), fast),
             *pieces,
             ((8, width), f32, fixed(8, width)),
             ((8, model), f32, fixed(8, model)),
         ],
-        [big(model, width), big(width, model)] if fast else [],
+        [low(length, model)] + ([big(model, width), big(width, model)] if fast else []),
     )
 
     def backward(start, count, carry, after=()):
+        size = 2 * BLOCK if start % 2 == 0 and count % 2 == 0 else BLOCK
+        steps, base = count * BLOCK // size, start * BLOCK // size
+
         def behind(n):
-            return rows(n, lambda i, a: (start + count - 1 - i, 0))
+            return pl.BlockSpec((size, n), lambda i, a: (base + steps - 1 - i, 0))
 
         def local(n):
-            return rows(n, lambda i, a: (count - 1 - i, 0))
-
-        states = states_spec(lambda i, a: (start + count - 1 - i, 0, 0))
-        vectors = [(nstate, width), (8, width), (8, nstate2), (8, width), (8, nstate2), (8, LANES)]
-        out = call(
+            return pl.BlockSpec((size, n), lambda i, a: (steps - 1 - i, 0))
+
+        states = pl.BlockSpec(
+            (size // CHUNK, nstate, width), lambda i, a: (base + steps - 1 - i, 0, 0)
+        )
+        slabs = [(width // LANES, 8, LANES), (nstate2 // LANES, 8, LANES)]
+        vectors = [(nstate, width), *slabs, (8, width), (8, nstate2), (8, LANES)]
+        out = run(
             functools.partial(backward_kernel, bool(carry), len(after)),
-            count,
+            steps,
             at,
             [
                 (dy, behind(width)),
@@ -992,12 +1074,16 @@
                 (conv_s, behind(nstate2)),
                 (sp, behind(nstate2)),
                 (z, behind(LANES)),
+                (step, behind(LANES)),
+                (running, behind(LANES)),
+                (shifted, behind(LANES)),
+                (grownx, behind(width)),
+                (tailx, behind(width)),
                 (sin, states),
                 (vconv, None),
                 (state_conv, None),
                 (rate, None),
                 (skipx, None),
-                (spread, None),
                 (gather, None),
                 *[(c, None) for c in carry],
                 *[(a, pl.BlockSpec(memory_space=pl.ANY)) for a in after],
@@ -1009,16 +1095,15 @@
                 *[(shape, f32, fixed(*shape)) for shape in vectors],
             ],
             [
-                big(BLOCK + 8, width),
-                big(BLOCK + 8, nstate2),
+                big(width // LANES, size + 8, LANES),
+                big(nstate2 // LANES, size + 8, LANES),
                 big(nstate, width),
-                big(CHUNK, width),
-                big(CHUNK, width),
-                big(CHUNK, width),
-                big(CHUNK, width),
-                big(CHUNK, width),
-                low(CHUNK, width),
-                low(CHUNK, width),
+                big(size, width),
+                big(size, width),
+                low(size, width),
+                low(size, width),
+                low(size, 2 * width),
+                low(size, 2 * width),
             ],
         )
         return out[:3], out[3:]
@@ -1046,13 +1131,13 @@
     else:
         shapes = [(model, width), (model, nstate2), (model, LANES), (8, model)]
         pieces = [(shape, f32, fixed(*shape)) for shape in shapes]
-    late = call(
-        functools.partial(weights_kernel, fast, len(behind), cut),
-        blocks,
+    late = run(
+        functools.partial(weights_kernel, fast, len(behind)),
+        1,
         at,
         [
-            (normed, rows(model)),
-            *lows,
+            (normed, None),
+            *[(a, None) for a, _ in lows],
             (value_w, None),
             (state_proj, None),
             (step_w, None),
@@ -1067,7 +1152,7 @@
         pieces,
         [big(model, width), big(model, nstate2), big(model, LANES)],
     )
-    ng, ng_sent = call(
+    ng, ng_sent = run(
         functools.partial(normed_grad_kernel, half_blocks, cut),
         blocks,
         at,
@@ -1083,7 +1168,7 @@
         [],
     )
 
-    mixed, token = call(
+    mixed, token = run(
         functools.partial(mixed_kernel, inner_all),
         rows_here // BLOCK,
         at,
@@ -1100,7 +1185,7 @@
     ng_got = other_half(ng, ng_sent)
     if not two:
         ng = lax.dynamic_slice_in_dim(ng, own_from, rows_here, 0)
-    grad_input, token_b = call(
+    grad_input, token_b = run(
         input_kernel,
         rows_here // BLOCK,
         at,
@@ -1121,23 +1206,23 @@
         (kept, sent), (early,) = stage(at, steps)
         got = hop(sent, "line")
         early = [early] + [hop(early, k) for k in (1, 2, 3)]
-        steps = [("fold", 3, [kept, got], 4, True), ("join", 3, early)]
-        (kept, *sent), (early,) = stage(at, steps, (ng, token))
+        ((kept, *sent),) = stage(at, [("fold", 3, [kept, got], 4, True)], (ng,))
         got = [hop(a, k + 1) for k, a in enumerate(sent)]
+        steps = [("fold", 3, [kept, *got], 1, True), ("join", 3, early)]
+        (done,), (early,) = stage(at, steps, (token,))
         early = [early, hop(early, "line")]
-        steps = [("fold", 3, [kept, *got], 1, True), ("join", 2, early)]
-        (done,), (early,) = stage(at, steps, (ng_got,))
         theirs = lax.ppermute(done[:, width:], "heads", swap)
-        done = call(
+        done = run(
             heads_kernel,
             1,
             at,
             [(done, None), (theirs, None)],
             [(done.shape, bf16, fixed(*done.shape))],
             [],
-            16,
         )[0]
-        grad_gate, grad_out_proj, token_c = call(
+        done = [done] + [hop(done, k) for k in (1, 2, 3)]
+        (done,), (early,) = stage(at, [("join", 3, done), ("join", 2, early)], (token_b,))
+        grad_gate, grad_out_proj, token_c = run(
             early_kernel,
             1,
             at,
@@ -1146,9 +1231,7 @@
             + [((8, LANES), f32, fixed(8, LANES))],
             [],
         )
-        ((done,),) = stage(at, [("join", 3, [done] + [hop(done, k) for k in (1, 2, 3)])])
-        steps = [("join", 2, [done, hop(done, "line")])]
-        ((done,),) = stage(at, steps, (token_b, token_c))
+        ((done,),) = stage(at, [("join", 2, [done, hop(done, "line")])], (token_c,))
         shapes = [
             (model, width),
             (model, nstate2),
@@ -1176,7 +1259,7 @@
             grad_bias,
             grad_rate,
             grad_skip,
-        ) = call(
+        ) = run(
             late_kernel,
             1,
             at,

time: 191 us -> 163 us (0.85); the launches traced: 189 us -> 163 us
  Pallas kernels: 87.5 us -> 72.2 us
  waiting for transfers between devices: 48.1 us -> 43.8 us
  local copies, waits for them, and re-layouts: 18.4 us -> 14.1 us
    pallas_call x20 -> x22, Pallas kernels: 87.5 us -> 72.2 us  [call(): pl.pallas_call(kernel, name=title, grid_spec=pltpu.PrefetchScalarGridSpec...]
    unnamed x66 -> x70, local copies, waits for them, and re-layouts: 13.5 us -> 8.21 us
    ppermute x2, waiting for transfers between devices: 12.5 us -> 9.89 us  [per_device(): pair_of = lambda a: (a, lax.ppermute(a, 'heads', swap))]
  transfers between devices with their start and end apart: 26 -> 26, of which waited for: 12 -> 15; matrix products, arithmetic and copies ran while one was open for 4% -> 5% of each run, Pallas kernels for 34% -> 32%
where the time goes in v3:
time: 163 us
  Pallas kernels  72.2 us (44%)
  waiting for transfers between devices  43.8 us (27%)
  starting transfers between devices  31.2 us (19%)
  local copies, waits for them, and re-layouts  14.1 us (9%)
    pallas_call x22, Pallas kernels, call(): pl.pallas_call(kernel, name=title, grid_spec=pltpu.PrefetchScalarGridSpec...  72.2 us
    ppermute x20, waiting for transfers between devices, hop(): return lax.ppermute(a, 'batch', [(i, i ^ mask) for i in range(batch)])  30.9 us
    ppermute x20, starting transfers between devices, hop(): return lax.ppermute(a, 'batch', [(i, i ^ mask) for i in range(batch)])  23.3 us
    ppermute x2, waiting for transfers between devices, per_device(): pair_of = lambda a: (a, lax.ppermute(a, 'heads', swap))  9.89 us
    unnamed x70, local copies, waits for them, and re-layouts  8.21 us
  transfers between devices with their start and end apart: 26, of which 15 were waited for; matrix products, arithmetic and copies ran while one was open for 5% of the time, Pallas kernels for 32%

profile of v3, /device:TPU:0, one launch (start us, length us, event | category | flops | bytes accessed | tf_op | source)
XLA Modules:
  0.0 162.9 jit_solution(5233234881335691835)
XLA Ops:
  0.7 3.0 %collective-permute-start = (bf16[512,768]{1,0:T(8,128)(2,1)}, bf16[512,768]{1,0:T(8,128)(2,1)S(1)}, u32[]{:S(2)}, u32[]{:S(2)}) collective-permute-start(bf16[512,768]{1,0:T(8,128)(2,1)} %bitcast.13), channel_id=1, source_target_pairs={{0,1},{1,0},{2,3},{3,2},{4,5},{5,4},{6,7},{7,6},{8,9},{9,8},{10,11... | collective-permute-start | bytes 2359304 | tf_op jit(solution)/shard_map/ppermute | solution.py:854
  15.8 6.5 %collective-permute-done.other_ref = bf16[512,768]{1,0:T(8,128)(2,1)S(1)} collective-permute-done((bf16[512,768]{1,0:T(8,128)(2,1)}, bf16[512,768]{1,0:T(8,128)(2,1)S(1)}, u32[]{:S(2)}, u32[]{:S(2)}) %collective-permute-start) | collective-permute-done | bytes 786464 | tf_op jit(solution)/shard_map/ppermute | solution.py:854
  22.3 12.5 %forward_kernel.1 = (bf16[1024,768]{1,0:T(8,128)(2,1)S(1)}, f32[1024,768]{1,0:T(8,128)S(1)}, f32[1024,768]{1,0:T(8,128)S(1)}, bf16[1024,768]{1,0:T(8,128)(2,1)S(...) custom-call(s32[5]{0:T(128)S(1)} %stack.23.at_ref, ...), custom_call_target="tpu_custom_call" | custom-call | flops 17999998976 | tf_op jit(solution)/shard_map/forward_kernel/pallas_call | solution.py:779
  34.9 3.4 %collective-permute-done.2.other_ref = bf16[512,768]{1,0:T(8,128)(2,1)S(1)} collective-permute-done((bf16[512,768]{1,0:T(8,128)(2,1)}, bf16[512,768]{1,0:T(8,128)(2,1)S(1)}, u32[]{:S(2)}, u32[]{:S(2)}) %collective-permute-start.2) | collective-permute-done | bytes 786464 | tf_op jit(solution)/shard_map/ppermute | solution.py:854
  38.3 3.5 %stats_kernel.1 = (f32[1024,768]{1,0:T(8,128)S(1)}, f32[8,1024]{1,0:T(8,128)S(1)}) custom-call(s32[5]{0:T(128)S(1)} %stack.23.at_ref, bf16[512,768]{1,0:T(8,128)(2,1)S(1)} %bitcast.18, bf16[512,768]{1,0:T(8,128)(2,1)S(1)} %collective-permute-done.2.other_ref, bf16[1024,768]{1,0:T(8,128)(2,1)S(1)} %get-tuple-element.127.gg_ref, ...), custom_call_target="tpu_custom_call" | custom-call | flops 4000000000 | tf_op jit(solution)/shard_map/stats_kernel/pallas_call | solution.py:779
  43.7 2.6 %branch_kernel.1 = (bf16[512,768]{1,0:T(8,128)(2,1)S(1)}, bf16[512,768]{1,0:T(8,128)(2,1)S(1)}) custom-call(s32[5]{0:T(128)S(1)} %stack.23.at_ref, bf16[1024,768]{1,0:T(8,128)(2,1)S(1)} %get-tuple-element.127.gg_ref, bf16[768,768]{1,0:T(8,128)(2,1)S(1)} %get-tuple-element.128.out_w), custom_call_target="tpu_custom_call" | custom-call | flops 2400000000 | tf_op jit(solution)/shard_map/branch_kernel/pallas_call | solution.py:779
  48.5 7.3 %gate_kernel.1 = (bf16[1024,768]{1,0:T(8,128)(2,1)S(1)}, bf16[1024,768]{1,0:T(8,128)(2,1)S(1)}, bf16[384,1536]{1,0:T(8,128)(2,1)S(1)}, bf16[384,1536]{1,0:T(8,12...) custom-call(s32[5]{0:T(128)S(1)} %stack.23.at_ref, bf16[512,768]{1,0:T(8,128)(2,1)S(1)} %bitcast.19, ...), custom_call_target="tpu_custom_call" | custom-call | flops 9600000000 | tf_op jit(solution)/shard_map/gate_kernel/pallas_call | solution.py:779
  62.7 9.4 %backward_kernel.2 = (bf16[512,768]{1,0:T(8,128)(2,1)S(1)}, bf16[512,256]{1,0:T(8,128)(2,1)S(1)}, bf16[512,128]{1,0:T(8,128)(2,1)S(1)}, f32[128,768]{1,0:T(8,128...) custom-call(s32[5]{0:T(128)S(1)} %stack.23.at_ref, ...), custom_call_target="tpu_custom_call" | custom-call | flops 7000000000 | tf_op jit(solution)/shard_map/backward_kernel/pallas_call | solution.py:779
  72.1 3.4 %collective-permute-done.5.refs_1_ = bf16[192,1536]{1,0:T(8,128)(2,1)S(1)} collective-permute-done((bf16[192,1536]{1,0:T(8,128)(2,1)S(1)}, bf16[192,1536]{1,0:T(8,128)(2,1)S(1)}, u32[]{:S(2)}, u32[]{:S(2)}) %collective-permute-start.5) | collective-permute-done | bytes 589856 | tf_op jit(solution)/shard_map/ppermute | solution.py:866
  77.9 2.6 %collective-permute-start.8 = (bf16[48,1536]{1,0:T(8,128)(2,1)S(1)}, bf16[48,1536]{1,0:T(8,128)(2,1)S(1)}, u32[]{:S(2)}, u32[]{:S(2)}) collective-permute-start(bf16[48,1536]{1,0:T(8,128)(2,1)S(1)} %get-tuple-element.178), channel_id=1, source_target_pairs={{0,16},{2,18},{4,20},{6,22},{8,24},{10,26},{12,28},{14,30},{16,0},... | collective-permute-start | bytes 442376 | tf_op jit(solution)/shard_map/ppermute | solution.py:866
  80.8 10.2 %backward_kernel.3 = (bf16[512,768]{1,0:T(8,128)(2,1)S(1)}, bf16[512,256]{1,0:T(8,128)(2,1)S(1)}, bf16[512,128]{1,0:T(8,128)(2,1)S(1)}, f32[128,768]{1,0:T(8,128...) custom-call(s32[5]{0:T(128)S(1)} %stack.23.at_ref, ...), custom_call_target="tpu_custom_call" | custom-call | flops 7000000000 | tf_op jit(solution)/shard_map/backward_kernel/pallas_call | solution.py:779
  91.6 3.9 %weights_kernel.1 = (bf16[384,1152]{1,0:T(8,128)(2,1)S(1)}, bf16[384,1152]{1,0:T(8,128)(2,1)S(1)}) custom-call(s32[5]{0:T(128)S(1)} %stack.23.at_ref, bf16[1024,768]{1,0:T(8,128)(2,1)S(1)} %get-tuple-element.134.normed_ref, bf16[512,768]{1,0:T(8,128)(2,1)S(1)} %get-tuple-element.163.refs_0_, bf16[512,256]{1,0:T(8,128)(2,1)S(1)} %get-tuple-element.164.refs_1_, ...), custom_call_target="tpu_custom_call" | custom-call | flops 1200000000 | tf_op jit(solution)/shard_map/weights_kernel/pallas_call | solution.py:779
  95.5 2.4 %collective-permute-done.10.refs_1_ = bf16[384,1152]{1,0:T(8,128)(2,1)S(1)} collective-permute-done((bf16[384,1152]{1,0:T(8,128)(2,1)S(1)}, bf16[384,1152]{1,0:T(8,128)(2,1)S(1)}, u32[]{:S(2)}, u32[]{:S(2)}) %collective-permute-start.10) | collective-permute-done | bytes 884768 | tf_op jit(solution)/shard_map/ppermute | solution.py:866
  99.2 3.0 %collective-permute-start.17 = (bf16[48,1536]{1,0:T(8,128)(2,1)S(1)}, bf16[48,1536]{1,0:T(8,128)(2,1)S(1)}, u32[]{:S(2)}, u32[]{:S(2)}) collective-permute-start(bf16[48,1536]{1,0:T(8,128)(2,1)S(1)} %get-tuple-element.188.refs_4_), channel_id=1, source_target_pairs={{0,24},{2,26},{4,28},{6,30},{8,16},{10,18},{12,20},{14,22},{16,8},... | collective-permute-start | bytes 442376 | tf_op jit(solution)/shard_map/ppermute | solution.py:866
  104.3 4.8 %normed_grad_kernel.1 = (bf16[512,768]{1,0:T(8,128)(2,1)S(1)}, bf16[512,768]{1,0:T(8,128)(2,1)S(1)}) custom-call(s32[5]{0:T(128)S(1)} %stack.23.at_ref, bf16[1024,768]{1,0:T(8,128)(2,1)S(1)} %copy-done.31, bf16[512,768]{1,0:T(8,128)(2,1)S(1)} %get-tuple-element.163.refs_0_, bf16[512,256]{1,0:T(8,128)(2,1)S(1)} %get-tuple-element.164.refs_1_, ...), custom_call_target="tpu_custom_call" | custom-call | flops 4800000000 | tf_op jit(solution)/shard_map/normed_grad_kernel/pallas_call | solution.py:779
  111.0 3.5 %collective-permute-done.11.refs_1_ = bf16[192,1152]{1,0:T(8,128)(2,1)S(1)} collective-permute-done((bf16[192,1152]{1,0:T(8,128)(2,1)S(1)}, bf16[192,1152]{1,0:T(8,128)(2,1)S(1)}, u32[]{:S(2)}, u32[]{:S(2)}) %collective-permute-start.11) | collective-permute-done | bytes 442400 | tf_op jit(solution)/shard_map/ppermute | solution.py:866
  123.4 3.3 %collective-permute-done.13.refs_2_ = bf16[48,1152]{1,0:T(8,128)(2,1)S(1)} collective-permute-done((bf16[48,1152]{1,0:T(8,128)(2,1)S(1)}, bf16[48,1152]{1,0:T(8,128)(2,1)S(1)}, u32[]{:S(2)}, u32[]{:S(2)}) %collective-permute-start.13) | collective-permute-done | bytes 110624 | tf_op jit(solution)/shard_map/ppermute | solution.py:866
  130.0 3.0 %collective-permute-done.18.other_ref = bf16[48,384]{1,0:T(8,128)(2,1)S(1)} collective-permute-done((bf16[48,384]{1,0:T(8,128)(2,1)S(1)}, bf16[48,384]{1,0:T(8,128)(2,1)S(1)}, u32[]{:S(2)}, u32[]{:S(2)}) %collective-permute-start.18) | collective-permute-done | bytes 36896 | tf_op jit(solution)/shard_map/ppermute | solution.py:1214
  133.7 2.7 %collective-permute-start.21 = (bf16[48,1152]{1,0:T(8,128)(2,1)S(1)}, bf16[48,1152]{1,0:T(8,128)(2,1)S(1)}, u32[]{:S(2)}, u32[]{:S(2)}) collective-permute-start(bf16[48,1152]{1,0:T(8,128)(2,1)S(1)} %heads_kernel.1.refs_0_), channel_id=1, source_target_pairs={{0,24},{2,26},{4,28},{6,30},{8,16},{10,18},{12,20},{14,22},{16,8},... | collective-permute-start | bytes 331784 | tf_op jit(solution)/shard_map/ppermute | solution.py:866
  140.8 2.3 %collective-permute-done.20.refs_2_ = bf16[48,1152]{1,0:T(8,128)(2,1)S(1)} collective-permute-done((bf16[48,1152]{1,0:T(8,128)(2,1)S(1)}, bf16[48,1152]{1,0:T(8,128)(2,1)S(1)}, u32[]{:S(2)}, u32[]{:S(2)}) %collective-permute-start.20) | collective-permute-done | bytes 110624 | tf_op jit(solution)/shard_map/ppermute | solution.py:866
  146.8 3.0 %early_kernel.1 = (f32[768,768]{1,0:T(8,128)}, f32[768,768]{1,0:T(8,128)}, f32[8,128]{1,0:T(8,128)S(1)}) custom-call(s32[5]{0:T(128)S(1)} %stack.23.at_ref, bf16[384,1536]{1,0:T(8,128)(2,1)S(1)} %get-tuple-element.194.own_ref, bf16[384,1536]{1,0:T(8,128)(2,1)S(1)} %collective-permute-done.24.other_ref), custom_call_target="tpu_custom_call" | custom-call | flops 3000000000 | tf_op jit(solution)/shard_map/early_kernel/pallas_call | solution.py:779
  149.7 6.8 %collective-permute-done.23.refs_1_ = bf16[192,1152]{1,0:T(8,128)(2,1)S(1)} collective-permute-done((bf16[192,1152]{1,0:T(8,128)(2,1)S(1)}, bf16[192,1152]{1,0:T(8,128)(2,1)S(1)}, u32[]{:S(2)}, u32[]{:S(2)}) %collective-permute-start.23) | collective-permute-done | bytes 442400 | tf_op jit(solution)/shard_map/ppermute | solution.py:866
  157.2 2.4 %collective-permute-done.25.other_ref = bf16[384,1152]{1,0:T(8,128)(2,1)S(1)} collective-permute-done((bf16[384,1152]{1,0:T(8,128)(2,1)S(1)}, bf16[384,1152]{1,0:T(8,128)(2,1)S(1)}, u32[]{:S(2)}, u32[]{:S(2)}) %collective-permute-start.25) | collective-permute-done | bytes 884768 | tf_op jit(solution)/shard_map/ppermute | solution.py:866
  159.6 2.5 %late_kernel.1 = (f32[768,768]{1,0:T(8,128)}, f32[768,256]{1,0:T(8,128)}, f32[768,12]{1,0:T(8,128)S(1)}, f32[4,768]{1,0:T(4,128)}, f32[768]{0:T(1024)}, /*index=...) custom-call(s32[5]{0:T(128)S(1)} %stack.23.at_ref, ...), custom_call_target="tpu_custom_call" | custom-call | flops 3000000000 | tf_op jit(solution)/shard_map/late_kernel/pallas_call | solution.py:779
  (139 shorter events, 53.9 us)
Async XLA Ops:
  0.7 21.6 %collective-permute-start = (bf16[512,768]{1,0:T(8,128)(2,1)}, bf16[512,768]{1,0:T(8,128)(2,1)S(1)}, u32[]{:S(2)}, u32[]{:S(2)}) collective-permute-start(bf16[512,768]{1,0:T(8,128)(2,1)} %bitcast.13), channel_id=1, source_target_pairs={{0,1},{1,0},{2,3},{3,2},{4,5},{5,4},{6,7},{7,6},{8,9},{9,8},{10,11... | collective-permute-start | bytes 2359304 | tf_op jit(solution)/shard_map/ppermute | solution.py:854
  3.7 34.6 %collective-permute-start.2 = (bf16[512,768]{1,0:T(8,128)(2,1)}, bf16[512,768]{1,0:T(8,128)(2,1)S(1)}, u32[]{:S(2)}, u32[]{:S(2)}) collective-permute-start(bf16[512,768]{1,0:T(8,128)(2,1)} %bitcast.17), channel_id=1, source_target_pairs={{0,1},{1,0},{2,3},{3,2},{4,5},{5,4},{6,7},{7,6},{8,9},{9,8},{10,11... | collective-permute-start | bytes 2359304 | tf_op jit(solution)/shard_map/ppermute | solution.py:854
  41.9 4.5 %collective-permute-start.3 = (f32[8,1024]{1,0:T(8,128)S(1)}, f32[8,1024]{1,0:T(8,128)S(1)}, u32[]{:S(2)}, u32[]{:S(2)}) collective-permute-start(f32[8,1024]{1,0:T(8,128)S(1)} %get-tuple-element.132.here_ref), channel_id=1, source_target_pairs={{0,1},{1,0},{2,3},{3,2},{4,5},{5,4},{6,7},{7,6},{8,9},{9,8},{10,11... | collective-permute-start | bytes 98312 | tf_op jit(solution)/shard_map/ppermute | solution.py:855
  55.8 2.9 %collective-permute-start.4 = (bf16[384,1536]{1,0:T(8,128)(2,1)S(1)}, bf16[384,1536]{1,0:T(8,128)(2,1)S(1)}, u32[]{:S(2)}, u32[]{:S(2)}) collective-permute-start(bf16[384,1536]{1,0:T(8,128)(2,1)S(1)} %get-tuple-element.153), channel_id=1, source_target_pairs={{0,2},{2,0},{4,6},{6,4},{8,10},{10,8},{12,14},{14,12},{16,18},{18,... | collective-permute-start | bytes 3538952 | tf_op jit(solution)/shard_map/ppermute | solution.py:866
  55.9 24.9 %collective-permute-start.1 = (bf16[512,768]{1,0:T(8,128)(2,1)S(1)}, bf16[512,768]{1,0:T(8,128)(2,1)S(1)}, u32[]{:S(2)}, u32[]{:S(2)}) collective-permute-start(bf16[512,768]{1,0:T(8,128)(2,1)S(1)} %get-tuple-element.130), channel_id=1, source_target_pairs={{0,1},{1,0},{2,3},{3,2},{4,5},{5,4},{6,7},{7,6},{8,9},{9,8},{10,11... | collective-permute-start | bytes 2359304 | tf_op jit(solution)/shard_map/ppermute | solution.py:1008
  60.0 15.4 %collective-permute-start.5 = (bf16[192,1536]{1,0:T(8,128)(2,1)S(1)}, bf16[192,1536]{1,0:T(8,128)(2,1)S(1)}, u32[]{:S(2)}, u32[]{:S(2)}) collective-permute-start(bf16[192,1536]{1,0:T(8,128)(2,1)S(1)} %get-tuple-element.161), channel_id=1, source_target_pairs={{0,4},{2,6},{4,0},{6,2},{8,12},{10,14},{12,8},{14,10},{16,20},{18,... | collective-permute-start | bytes 1769480 | tf_op jit(solution)/shard_map/ppermute | solution.py:866
  76.3 14.6 %collective-permute-start.7 = (bf16[48,1536]{1,0:T(8,128)(2,1)S(1)}, bf16[48,1536]{1,0:T(8,128)(2,1)S(1)}, u32[]{:S(2)}, u32[]{:S(2)}) collective-permute-start(bf16[48,1536]{1,0:T(8,128)(2,1)S(1)} %get-tuple-element.177), channel_id=1, source_target_pairs={{0,8},{2,10},{4,12},{6,14},{8,0},{10,2},{12,4},{14,6},{16,24},{18,... | collective-permute-start | bytes 442376 | tf_op jit(solution)/shard_map/ppermute | solution.py:866
  77.9 13.6 %collective-permute-start.8 = (bf16[48,1536]{1,0:T(8,128)(2,1)S(1)}, bf16[48,1536]{1,0:T(8,128)(2,1)S(1)}, u32[]{:S(2)}, u32[]{:S(2)}) collective-permute-start(bf16[48,1536]{1,0:T(8,128)(2,1)S(1)} %get-tuple-element.178), channel_id=1, source_target_pairs={{0,16},{2,18},{4,20},{6,22},{8,24},{10,26},{12,28},{14,30},{16,0},... | collective-permute-start | bytes 442376 | tf_op jit(solution)/shard_map/ppermute | solution.py:866
  80.5 11.1 %collective-permute-start.9 = (bf16[48,1536]{1,0:T(8,128)(2,1)S(1)}, bf16[48,1536]{1,0:T(8,128)(2,1)S(1)}, u32[]{:S(2)}, u32[]{:S(2)}) collective-permute-start(bf16[48,1536]{1,0:T(8,128)(2,1)S(1)} %get-tuple-element.179), channel_id=1, source_target_pairs={{0,24},{2,26},{4,28},{6,30},{8,16},{10,18},{12,20},{14,22},{16,8},... | collective-permute-start | bytes 442376 | tf_op jit(solution)/shard_map/ppermute | solution.py:866
  99.2 17.0 %collective-permute-start.17 = (bf16[48,1536]{1,0:T(8,128)(2,1)S(1)}, bf16[48,1536]{1,0:T(8,128)(2,1)S(1)}, u32[]{:S(2)}, u32[]{:S(2)}) collective-permute-start(bf16[48,1536]{1,0:T(8,128)(2,1)S(1)} %get-tuple-element.188.refs_4_), channel_id=1, source_target_pairs={{0,24},{2,26},{4,28},{6,30},{8,16},{10,18},{12,20},{14,22},{16,8},... | collective-permute-start | bytes 442376 | tf_op jit(solution)/shard_map/ppermute | solution.py:866
  102.2 16.2 %collective-permute-start.16 = (bf16[48,1536]{1,0:T(8,128)(2,1)S(1)}, bf16[48,1536]{1,0:T(8,128)(2,1)S(1)}, u32[]{:S(2)}, u32[]{:S(2)}) collective-permute-start(bf16[48,1536]{1,0:T(8,128)(2,1)S(1)} %get-tuple-element.188.refs_4_), channel_id=1, source_target_pairs={{0,16},{2,18},{4,20},{6,22},{8,24},{10,26},{12,28},{14,30},{16,0},... | collective-permute-start | bytes 442376 | tf_op jit(solution)/shard_map/ppermute | solution.py:866
  102.8 11.6 %collective-permute-start.11 = (bf16[192,1152]{1,0:T(8,128)(2,1)S(1)}, bf16[192,1152]{1,0:T(8,128)(2,1)S(1)}, u32[]{:S(2)}, u32[]{:S(2)}) collective-permute-start(bf16[192,1152]{1,0:T(8,128)(2,1)S(1)} %get-tuple-element.183), channel_id=1, source_target_pairs={{0,4},{2,6},{4,0},{6,2},{8,12},{10,14},{12,8},{14,10},{16,20},{18,... | collective-permute-start | bytes 1327112 | tf_op jit(solution)/shard_map/ppermute | solution.py:866
  109.2 28.9 %collective-permute-start.6 = (bf16[512,768]{1,0:T(8,128)(2,1)S(1)}, bf16[512,768]{1,0:T(8,128)(2,1)S(1)}, u32[]{:S(2)}, u32[]{:S(2)}) collective-permute-start(bf16[512,768]{1,0:T(8,128)(2,1)S(1)} %get-tuple-element.170), channel_id=1, source_target_pairs={{0,1},{1,0},{2,3},{3,2},{4,5},{5,4},{6,7},{7,6},{8,9},{9,8},{10,11... | collective-permute-start | bytes 2359304 | tf_op jit(solution)/shard_map/ppermute | solution.py:1008
  110.2 11.7 %collective-permute-start.15 = (bf16[48,1536]{1,0:T(8,128)(2,1)S(1)}, bf16[48,1536]{1,0:T(8,128)(2,1)S(1)}, u32[]{:S(2)}, u32[]{:S(2)}) collective-permute-start(bf16[48,1536]{1,0:T(8,128)(2,1)S(1)} %get-tuple-element.188.refs_4_), channel_id=1, source_target_pairs={{0,8},{2,10},{4,12},{6,14},{8,0},{10,2},{12,4},{14,6},{16,24},{18,... | collective-permute-start | bytes 442376 | tf_op jit(solution)/shard_map/ppermute | solution.py:866
  115.3 8.1 %collective-permute-start.12 = (bf16[48,1152]{1,0:T(8,128)(2,1)S(1)}, bf16[48,1152]{1,0:T(8,128)(2,1)S(1)}, u32[]{:S(2)}, u32[]{:S(2)}) collective-permute-start(bf16[48,1152]{1,0:T(8,128)(2,1)S(1)} %get-tuple-element.185), channel_id=1, source_target_pairs={{0,8},{2,10},{4,12},{6,14},{8,0},{10,2},{12,4},{14,6},{16,24},{18,... | collective-permute-start | bytes 331784 | tf_op jit(solution)/shard_map/ppermute | solution.py:866
  116.2 10.5 %collective-permute-start.13 = (bf16[48,1152]{1,0:T(8,128)(2,1)S(1)}, bf16[48,1152]{1,0:T(8,128)(2,1)S(1)}, u32[]{:S(2)}, u32[]{:S(2)}) collective-permute-start(bf16[48,1152]{1,0:T(8,128)(2,1)S(1)} %get-tuple-element.186), channel_id=1, source_target_pairs={{0,16},{2,18},{4,20},{6,22},{8,24},{10,26},{12,28},{14,30},{16,0},... | collective-permute-start | bytes 331784 | tf_op jit(solution)/shard_map/ppermute | solution.py:866
  118.4 8.3 %collective-permute-start.14 = (bf16[48,1152]{1,0:T(8,128)(2,1)S(1)}, bf16[48,1152]{1,0:T(8,128)(2,1)S(1)}, u32[]{:S(2)}, u32[]{:S(2)}) collective-permute-start(bf16[48,1152]{1,0:T(8,128)(2,1)S(1)} %get-tuple-element.187), channel_id=1, source_target_pairs={{0,24},{2,26},{4,28},{6,30},{8,16},{10,18},{12,20},{14,22},{16,8},... | collective-permute-start | bytes 331784 | tf_op jit(solution)/shard_map/ppermute | solution.py:866
  127.4 15.8 %collective-permute-start.22 = (bf16[192,1536]{1,0:T(8,128)(2,1)S(1)}, bf16[192,1536]{1,0:T(8,128)(2,1)S(1)}, u32[]{:S(2)}, u32[]{:S(2)}) collective-permute-start(bf16[192,1536]{1,0:T(8,128)(2,1)S(1)} %get-tuple-element.191.refs_4_), channel_id=1, source_target_pairs={{0,4},{2,6},{4,0},{6,2},{8,12},{10,14},{12,8},{14,10},{16,20},{18,... | collective-permute-start | bytes 1769480 | tf_op jit(solution)/shard_map/ppermute | solution.py:866
  129.0 4.0 %collective-permute-start.18 = (bf16[48,384]{1,0:T(8,128)(2,1)S(1)}, bf16[48,384]{1,0:T(8,128)(2,1)S(1)}, u32[]{:S(2)}, u32[]{:S(2)}) collective-permute-start(bf16[48,384]{1,0:T(8,128)(2,1)S(1)} %slice.3), channel_id=1, source_target_pairs={{0,1},{1,0},{2,3},{3,2},{4,5},{5,4},{6,7},{7,6},{8,9},{9,8},{10,11... | collective-permute-start | bytes 110600 | tf_op jit(solution)/shard_map/ppermute | solution.py:1214
  133.7 7.2 %collective-permute-start.21 = (bf16[48,1152]{1,0:T(8,128)(2,1)S(1)}, bf16[48,1152]{1,0:T(8,128)(2,1)S(1)}, u32[]{:S(2)}, u32[]{:S(2)}) collective-permute-start(bf16[48,1152]{1,0:T(8,128)(2,1)S(1)} %heads_kernel.1.refs_0_), channel_id=1, source_target_pairs={{0,24},{2,26},{4,28},{6,30},{8,16},{10,18},{12,20},{14,22},{16,8},... | collective-permute-start | bytes 331784 | tf_op jit(solution)/shard_map/ppermute | solution.py:866
  136.3 6.8 %collective-permute-start.20 = (bf16[48,1152]{1,0:T(8,128)(2,1)S(1)}, bf16[48,1152]{1,0:T(8,128)(2,1)S(1)}, u32[]{:S(2)}, u32[]{:S(2)}) collective-permute-start(bf16[48,1152]{1,0:T(8,128)(2,1)S(1)} %heads_kernel.1.refs_0_), channel_id=1, source_target_pairs={{0,16},{2,18},{4,20},{6,22},{8,24},{10,26},{12,28},{14,30},{16,0},... | collective-permute-start | bytes 331784 | tf_op jit(solution)/shard_map/ppermute | solution.py:866
  136.9 6.3 %collective-permute-start.19 = (bf16[48,1152]{1,0:T(8,128)(2,1)S(1)}, bf16[48,1152]{1,0:T(8,128)(2,1)S(1)}, u32[]{:S(2)}, u32[]{:S(2)}) collective-permute-start(bf16[48,1152]{1,0:T(8,128)(2,1)S(1)} %heads_kernel.1.refs_0_), channel_id=1, source_target_pairs={{0,8},{2,10},{4,12},{6,14},{8,0},{10,2},{12,4},{14,6},{16,24},{18,... | collective-permute-start | bytes 331784 | tf_op jit(solution)/shard_map/ppermute | solution.py:866
  143.8 2.9 %collective-permute-start.24 = (bf16[384,1536]{1,0:T(8,128)(2,1)S(1)}, bf16[384,1536]{1,0:T(8,128)(2,1)S(1)}, u32[]{:S(2)}, u32[]{:S(2)}) collective-permute-start(bf16[384,1536]{1,0:T(8,128)(2,1)S(1)} %get-tuple-element.194.own_ref), channel_id=1, source_target_pairs={{0,2},{2,0},{4,6},{6,4},{8,10},{10,8},{12,14},{14,12},{16,18},{18,... | collective-permute-start | bytes 3538952 | tf_op jit(solution)/shard_map/ppermute | solution.py:866
  143.9 12.6 %collective-permute-start.23 = (bf16[192,1152]{1,0:T(8,128)(2,1)S(1)}, bf16[192,1152]{1,0:T(8,128)(2,1)S(1)}, u32[]{:S(2)}, u32[]{:S(2)}) collective-permute-start(bf16[192,1152]{1,0:T(8,128)(2,1)S(1)} %get-tuple-element.193.refs_0_), channel_id=1, source_target_pairs={{0,4},{2,6},{4,0},{6,2},{8,12},{10,14},{12,8},{14,10},{16,20},{18,... | collective-permute-start | bytes 1327112 | tf_op jit(solution)/shard_map/ppermute | solution.py:866
  (36 other events, 249.1 us)

commit v4 on v3

--- a/solution.py
+++ b/solution.py
@@ -49,6 +49,7 @@
 def causal_back(buf, slab, r0, grad, pre, taps, extra):
     buf[slab, pl.ds(r0, CHUNK), :] = grad
     lanes = slice(slab * LANES, (slab + 1) * LANES)
+    pre = pre.astype(f32)
     out, rows = 0.0, []
     for tap in range(4):
         moved = grad if tap == 3 else buf[slab, pl.ds(r0 + 3 - tap, CHUNK), :]
@@ -150,7 +151,8 @@
     g_ref,
     y_ref,
     gg_ref,
-    av_ref,
+    low_ref,
+    slope_ref,
     vp_ref,
     as_ref,
     sp_ref,
@@ -167,7 +169,6 @@
     state,
     carried,
     values,
-    low,
     vtail,
 ):
     step_at = pl.program_id(0)
@@ -189,7 +190,7 @@
     z_ref[...] = z
     for out, buf, w in ((sp_ref, sbuf, state_w), (vp_ref, vbuf, value_w)):
         pre = dot(normed, w[...])
-        out[...] = pre
+        out[...] = pre.astype(bf16)
         for slab in range(buf.shape[0]):
             buf[slab, 8:, :] = pre[:, slab * LANES : (slab + 1) * LANES]
     g_ref[...] = dot(normed, gate_w[...])
@@ -206,11 +207,10 @@
         states.append(silu(conv))
     for pair in range(pairs):
         lanes = slice(pair * LANES, (pair + 1) * LANES)
-        conv = causal(vbuf, pair, vconv_ref, vshift_ref)
-        av_ref[:, lanes] = conv
-        out = silu(conv)
+        out, slope = silu_slope(causal(vbuf, pair, vconv_ref, vshift_ref))
+        slope_ref[:, lanes] = slope.astype(bf16)
         values[:, lanes] = out
-        low[:, lanes] = out.astype(bf16)
+        low_ref[:, lanes] = out.astype(bf16)
         vtail[:, lanes] = (out * tailx[:, lanes]).astype(bf16)
     parts = []
     for chunk in chunks:
@@ -232,7 +232,7 @@
             _, mixes = quad_mixing(parts[chunk], run, run_t, quad, mask)
             sides = [slice((2 * quad + k) * LANES, (2 * quad + k + 1) * LANES) for k in range(2)]
             both = dot(
-                jnp.concatenate(mixes, axis=1), heads_apart(*(low[here, lanes] for lanes in sides))
+                jnp.concatenate(mixes, axis=1), heads_apart(*(low_ref[here, lanes] for lanes in sides))
             )
             for k, lanes in enumerate(sides):
                 scanned = both[:, k * LANES : (k + 1) * LANES]
@@ -247,10 +247,8 @@
         buf[:, 0:8, :] = buf[:, BLOCK : BLOCK + 8, :]
 
 
-def stats_kernel(half_blocks, at_ref, own_ref, other_ref, gg_ref, sq_ref, out_w, og_ref, stats_ref):
-    mine = (pl.program_id(0) // half_blocks) == at_ref[0]
-    cot = jnp.where(mine, own_ref[...], other_ref[...])
-    og = dot(cot, out_w[...], NT)
+def stats_kernel(at_ref, cot_ref, gg_ref, sq_ref, out_w, og_ref, stats_ref):
+    og = dot(cot_ref[...], out_w[...], NT)
     og_ref[...] = og
     prod = (og * gg_ref[...].astype(f32)).astype(bf16)
     dots = dot(jnp.ones((8, prod.shape[1]), bf16), prod, NT)
@@ -277,16 +275,20 @@
         other_ref[...] = rows
 
 
+def gate_back_kernel(at_ref, dg_ref, gate_w, out_ref):
+    out_ref[...] = dot(dg_ref[...], gate_w[...], NT)
+
+
 def picked(cut, early, late):
     return jnp.where(pl.program_id(0) < cut, early[...], late[...])
 
 
-def normed_grad_kernel(half_blocks, cut, at_ref, dg_ref, *refs):
-    lows, (gate_w, value_w, state_w, step_w, own_ref, other_ref) = refs[:6], refs[6:]
+def normed_grad_kernel(half_blocks, cut, at_ref, from_gate, *refs):
+    lows, (value_w, state_w, step_w, own_ref, other_ref) = refs[:6], refs[6:]
     dv, ds, dz = (picked(cut, a, b) for a, b in zip(lows[:3], lows[3:]))
     mine = (pl.program_id(0) // half_blocks) == at_ref[0]
     rows = (
-        dot(dg_ref[...], gate_w[...], NT)
+        from_gate[...]
         + dot(dv, value_w[...], NT)
         + dot(ds, state_w[...], NT)
         + dot(dz, step_w[...], NT)
@@ -344,10 +346,13 @@
     at_ref,
     own_ref,
     other_ref,
-    here_ref,
-    there_ref,
+    here_a,
+    there_a,
+    here_b,
+    there_b,
     normed_ref,
-    og_ref,
+    og_a,
+    og_b,
     y_ref,
     g_ref,
     gg_ref,
@@ -365,24 +370,24 @@
 ):
     step_at = pl.program_id(0)
     here = pl.ds(pl.multiple_of(step_at * BLOCK, BLOCK), BLOCK)
-    pairs = og_ref.shape[1] // LANES
+    pairs = og_a.shape[1] // LANES
     grad_gate, grad_out = scratch if fast else (first_ref, second_ref)
 
     @pl.when(step_at == 0)
     def _():
         grad_gain_ref[...] = jnp.zeros_like(grad_gain_ref)
 
-    sums = here_ref[...] + there_ref[...]
+    mine = (step_at // half_blocks) == at_ref[0]
+    sums = jnp.where(mine, here_a[...] + there_a[...], here_b[...] + there_b[...])
     scale_row = lax.rsqrt(sums[0:1, :] / inner_all + EPSILON)
     pull_row = scale_row * scale_row * scale_row * sums[1:2, :] / inner_all
     columns = row_column(jnp.concatenate([scale_row, pull_row], axis=0))
     scale, pull = columns[:, 0:1], columns[:, 1:2]
-    mine = (step_at // half_blocks) == at_ref[0]
     cot = jnp.where(mine, own_ref[...], other_ref[...]).astype(f32)
     scaled_ref[here, :] = (cot * scale).astype(bf16)
     for pair in range(pairs):
         lanes = slice(pair * LANES, (pair + 1) * LANES)
-        og = og_ref[:, lanes] * scale
+        og = jnp.where(mine, og_a[:, lanes], og_b[:, lanes]) * scale
         y = y_ref[:, lanes]
         g = g_ref[:, lanes]
         gate, slope = silu_slope(g)
@@ -401,10 +406,16 @@
             emit(at_ref, (grad_gate, grad_out), (first_ref, second_ref))
 
 
-def weights_kernel(fast, extra, at_ref, normed_ref, *refs):
+def weights_kernel(fast, at_ref, normed_ref, *refs):
     lows, refs = refs[:6], refs[6:]
     value_w, state_w, step_w, gain_ref, vec_ref, svec_ref, head_ref, ggain_ref, norm_ref = refs[:9]
-    outs, acc = refs[9 + extra : -3], refs[-3:]
+    outs, acc = refs[9:-3], refs[-3:]
+    if fast:
+        pieces, outs, done_ref = outs[:4], outs[4:6], outs[6]
+        total = pieces[0][...].astype(f32)
+        for r in pieces[1:]:
+            total = total + r[...].astype(f32)
+        done_ref[...] = total.astype(bf16)
     for a, early, late in zip(acc, lows[:3], lows[3:]):
         a[...] = dot(normed_ref[...], jnp.concatenate([early[...], late[...]], axis=0), TN)
     norm = norm_ref[...]
@@ -470,8 +481,11 @@
             last = last + r[:, width:].astype(f32)
         buf[:, width:] = carry_rest(join_rest(last)).astype(bf16)
     rows = outs[0].shape[0]
-    if len(outs) == 1:
-        outs[0][...] = buf[...]
+    if rows == buf.shape[0]:
+        left = 0
+        for o in outs:
+            o[...] = buf[:, left : left + o.shape[1]]
+            left += o.shape[1]
         return
     for j, o in enumerate(outs):
         o[...] = buf[pl.ds(pl.multiple_of((me ^ j) * rows, 16), rows), :]
@@ -479,8 +493,13 @@
 
 def join_step(me, ins, out):
     rows = ins[0].shape[0]
-    for j, r in enumerate(ins):
-        out[pl.ds(pl.multiple_of((me ^ j) * rows, 16), rows), :] = r[...]
+    count = out.shape[0] // rows
+    left = 0
+    for first in range(0, len(ins), count):
+        right = left + ins[first].shape[1]
+        for j, r in enumerate(ins[first : first + count]):
+            out[pl.ds(pl.multiple_of((me ^ j) * rows, 16), rows), left:right] = r[...]
+        left = right
 
 
 def stage_kernel(plan, extra, at_ref, *refs):
@@ -489,8 +508,8 @@
     n_out = sum(count for _, _, _, count, _ in plan)
     outs, bufs = refs[:n_out], list(refs[n_out:])
     for kind, axis, take, give, vectors in plan:
-        if kind == "fold":
-            fold_step(at_ref[axis], ins[:take], outs[:give], bufs.pop(0), vectors)
+        if kind != "join":
+            fold_step(at_ref[axis if kind == "fold" else 0], ins[:take], outs[:give], bufs.pop(0), vectors)
         else:
             join_step(at_ref[axis], ins[:take], outs[0])
         ins, outs = ins[take:], outs[give:]
@@ -503,9 +522,13 @@
         count, vectors = rest if rest else (1, False)
         if kind == "fold":
             shapes += [(rows // count, width)] * count
+        elif kind == "part":
+            shapes += [(rows, axis), (rows, width - axis)]
+        else:
+            widths = {a.shape[1] for a in ins}
+            shapes.append((rows * len(ins) // len(widths), sum(widths)))
+        if kind != "join":
             scratch.append(pltpu.VMEM((rows, width), bf16))
-        else:
-            shapes.append((rows * len(ins), width))
         plan.append((kind, axis, len(ins), count, vectors))
         arrays += ins
     out = call(
@@ -523,20 +546,17 @@
     return results
 
 
-def heads_kernel(at_ref, own_ref, other_ref, out_ref):
-    split_at = out_ref.shape[1] - other_ref.shape[1]
-    state = other_ref.shape[1] - LANES
-    out_ref[:, :split_at] = own_ref[:, :split_at]
-    out_ref[:, split_at : split_at + state] = (
-        own_ref[:, split_at : split_at + state].astype(f32) + other_ref[:, :state].astype(f32)
-    ).astype(bf16)
+def heads_kernel(at_ref, done_ref, own_ref, other_ref, out_ref):
+    start = done_ref.shape[1]
+    state = own_ref.shape[1] - LANES
+    out_ref[:, :start] = done_ref[...]
+    sums = own_ref[:, :state].astype(f32) + other_ref[:, :state].astype(f32)
+    out_ref[:, start : start + state] = sums.astype(bf16)
     lane = lax.broadcasted_iota(jnp.int32, (1, LANES), 1)
     shared = (lane == VEC_AT + 6) | ((lane >= SVEC_AT) & (lane < HEAD_AT))
-    mine = join_rest(own_ref[:, split_at + state :].astype(f32))
+    mine = join_rest(own_ref[:, state:].astype(f32))
     theirs = join_rest(other_ref[:, state:].astype(f32))
-    out_ref[:, split_at + state :] = carry_rest(
-        mine + jnp.where(shared, theirs, 0.0)
-    ).astype(bf16)
+    out_ref[:, start + state :] = carry_rest(mine + jnp.where(shared, theirs, 0.0)).astype(bf16)
 
 
 def halves_of(at_ref, own_ref, other_ref, left, right):
@@ -564,9 +584,8 @@
             o[at, :] = v
         left = right
     full = join_rest(block[...])
-    heads = outs[2].shape[1]
-    outs[2][...] = full[:, :heads]
     rows = full.T
+    outs[2][...] = rows[: outs[2].shape[0]]
     vec, svec = rows[VEC_AT : VEC_AT + 8], rows[SVEC_AT : SVEC_AT + 8]
     head = rows[HEAD_AT : HEAD_AT + 8]
     vconv, vshift, ggain, norm, sconv, sshift, bias, rate, skip = outs[3:]
@@ -579,11 +598,14 @@
 
 
 def backward_kernel(
+    size,
+    from_row,
     carried_in,
     extra,
     at_ref,
     dy_ref,
-    av_ref,
+    low_ref,
+    slope_ref,
     vp_ref,
     as_ref,
     sp_ref,
@@ -607,8 +629,11 @@
     dabuf, dsbuf, dstate, carried, pulled, ubuf, vtail, inner, outer = refs[9:]
     step_at = pl.program_id(0)
     nstate, width = dstate.shape
-    size = dy_ref.shape[0]
     pairs = width // LANES
+
+    def row_at(start, count=CHUNK):
+        return slice(from_row + start, from_row + start + count)
+
 
     @pl.when(step_at == 0)
     def _():
@@ -636,19 +661,20 @@
     rate = -jnp.exp(rate_ref[...])
     states, slopes = [], []
     for slab in range(2):
-        out, slope = silu_slope(as_ref[:, slab * LANES : (slab + 1) * LANES])
+        out, slope = silu_slope(as_ref[row_at(0, size), slab * LANES : (slab + 1) * LANES])
         states.append(out)
         slopes.append(slope)
     for pair in range(pairs):
         lanes = slice(pair * LANES, (pair + 1) * LANES)
-        ubuf[:, lanes] = (dy_ref[:, lanes].astype(f32) * grownx[:, lanes]).astype(bf16)
+        there = (row_at(0, size), lanes)
+        ubuf[:, lanes] = (dy_ref[there].astype(f32) * grownx[there]).astype(bf16)
     two = [chunk_scores(*(v[here] for v in states)) for here in chunks]
     helds, afters = [None] * len(chunks), [None] * len(chunks)
     for chunk in reversed(range(len(chunks))):
         here = chunks[chunk]
         b_two, c_two, _ = two[chunk]
-        before = sin_ref[chunk, :, :]
-        last = grownx[here.stop - 1 : here.stop, :]
+        before = sin_ref[from_row // CHUNK + chunk, :, :]
+        last = grownx[row_at(here.stop - 1, 1), :]
         grad = dstate[...]
         afters[chunk] = grad.astype(bf16)
         carried[here, :] = dot(c_two[:, :nstate], before)
@@ -664,15 +690,15 @@
     for chunk in reversed(range(len(chunks))):
         here = chunks[chunk]
         b_two, c_two, scores = two[chunk]
-        run = running_ref[here, :]
-        run_t = shifted_ref[here, :].T
+        rows_in = row_at(here.start)
+        run = running_ref[rows_in, :]
+        run_t = shifted_ref[rows_in, :].T
         dscores = jnp.zeros((CHUNK, CHUNK), f32)
         for quad in range(pairs // 2):
             factors, mixes = quad_mixing(scores, run, run_t, quad, mask)
             both = [slice((2 * quad + k) * LANES, (2 * quad + k + 1) * LANES) for k in range(2)]
-            values, slope = zip(*(silu_slope(av_ref[here, lanes]) for lanes in both))
-            low = [v.astype(bf16) for v in values]
-            dy_low = [dy_ref[here, lanes] for lanes in both]
+            low = [low_ref[rows_in, lanes] for lanes in both]
+            dy_low = [dy_ref[rows_in, lanes] for lanes in both]
             apart = heads_apart(*low)
             scanned = dot(jnp.concatenate(mixes, axis=1), apart)
             dsteps = dot(jnp.concatenate(mixes, axis=0), heads_apart(*dy_low), TN)
@@ -684,21 +710,21 @@
                 dscores = dscores + dmixing[:, CHUNK:] * factors[2 * k + 1]
                 wide = slice(2 * pair * LANES, (2 * pair + 1) * LANES)
                 wide_b = slice((2 * pair + 1) * LANES, (2 * pair + 2) * LANES)
-                dy = dy_low[k].astype(f32)
+                dy, values = dy_low[k].astype(f32), low[k].astype(f32)
                 dvalues = dsteps[:, own]
-                pulls = low[k].astype(f32) * dvalues
+                pulls = values * dvalues
                 inside = dy * scanned[:, own] - pulls + ubuf[here, lanes].astype(f32) * carried[here, lanes]
                 high = inside.astype(bf16)
                 inner[here, wide] = high
                 inner[here, wide_b] = (inside - high.astype(f32)).astype(bf16)
-                tails, pull = tailx[here, lanes], pulled[here, lanes]
-                v = (values[k] * tails).astype(bf16)
+                tails, pull = tailx[rows_in, lanes], pulled[here, lanes]
+                v = (values * tails).astype(bf16)
                 vtail[here, lanes] = v
                 outer[here, wide] = pulls.astype(bf16)
                 outer[here, wide_b] = (v.astype(f32) * pull).astype(bf16)
-                da = (dvalues + tails * pull + skip_ref[:, lanes] * dy) * slope[k]
-                skips = jnp.sum(values[k] * dy, axis=0, keepdims=True)
-                dv, rows = causal_back(dabuf, pair, here.start, da, vp_ref[here, lanes], vconv_ref, skips)
+                da = (dvalues + tails * pull + skip_ref[:, lanes] * dy) * slope_ref[rows_in, lanes].astype(f32)
+                skips = jnp.sum(values * dy, axis=0, keepdims=True)
+                dv, rows = causal_back(dabuf, pair, here.start, da, vp_ref[rows_in, lanes], vconv_ref, skips)
                 grad_vconv_ref[:, lanes] += rows
                 dvalue[here, lanes] = dv.astype(bf16)
         dlow = dscores.astype(bf16)
@@ -706,7 +732,7 @@
         b_rows, c_rows = b_two[:, :nstate], c_two[:, :nstate]
         cross = dot(
             jnp.concatenate([vtail[here, :], ubuf[here, :]], axis=0),
-            jnp.concatenate([afters[chunk], sin_ref[chunk, :, :]], axis=0),
+            jnp.concatenate([afters[chunk], sin_ref[from_row // CHUNK + chunk, :, :]], axis=0),
             NT,
         )
         db = cross[:CHUNK, :nstate] + dot(
@@ -721,7 +747,7 @@
         for slab, d in enumerate((db, dc)):
             lanes = slice(slab * LANES, (slab + 1) * LANES)
             d = d * slopes[slab][here]
-            dpre, rows = causal_back(dsbuf, slab, here.start, d, sp_ref[here, lanes], sconv_ref, zero_row)
+            dpre, rows = causal_back(dsbuf, slab, here.start, d, sp_ref[rows_in, lanes], sconv_ref, zero_row)
             grad_sconv_ref[:, lanes] += rows
             dstates[here, lanes] = dpre.astype(bf16)
 
@@ -735,9 +761,10 @@
         ddecay = ddecay + dot(chunk_mask(True), outs[:, LANES:].astype(bf16))
         held = [jnp.broadcast_to(helds[k // CHUNK], (CHUNK, LANES)) for k in range(r, r + BLOCK, CHUNK)]
         ddecay = ddecay + jnp.concatenate(held, axis=0)
-        step = step_ref[here, :]
+        rows_in = row_at(r, BLOCK)
+        step = step_ref[rows_in, :]
         direct = (outs[:, :LANES] + outs[:, LANES:]) / jnp.maximum(step, 1e-37)
-        dz = (direct + ddecay * rate) * sigmoid(z_ref[here, :])
+        dz = (direct + ddecay * rate) * sigmoid(z_ref[rows_in, :])
         dstep[here, :] = dz.astype(bf16)
         heads[0] = heads[0] + jnp.sum(dz, axis=0, keepdims=True)
         heads[1] = heads[1] + jnp.sum(ddecay * step, axis=0, keepdims=True) * rate
@@ -758,8 +785,8 @@
     forward_kernel=14,
     stats_kernel=8,
     branch_kernel=8,
-    gate_kernel=16,
-    backward_kernel=22,
+    gate_kernel=12,
+    backward_kernel=24,
     weights_kernel=14,
     normed_grad_kernel=12,
     mixed_kernel=8,
@@ -923,7 +950,7 @@
         ((rows_here if two else BLOCK, model), bf16, rows(model, other_block)),
     ]
 
-    normed, g, y, gg, av, vp, conv_s, sp, z, sin, sq, step, running, shifted, grownx, tailx = run(
+    normed, g, y, gg, values, slope, vp, conv_s, sp, z, sin, sq, step, running, shifted, grownx, tailx = run(
         functools.partial(forward_kernel, half_blocks),
         blocks,
         at,
@@ -953,10 +980,11 @@
                     ((length, width), f32, rows(width)),
                     ((length, width), f32, rows(width)),
                     ((length, width), bf16, rows(width)),
-                    ((length, width), f32, rows(width)),
-                    ((length, width), f32, rows(width)),
+                    ((length, width), bf16, rows(width)),
+                    ((length, width), bf16, rows(width)),
+                    ((length, width), bf16, rows(width)),
                     ((length, nstate2), f32, rows(nstate2)),
-                    ((length, nstate2), f32, rows(nstate2)),
+                    ((length, nstate2), bf16, rows(nstate2)),
                     ((length, LANES), f32, rows(LANES)),
                     ((blocks * chunks, nstate, width), bf16, states_spec(lambda i, a: (i, 0, 0))),
                     ((8, length), f32, along),
@@ -975,25 +1003,39 @@
             big(BLOCK, width),
             big(BLOCK, width),
             low(BLOCK, width),
-            low(BLOCK, width),
         ],
     )
-    og, stats = run(
-        functools.partial(stats_kernel, half_blocks),
-        blocks,
-        at,
-        [
-            (own_cot, rows(model, own_block)),
-            (other_cot, rows(model, other_read)),
-            (gg, rows(width)),
-            (sq, along),
-            (out_w, None),
-        ],
-        [((length, width), f32, rows(width), fast), ((8, length), f32, along)],
-        [],
-    )
-    other_stats = add_other(stats)
-    own_along = pl.BlockSpec((8, BLOCK), lambda i, a: (0, i + a[4] // BLOCK))
+    def stats_of(cot_rows, theirs):
+        first = (lambda a: (1 - a[0]) * half_blocks) if theirs else (lambda a: a[0] * half_blocks)
+        count = cot_rows.shape[0]
+        return run(
+            stats_kernel,
+            count // BLOCK,
+            at,
+            [
+                (cot_rows, rows(model)),
+                (gg, rows(width, lambda i, a: (first(a) + i, 0))),
+                (sq, pl.BlockSpec((8, BLOCK), lambda i, a: (0, first(a) + i))),
+                (out_w, None),
+            ],
+            [((count, width), f32, rows(width), fast), ((8, count), f32, along)],
+            [],
+        )
+
+    og, stats = stats_of(own_cot, False)
+    if two:
+        og_b, stats_b = stats_of(other_cot, True)
+        got_b, got = add_other(stats), add_other(stats_b)
+    else:
+        og_b, stats_b, got = og, stats, add_other(stats)
+        got_b = got
+
+    def own_along(i, a):
+        return own_block(i, a)[::-1]
+
+    def other_along(i, a):
+        return other_read(i, a)[::-1]
+
     branch, branch_sent = run(
         functools.partial(branch_kernel, half_blocks),
         blocks,
@@ -1027,10 +1069,13 @@
         [
             (own_cot, rows(model, own_block)),
             (other_cot, rows(model, other_read)),
-            (stats, along),
-            (other_stats, along),
+            (stats, pl.BlockSpec((8, BLOCK), own_along)),
+            (got, pl.BlockSpec((8, BLOCK), own_along)),
+            (stats_b, pl.BlockSpec((8, BLOCK), other_along)),
+            (got_b, pl.BlockSpec((8, BLOCK), other_along)),
             (normed, None),
-            (og, rows(width)),
+            (og, rows(width, own_block)),
+            (og_b, rows(width, other_read)),
             (y, rows(width)),
             (g, rows(width)),
             (gg, None),
@@ -1050,36 +1095,32 @@
 
     def backward(start, count, carry, after=()):
         size = 2 * BLOCK if start % 2 == 0 and count % 2 == 0 else BLOCK
+        size = count * BLOCK if fast else size
         steps, base = count * BLOCK // size, start * BLOCK // size
-
-        def behind(n):
-            return pl.BlockSpec((size, n), lambda i, a: (base + steps - 1 - i, 0))
 
         def local(n):
             return pl.BlockSpec((size, n), lambda i, a: (steps - 1 - i, 0))
 
-        states = pl.BlockSpec(
-            (size // CHUNK, nstate, width), lambda i, a: (base + steps - 1 - i, 0, 0)
-        )
+        def taken(array):
+            if fast:
+                return (array, None)
+            shape = (size // CHUNK if array.ndim == 3 else size, *array.shape[1:])
+            rest = (0,) * (array.ndim - 1)
+            return (array, pl.BlockSpec(shape, lambda i, a: (base + steps - 1 - i, *rest)))
+
         slabs = [(width // LANES, 8, LANES), (nstate2 // LANES, 8, LANES)]
         vectors = [(nstate, width), *slabs, (8, width), (8, nstate2), (8, LANES)]
         out = run(
-            functools.partial(backward_kernel, bool(carry), len(after)),
+            functools.partial(
+                backward_kernel, size, start * BLOCK if fast else 0, bool(carry), len(after)
+            ),
             steps,
             at,
             [
-                (dy, behind(width)),
-                (av, behind(width)),
-                (vp, behind(width)),
-                (conv_s, behind(nstate2)),
-                (sp, behind(nstate2)),
-                (z, behind(LANES)),
-                (step, behind(LANES)),
-                (running, behind(LANES)),
-                (shifted, behind(LANES)),
-                (grownx, behind(width)),
-                (tailx, behind(width)),
-                (sin, states),
+                *[
+                    taken(a)
+                    for a in (dy, values, slope, vp, conv_s, sp, z, step, running, shifted, grownx, tailx, sin)
+                ],
                 (vconv, None),
                 (state_conv, None),
                 (rate, None),
@@ -1108,10 +1149,34 @@
         )
         return out[:3], out[3:]
 
+    own_stats = along if two else pl.BlockSpec((8, BLOCK), lambda i, a: (0, i + a[4] // BLOCK))
+    mixed, token = run(
+        functools.partial(mixed_kernel, inner_all),
+        rows_here // BLOCK,
+        at,
+        [
+            (residual, rows(model)),
+            (branch, rows(model)),
+            (branch_got, rows(model)),
+            (stats, own_stats),
+            (got, own_stats),
+        ],
+        [((rows_here, model), f32, rows(model)), ((8, LANES), f32, fixed(8, LANES))],
+        [],
+    )
+    from_gate = run(
+        gate_back_kernel,
+        blocks,
+        at,
+        [(dg, rows(width)), (gate_w, None)],
+        [((length, model), f32, rows(model), fast)],
+        [],
+    )[0]
     cut = blocks // 2
     behind = ()
     if fast:
-        ((kept, sent),) = stage(at, [("fold", 2, [early_a, hop(early_b, "core")], 2, False)])
+        steps = [("fold", 2, [early_a, hop(early_b, "core")], 2, False)]
+        ((kept, sent),) = stage(at, steps, (from_gate,))
         early = [kept, hop(sent, "line")]
         behind = (kept,)
     low_b, carry = backward(cut, blocks - cut, (), behind)
@@ -1121,18 +1186,19 @@
         behind = (kept, branch_got)
     low_a, carry = backward(0, cut, carry, behind)
     vec, svec, head = carry[3:]
+    early = early if fast else ()
     lows = [(a, rows(a.shape[1], lambda i, at: (jnp.minimum(i, cut - 1), 0))) for a in low_a]
     lows += [(a, rows(a.shape[1], lambda i, at: (jnp.maximum(i - cut, 0), 0))) for a in low_b]
-    behind = early[1:] if fast else ()
 
     if fast:
         shape = (model // 2, width + nstate2 + LANES)
         pieces = [(shape, bf16, fixed(*shape))] * 2
+        pieces.append((early[0].shape, bf16, fixed(*early[0].shape)))
     else:
         shapes = [(model, width), (model, nstate2), (model, LANES), (8, model)]
         pieces = [(shape, f32, fixed(*shape)) for shape in shapes]
     late = run(
-        functools.partial(weights_kernel, fast, len(behind)),
+        functools.partial(weights_kernel, fast),
         1,
         at,
         [
@@ -1147,7 +1213,7 @@
             (head, None),
             (grad_gain, None),
             (norm, None),
-            *[(a, pl.BlockSpec(memory_space=pl.ANY)) for a in behind],
+            *[(a, None) for a in early],
         ],
         pieces,
         [big(model, width), big(model, nstate2), big(model, LANES)],
@@ -1157,9 +1223,8 @@
         blocks,
         at,
         [
-            (dg, rows(width)),
+            (from_gate, rows(model)),
             *lows,
-            (gate_w, None),
             (value_w, None),
             (state_proj, None),
             (step_w, None),
@@ -1168,20 +1233,6 @@
         [],
     )
 
-    mixed, token = run(
-        functools.partial(mixed_kernel, inner_all),
-        rows_here // BLOCK,
-        at,
-        [
-            (residual, rows(model)),
-            (branch, rows(model)),
-            (branch_got, rows(model)),
-            (stats, own_along),
-            (other_stats, own_along),
-        ],
-        [((rows_here, model), f32, rows(model)), ((8, LANES), f32, fixed(8, LANES))],
-        [],
-    )
     ng_got = other_half(ng, ng_sent)
     if not two:
         ng = lax.dynamic_slice_in_dim(ng, own_from, rows_here, 0)
@@ -1201,23 +1252,22 @@
     )
 
     if fast:
-        kept, sent = late
-        steps = [("fold", 2, [kept, hop(sent, "core")], 2, True), ("fold", 3, early, 1, False)]
-        (kept, sent), (early,) = stage(at, steps)
+        kept, sent, early = late
+        ((kept, sent),) = stage(at, [("fold", 2, [kept, hop(sent, "core")], 2, True)])
         got = hop(sent, "line")
         early = [early] + [hop(early, k) for k in (1, 2, 3)]
         ((kept, *sent),) = stage(at, [("fold", 3, [kept, got], 4, True)], (ng,))
         got = [hop(a, k + 1) for k, a in enumerate(sent)]
-        steps = [("fold", 3, [kept, *got], 1, True), ("join", 3, early)]
-        (done,), (early,) = stage(at, steps, (token,))
+        steps = [("part", width, [kept, *got], 2, True), ("join", 3, early)]
+        (done, rest), (early,) = stage(at, steps, (token,))
         early = [early, hop(early, "line")]
-        theirs = lax.ppermute(done[:, width:], "heads", swap)
+        theirs = lax.ppermute(rest, "heads", swap)
         done = run(
             heads_kernel,
             1,
             at,
-            [(done, None), (theirs, None)],
-            [(done.shape, bf16, fixed(*done.shape))],
+            [(done, None), (rest, None), (theirs, None)],
+            [((rest.shape[0], width + rest.shape[1]), bf16, fixed(rest.shape[0], width + rest.shape[1]))],
             [],
         )[0]
         done = [done] + [hop(done, k) for k in (1, 2, 3)]
@@ -1235,7 +1285,7 @@
         shapes = [
             (model, width),
             (model, nstate2),
-            (model, heads),
+            (heads, model),
             (4, width),
             (width,),
             (width,),
@@ -1274,7 +1324,7 @@
             grad_gate,
             grad_value,
             grad_state,
-            grad_step,
+            grad_step.T,
             grad_vconv,
             grad_vshift,
             grad_sconv,

time: 163 us -> 160 us (0.982)
  local copies, waits for them, and re-layouts: 14.1 us -> 10.3 us
  waiting for transfers between devices: 43.8 us -> 41.3 us
  Pallas kernels: 72.2 us -> 74.4 us
    unnamed x70 -> x29, local copies, waits for them, and re-layouts: 8.21 us -> 4.35 us
    ppermute x2, waiting for transfers between devices: 9.89 us -> 7.41 us  [per_device(): pair_of = lambda a: (a, lax.ppermute(a, 'heads', swap))]
    pallas_call x22 -> x24, Pallas kernels: 72.2 us -> 74.4 us  [call(): pl.pallas_call(kernel, name=title, grid_spec=pltpu.PrefetchScalarGridSpec...]
  transfers between devices with their start and end apart: 26 -> 27, of which waited for: 15 -> 13; matrix products, arithmetic and copies ran while one was open for 5% -> 5% of each run, Pallas kernels for 32% -> 36%
where the time goes in v4:
time: 160 us; the launch traced here: 159 us
  Pallas kernels  74.4 us (47%)
  waiting for transfers between devices  41.3 us (26%)
  starting transfers between devices  31.7 us (20%)
  local copies, waits for them, and re-layouts  10.3 us (6%)
    pallas_call x24, Pallas kernels, call(): pl.pallas_call(kernel, name=title, grid_spec=pltpu.PrefetchScalarGridSpec...  74.4 us
    ppermute x20, waiting for transfers between devices, hop(): return lax.ppermute(a, 'batch', [(i, i ^ mask) for i in range(batch)])  30.2 us
    ppermute x20, starting transfers between devices, hop(): return lax.ppermute(a, 'batch', [(i, i ^ mask) for i in range(batch)])  23.4 us
    ppermute x2, waiting for transfers between devices, per_device(): pair_of = lambda a: (a, lax.ppermute(a, 'heads', swap))  7.41 us
    unnamed x29, local copies, waits for them, and re-layouts  4.35 us
  transfers between devices with their start and end apart: 27, of which 13 were waited for; matrix products, arithmetic and copies ran while one was open for 5% of the time, Pallas kernels for 36%

profile of v4, /device:TPU:0, one launch (start us, length us, event | category | flops | bytes accessed | tf_op | source)
XLA Modules:
  0.0 159.3 jit_solution(12591215418559378816)
XLA Ops:
  0.7 3.0 %collective-permute-start = (bf16[512,768]{1,0:T(8,128)(2,1)}, bf16[512,768]{1,0:T(8,128)(2,1)S(1)}, u32[]{:S(2)}, u32[]{:S(2)}) collective-permute-start(bf16[512,768]{1,0:T(8,128)(2,1)} %bitcast.14), channel_id=1, source_target_pairs={{0,1},{1,0},{2,3},{3,2},{4,5},{5,4},{6,7},{7,6},{8,9},{9,8},{10,11... | collective-permute-start | bytes 2359304 | tf_op jit(solution)/shard_map/ppermute | solution.py:881
  15.8 6.5 %collective-permute-done.other_ref = bf16[512,768]{1,0:T(8,128)(2,1)S(1)} collective-permute-done((bf16[512,768]{1,0:T(8,128)(2,1)}, bf16[512,768]{1,0:T(8,128)(2,1)S(1)}, u32[]{:S(2)}, u32[]{:S(2)}) %collective-permute-start) | collective-permute-done | bytes 786464 | tf_op jit(solution)/shard_map/ppermute | solution.py:881
  22.3 12.9 %forward_kernel.1 = (bf16[1024,768]{1,0:T(8,128)(2,1)S(1)}, f32[1024,768]{1,0:T(8,128)S(1)}, f32[1024,768]{1,0:T(8,128)S(1)}, bf16[1024,768]{1,0:T(8,128)(2,1)S(...) custom-call(s32[5]{0:T(128)S(1)} %stack.23.at_ref, ...), custom_call_target="tpu_custom_call" | custom-call | flops 17999998976 | tf_op jit(solution)/shard_map/forward_kernel/pallas_call | solution.py:806
  42.3 2.6 %branch_kernel.1 = (bf16[512,768]{1,0:T(8,128)(2,1)S(1)}, bf16[512,768]{1,0:T(8,128)(2,1)S(1)}) custom-call(s32[5]{0:T(128)S(1)} %stack.23.at_ref, bf16[1024,768]{1,0:T(8,128)(2,1)S(1)} %get-tuple-element.131.gg_ref, bf16[768,768]{1,0:T(8,128)(2,1)S(1)} %get-tuple-element.132.out_w), custom_call_target="tpu_custom_call" | custom-call | flops 2400000000 | tf_op jit(solution)/shard_map/branch_kernel/pallas_call | solution.py:806
  45.8 7.1 %gate_kernel.1 = (bf16[1024,768]{1,0:T(8,128)(2,1)S(1)}, bf16[1024,768]{1,0:T(8,128)(2,1)S(1)}, bf16[384,1536]{1,0:T(8,128)(2,1)S(1)}, bf16[384,1536]{1,0:T(8,12...) custom-call(s32[5]{0:T(128)S(1)} %stack.23.at_ref, bf16[512,768]{1,0:T(8,128)(2,1)S(1)} %bitcast.20, ...), custom_call_target="tpu_custom_call" | custom-call | flops 9600000000 | tf_op jit(solution)/shard_map/gate_kernel/pallas_call | solution.py:806
  53.9 2.8 %gate_back_kernel.1.refs_2_.from_gate = f32[1024,768]{1,0:T(8,128)S(1)} custom-call(s32[5]{0:T(128)S(1)} %stack.23.at_ref, bf16[1024,768]{1,0:T(8,128)(2,1)S(1)} %get-tuple-element.144.dg_ref, bf16[768,768]{1,0:T(8,128)(2,1)S(1)} %get-tuple-element.118.gate_w), custom_call_target="tpu_custom_call" | custom-call | flops 4000000000 | tf_op jit(solution)/shard_map/gate_back_kernel/pallas_call | solution.py:806
  59.6 9.3 %backward_kernel.2 = (bf16[512,768]{1,0:T(8,128)(2,1)S(1)}, bf16[512,256]{1,0:T(8,128)(2,1)S(1)}, bf16[512,128]{1,0:T(8,128)(2,1)S(1)}, f32[128,768]{1,0:T(8,128...) custom-call(s32[5]{0:T(128)S(1)} %stack.23.at_ref, ...), custom_call_target="tpu_custom_call" | custom-call | flops 7000000000 | tf_op jit(solution)/shard_map/backward_kernel/pallas_call | solution.py:806
  68.8 4.6 %collective-permute-done.6.refs_1_ = bf16[192,1536]{1,0:T(8,128)(2,1)S(1)} collective-permute-done((bf16[192,1536]{1,0:T(8,128)(2,1)S(1)}, bf16[192,1536]{1,0:T(8,128)(2,1)S(1)}, u32[]{:S(2)}, u32[]{:S(2)}) %collective-permute-start.6) | collective-permute-done | bytes 589856 | tf_op jit(solution)/shard_map/ppermute | solution.py:893
  76.0 2.6 %collective-permute-start.9 = (bf16[48,1536]{1,0:T(8,128)(2,1)S(1)}, bf16[48,1536]{1,0:T(8,128)(2,1)S(1)}, u32[]{:S(2)}, u32[]{:S(2)}) collective-permute-start(bf16[48,1536]{1,0:T(8,128)(2,1)S(1)} %get-tuple-element.185), channel_id=1, source_target_pairs={{0,16},{2,18},{4,20},{6,22},{8,24},{10,26},{12,28},{14,30},{16,0},... | collective-permute-start | bytes 442376 | tf_op jit(solution)/shard_map/ppermute | solution.py:893
  78.8 10.1 %backward_kernel.3 = (bf16[512,768]{1,0:T(8,128)(2,1)S(1)}, bf16[512,256]{1,0:T(8,128)(2,1)S(1)}, bf16[512,128]{1,0:T(8,128)(2,1)S(1)}, f32[128,768]{1,0:T(8,128...) custom-call(s32[5]{0:T(128)S(1)} %stack.23.at_ref, ...), custom_call_target="tpu_custom_call" | custom-call | flops 7000000000 | tf_op jit(solution)/shard_map/backward_kernel/pallas_call | solution.py:806
  89.7 4.0 %weights_kernel.1 = (bf16[384,1152]{1,0:T(8,128)(2,1)S(1)}, bf16[384,1152]{1,0:T(8,128)(2,1)S(1)}, bf16[48,1536]{1,0:T(8,128)(2,1)S(1)}) custom-call(s32[5]{0:T(128)S(1)} %stack.23.at_ref, bf16[1024,768]{1,0:T(8,128)(2,1)S(1)} %get-tuple-element.139.normed_ref, bf16[512,768]{1,0:T(8,128)(2,1)S(1)} %get-tuple-element.170.refs_0_, ...), custom_call_target="tpu_custom_call" | custom-call | flops 1200000000 | tf_op jit(solution)/shard_map/weights_kernel/pallas_call | solution.py:806
  93.7 2.9 %collective-permute-start.18 = (bf16[48,1536]{1,0:T(8,128)(2,1)S(1)}, bf16[48,1536]{1,0:T(8,128)(2,1)S(1)}, u32[]{:S(2)}, u32[]{:S(2)}) collective-permute-start(bf16[48,1536]{1,0:T(8,128)(2,1)S(1)} %get-tuple-element.195.refs_4_), channel_id=1, source_target_pairs={{0,24},{2,26},{4,28},{6,30},{8,16},{10,18},{12,20},{14,22},{16,8},... | collective-permute-start | bytes 442376 | tf_op jit(solution)/shard_map/ppermute | solution.py:893
  100.1 3.6 %normed_grad_kernel.1 = (bf16[512,768]{1,0:T(8,128)(2,1)S(1)}, bf16[512,768]{1,0:T(8,128)(2,1)S(1)}) custom-call(s32[5]{0:T(128)S(1)} %stack.23.at_ref, f32[1024,768]{1,0:T(8,128)S(1)} %gate_back_kernel.1.refs_2_.from_gate, bf16[512,768]{1,0:T(8,128)(2,1)S(1)} %get-tuple-element.170.refs_0_, bf16[512,256]{1,0:T(8,128)(2,1)S(1)} %get-tuple-element.171.refs_1_, ...), custom_call_target="tpu_custom_call" | custom-call | flops 4800000000 | tf_op jit(solution)/shard_map/normed_grad_kernel/pallas_call | solution.py:806
  105.7 4.8 %collective-permute-done.12.refs_1_ = bf16[192,1152]{1,0:T(8,128)(2,1)S(1)} collective-permute-done((bf16[192,1152]{1,0:T(8,128)(2,1)S(1)}, bf16[192,1152]{1,0:T(8,128)(2,1)S(1)}, u32[]{:S(2)}, u32[]{:S(2)}) %collective-permute-start.12) | collective-permute-done | bytes 442400 | tf_op jit(solution)/shard_map/ppermute | solution.py:893
  117.9 5.3 %collective-permute-done.14.refs_2_ = bf16[48,1152]{1,0:T(8,128)(2,1)S(1)} collective-permute-done((bf16[48,1152]{1,0:T(8,128)(2,1)S(1)}, bf16[48,1152]{1,0:T(8,128)(2,1)S(1)}, u32[]{:S(2)}, u32[]{:S(2)}) %collective-permute-start.14) | collective-permute-done | bytes 110624 | tf_op jit(solution)/shard_map/ppermute | solution.py:893
  126.6 2.9 %collective-permute-done.19.other_ref = bf16[48,384]{1,0:T(8,128)(2,1)S(1)} collective-permute-done((bf16[48,384]{1,0:T(8,128)(2,1)S(1)}, bf16[48,384]{1,0:T(8,128)(2,1)S(1)}, u32[]{:S(2)}, u32[]{:S(2)}) %collective-permute-start.19) | collective-permute-done | bytes 36896 | tf_op jit(solution)/shard_map/ppermute | solution.py:1264
  130.2 2.4 %collective-permute-start.22 = (bf16[48,1152]{1,0:T(8,128)(2,1)S(1)}, bf16[48,1152]{1,0:T(8,128)(2,1)S(1)}, u32[]{:S(2)}, u32[]{:S(2)}) collective-permute-start(bf16[48,1152]{1,0:T(8,128)(2,1)S(1)} %heads_kernel.1.refs_0_), channel_id=1, source_target_pairs={{0,24},{2,26},{4,28},{6,30},{8,16},{10,18},{12,20},{14,22},{16,8},... | collective-permute-start | bytes 331784 | tf_op jit(solution)/shard_map/ppermute | solution.py:893
  134.6 2.3 %input_kernel.1 = (f32[512,768]{1,0:T(8,128)}, f32[8,128]{1,0:T(8,128)S(1)}) custom-call(s32[5]{0:T(128)S(1)} %stack.23.at_ref, bf16[512,768]{1,0:T(8,128)(2,1)S(1)} %bitcast.17, bf16[512,768]{1,0:T(8,128)(2,1)S(1)} %bitcast.21, bf16[512,768]{1,0:T(8,128)(2,1)S(1)} %get-tuple-element.176.own_ref.refs_2_, ...), custom_call_target="tpu_custom_call" | custom-call | flops 2000000000 | tf_op jit(solution)/shard_map/input_kernel/pallas_call | solution.py:806
  137.3 2.8 %collective-permute-done.21.refs_2_ = bf16[48,1152]{1,0:T(8,128)(2,1)S(1)} collective-permute-done((bf16[48,1152]{1,0:T(8,128)(2,1)S(1)}, bf16[48,1152]{1,0:T(8,128)(2,1)S(1)}, u32[]{:S(2)}, u32[]{:S(2)}) %collective-permute-start.21) | collective-permute-done | bytes 110624 | tf_op jit(solution)/shard_map/ppermute | solution.py:893
  141.5 2.3 %collective-permute-done.25.other_ref = bf16[384,1536]{1,0:T(8,128)(2,1)S(1)} collective-permute-done((bf16[384,1536]{1,0:T(8,128)(2,1)S(1)}, bf16[384,1536]{1,0:T(8,128)(2,1)S(1)}, u32[]{:S(2)}, u32[]{:S(2)}) %collective-permute-start.25) | collective-permute-done | bytes 1179680 | tf_op jit(solution)/shard_map/ppermute | solution.py:893
  143.7 3.0 %early_kernel.1 = (f32[768,768]{1,0:T(8,128)}, f32[768,768]{1,0:T(8,128)}, f32[8,128]{1,0:T(8,128)S(1)}) custom-call(s32[5]{0:T(128)S(1)} %stack.23.at_ref, bf16[384,1536]{1,0:T(8,128)(2,1)S(1)} %get-tuple-element.202.own_ref, bf16[384,1536]{1,0:T(8,128)(2,1)S(1)} %collective-permute-done.25.other_ref), custom_call_target="tpu_custom_call" | custom-call | flops 3000000000 | tf_op jit(solution)/shard_map/early_kernel/pallas_call | solution.py:806
  146.7 6.8 %collective-permute-done.24.refs_1_ = bf16[192,1152]{1,0:T(8,128)(2,1)S(1)} collective-permute-done((bf16[192,1152]{1,0:T(8,128)(2,1)S(1)}, bf16[192,1152]{1,0:T(8,128)(2,1)S(1)}, u32[]{:S(2)}, u32[]{:S(2)}) %collective-permute-start.24) | collective-permute-done | bytes 442400 | tf_op jit(solution)/shard_map/ppermute | solution.py:893
  154.2 2.4 %collective-permute-done.26.other_ref = bf16[384,1152]{1,0:T(8,128)(2,1)S(1)} collective-permute-done((bf16[384,1152]{1,0:T(8,128)(2,1)S(1)}, bf16[384,1152]{1,0:T(8,128)(2,1)S(1)}, u32[]{:S(2)}, u32[]{:S(2)}) %collective-permute-start.26) | collective-permute-done | bytes 884768 | tf_op jit(solution)/shard_map/ppermute | solution.py:893
  156.6 2.5 %late_kernel.1 = (f32[768,768]{1,0:T(8,128)}, f32[768,256]{1,0:T(8,128)}, f32[12,768]{1,0:T(8,128)}, f32[4,768]{1,0:T(4,128)}, f32[768]{0:T(1024)}, /*index=5*/f...) custom-call(s32[5]{0:T(128)S(1)} %stack.23.at_ref, ...), custom_call_target="tpu_custom_call" | custom-call | flops 3000000000 | tf_op jit(solution)/shard_map/late_kernel/pallas_call | solution.py:806
  (101 shorter events, 48.7 us)
Async XLA Ops:
  0.7 21.6 %collective-permute-start = (bf16[512,768]{1,0:T(8,128)(2,1)}, bf16[512,768]{1,0:T(8,128)(2,1)S(1)}, u32[]{:S(2)}, u32[]{:S(2)}) collective-permute-start(bf16[512,768]{1,0:T(8,128)(2,1)} %bitcast.14), channel_id=1, source_target_pairs={{0,1},{1,0},{2,3},{3,2},{4,5},{5,4},{6,7},{7,6},{8,9},{9,8},{10,11... | collective-permute-start | bytes 2359304 | tf_op jit(solution)/shard_map/ppermute | solution.py:881
  3.7 34.6 %collective-permute-start.2 = (bf16[512,768]{1,0:T(8,128)(2,1)}, bf16[512,768]{1,0:T(8,128)(2,1)S(1)}, u32[]{:S(2)}, u32[]{:S(2)}) collective-permute-start(bf16[512,768]{1,0:T(8,128)(2,1)} %bitcast.18), channel_id=1, source_target_pairs={{0,1},{1,0},{2,3},{3,2},{4,5},{5,4},{6,7},{7,6},{8,9},{9,8},{10,11... | collective-permute-start | bytes 2359304 | tf_op jit(solution)/shard_map/ppermute | solution.py:881
  40.3 4.7 %collective-permute-start.3 = (f32[8,512]{1,0:T(8,128)S(1)}, f32[8,512]{1,0:T(8,128)S(1)}, u32[]{:S(2)}, u32[]{:S(2)}) collective-permute-start(f32[8,512]{1,0:T(8,128)S(1)} %get-tuple-element.137.here_b), channel_id=1, source_target_pairs={{0,1},{1,0},{2,3},{3,2},{4,5},{5,4},{6,7},{7,6},{8,9},{9,8},{10,11... | collective-permute-start | bytes 49160 | tf_op jit(solution)/shard_map/ppermute | solution.py:882
  52.9 3.8 %collective-permute-start.5 = (bf16[384,1536]{1,0:T(8,128)(2,1)S(1)}, bf16[384,1536]{1,0:T(8,128)(2,1)S(1)}, u32[]{:S(2)}, u32[]{:S(2)}) collective-permute-start(bf16[384,1536]{1,0:T(8,128)(2,1)S(1)} %get-tuple-element.160), channel_id=1, source_target_pairs={{0,2},{2,0},{4,6},{6,4},{8,10},{10,8},{12,14},{14,12},{16,18},{18,... | collective-permute-start | bytes 3538952 | tf_op jit(solution)/shard_map/ppermute | solution.py:893
  52.9 25.9 %collective-permute-start.1 = (bf16[512,768]{1,0:T(8,128)(2,1)S(1)}, bf16[512,768]{1,0:T(8,128)(2,1)S(1)}, u32[]{:S(2)}, u32[]{:S(2)}) collective-permute-start(bf16[512,768]{1,0:T(8,128)(2,1)S(1)} %get-tuple-element.134), channel_id=1, source_target_pairs={{0,1},{1,0},{2,3},{3,2},{4,5},{5,4},{6,7},{7,6},{8,9},{9,8},{10,11... | collective-permute-start | bytes 2359304 | tf_op jit(solution)/shard_map/ppermute | solution.py:1050
  58.0 15.5 %collective-permute-start.6 = (bf16[192,1536]{1,0:T(8,128)(2,1)S(1)}, bf16[192,1536]{1,0:T(8,128)(2,1)S(1)}, u32[]{:S(2)}, u32[]{:S(2)}) collective-permute-start(bf16[192,1536]{1,0:T(8,128)(2,1)S(1)} %get-tuple-element.168), channel_id=1, source_target_pairs={{0,4},{2,6},{4,0},{6,2},{8,12},{10,14},{12,8},{14,10},{16,20},{18,... | collective-permute-start | bytes 1769480 | tf_op jit(solution)/shard_map/ppermute | solution.py:893
  74.3 14.6 %collective-permute-start.8 = (bf16[48,1536]{1,0:T(8,128)(2,1)S(1)}, bf16[48,1536]{1,0:T(8,128)(2,1)S(1)}, u32[]{:S(2)}, u32[]{:S(2)}) collective-permute-start(bf16[48,1536]{1,0:T(8,128)(2,1)S(1)} %get-tuple-element.184), channel_id=1, source_target_pairs={{0,8},{2,10},{4,12},{6,14},{8,0},{10,2},{12,4},{14,6},{16,24},{18,... | collective-permute-start | bytes 442376 | tf_op jit(solution)/shard_map/ppermute | solution.py:893
  76.0 13.7 %collective-permute-start.9 = (bf16[48,1536]{1,0:T(8,128)(2,1)S(1)}, bf16[48,1536]{1,0:T(8,128)(2,1)S(1)}, u32[]{:S(2)}, u32[]{:S(2)}) collective-permute-start(bf16[48,1536]{1,0:T(8,128)(2,1)S(1)} %get-tuple-element.185), channel_id=1, source_target_pairs={{0,16},{2,18},{4,20},{6,22},{8,24},{10,26},{12,28},{14,30},{16,0},... | collective-permute-start | bytes 442376 | tf_op jit(solution)/shard_map/ppermute | solution.py:893
  78.6 11.1 %collective-permute-start.10 = (bf16[48,1536]{1,0:T(8,128)(2,1)S(1)}, bf16[48,1536]{1,0:T(8,128)(2,1)S(1)}, u32[]{:S(2)}, u32[]{:S(2)}) collective-permute-start(bf16[48,1536]{1,0:T(8,128)(2,1)S(1)} %get-tuple-element.186), channel_id=1, source_target_pairs={{0,24},{2,26},{4,28},{6,30},{8,16},{10,18},{12,20},{14,22},{16,8},... | collective-permute-start | bytes 442376 | tf_op jit(solution)/shard_map/ppermute | solution.py:893
  93.6 3.7 %collective-permute-start.11 = (bf16[384,1152]{1,0:T(8,128)(2,1)S(1)}, bf16[384,1152]{1,0:T(8,128)(2,1)S(1)}, u32[]{:S(2)}, u32[]{:S(2)}) collective-permute-start(bf16[384,1152]{1,0:T(8,128)(2,1)S(1)} %get-tuple-element.188), channel_id=1, source_target_pairs={{0,2},{2,0},{4,6},{6,4},{8,10},{10,8},{12,14},{14,12},{16,18},{18,... | collective-permute-start | bytes 2654216 | tf_op jit(solution)/shard_map/ppermute | solution.py:893
  93.7 18.9 %collective-permute-start.18 = (bf16[48,1536]{1,0:T(8,128)(2,1)S(1)}, bf16[48,1536]{1,0:T(8,128)(2,1)S(1)}, u32[]{:S(2)}, u32[]{:S(2)}) collective-permute-start(bf16[48,1536]{1,0:T(8,128)(2,1)S(1)} %get-tuple-element.195.refs_4_), channel_id=1, source_target_pairs={{0,24},{2,26},{4,28},{6,30},{8,16},{10,18},{12,20},{14,22},{16,8},... | collective-permute-start | bytes 442376 | tf_op jit(solution)/shard_map/ppermute | solution.py:893
  96.6 17.9 %collective-permute-start.17 = (bf16[48,1536]{1,0:T(8,128)(2,1)S(1)}, bf16[48,1536]{1,0:T(8,128)(2,1)S(1)}, u32[]{:S(2)}, u32[]{:S(2)}) collective-permute-start(bf16[48,1536]{1,0:T(8,128)(2,1)S(1)} %get-tuple-element.195.refs_4_), channel_id=1, source_target_pairs={{0,16},{2,18},{4,20},{6,22},{8,24},{10,26},{12,28},{14,30},{16,0},... | collective-permute-start | bytes 442376 | tf_op jit(solution)/shard_map/ppermute | solution.py:893
  98.5 12.0 %collective-permute-start.12 = (bf16[192,1152]{1,0:T(8,128)(2,1)S(1)}, bf16[192,1152]{1,0:T(8,128)(2,1)S(1)}, u32[]{:S(2)}, u32[]{:S(2)}) collective-permute-start(bf16[192,1152]{1,0:T(8,128)(2,1)S(1)} %get-tuple-element.190), channel_id=1, source_target_pairs={{0,4},{2,6},{4,0},{6,2},{8,12},{10,14},{12,8},{14,10},{16,20},{18,... | collective-permute-start | bytes 1327112 | tf_op jit(solution)/shard_map/ppermute | solution.py:893
  103.7 30.9 %collective-permute-start.7 = (bf16[512,768]{1,0:T(8,128)(2,1)S(1)}, bf16[512,768]{1,0:T(8,128)(2,1)S(1)}, u32[]{:S(2)}, u32[]{:S(2)}) collective-permute-start(bf16[512,768]{1,0:T(8,128)(2,1)S(1)} %get-tuple-element.177), channel_id=1, source_target_pairs={{0,1},{1,0},{2,3},{3,2},{4,5},{5,4},{6,7},{7,6},{8,9},{9,8},{10,11... | collective-permute-start | bytes 2359304 | tf_op jit(solution)/shard_map/ppermute | solution.py:1050
  104.8 13.1 %collective-permute-start.16 = (bf16[48,1536]{1,0:T(8,128)(2,1)S(1)}, bf16[48,1536]{1,0:T(8,128)(2,1)S(1)}, u32[]{:S(2)}, u32[]{:S(2)}) collective-permute-start(bf16[48,1536]{1,0:T(8,128)(2,1)S(1)} %get-tuple-element.195.refs_4_), channel_id=1, source_target_pairs={{0,8},{2,10},{4,12},{6,14},{8,0},{10,2},{12,4},{14,6},{16,24},{18,... | collective-permute-start | bytes 442376 | tf_op jit(solution)/shard_map/ppermute | solution.py:893
  111.4 6.5 %collective-permute-start.13 = (bf16[48,1152]{1,0:T(8,128)(2,1)S(1)}, bf16[48,1152]{1,0:T(8,128)(2,1)S(1)}, u32[]{:S(2)}, u32[]{:S(2)}) collective-permute-start(bf16[48,1152]{1,0:T(8,128)(2,1)S(1)} %get-tuple-element.192), channel_id=1, source_target_pairs={{0,8},{2,10},{4,12},{6,14},{8,0},{10,2},{12,4},{14,6},{16,24},{18,... | collective-permute-start | bytes 331784 | tf_op jit(solution)/shard_map/ppermute | solution.py:893
  112.6 10.6 %collective-permute-start.14 = (bf16[48,1152]{1,0:T(8,128)(2,1)S(1)}, bf16[48,1152]{1,0:T(8,128)(2,1)S(1)}, u32[]{:S(2)}, u32[]{:S(2)}) collective-permute-start(bf16[48,1152]{1,0:T(8,128)(2,1)S(1)} %get-tuple-element.193), channel_id=1, source_target_pairs={{0,16},{2,18},{4,20},{6,22},{8,24},{10,26},{12,28},{14,30},{16,0},... | collective-permute-start | bytes 331784 | tf_op jit(solution)/shard_map/ppermute | solution.py:893
  114.5 8.7 %collective-permute-start.15 = (bf16[48,1152]{1,0:T(8,128)(2,1)S(1)}, bf16[48,1152]{1,0:T(8,128)(2,1)S(1)}, u32[]{:S(2)}, u32[]{:S(2)}) collective-permute-start(bf16[48,1152]{1,0:T(8,128)(2,1)S(1)} %get-tuple-element.194), channel_id=1, source_target_pairs={{0,24},{2,26},{4,28},{6,30},{8,16},{10,18},{12,20},{14,22},{16,8},... | collective-permute-start | bytes 331784 | tf_op jit(solution)/shard_map/ppermute | solution.py:893
  124.0 16.2 %collective-permute-start.23 = (bf16[192,1536]{1,0:T(8,128)(2,1)S(1)}, bf16[192,1536]{1,0:T(8,128)(2,1)S(1)}, u32[]{:S(2)}, u32[]{:S(2)}) collective-permute-start(bf16[192,1536]{1,0:T(8,128)(2,1)S(1)} %get-tuple-element.199.refs_4_), channel_id=1, source_target_pairs={{0,4},{2,6},{4,0},{6,2},{8,12},{10,14},{12,8},{14,10},{16,20},{18,... | collective-permute-start | bytes 1769480 | tf_op jit(solution)/shard_map/ppermute | solution.py:893
  125.5 4.0 %collective-permute-start.19 = (bf16[48,384]{1,0:T(8,128)(2,1)S(1)}, bf16[48,384]{1,0:T(8,128)(2,1)S(1)}, u32[]{:S(2)}, u32[]{:S(2)}) collective-permute-start(bf16[48,384]{1,0:T(8,128)(2,1)S(1)} %get-tuple-element.198.own_ref), channel_id=1, source_target_pairs={{0,1},{1,0},{2,3},{3,2},{4,5},{5,4},{6,7},{7,6},{8,9},{9,8},{10,11... | collective-permute-start | bytes 110600 | tf_op jit(solution)/shard_map/ppermute | solution.py:1264
  130.2 7.1 %collective-permute-start.22 = (bf16[48,1152]{1,0:T(8,128)(2,1)S(1)}, bf16[48,1152]{1,0:T(8,128)(2,1)S(1)}, u32[]{:S(2)}, u32[]{:S(2)}) collective-permute-start(bf16[48,1152]{1,0:T(8,128)(2,1)S(1)} %heads_kernel.1.refs_0_), channel_id=1, source_target_pairs={{0,24},{2,26},{4,28},{6,30},{8,16},{10,18},{12,20},{14,22},{16,8},... | collective-permute-start | bytes 331784 | tf_op jit(solution)/shard_map/ppermute | solution.py:893
  132.6 7.6 %collective-permute-start.21 = (bf16[48,1152]{1,0:T(8,128)(2,1)S(1)}, bf16[48,1152]{1,0:T(8,128)(2,1)S(1)}, u32[]{:S(2)}, u32[]{:S(2)}) collective-permute-start(bf16[48,1152]{1,0:T(8,128)(2,1)S(1)} %heads_kernel.1.refs_0_), channel_id=1, source_target_pairs={{0,16},{2,18},{4,20},{6,22},{8,24},{10,26},{12,28},{14,30},{16,0},... | collective-permute-start | bytes 331784 | tf_op jit(solution)/shard_map/ppermute | solution.py:893
  133.6 6.6 %collective-permute-start.20 = (bf16[48,1152]{1,0:T(8,128)(2,1)S(1)}, bf16[48,1152]{1,0:T(8,128)(2,1)S(1)}, u32[]{:S(2)}, u32[]{:S(2)}) collective-permute-start(bf16[48,1152]{1,0:T(8,128)(2,1)S(1)} %heads_kernel.1.refs_0_), channel_id=1, source_target_pairs={{0,8},{2,10},{4,12},{6,14},{8,0},{10,2},{12,4},{14,6},{16,24},{18,... | collective-permute-start | bytes 331784 | tf_op jit(solution)/shard_map/ppermute | solution.py:893
  140.9 12.6 %collective-permute-start.24 = (bf16[192,1152]{1,0:T(8,128)(2,1)S(1)}, bf16[192,1152]{1,0:T(8,128)(2,1)S(1)}, u32[]{:S(2)}, u32[]{:S(2)}) collective-permute-start(bf16[192,1152]{1,0:T(8,128)(2,1)S(1)} %get-tuple-element.201.refs_0_), channel_id=1, source_target_pairs={{0,4},{2,6},{4,0},{6,2},{8,12},{10,14},{12,8},{14,10},{16,20},{18,... | collective-permute-start | bytes 1327112 | tf_op jit(solution)/shard_map/ppermute | solution.py:893
  (17 other events, 70.5 us)

commit v5 on v4

--- a/solution.py
+++ b/solution.py
@@ -247,13 +247,16 @@
         buf[:, 0:8, :] = buf[:, BLOCK : BLOCK + 8, :]
 
 
-def stats_kernel(at_ref, cot_ref, gg_ref, sq_ref, out_w, og_ref, stats_ref):
+def stats_kernel(at_ref, cot_ref, gg_ref, sq_ref, out_w, *refs):
+    og_ref, stats_ref = refs[-2:]
+    if len(refs) > 2:
+        stats_ref[8:, :] = refs[0][...]
     og = dot(cot_ref[...], out_w[...], NT)
     og_ref[...] = og
     prod = (og * gg_ref[...].astype(f32)).astype(bf16)
     dots = dot(jnp.ones((8, prod.shape[1]), bf16), prod, NT)
     row = lax.broadcasted_iota(jnp.int32, dots.shape, 0)
-    stats_ref[...] = jnp.where(row == 0, sq_ref[...], dots)
+    stats_ref[:8, :] = jnp.where(row == 0, sq_ref[...], dots)
 
 
 def bring_kernel(at_ref, *refs):
@@ -406,6 +409,11 @@
             emit(at_ref, (grad_gate, grad_out), (first_ref, second_ref))
 
 
+def partial_kernel(from_row, at_ref, normed_ref, *refs):
+    for low, out in zip(refs[:3], refs[3:]):
+        out[...] = dot(normed_ref[from_row:, :], low[...], TN)
+
+
 def weights_kernel(fast, at_ref, normed_ref, *refs):
     lows, refs = refs[:6], refs[6:]
     value_w, state_w, step_w, gain_ref, vec_ref, svec_ref, head_ref, ggain_ref, norm_ref = refs[:9]
@@ -416,8 +424,8 @@
         for r in pieces[1:]:
             total = total + r[...].astype(f32)
         done_ref[...] = total.astype(bf16)
-    for a, early, late in zip(acc, lows[:3], lows[3:]):
-        a[...] = dot(normed_ref[...], jnp.concatenate([early[...], late[...]], axis=0), TN)
+    for a, low, rest in zip(acc, lows[:3], lows[3:]):
+        a[...] = rest[...] + dot(normed_ref[: low.shape[0], :], low[...], TN)
     norm = norm_ref[...]
     for a, w in zip(acc, (value_w, state_w, step_w)):
         norm = norm + row_sums(a[...], w[...])
@@ -494,6 +502,9 @@
 def join_step(me, ins, out):
     rows = ins[0].shape[0]
     count = out.shape[0] // rows
+    if count == 1:
+        out[...] = ins[0][...]
+        return
     left = 0
     for first in range(0, len(ins), count):
         right = left + ins[first].shape[1]
@@ -575,14 +586,27 @@
         left = right
 
 
-def late_kernel(at_ref, own_ref, other_ref, *refs):
-    outs, block = refs[:-1], refs[-1]
+def widen(piece, outs):
     left = 0
-    for o in (outs[0], outs[1], block):
+    for o in outs:
         right = left + o.shape[1]
-        for at, v in halves_of(at_ref, own_ref, other_ref, left, right):
-            o[at, :] = v
+        o[...] = piece[:, left:right].astype(f32)
         left = right
+
+
+def place_kernel(at_ref, piece_ref, *refs):
+    widen(piece_ref, refs[-3:-1])
+    refs[-1][...] = jnp.zeros_like(refs[-1])
+
+
+def late_kernel(at_ref, *refs):
+    pieces, outs, block = refs[:4], refs[6:-1], refs[-1]
+    widen(pieces[3], outs[:2])
+    rows, right = pieces[0].shape
+    for n, piece in enumerate(pieces):
+        start = (at_ref[1] ^ (n // 2)) * 2 + (at_ref[2] ^ (n % 2))
+        at = pl.ds(pl.multiple_of(start * rows, 16), rows)
+        block[at, :] = piece[:, right - LANES :].astype(f32)
     full = join_rest(block[...])
     rows = full.T
     outs[2][...] = rows[: outs[2].shape[0]]
@@ -782,26 +806,28 @@
 
 
 MIB = dict(
-    forward_kernel=14,
-    stats_kernel=8,
-    branch_kernel=8,
-    gate_kernel=12,
-    backward_kernel=24,
-    weights_kernel=14,
+    forward_kernel=11,
+    stats_kernel=6,
+    branch_kernel=6,
+    gate_kernel=10,
+    backward_kernel=17,
+    weights_kernel=11,
     normed_grad_kernel=12,
     mixed_kernel=8,
     input_kernel=8,
     early_kernel=10,
     late_kernel=10,
+    place_kernel=8,
+    partial_kernel=8,
 )
-COST = dict(forward_kernel=4.5, backward_kernel=7, stats_kernel=1, branch_kernel=.6, gate_kernel=2.4, weights_kernel=1.2, normed_grad_kernel=1.2, mixed_kernel=1, input_kernel=1, early_kernel=3, late_kernel=3)
+COST = dict(forward_kernel=4.5, backward_kernel=7, stats_kernel=1, branch_kernel=.6, gate_kernel=2.4, weights_kernel=1.2, normed_grad_kernel=1.2, mixed_kernel=1, input_kernel=1, early_kernel=3, late_kernel=3, place_kernel=1, partial_kernel=2)
 
 
 def whole(array):
     return pl.BlockSpec(array.shape, lambda i, at: (0,) * array.ndim)
 
 
-def call(kernel, blocks, at, ins, outs, scratch, small=True):
+def call(kernel, blocks, at, ins, outs, scratch, small=True, aliases=()):
     title = getattr(kernel, "func", kernel).__name__
     return pl.pallas_call(
         kernel,
@@ -818,6 +844,7 @@
             for shape, dtype, _, *rest in outs
         ],
         cost_estimate=pl.CostEstimate(flops=int(COST.get(title, 1)*blocks * 10**9), bytes_accessed=0, transcendentals=0),
+        input_output_aliases=dict(aliases),
         compiler_params=pltpu.CompilerParams(
             dimension_semantics=("arbitrary",), vmem_limit_bytes=(MIB.get(title, 16) if small else 48) * 2**20
         ),
@@ -1005,7 +1032,7 @@
             low(BLOCK, width),
         ],
     )
-    def stats_of(cot_rows, theirs):
+    def stats_of(cot_rows, theirs, *before):
         first = (lambda a: (1 - a[0]) * half_blocks) if theirs else (lambda a: a[0] * half_blocks)
         count = cot_rows.shape[0]
         return run(
@@ -1017,24 +1044,29 @@
                 (gg, rows(width, lambda i, a: (first(a) + i, 0))),
                 (sq, pl.BlockSpec((8, BLOCK), lambda i, a: (0, first(a) + i))),
                 (out_w, None),
+                *[(b, along) for b in before],
             ],
-            [((count, width), f32, rows(width), fast), ((8, count), f32, along)],
+            [
+                ((count, width), f32, rows(width), fast),
+                (
+                    (8 + 8 * len(before), count),
+                    f32,
+                    pl.BlockSpec((8 + 8 * len(before), BLOCK), lambda i, a: (0, i)),
+                ),
+            ],
             [],
         )
 
     og, stats = stats_of(own_cot, False)
     if two:
-        og_b, stats_b = stats_of(other_cot, True)
-        got_b, got = add_other(stats), add_other(stats_b)
+        og_b, stats = stats_of(other_cot, True, stats)
     else:
-        og_b, stats_b, got = og, stats, add_other(stats)
-        got_b = got
-
-    def own_along(i, a):
-        return own_block(i, a)[::-1]
-
-    def other_along(i, a):
-        return other_read(i, a)[::-1]
+        og_b = og
+    got = add_other(stats)
+    above = 1 if two else 0
+
+    def stats_at(row, block):
+        return pl.BlockSpec((8, BLOCK), lambda i, a: (row, block(i, a)[0]))
 
     branch, branch_sent = run(
         functools.partial(branch_kernel, half_blocks),
@@ -1069,10 +1101,10 @@
         [
             (own_cot, rows(model, own_block)),
             (other_cot, rows(model, other_read)),
-            (stats, pl.BlockSpec((8, BLOCK), own_along)),
-            (got, pl.BlockSpec((8, BLOCK), own_along)),
-            (stats_b, pl.BlockSpec((8, BLOCK), other_along)),
-            (got_b, pl.BlockSpec((8, BLOCK), other_along)),
+            (stats, stats_at(above, own_block)),
+            (got, stats_at(0, own_block)),
+            (stats, stats_at(0, other_read)),
+            (got, stats_at(above, other_read)),
             (normed, None),
             (og, rows(width, own_block)),
             (og_b, rows(width, other_read)),
@@ -1149,7 +1181,10 @@
         )
         return out[:3], out[3:]
 
-    own_stats = along if two else pl.BlockSpec((8, BLOCK), lambda i, a: (0, i + a[4] // BLOCK))
+    if two:
+        own_stats, their_stats = stats_at(1, lambda i, a: (i, 0)), along
+    else:
+        own_stats = their_stats = stats_at(0, lambda i, a: (i + a[4] // BLOCK, 0))
     mixed, token = run(
         functools.partial(mixed_kernel, inner_all),
         rows_here // BLOCK,
@@ -1159,7 +1194,7 @@
             (branch, rows(model)),
             (branch_got, rows(model)),
             (stats, own_stats),
-            (got, own_stats),
+            (got, their_stats),
         ],
         [((rows_here, model), f32, rows(model)), ((8, LANES), f32, fixed(8, LANES))],
         [],
@@ -1180,10 +1215,20 @@
         early = [kept, hop(sent, "line")]
         behind = (kept,)
     low_b, carry = backward(cut, blocks - cut, (), behind)
+    partial = run(
+        functools.partial(partial_kernel, cut * BLOCK),
+        1,
+        at,
+        [(normed, None), *[(a, None) for a in low_b]],
+        [
+            ((model, a.shape[1]), f32, fixed(model, a.shape[1])) for a in low_b
+        ],
+        [],
+    )
     if fast:
         ((kept, *sent),) = stage(at, [("fold", 3, early, 4, False)])
         early = [kept] + [hop(a, k + 1) for k, a in enumerate(sent)]
-        behind = (kept, branch_got)
+        behind = (kept, branch_got, partial[2])
     low_a, carry = backward(0, cut, carry, behind)
     vec, svec, head = carry[3:]
     early = early if fast else ()
@@ -1203,7 +1248,8 @@
         at,
         [
             (normed, None),
-            *[(a, None) for a, _ in lows],
+            *[(a, None) for a in low_a],
+            *[(a, None) for a in partial],
             (value_w, None),
             (state_proj, None),
             (step_w, None),
@@ -1281,10 +1327,31 @@
             + [((8, LANES), f32, fixed(8, LANES))],
             [],
         )
-        ((done,),) = stage(at, [("join", 2, [done, hop(done, "line")])], (token_c,))
+        quarter = done.shape[0]
+
+        def wide(n):
+            def index(i, a):
+                return ((a[1] ^ (n // 2)) * 2 + (a[2] ^ (n % 2)), 0)
+
+            return [((model, w), f32, pl.BlockSpec((quarter, w), index)) for w in (width, nstate2)]
+
+        def kept_in(arrays):
+            return [(a, pl.BlockSpec(memory_space=pl.ANY)) for a in arrays]
+
+        def place(n, piece, filled=()):
+            aliases = ((2, 0), (3, 1)) if filled else ()
+            ins = [(piece, None), *kept_in(filled)]
+            outs = wide(n) + [((8, LANES), f32, fixed(8, LANES))]
+            return run(place_kernel, 1, at, ins, outs, [], aliases=aliases)
+
+        got = hop(done, "line")
+        across = hop(done, "core")
+        *filled, token_d = place(0, done)
+        *filled, token_e = place(2, across, filled)
+        ((got,),) = stage(at, [("join", 2, [got])], (token_c, token_e))
+        done = [done, got, across, hop(got, "core")]
+        *filled, token_d = place(1, got, filled)
         shapes = [
-            (model, width),
-            (model, nstate2),
             (heads, model),
             (4, width),
             (width,),
@@ -1313,9 +1380,10 @@
             late_kernel,
             1,
             at,
-            [(done, None), (hop(done, "core"), None)],
-            [(shape, f32, fixed(*shape)) for shape in shapes],
+            [*[(a, None) for a in done], *kept_in(filled)],
+            wide(3) + [(shape, f32, fixed(*shape)) for shape in shapes],
             [big(model, LANES)],
+            aliases=((5, 0), (6, 1)),
         )
         return (
             mixed[None],

time: 160 us -> 157 us (0.981)
  waiting for transfers between devices: 41.3 us -> 33.8 us
  Pallas kernels: 74.4 us -> 79.2 us
    ppermute x20 -> x21, waiting for transfers between devices: 30.2 us -> 23.5 us  [hop(): return lax.ppermute(a, 'batch', [(i, i ^ mask) for i in range(batch)])]
    pallas_call x24 -> x28, Pallas kernels: 74.4 us -> 79.2 us  [call(): pl.pallas_call(kernel, name=title, grid_spec=pltpu.PrefetchScalarGridSpec...]
    ppermute x20 -> x21, starting transfers between devices: 23.4 us -> 23.8 us  [hop(): return lax.ppermute(a, 'batch', [(i, i ^ mask) for i in range(batch)])]
    unnamed x29 -> x17, local copies, waits for them, and re-layouts: 4.35 us -> 4.13 us
  transfers between devices with their start and end apart: 27 -> 27, of which waited for: 13 -> 12; matrix products, arithmetic and copies ran while one was open for 5% -> 5% of each run, Pallas kernels for 36% -> 41%
where the time goes in v5:
time: 157 us; the launch traced here: 156 us
  Pallas kernels  79.2 us (50%)
  waiting for transfers between devices  33.8 us (22%)
  starting transfers between devices  31.6 us (20%)
  local copies, waits for them, and re-layouts  10 us (6%)
    pallas_call x28, Pallas kernels, call(): pl.pallas_call(kernel, name=title, grid_spec=pltpu.PrefetchScalarGridSpec...  79.2 us
    ppermute x21, starting transfers between devices, hop(): return lax.ppermute(a, 'batch', [(i, i ^ mask) for i in range(batch)])  23.8 us
    ppermute x21, waiting for transfers between devices, hop(): return lax.ppermute(a, 'batch', [(i, i ^ mask) for i in range(batch)])  23.5 us
    ppermute x2, waiting for transfers between devices, per_device(): pair_of = lambda a: (a, lax.ppermute(a, 'heads', swap))  7.16 us
    unnamed x17, local copies, waits for them, and re-layouts  4.13 us
    ppermute x1, waiting for transfers between devices, per_device(): theirs = lax.ppermute(rest, 'heads', swap)  3.18 us
  transfers between devices with their start and end apart: 27, of which 12 were waited for; matrix products, arithmetic and copies ran while one was open for 5% of the time, Pallas kernels for 41%

profile of v5, /device:TPU:0, one launch (start us, length us, event | category | flops | bytes accessed | tf_op | source)
XLA Modules:
  0.0 156.1 jit_solution(13985246368779994975)
XLA Ops:
  0.7 3.0 %collective-permute-start = (bf16[512,768]{1,0:T(8,128)(2,1)}, bf16[512,768]{1,0:T(8,128)(2,1)S(1)}, u32[]{:S(2)}, u32[]{:S(2)}) collective-permute-start(bf16[512,768]{1,0:T(8,128)(2,1)} %bitcast.14), channel_id=1, source_target_pairs={{0,1},{1,0},{2,3},{3,2},{4,5},{5,4},{6,7},{7,6},{8,9},{9,8},{10,11... | collective-permute-start | bytes 2359304 | tf_op jit(solution)/shard_map/ppermute | solution.py:908
  15.8 6.5 %collective-permute-done.other_ref = bf16[512,768]{1,0:T(8,128)(2,1)S(1)} collective-permute-done((bf16[512,768]{1,0:T(8,128)(2,1)}, bf16[512,768]{1,0:T(8,128)(2,1)S(1)}, u32[]{:S(2)}, u32[]{:S(2)}) %collective-permute-start) | collective-permute-done | bytes 786464 | tf_op jit(solution)/shard_map/ppermute | solution.py:908
  22.3 13.3 %forward_kernel.1 = (bf16[1024,768]{1,0:T(8,128)(2,1)S(1)}, f32[1024,768]{1,0:T(8,128)S(1)}, f32[1024,768]{1,0:T(8,128)S(1)}, bf16[1024,768]{1,0:T(8,128)(2,1)S(...) custom-call(s32[5]{0:T(128)S(1)} %stack.23.at_ref, ...), custom_call_target="tpu_custom_call" | custom-call | flops 17999998976 | tf_op jit(solution)/shard_map/forward_kernel/pallas_call | solution.py:832
  35.6 2.0 %stats_kernel.2 = (f32[512,768]{1,0:T(8,128)S(1)}, f32[8,512]{1,0:T(8,128)S(1)}) custom-call(s32[5]{0:T(128)S(1)} %stack.23.at_ref, bf16[512,768]{1,0:T(8,128)(2,1)S(1)} %bitcast.19, bf16[1024,768]{1,0:T(8,128)(2,1)S(1)} %get-tuple-element.141.gg_ref, f32[8,1024]{1,0:T(8,128)S(1)} %get-tuple-element.145.sq_ref, bf16[768,768]{1,0:T(8,128)(2,1)S(1)} %get-tuple-element.142.out_w), custom_call_target="tpu_custom_call" | custom-call | flops 2000000000 | tf_op jit(solution)/shard_map/stats_kernel/pallas_call | solution.py:832
  38.3 2.0 %stats_kernel.3 = (f32[512,768]{1,0:T(8,128)S(1)}, f32[16,512]{1,0:T(8,128)S(1)}) custom-call(s32[5]{0:T(128)S(1)} %stack.23.at_ref, bf16[512,768]{1,0:T(8,128)(2,1)S(1)} %collective-permute-done.2.cot_ref.other_ref, bf16[1024,768]{1,0:T(8,128)(2,1)S(1)} %get-tuple-element.141.gg_ref, f32[8,1024]{1,0:T(8,128)S(1)} %get-tuple-element.145.sq_ref, ...), custom_call_target="tpu_custom_call" | custom-call | flops 2000000000 | tf_op jit(solution)/shard_map/stats_kernel/pallas_call | solution.py:832
  42.0 2.6 %branch_kernel.1 = (bf16[512,768]{1,0:T(8,128)(2,1)S(1)}, bf16[512,768]{1,0:T(8,128)(2,1)S(1)}) custom-call(s32[5]{0:T(128)S(1)} %stack.23.at_ref, bf16[1024,768]{1,0:T(8,128)(2,1)S(1)} %get-tuple-element.141.gg_ref, bf16[768,768]{1,0:T(8,128)(2,1)S(1)} %get-tuple-element.142.out_w), custom_call_target="tpu_custom_call" | custom-call | flops 2400000000 | tf_op jit(solution)/shard_map/branch_kernel/pallas_call | solution.py:832
  44.7 7.3 %gate_kernel.1 = (bf16[1024,768]{1,0:T(8,128)(2,1)S(1)}, bf16[1024,768]{1,0:T(8,128)(2,1)S(1)}, bf16[384,1536]{1,0:T(8,128)(2,1)S(1)}, bf16[384,1536]{1,0:T(8,12...) custom-call(s32[5]{0:T(128)S(1)} %stack.23.at_ref, bf16[512,768]{1,0:T(8,128)(2,1)S(1)} %bitcast.20, ...), custom_call_target="tpu_custom_call" | custom-call | flops 9600000000 | tf_op jit(solution)/shard_map/gate_kernel/pallas_call | solution.py:832
  53.3 2.8 %gate_back_kernel.1.refs_2_.from_gate = f32[1024,768]{1,0:T(8,128)S(1)} custom-call(s32[5]{0:T(128)S(1)} %stack.23.at_ref, bf16[1024,768]{1,0:T(8,128)(2,1)S(1)} %get-tuple-element.154.dg_ref, bf16[768,768]{1,0:T(8,128)(2,1)S(1)} %get-tuple-element.128.gate_w), custom_call_target="tpu_custom_call" | custom-call | flops 4000000000 | tf_op jit(solution)/shard_map/gate_back_kernel/pallas_call | solution.py:832
  59.0 9.2 %backward_kernel.2 = (bf16[512,768]{1,0:T(8,128)(2,1)S(1)}, bf16[512,256]{1,0:T(8,128)(2,1)S(1)}, bf16[512,128]{1,0:T(8,128)(2,1)S(1)}, f32[128,768]{1,0:T(8,128...) custom-call(s32[5]{0:T(128)S(1)} %stack.23.at_ref, ...), custom_call_target="tpu_custom_call" | custom-call | flops 7000000000 | tf_op jit(solution)/shard_map/backward_kernel/pallas_call | solution.py:832
  70.0 2.9 %collective-permute-done.5.refs_1_ = bf16[192,1536]{1,0:T(8,128)(2,1)S(1)} collective-permute-done((bf16[192,1536]{1,0:T(8,128)(2,1)S(1)}, bf16[192,1536]{1,0:T(8,128)(2,1)S(1)}, u32[]{:S(2)}, u32[]{:S(2)}) %collective-permute-start.5) | collective-permute-done | bytes 589856 | tf_op jit(solution)/shard_map/ppermute | solution.py:920
  75.4 2.6 %collective-permute-start.8 = (bf16[48,1536]{1,0:T(8,128)(2,1)S(1)}, bf16[48,1536]{1,0:T(8,128)(2,1)S(1)}, u32[]{:S(2)}, u32[]{:S(2)}) collective-permute-start(bf16[48,1536]{1,0:T(8,128)(2,1)S(1)} %get-tuple-element.198), channel_id=1, source_target_pairs={{0,16},{2,18},{4,20},{6,22},{8,24},{10,26},{12,28},{14,30},{16,0},... | collective-permute-start | bytes 442376 | tf_op jit(solution)/shard_map/ppermute | solution.py:920
  78.2 10.1 %backward_kernel.3 = (bf16[512,768]{1,0:T(8,128)(2,1)S(1)}, bf16[512,256]{1,0:T(8,128)(2,1)S(1)}, bf16[512,128]{1,0:T(8,128)(2,1)S(1)}, f32[128,768]{1,0:T(8,128...) custom-call(s32[5]{0:T(128)S(1)} %stack.23.at_ref, ...), custom_call_target="tpu_custom_call" | custom-call | flops 7000000000 | tf_op jit(solution)/shard_map/backward_kernel/pallas_call | solution.py:832
  89.1 2.8 %weights_kernel.1 = (bf16[384,1152]{1,0:T(8,128)(2,1)S(1)}, bf16[384,1152]{1,0:T(8,128)(2,1)S(1)}, bf16[48,1536]{1,0:T(8,128)(2,1)S(1)}) custom-call(s32[5]{0:T(128)S(1)} %stack.23.at_ref, bf16[1024,768]{1,0:T(8,128)(2,1)S(1)} %get-tuple-element.149.normed_ref, bf16[512,768]{1,0:T(8,128)(2,1)S(1)} %get-tuple-element.184.refs_0_, ...), custom_call_target="tpu_custom_call" | custom-call | flops 1200000000 | tf_op jit(solution)/shard_map/weights_kernel/pallas_call | solution.py:832
  92.0 2.9 %collective-permute-start.17 = (bf16[48,1536]{1,0:T(8,128)(2,1)S(1)}, bf16[48,1536]{1,0:T(8,128)(2,1)S(1)}, u32[]{:S(2)}, u32[]{:S(2)}) collective-permute-start(bf16[48,1536]{1,0:T(8,128)(2,1)S(1)} %get-tuple-element.208.refs_4_), channel_id=1, source_target_pairs={{0,24},{2,26},{4,28},{6,30},{8,16},{10,18},{12,20},{14,22},{16,8},... | collective-permute-start | bytes 442376 | tf_op jit(solution)/shard_map/ppermute | solution.py:920
  98.4 3.6 %normed_grad_kernel.1 = (bf16[512,768]{1,0:T(8,128)(2,1)S(1)}, bf16[512,768]{1,0:T(8,128)(2,1)S(1)}) custom-call(s32[5]{0:T(128)S(1)} %stack.23.at_ref, f32[1024,768]{1,0:T(8,128)S(1)} %gate_back_kernel.1.refs_2_.from_gate, bf16[512,768]{1,0:T(8,128)(2,1)S(1)} %get-tuple-element.184.refs_0_, bf16[512,256]{1,0:T(8,128)(2,1)S(1)} %get-tuple-element.185.refs_1_, ...), custom_call_target="tpu_custom_call" | custom-call | flops 4800000000 | tf_op jit(solution)/shard_map/normed_grad_kernel/pallas_call | solution.py:832
  103.7 5.1 %collective-permute-done.11.refs_1_ = bf16[192,1152]{1,0:T(8,128)(2,1)S(1)} collective-permute-done((bf16[192,1152]{1,0:T(8,128)(2,1)S(1)}, bf16[192,1152]{1,0:T(8,128)(2,1)S(1)}, u32[]{:S(2)}, u32[]{:S(2)}) %collective-permute-start.11) | collective-permute-done | bytes 442400 | tf_op jit(solution)/shard_map/ppermute | solution.py:920
  114.2 2.1 %mixed_kernel.1 = (f32[512,768]{1,0:T(8,128)}, f32[8,128]{1,0:T(8,128)S(1)}) custom-call(s32[5]{0:T(128)S(1)} %stack.23.at_ref, bf16[512,768]{1,0:T(8,128)(2,1)S(1)} %bitcast.16, bf16[512,768]{1,0:T(8,128)(2,1)S(1)} %get-tuple-element.143.own_ref._, bf16[512,768]{1,0:T(8,128)(2,1)S(1)} %collective-permute-done.1.other_ref.refs_7_, ...), custom_call_target="tpu_custom_call" | custom-call | flops 2000000000 | tf_op jit(solution)/shard_map/mixed_kernel/pallas_call | solution.py:832
  116.2 5.3 %collective-permute-done.13.refs_2_ = bf16[48,1152]{1,0:T(8,128)(2,1)S(1)} collective-permute-done((bf16[48,1152]{1,0:T(8,128)(2,1)S(1)}, bf16[48,1152]{1,0:T(8,128)(2,1)S(1)}, u32[]{:S(2)}, u32[]{:S(2)}) %collective-permute-start.13) | collective-permute-done | bytes 110624 | tf_op jit(solution)/shard_map/ppermute | solution.py:920
  124.6 3.2 %collective-permute-done.18.other_ref = bf16[48,384]{1,0:T(8,128)(2,1)S(1)} collective-permute-done((bf16[48,384]{1,0:T(8,128)(2,1)S(1)}, bf16[48,384]{1,0:T(8,128)(2,1)S(1)}, u32[]{:S(2)}, u32[]{:S(2)}) %collective-permute-start.18) | collective-permute-done | bytes 36896 | tf_op jit(solution)/shard_map/ppermute | solution.py:1310
  128.5 2.4 %collective-permute-start.21 = (bf16[48,1152]{1,0:T(8,128)(2,1)S(1)}, bf16[48,1152]{1,0:T(8,128)(2,1)S(1)}, u32[]{:S(2)}, u32[]{:S(2)}) collective-permute-start(bf16[48,1152]{1,0:T(8,128)(2,1)S(1)} %heads_kernel.1.refs_0_), channel_id=1, source_target_pairs={{0,24},{2,26},{4,28},{6,30},{8,16},{10,18},{12,20},{14,22},{16,8},... | collective-permute-start | bytes 331784 | tf_op jit(solution)/shard_map/ppermute | solution.py:920
  132.9 2.3 %input_kernel.1 = (f32[512,768]{1,0:T(8,128)}, f32[8,128]{1,0:T(8,128)S(1)}) custom-call(s32[5]{0:T(128)S(1)} %stack.23.at_ref, bf16[512,768]{1,0:T(8,128)(2,1)S(1)} %bitcast.17, bf16[512,768]{1,0:T(8,128)(2,1)S(1)} %bitcast.21, bf16[512,768]{1,0:T(8,128)(2,1)S(1)} %get-tuple-element.187.own_ref.refs_2_, ...), custom_call_target="tpu_custom_call" | custom-call | flops 2000000000 | tf_op jit(solution)/shard_map/input_kernel/pallas_call | solution.py:832
  135.6 2.8 %collective-permute-done.20.refs_2_ = bf16[48,1152]{1,0:T(8,128)(2,1)S(1)} collective-permute-done((bf16[48,1152]{1,0:T(8,128)(2,1)S(1)}, bf16[48,1152]{1,0:T(8,128)(2,1)S(1)}, u32[]{:S(2)}, u32[]{:S(2)}) %collective-permute-start.20) | collective-permute-done | bytes 110624 | tf_op jit(solution)/shard_map/ppermute | solution.py:920
  144.1 3.0 %early_kernel.1 = (f32[768,768]{1,0:T(8,128)}, f32[768,768]{1,0:T(8,128)}, f32[8,128]{1,0:T(8,128)S(1)}) custom-call(s32[5]{0:T(128)S(1)} %stack.23.at_ref, bf16[384,1536]{1,0:T(8,128)(2,1)S(1)} %get-tuple-element.215.own_ref, bf16[384,1536]{1,0:T(8,128)(2,1)S(1)} %collective-permute-done.24.other_ref), custom_call_target="tpu_custom_call" | custom-call | flops 3000000000 | tf_op jit(solution)/shard_map/early_kernel/pallas_call | solution.py:832
  147.1 4.8 %collective-permute-done.23.refs_0_ = bf16[192,1152]{1,0:T(8,128)(2,1)S(1)} collective-permute-done((bf16[192,1152]{1,0:T(8,128)(2,1)S(1)}, bf16[192,1152]{1,0:T(8,128)(2,1)S(1)}, u32[]{:S(2)}, u32[]{:S(2)}) %collective-permute-start.23) | collective-permute-done | bytes 442400 | tf_op jit(solution)/shard_map/ppermute | solution.py:920
  (93 shorter events, 50.4 us)
Async XLA Ops:
  0.7 21.6 %collective-permute-start = (bf16[512,768]{1,0:T(8,128)(2,1)}, bf16[512,768]{1,0:T(8,128)(2,1)S(1)}, u32[]{:S(2)}, u32[]{:S(2)}) collective-permute-start(bf16[512,768]{1,0:T(8,128)(2,1)} %bitcast.14), channel_id=1, source_target_pairs={{0,1},{1,0},{2,3},{3,2},{4,5},{5,4},{6,7},{7,6},{8,9},{9,8},{10,11... | collective-permute-start | bytes 2359304 | tf_op jit(solution)/shard_map/ppermute | solution.py:908
  3.7 34.6 %collective-permute-start.2 = (bf16[512,768]{1,0:T(8,128)(2,1)}, bf16[512,768]{1,0:T(8,128)(2,1)S(1)}, u32[]{:S(2)}, u32[]{:S(2)}) collective-permute-start(bf16[512,768]{1,0:T(8,128)(2,1)} %bitcast.18), channel_id=1, source_target_pairs={{0,1},{1,0},{2,3},{3,2},{4,5},{5,4},{6,7},{7,6},{8,9},{9,8},{10,11... | collective-permute-start | bytes 2359304 | tf_op jit(solution)/shard_map/ppermute | solution.py:908
  40.3 4.4 %collective-permute-start.3 = (f32[16,512]{1,0:T(8,128)S(1)}, f32[16,512]{1,0:T(8,128)S(1)}, u32[]{:S(2)}, u32[]{:S(2)}) collective-permute-start(f32[16,512]{1,0:T(8,128)S(1)} %get-tuple-element.147.here_ref.here_a.here_b), channel_id=1, source_target_pairs={{0,1},{1,0},{2,3},{3,2},{4,5},{5,4},{6,7},{7,6},{8,9},{9,8},{10,11... | collective-permute-start | bytes 98312 | tf_op jit(solution)/shard_map/ppermute | solution.py:909
  52.0 4.1 %collective-permute-start.4 = (bf16[384,1536]{1,0:T(8,128)(2,1)S(1)}, bf16[384,1536]{1,0:T(8,128)(2,1)S(1)}, u32[]{:S(2)}, u32[]{:S(2)}) collective-permute-start(bf16[384,1536]{1,0:T(8,128)(2,1)S(1)} %get-tuple-element.170), channel_id=1, source_target_pairs={{0,2},{2,0},{4,6},{6,4},{8,10},{10,8},{12,14},{14,12},{16,18},{18,... | collective-permute-start | bytes 3538952 | tf_op jit(solution)/shard_map/ppermute | solution.py:920
  52.0 26.2 %collective-permute-start.1 = (bf16[512,768]{1,0:T(8,128)(2,1)S(1)}, bf16[512,768]{1,0:T(8,128)(2,1)S(1)}, u32[]{:S(2)}, u32[]{:S(2)}) collective-permute-start(bf16[512,768]{1,0:T(8,128)(2,1)S(1)} %get-tuple-element.144), channel_id=1, source_target_pairs={{0,1},{1,0},{2,3},{3,2},{4,5},{5,4},{6,7},{7,6},{8,9},{9,8},{10,11... | collective-permute-start | bytes 2359304 | tf_op jit(solution)/shard_map/ppermute | solution.py:1082
  57.4 15.5 %collective-permute-start.5 = (bf16[192,1536]{1,0:T(8,128)(2,1)S(1)}, bf16[192,1536]{1,0:T(8,128)(2,1)S(1)}, u32[]{:S(2)}, u32[]{:S(2)}) collective-permute-start(bf16[192,1536]{1,0:T(8,128)(2,1)S(1)} %get-tuple-element.178), channel_id=1, source_target_pairs={{0,4},{2,6},{4,0},{6,2},{8,12},{10,14},{12,8},{14,10},{16,20},{18,... | collective-permute-start | bytes 1769480 | tf_op jit(solution)/shard_map/ppermute | solution.py:920
  73.7 14.5 %collective-permute-start.7 = (bf16[48,1536]{1,0:T(8,128)(2,1)S(1)}, bf16[48,1536]{1,0:T(8,128)(2,1)S(1)}, u32[]{:S(2)}, u32[]{:S(2)}) collective-permute-start(bf16[48,1536]{1,0:T(8,128)(2,1)S(1)} %get-tuple-element.197), channel_id=1, source_target_pairs={{0,8},{2,10},{4,12},{6,14},{8,0},{10,2},{12,4},{14,6},{16,24},{18,... | collective-permute-start | bytes 442376 | tf_op jit(solution)/shard_map/ppermute | solution.py:920
  75.4 13.7 %collective-permute-start.8 = (bf16[48,1536]{1,0:T(8,128)(2,1)S(1)}, bf16[48,1536]{1,0:T(8,128)(2,1)S(1)}, u32[]{:S(2)}, u32[]{:S(2)}) collective-permute-start(bf16[48,1536]{1,0:T(8,128)(2,1)S(1)} %get-tuple-element.198), channel_id=1, source_target_pairs={{0,16},{2,18},{4,20},{6,22},{8,24},{10,26},{12,28},{14,30},{16,0},... | collective-permute-start | bytes 442376 | tf_op jit(solution)/shard_map/ppermute | solution.py:920
  78.0 11.1 %collective-permute-start.9 = (bf16[48,1536]{1,0:T(8,128)(2,1)S(1)}, bf16[48,1536]{1,0:T(8,128)(2,1)S(1)}, u32[]{:S(2)}, u32[]{:S(2)}) collective-permute-start(bf16[48,1536]{1,0:T(8,128)(2,1)S(1)} %get-tuple-element.199), channel_id=1, source_target_pairs={{0,24},{2,26},{4,28},{6,30},{8,16},{10,18},{12,20},{14,22},{16,8},... | collective-permute-start | bytes 442376 | tf_op jit(solution)/shard_map/ppermute | solution.py:920
  92.0 18.9 %collective-permute-start.17 = (bf16[48,1536]{1,0:T(8,128)(2,1)S(1)}, bf16[48,1536]{1,0:T(8,128)(2,1)S(1)}, u32[]{:S(2)}, u32[]{:S(2)}) collective-permute-start(bf16[48,1536]{1,0:T(8,128)(2,1)S(1)} %get-tuple-element.208.refs_4_), channel_id=1, source_target_pairs={{0,24},{2,26},{4,28},{6,30},{8,16},{10,18},{12,20},{14,22},{16,8},... | collective-permute-start | bytes 442376 | tf_op jit(solution)/shard_map/ppermute | solution.py:920
  94.9 17.9 %collective-permute-start.16 = (bf16[48,1536]{1,0:T(8,128)(2,1)S(1)}, bf16[48,1536]{1,0:T(8,128)(2,1)S(1)}, u32[]{:S(2)}, u32[]{:S(2)}) collective-permute-start(bf16[48,1536]{1,0:T(8,128)(2,1)S(1)} %get-tuple-element.208.refs_4_), channel_id=1, source_target_pairs={{0,16},{2,18},{4,20},{6,22},{8,24},{10,26},{12,28},{14,30},{16,0},... | collective-permute-start | bytes 442376 | tf_op jit(solution)/shard_map/ppermute | solution.py:920
  96.8 12.0 %collective-permute-start.11 = (bf16[192,1152]{1,0:T(8,128)(2,1)S(1)}, bf16[192,1152]{1,0:T(8,128)(2,1)S(1)}, u32[]{:S(2)}, u32[]{:S(2)}) collective-permute-start(bf16[192,1152]{1,0:T(8,128)(2,1)S(1)} %get-tuple-element.203), channel_id=1, source_target_pairs={{0,4},{2,6},{4,0},{6,2},{8,12},{10,14},{12,8},{14,10},{16,20},{18,... | collective-permute-start | bytes 1327112 | tf_op jit(solution)/shard_map/ppermute | solution.py:920
  102.0 30.9 %collective-permute-start.6 = (bf16[512,768]{1,0:T(8,128)(2,1)S(1)}, bf16[512,768]{1,0:T(8,128)(2,1)S(1)}, u32[]{:S(2)}, u32[]{:S(2)}) collective-permute-start(bf16[512,768]{1,0:T(8,128)(2,1)S(1)} %get-tuple-element.188), channel_id=1, source_target_pairs={{0,1},{1,0},{2,3},{3,2},{4,5},{5,4},{6,7},{7,6},{8,9},{9,8},{10,11... | collective-permute-start | bytes 2359304 | tf_op jit(solution)/shard_map/ppermute | solution.py:1082
  102.8 13.4 %collective-permute-start.15 = (bf16[48,1536]{1,0:T(8,128)(2,1)S(1)}, bf16[48,1536]{1,0:T(8,128)(2,1)S(1)}, u32[]{:S(2)}, u32[]{:S(2)}) collective-permute-start(bf16[48,1536]{1,0:T(8,128)(2,1)S(1)} %get-tuple-element.208.refs_4_), channel_id=1, source_target_pairs={{0,8},{2,10},{4,12},{6,14},{8,0},{10,2},{12,4},{14,6},{16,24},{18,... | collective-permute-start | bytes 442376 | tf_op jit(solution)/shard_map/ppermute | solution.py:920
  109.7 6.5 %collective-permute-start.12 = (bf16[48,1152]{1,0:T(8,128)(2,1)S(1)}, bf16[48,1152]{1,0:T(8,128)(2,1)S(1)}, u32[]{:S(2)}, u32[]{:S(2)}) collective-permute-start(bf16[48,1152]{1,0:T(8,128)(2,1)S(1)} %get-tuple-element.205), channel_id=1, source_target_pairs={{0,8},{2,10},{4,12},{6,14},{8,0},{10,2},{12,4},{14,6},{16,24},{18,... | collective-permute-start | bytes 331784 | tf_op jit(solution)/shard_map/ppermute | solution.py:920
  110.9 10.6 %collective-permute-start.13 = (bf16[48,1152]{1,0:T(8,128)(2,1)S(1)}, bf16[48,1152]{1,0:T(8,128)(2,1)S(1)}, u32[]{:S(2)}, u32[]{:S(2)}) collective-permute-start(bf16[48,1152]{1,0:T(8,128)(2,1)S(1)} %get-tuple-element.206), channel_id=1, source_target_pairs={{0,16},{2,18},{4,20},{6,22},{8,24},{10,26},{12,28},{14,30},{16,0},... | collective-permute-start | bytes 331784 | tf_op jit(solution)/shard_map/ppermute | solution.py:920
  112.8 8.7 %collective-permute-start.14 = (bf16[48,1152]{1,0:T(8,128)(2,1)S(1)}, bf16[48,1152]{1,0:T(8,128)(2,1)S(1)}, u32[]{:S(2)}, u32[]{:S(2)}) collective-permute-start(bf16[48,1152]{1,0:T(8,128)(2,1)S(1)} %get-tuple-element.207), channel_id=1, source_target_pairs={{0,24},{2,26},{4,28},{6,30},{8,16},{10,18},{12,20},{14,22},{16,8},... | collective-permute-start | bytes 331784 | tf_op jit(solution)/shard_map/ppermute | solution.py:920
  122.2 16.2 %collective-permute-start.22 = (bf16[192,1536]{1,0:T(8,128)(2,1)S(1)}, bf16[192,1536]{1,0:T(8,128)(2,1)S(1)}, u32[]{:S(2)}, u32[]{:S(2)}) collective-permute-start(bf16[192,1536]{1,0:T(8,128)(2,1)S(1)} %get-tuple-element.212.refs_4_), channel_id=1, source_target_pairs={{0,4},{2,6},{4,0},{6,2},{8,12},{10,14},{12,8},{14,10},{16,20},{18,... | collective-permute-start | bytes 1769480 | tf_op jit(solution)/shard_map/ppermute | solution.py:920
  123.8 4.0 %collective-permute-start.18 = (bf16[48,384]{1,0:T(8,128)(2,1)S(1)}, bf16[48,384]{1,0:T(8,128)(2,1)S(1)}, u32[]{:S(2)}, u32[]{:S(2)}) collective-permute-start(bf16[48,384]{1,0:T(8,128)(2,1)S(1)} %get-tuple-element.211.own_ref), channel_id=1, source_target_pairs={{0,1},{1,0},{2,3},{3,2},{4,5},{5,4},{6,7},{7,6},{8,9},{9,8},{10,11... | collective-permute-start | bytes 110600 | tf_op jit(solution)/shard_map/ppermute | solution.py:1310
  128.5 7.1 %collective-permute-start.21 = (bf16[48,1152]{1,0:T(8,128)(2,1)S(1)}, bf16[48,1152]{1,0:T(8,128)(2,1)S(1)}, u32[]{:S(2)}, u32[]{:S(2)}) collective-permute-start(bf16[48,1152]{1,0:T(8,128)(2,1)S(1)} %heads_kernel.1.refs_0_), channel_id=1, source_target_pairs={{0,24},{2,26},{4,28},{6,30},{8,16},{10,18},{12,20},{14,22},{16,8},... | collective-permute-start | bytes 331784 | tf_op jit(solution)/shard_map/ppermute | solution.py:920
  130.9 7.6 %collective-permute-start.20 = (bf16[48,1152]{1,0:T(8,128)(2,1)S(1)}, bf16[48,1152]{1,0:T(8,128)(2,1)S(1)}, u32[]{:S(2)}, u32[]{:S(2)}) collective-permute-start(bf16[48,1152]{1,0:T(8,128)(2,1)S(1)} %heads_kernel.1.refs_0_), channel_id=1, source_target_pairs={{0,16},{2,18},{4,20},{6,22},{8,24},{10,26},{12,28},{14,30},{16,0},... | collective-permute-start | bytes 331784 | tf_op jit(solution)/shard_map/ppermute | solution.py:920
  131.9 6.6 %collective-permute-start.19 = (bf16[48,1152]{1,0:T(8,128)(2,1)S(1)}, bf16[48,1152]{1,0:T(8,128)(2,1)S(1)}, u32[]{:S(2)}, u32[]{:S(2)}) collective-permute-start(bf16[48,1152]{1,0:T(8,128)(2,1)S(1)} %heads_kernel.1.refs_0_), channel_id=1, source_target_pairs={{0,8},{2,10},{4,12},{6,14},{8,0},{10,2},{12,4},{14,6},{16,24},{18,... | collective-permute-start | bytes 331784 | tf_op jit(solution)/shard_map/ppermute | solution.py:920
  139.1 5.0 %collective-permute-start.24 = (bf16[384,1536]{1,0:T(8,128)(2,1)S(1)}, bf16[384,1536]{1,0:T(8,128)(2,1)S(1)}, u32[]{:S(2)}, u32[]{:S(2)}) collective-permute-start(bf16[384,1536]{1,0:T(8,128)(2,1)S(1)} %get-tuple-element.215.own_ref), channel_id=1, source_target_pairs={{0,2},{2,0},{4,6},{6,4},{8,10},{10,8},{12,14},{14,12},{16,18},{18,... | collective-permute-start | bytes 3538952 | tf_op jit(solution)/shard_map/ppermute | solution.py:920
  139.7 12.2 %collective-permute-start.23 = (bf16[192,1152]{1,0:T(8,128)(2,1)S(1)}, bf16[192,1152]{1,0:T(8,128)(2,1)S(1)}, u32[]{:S(2)}, u32[]{:S(2)}) collective-permute-start(bf16[192,1152]{1,0:T(8,128)(2,1)S(1)} %get-tuple-element.214.piece_ref.refs_0_), channel_id=1, source_target_pairs={{0,4},{2,6},{4,0},{6,2},{8,12},{10,14},{12,8},{14,10},{16,20},{18,... | collective-permute-start | bytes 1327112 | tf_op jit(solution)/shard_map/ppermute | solution.py:920
  (11 other events, 55.9 us)

commit v6 on v5

--- a/solution.py
+++ b/solution.py
@@ -238,8 +238,10 @@
                 scanned = both[:, k * LANES : (k + 1) * LANES]
                 scanned = scanned + grownx[here, lanes] * carried[here, lanes]
                 scanned = scanned + skip_ref[:, lanes] * values[here, lanes]
-                y_ref[here, lanes] = scanned
-                gated = scanned * silu(g_ref[here, lanes])
+                gate, slope = silu_slope(g_ref[here, lanes])
+                y_ref[here, lanes] = scanned * slope
+                g_ref[here, lanes] = gate
+                gated = scanned * gate
                 gg_ref[here, lanes] = (gated * ggain_ref[:, lanes].astype(f32)).astype(bf16)
                 squares = squares + gated * gated
         sq_ref[:, here] = dot(jnp.ones((8, LANES), f32), squares, NT, HIGHEST)
@@ -322,7 +324,7 @@
 
 
 def row_column(rows):
-    return jnp.concatenate([rows, jnp.zeros((LANES - rows.shape[0], BLOCK), f32)], axis=0).T
+    return jnp.concatenate([rows, jnp.zeros((LANES - rows.shape[0], rows.shape[1]), f32)], axis=0).T
 
 
 def mixed_kernel(inner_all, at_ref, rows_ref, own_ref, other_ref, here_ref, there_ref, out_ref, token_ref):
@@ -372,7 +374,8 @@
     *scratch,
 ):
     step_at = pl.program_id(0)
-    here = pl.ds(pl.multiple_of(step_at * BLOCK, BLOCK), BLOCK)
+    size = own_ref.shape[0]
+    here = pl.ds(pl.multiple_of(step_at * size, BLOCK), size)
     pairs = og_a.shape[1] // LANES
     grad_gate, grad_out = scratch if fast else (first_ref, second_ref)
 
@@ -391,14 +394,13 @@
     for pair in range(pairs):
         lanes = slice(pair * LANES, (pair + 1) * LANES)
         og = jnp.where(mine, og_a[:, lanes], og_b[:, lanes]) * scale
-        y = y_ref[:, lanes]
-        g = g_ref[:, lanes]
-        gate, slope = silu_slope(g)
-        gated = y * gate
-        grad_gain_ref[0:1, lanes] += jnp.sum(og * gated, axis=0, keepdims=True)
-        gated_grad = ggain_ref[:, lanes].astype(f32) * og - gated * pull
-        dy_ref[:, lanes] = (gated_grad * gate).astype(bf16)
-        dg_ref[here, lanes] = (gated_grad * y * slope).astype(bf16)
+        gain = ggain_ref[:, lanes].astype(f32)
+        inverse = 1.0 / gain
+        low = gg_ref[here, lanes].astype(f32)
+        grad_gain_ref[0:1, lanes] += jnp.sum(og * low, axis=0, keepdims=True) * inverse
+        gated_grad = gain * og - (low * inverse) * pull
+        dy_ref[:, lanes] = (gated_grad * g_ref[:, lanes]).astype(bf16)
+        dg_ref[here, lanes] = (gated_grad * y_ref[:, lanes]).astype(bf16)
 
     @pl.when(step_at == pl.num_programs(0) - 1)
     def _():
@@ -477,26 +479,26 @@
     return jnp.where(lane < HALF, block + pltpu.roll(block, HALF, 1), 0.0)
 
 
-def fold_step(me, ins, outs, buf, vectors):
-    width = buf.shape[1] - (LANES if vectors else 0)
-    total = ins[0][:, :width].astype(f32)
-    for r in ins[1:]:
-        total = total + r[:, :width].astype(f32)
-    buf[:, :width] = total.astype(bf16)
-    if vectors:
-        last = ins[0][:, width:].astype(f32)
-        for r in ins[1:]:
-            last = last + r[:, width:].astype(f32)
-        buf[:, width:] = carry_rest(join_rest(last)).astype(bf16)
-    rows = outs[0].shape[0]
-    if rows == buf.shape[0]:
-        left = 0
-        for o in outs:
-            o[...] = buf[:, left : left + o.shape[1]]
-            left += o.shape[1]
-        return
+def fold_step(me, ins, outs, vectors):
+    rows, width = outs[0].shape
+    width -= LANES if vectors else 0
     for j, o in enumerate(outs):
-        o[...] = buf[pl.ds(pl.multiple_of((me ^ j) * rows, 16), rows), :]
+        at = slice(0, rows)
+        if len(outs) > 1:
+            at = pl.ds(pl.multiple_of((me ^ j) * rows, 16), rows)
+        o[:, :width] = sum(r[at, :width].astype(f32) for r in ins).astype(bf16)
+        if vectors:
+            last = sum(r[at, width:].astype(f32) for r in ins)
+            o[:, width:] = carry_rest(join_rest(last)).astype(bf16)
+
+
+def part_step(ins, outs, vectors):
+    width = outs[0].shape[1]
+    outs[0][...] = sum(r[:, :width].astype(f32) for r in ins).astype(bf16)
+    state = outs[1].shape[1] - LANES
+    outs[1][:, :state] = sum(r[:, width : width + state].astype(f32) for r in ins).astype(bf16)
+    last = sum(r[:, width + state :].astype(f32) for r in ins)
+    outs[1][:, state:] = carry_rest(join_rest(last)).astype(bf16)
 
 
 def join_step(me, ins, out):
@@ -515,19 +517,19 @@
 
 def stage_kernel(plan, extra, at_ref, *refs):
     n_in = sum(count for _, _, count, _, _ in plan)
-    ins, refs = refs[:n_in], refs[n_in + extra :]
-    n_out = sum(count for _, _, _, count, _ in plan)
-    outs, bufs = refs[:n_out], list(refs[n_out:])
+    ins, outs = refs[:n_in], refs[n_in + extra :]
     for kind, axis, take, give, vectors in plan:
-        if kind != "join":
-            fold_step(at_ref[axis if kind == "fold" else 0], ins[:take], outs[:give], bufs.pop(0), vectors)
+        if kind == "fold":
+            fold_step(at_ref[axis], ins[:take], outs[:give], vectors)
+        elif kind == "part":
+            part_step(ins[:take], outs[:give], vectors)
         else:
             join_step(at_ref[axis], ins[:take], outs[0])
         ins, outs = ins[take:], outs[give:]
 
 
 def stage(at, steps, after=()):
-    plan, arrays, shapes, scratch = [], [], [], []
+    plan, arrays, shapes = [], [], []
     for kind, axis, ins, *rest in steps:
         rows, width = ins[0].shape
         count, vectors = rest if rest else (1, False)
@@ -538,8 +540,6 @@
         else:
             widths = {a.shape[1] for a in ins}
             shapes.append((rows * len(ins) // len(widths), sum(widths)))
-        if kind != "join":
-            scratch.append(pltpu.VMEM((rows, width), bf16))
         plan.append((kind, axis, len(ins), count, vectors))
         arrays += ins
     out = call(
@@ -548,7 +548,7 @@
         at,
         [(a, None) for a in arrays] + [(a, pl.BlockSpec(memory_space=pl.ANY)) for a in after],
         [(shape, bf16, pl.BlockSpec(shape, lambda i, a: (0, 0))) for shape in shapes],
-        scratch,
+        [],
     )
     out, results = list(out), []
     for _, _, _, give, _ in plan:
@@ -885,10 +885,10 @@
     chunks = BLOCK // CHUNK
     half_blocks = rows_here // BLOCK if two else blocks
 
-    def wide(a, axis):
+    def wide(a, axis, fill=0):
         pads = [(0, 0)] * a.ndim
         pads[axis] = (0, width - inner)
-        return jnp.pad(a, pads) if width > inner else a
+        return jnp.pad(a, pads, constant_values=fill) if width > inner else a
 
     def lanes_of(a):
         return jnp.pad(a, [(0, 0)] * (a.ndim - 1) + [(0, LANES - a.shape[-1])])
@@ -942,7 +942,7 @@
     sshift = state_shift[None, :]
     sbias, rate = lanes_of(step_bias[None, :]), lanes_of(log_rate[None, :])
     skipx = wide(jnp.repeat(skip_gain, head_width)[None, :], 1)
-    ggain = wide(gated_gain[None, :], 1)
+    ggain = wide(gated_gain[None, :], 1, 1)
     head_of = jnp.arange(width) // head_width
     spread = (jnp.arange(LANES)[:, None] == head_of[None, :]).astype(bf16)
     spread = jnp.concatenate([spread, spread], axis=0)
@@ -968,6 +968,20 @@
         return pl.BlockSpec((BLOCK, n), index)
 
     along = pl.BlockSpec((8, BLOCK), lambda i, a: (0, i))
+    unit = 2 * BLOCK if two and rows_here % (2 * BLOCK) == 0 else BLOCK
+    units, half_units = length // unit, half_blocks * BLOCK // unit
+
+    def own_unit(i, a):
+        return (jnp.clip(i - a[0] * half_units, 0, half_units - 1), 0)
+
+    def other_unit(i, a):
+        return (jnp.clip(i - (1 - a[0]) * half_units, 0, half_units - 1), 0)
+
+    other_taken = other_unit if two else own_unit
+
+    def tall(n, index=lambda i, a: (i, 0)):
+        return pl.BlockSpec((unit, n), index)
+
     fixed = lambda *shape: pl.BlockSpec(shape, lambda i, a: (0,) * len(shape))
     states_spec = lambda index: pl.BlockSpec((chunks, nstate, width), index)
     big = lambda *shape: pltpu.VMEM(shape, f32)
@@ -1033,25 +1047,25 @@
         ],
     )
     def stats_of(cot_rows, theirs, *before):
-        first = (lambda a: (1 - a[0]) * half_blocks) if theirs else (lambda a: a[0] * half_blocks)
+        first = (lambda a: (1 - a[0]) * half_units) if theirs else (lambda a: a[0] * half_units)
         count = cot_rows.shape[0]
         return run(
             stats_kernel,
-            count // BLOCK,
+            count // unit,
             at,
             [
-                (cot_rows, rows(model)),
-                (gg, rows(width, lambda i, a: (first(a) + i, 0))),
-                (sq, pl.BlockSpec((8, BLOCK), lambda i, a: (0, first(a) + i))),
+                (cot_rows, tall(model)),
+                (gg, tall(width, lambda i, a: (first(a) + i, 0))),
+                (sq, pl.BlockSpec((8, unit), lambda i, a: (0, first(a) + i))),
                 (out_w, None),
-                *[(b, along) for b in before],
+                *[(b, pl.BlockSpec((8, unit), lambda i, a: (0, i))) for b in before],
             ],
             [
-                ((count, width), f32, rows(width), fast),
+                ((count, width), f32, tall(width), fast),
                 (
                     (8 + 8 * len(before), count),
                     f32,
-                    pl.BlockSpec((8 + 8 * len(before), BLOCK), lambda i, a: (0, i)),
+                    pl.BlockSpec((8 + 8 * len(before), unit), lambda i, a: (0, i)),
                 ),
             ],
             [],
@@ -1065,15 +1079,18 @@
     got = add_other(stats)
     above = 1 if two else 0
 
-    def stats_at(row, block):
-        return pl.BlockSpec((8, BLOCK), lambda i, a: (row, block(i, a)[0]))
+    def stats_at(row, block, size=BLOCK):
+        return pl.BlockSpec((8, size), lambda i, a: (row, block(i, a)[0]))
 
     branch, branch_sent = run(
-        functools.partial(branch_kernel, half_blocks),
-        blocks,
+        functools.partial(branch_kernel, half_units),
+        units,
         at,
-        [(gg, rows(width)), (out_w, None)],
-        halves,
+        [(gg, tall(width)), (out_w, None)],
+        [
+            ((rows_here if two else length, model), bf16, tall(model, own_unit)),
+            ((rows_here if two else BLOCK, model), bf16, tall(model, other_unit if two else other_block)),
+        ],
         [],
     )
 
@@ -1095,21 +1112,21 @@
             ((width, model), f32, fixed(width, model)),
         ]
     dg, dy, early_a, early_b, grad_gain, norm = run(
-        functools.partial(gate_kernel, half_blocks, inner_all, fast),
-        blocks,
+        functools.partial(gate_kernel, half_units, inner_all, fast),
+        units,
         at,
         [
-            (own_cot, rows(model, own_block)),
-            (other_cot, rows(model, other_read)),
-            (stats, stats_at(above, own_block)),
-            (got, stats_at(0, own_block)),
-            (stats, stats_at(0, other_read)),
-            (got, stats_at(above, other_read)),
+            (own_cot, tall(model, own_unit)),
+            (other_cot, tall(model, other_taken)),
+            (stats, stats_at(above, own_unit, unit)),
+            (got, stats_at(0, own_unit, unit)),
+            (stats, stats_at(0, other_taken, unit)),
+            (got, stats_at(above, other_taken, unit)),
             (normed, None),
-            (og, rows(width, own_block)),
-            (og_b, rows(width, other_read)),
-            (y, rows(width)),
-            (g, rows(width)),
+            (og, tall(width, own_unit)),
+            (og_b, tall(width, other_taken)),
+            (y, tall(width)),
+            (g, tall(width)),
             (gg, None),
             (ggain, None),
             (gate_w, None),
@@ -1117,7 +1134,7 @@
         ],
         [
             ((length, width), bf16, fixed(length, width), fast),
-            ((length, width), bf16, rows(width), fast),
+            ((length, width), bf16, tall(width), fast),
             *pieces,
             ((8, width), f32, fixed(8, width)),
             ((8, model), f32, fixed(8, model)),

time: 157 us -> 154 us (0.981)
  Pallas kernels: 79.2 us -> 76.5 us
    pallas_call x28, Pallas kernels: 79.2 us -> 76.5 us  [call(): pl.pallas_call(kernel, name=title, grid_spec=pltpu.PrefetchScalarGridSpec...]
where the time goes in v6:
time: 154 us
  Pallas kernels  76.5 us (50%)
  waiting for transfers between devices  34.2 us (22%)
  starting transfers between devices  31.5 us (20%)
  local copies, waits for them, and re-layouts  10 us (6%)
    pallas_call x28, Pallas kernels, call(): pl.pallas_call(kernel, name=title, grid_spec=pltpu.PrefetchScalarGridSpec...  76.5 us
    ppermute x21, starting transfers between devices, hop(): return lax.ppermute(a, 'batch', [(i, i ^ mask) for i in range(batch)])  23.8 us
    ppermute x21, waiting for transfers between devices, hop(): return lax.ppermute(a, 'batch', [(i, i ^ mask) for i in range(batch)])  23.7 us
    ppermute x2, waiting for transfers between devices, per_device(): pair_of = lambda a: (a, lax.ppermute(a, 'heads', swap))  7.12 us
    unnamed x17, local copies, waits for them, and re-layouts  4.13 us
    ppermute x1, waiting for transfers between devices, per_device(): theirs = lax.ppermute(rest, 'heads', swap)  3.42 us
    ppermute x2, starting transfers between devices, per_device(): pair_of = lambda a: (a, lax.ppermute(a, 'heads', swap))  3.08 us
  transfers between devices with their start and end apart: 27, of which 12 were waited for; matrix products, arithmetic and copies ran while one was open for 5% of the time, Pallas kernels for 41%

profile of v6, /device:TPU:0, one launch (start us, length us, event | category | flops | bytes accessed | tf_op | source)
XLA Modules:
  0.0 153.8 jit_solution(15075112602436216017)
XLA Ops:
  0.7 3.0 %collective-permute-start = (bf16[512,768]{1,0:T(8,128)(2,1)}, bf16[512,768]{1,0:T(8,128)(2,1)S(1)}, u32[]{:S(2)}, u32[]{:S(2)}) collective-permute-start(bf16[512,768]{1,0:T(8,128)(2,1)} %bitcast.14), channel_id=1, source_target_pairs={{0,1},{1,0},{2,3},{3,2},{4,5},{5,4},{6,7},{7,6},{8,9},{9,8},{10,11... | collective-permute-start | bytes 2359304 | tf_op jit(solution)/shard_map/ppermute | solution.py:908
  15.8 6.5 %collective-permute-done.other_ref = bf16[512,768]{1,0:T(8,128)(2,1)S(1)} collective-permute-done((bf16[512,768]{1,0:T(8,128)(2,1)}, bf16[512,768]{1,0:T(8,128)(2,1)S(1)}, u32[]{:S(2)}, u32[]{:S(2)}) %collective-permute-start) | collective-permute-done | bytes 786464 | tf_op jit(solution)/shard_map/ppermute | solution.py:908
  22.3 13.6 %forward_kernel.1 = (bf16[1024,768]{1,0:T(8,128)(2,1)S(1)}, f32[1024,768]{1,0:T(8,128)S(1)}, f32[1024,768]{1,0:T(8,128)S(1)}, bf16[1024,768]{1,0:T(8,128)(2,1)S(...) custom-call(s32[5]{0:T(128)S(1)} %stack.23.at_ref, ...), custom_call_target="tpu_custom_call" | custom-call | flops 17999998976 | tf_op jit(solution)/shard_map/forward_kernel/pallas_call | solution.py:832
  35.8 1.8 %stats_kernel.2 = (f32[512,768]{1,0:T(8,128)S(1)}, f32[8,512]{1,0:T(8,128)S(1)}) custom-call(s32[5]{0:T(128)S(1)} %stack.23.at_ref, bf16[512,768]{1,0:T(8,128)(2,1)S(1)} %bitcast.19, bf16[1024,768]{1,0:T(8,128)(2,1)S(1)} %get-tuple-element.141.gg_ref, f32[8,1024]{1,0:T(8,128)S(1)} %get-tuple-element.145.sq_ref, bf16[768,768]{1,0:T(8,128)(2,1)S(1)} %get-tuple-element.142.out_w), custom_call_target="tpu_custom_call" | custom-call | flops 1000000000 | tf_op jit(solution)/shard_map/stats_kernel/pallas_call | solution.py:832
  41.8 2.3 %branch_kernel.1 = (bf16[512,768]{1,0:T(8,128)(2,1)S(1)}, bf16[512,768]{1,0:T(8,128)(2,1)S(1)}) custom-call(s32[5]{0:T(128)S(1)} %stack.23.at_ref, bf16[1024,768]{1,0:T(8,128)(2,1)S(1)} %get-tuple-element.141.gg_ref, bf16[768,768]{1,0:T(8,128)(2,1)S(1)} %get-tuple-element.142.out_w), custom_call_target="tpu_custom_call" | custom-call | flops 1200000000 | tf_op jit(solution)/shard_map/branch_kernel/pallas_call | solution.py:832
  44.1 6.0 %gate_kernel.1 = (bf16[1024,768]{1,0:T(8,128)(2,1)S(1)}, bf16[1024,768]{1,0:T(8,128)(2,1)S(1)}, bf16[384,1536]{1,0:T(8,128)(2,1)S(1)}, bf16[384,1536]{1,0:T(8,12...) custom-call(s32[5]{0:T(128)S(1)} %stack.23.at_ref, bf16[512,768]{1,0:T(8,128)(2,1)S(1)} %bitcast.20, ...), custom_call_target="tpu_custom_call" | custom-call | flops 4800000000 | tf_op jit(solution)/shard_map/gate_kernel/pallas_call | solution.py:832
  51.8 2.8 %gate_back_kernel.1.refs_2_.from_gate = f32[1024,768]{1,0:T(8,128)S(1)} custom-call(s32[5]{0:T(128)S(1)} %stack.23.at_ref, bf16[1024,768]{1,0:T(8,128)(2,1)S(1)} %get-tuple-element.154.dg_ref, bf16[768,768]{1,0:T(8,128)(2,1)S(1)} %get-tuple-element.128.gate_w), custom_call_target="tpu_custom_call" | custom-call | flops 4000000000 | tf_op jit(solution)/shard_map/gate_back_kernel/pallas_call | solution.py:832
  57.0 9.2 %backward_kernel.2 = (bf16[512,768]{1,0:T(8,128)(2,1)S(1)}, bf16[512,256]{1,0:T(8,128)(2,1)S(1)}, bf16[512,128]{1,0:T(8,128)(2,1)S(1)}, f32[128,768]{1,0:T(8,128...) custom-call(s32[5]{0:T(128)S(1)} %stack.23.at_ref, ...), custom_call_target="tpu_custom_call" | custom-call | flops 7000000000 | tf_op jit(solution)/shard_map/backward_kernel/pallas_call | solution.py:832
  68.0 2.9 %collective-permute-done.5.refs_1_ = bf16[192,1536]{1,0:T(8,128)(2,1)S(1)} collective-permute-done((bf16[192,1536]{1,0:T(8,128)(2,1)S(1)}, bf16[192,1536]{1,0:T(8,128)(2,1)S(1)}, u32[]{:S(2)}, u32[]{:S(2)}) %collective-permute-start.5) | collective-permute-done | bytes 589856 | tf_op jit(solution)/shard_map/ppermute | solution.py:920
  73.2 2.6 %collective-permute-start.8 = (bf16[48,1536]{1,0:T(8,128)(2,1)S(1)}, bf16[48,1536]{1,0:T(8,128)(2,1)S(1)}, u32[]{:S(2)}, u32[]{:S(2)}) collective-permute-start(bf16[48,1536]{1,0:T(8,128)(2,1)S(1)} %get-tuple-element.198), channel_id=1, source_target_pairs={{0,16},{2,18},{4,20},{6,22},{8,24},{10,26},{12,28},{14,30},{16,0},... | collective-permute-start | bytes 442376 | tf_op jit(solution)/shard_map/ppermute | solution.py:920
  76.0 10.1 %backward_kernel.3 = (bf16[512,768]{1,0:T(8,128)(2,1)S(1)}, bf16[512,256]{1,0:T(8,128)(2,1)S(1)}, bf16[512,128]{1,0:T(8,128)(2,1)S(1)}, f32[128,768]{1,0:T(8,128...) custom-call(s32[5]{0:T(128)S(1)} %stack.23.at_ref, ...), custom_call_target="tpu_custom_call" | custom-call | flops 7000000000 | tf_op jit(solution)/shard_map/backward_kernel/pallas_call | solution.py:832
  86.9 2.8 %weights_kernel.1 = (bf16[384,1152]{1,0:T(8,128)(2,1)S(1)}, bf16[384,1152]{1,0:T(8,128)(2,1)S(1)}, bf16[48,1536]{1,0:T(8,128)(2,1)S(1)}) custom-call(s32[5]{0:T(128)S(1)} %stack.23.at_ref, bf16[1024,768]{1,0:T(8,128)(2,1)S(1)} %get-tuple-element.149.normed_ref, bf16[512,768]{1,0:T(8,128)(2,1)S(1)} %get-tuple-element.184.refs_0_, ...), custom_call_target="tpu_custom_call" | custom-call | flops 1200000000 | tf_op jit(solution)/shard_map/weights_kernel/pallas_call | solution.py:832
  89.8 2.9 %collective-permute-start.17 = (bf16[48,1536]{1,0:T(8,128)(2,1)S(1)}, bf16[48,1536]{1,0:T(8,128)(2,1)S(1)}, u32[]{:S(2)}, u32[]{:S(2)}) collective-permute-start(bf16[48,1536]{1,0:T(8,128)(2,1)S(1)} %get-tuple-element.208.refs_4_), channel_id=1, source_target_pairs={{0,24},{2,26},{4,28},{6,30},{8,16},{10,18},{12,20},{14,22},{16,8},... | collective-permute-start | bytes 442376 | tf_op jit(solution)/shard_map/ppermute | solution.py:920
  96.1 3.6 %normed_grad_kernel.1 = (bf16[512,768]{1,0:T(8,128)(2,1)S(1)}, bf16[512,768]{1,0:T(8,128)(2,1)S(1)}) custom-call(s32[5]{0:T(128)S(1)} %stack.23.at_ref, f32[1024,768]{1,0:T(8,128)S(1)} %gate_back_kernel.1.refs_2_.from_gate, bf16[512,768]{1,0:T(8,128)(2,1)S(1)} %get-tuple-element.184.refs_0_, bf16[512,256]{1,0:T(8,128)(2,1)S(1)} %get-tuple-element.185.refs_1_, ...), custom_call_target="tpu_custom_call" | custom-call | flops 4800000000 | tf_op jit(solution)/shard_map/normed_grad_kernel/pallas_call | solution.py:832
  101.2 5.3 %collective-permute-done.11.refs_1_ = bf16[192,1152]{1,0:T(8,128)(2,1)S(1)} collective-permute-done((bf16[192,1152]{1,0:T(8,128)(2,1)S(1)}, bf16[192,1152]{1,0:T(8,128)(2,1)S(1)}, u32[]{:S(2)}, u32[]{:S(2)}) %collective-permute-start.11) | collective-permute-done | bytes 442400 | tf_op jit(solution)/shard_map/ppermute | solution.py:920
  108.6 1.9 %collective-permute-start.13 = (bf16[48,1152]{1,0:T(8,128)(2,1)S(1)}, bf16[48,1152]{1,0:T(8,128)(2,1)S(1)}, u32[]{:S(2)}, u32[]{:S(2)}) collective-permute-start(bf16[48,1152]{1,0:T(8,128)(2,1)S(1)} %get-tuple-element.206), channel_id=1, source_target_pairs={{0,16},{2,18},{4,20},{6,22},{8,24},{10,26},{12,28},{14,30},{16,0},... | collective-permute-start | bytes 331784 | tf_op jit(solution)/shard_map/ppermute | solution.py:920
  111.8 2.1 %mixed_kernel.1 = (f32[512,768]{1,0:T(8,128)}, f32[8,128]{1,0:T(8,128)S(1)}) custom-call(s32[5]{0:T(128)S(1)} %stack.23.at_ref, bf16[512,768]{1,0:T(8,128)(2,1)S(1)} %bitcast.16, bf16[512,768]{1,0:T(8,128)(2,1)S(1)} %get-tuple-element.143.own_ref._, bf16[512,768]{1,0:T(8,128)(2,1)S(1)} %collective-permute-done.1.other_ref.refs_7_, ...), custom_call_target="tpu_custom_call" | custom-call | flops 2000000000 | tf_op jit(solution)/shard_map/mixed_kernel/pallas_call | solution.py:832
  113.9 5.3 %collective-permute-done.13.refs_2_ = bf16[48,1152]{1,0:T(8,128)(2,1)S(1)} collective-permute-done((bf16[48,1152]{1,0:T(8,128)(2,1)S(1)}, bf16[48,1152]{1,0:T(8,128)(2,1)S(1)}, u32[]{:S(2)}, u32[]{:S(2)}) %collective-permute-start.13) | collective-permute-done | bytes 110624 | tf_op jit(solution)/shard_map/ppermute | solution.py:920
  122.0 3.4 %collective-permute-done.18.other_ref = bf16[48,384]{1,0:T(8,128)(2,1)S(1)} collective-permute-done((bf16[48,384]{1,0:T(8,128)(2,1)S(1)}, bf16[48,384]{1,0:T(8,128)(2,1)S(1)}, u32[]{:S(2)}, u32[]{:S(2)}) %collective-permute-start.18) | collective-permute-done | bytes 36896 | tf_op jit(solution)/shard_map/ppermute | solution.py:1327
  126.1 2.4 %collective-permute-start.21 = (bf16[48,1152]{1,0:T(8,128)(2,1)S(1)}, bf16[48,1152]{1,0:T(8,128)(2,1)S(1)}, u32[]{:S(2)}, u32[]{:S(2)}) collective-permute-start(bf16[48,1152]{1,0:T(8,128)(2,1)S(1)} %heads_kernel.1.refs_0_), channel_id=1, source_target_pairs={{0,24},{2,26},{4,28},{6,30},{8,16},{10,18},{12,20},{14,22},{16,8},... | collective-permute-start | bytes 331784 | tf_op jit(solution)/shard_map/ppermute | solution.py:920
  130.5 2.3 %input_kernel.1 = (f32[512,768]{1,0:T(8,128)}, f32[8,128]{1,0:T(8,128)S(1)}) custom-call(s32[5]{0:T(128)S(1)} %stack.23.at_ref, bf16[512,768]{1,0:T(8,128)(2,1)S(1)} %bitcast.17, bf16[512,768]{1,0:T(8,128)(2,1)S(1)} %bitcast.21, bf16[512,768]{1,0:T(8,128)(2,1)S(1)} %get-tuple-element.187.own_ref.refs_2_, ...), custom_call_target="tpu_custom_call" | custom-call | flops 2000000000 | tf_op jit(solution)/shard_map/input_kernel/pallas_call | solution.py:832
  133.3 2.8 %collective-permute-done.20.refs_2_ = bf16[48,1152]{1,0:T(8,128)(2,1)S(1)} collective-permute-done((bf16[48,1152]{1,0:T(8,128)(2,1)S(1)}, bf16[48,1152]{1,0:T(8,128)(2,1)S(1)}, u32[]{:S(2)}, u32[]{:S(2)}) %collective-permute-start.20) | collective-permute-done | bytes 110624 | tf_op jit(solution)/shard_map/ppermute | solution.py:920
  141.8 3.0 %early_kernel.1 = (f32[768,768]{1,0:T(8,128)}, f32[768,768]{1,0:T(8,128)}, f32[8,128]{1,0:T(8,128)S(1)}) custom-call(s32[5]{0:T(128)S(1)} %stack.23.at_ref, bf16[384,1536]{1,0:T(8,128)(2,1)S(1)} %get-tuple-element.215.own_ref, bf16[384,1536]{1,0:T(8,128)(2,1)S(1)} %collective-permute-done.24.other_ref), custom_call_target="tpu_custom_call" | custom-call | flops 3000000000 | tf_op jit(solution)/shard_map/early_kernel/pallas_call | solution.py:832
  144.7 4.8 %collective-permute-done.23.refs_0_ = bf16[192,1152]{1,0:T(8,128)(2,1)S(1)} collective-permute-done((bf16[192,1152]{1,0:T(8,128)(2,1)S(1)}, bf16[192,1152]{1,0:T(8,128)(2,1)S(1)}, u32[]{:S(2)}, u32[]{:S(2)}) %collective-permute-start.23) | collective-permute-done | bytes 442400 | tf_op jit(solution)/shard_map/ppermute | solution.py:920
  (93 shorter events, 49.4 us)
Async XLA Ops:
  0.7 21.6 %collective-permute-start = (bf16[512,768]{1,0:T(8,128)(2,1)}, bf16[512,768]{1,0:T(8,128)(2,1)S(1)}, u32[]{:S(2)}, u32[]{:S(2)}) collective-permute-start(bf16[512,768]{1,0:T(8,128)(2,1)} %bitcast.14), channel_id=1, source_target_pairs={{0,1},{1,0},{2,3},{3,2},{4,5},{5,4},{6,7},{7,6},{8,9},{9,8},{10,11... | collective-permute-start | bytes 2359304 | tf_op jit(solution)/shard_map/ppermute | solution.py:908
  3.7 34.6 %collective-permute-start.2 = (bf16[512,768]{1,0:T(8,128)(2,1)}, bf16[512,768]{1,0:T(8,128)(2,1)S(1)}, u32[]{:S(2)}, u32[]{:S(2)}) collective-permute-start(bf16[512,768]{1,0:T(8,128)(2,1)} %bitcast.18), channel_id=1, source_target_pairs={{0,1},{1,0},{2,3},{3,2},{4,5},{5,4},{6,7},{7,6},{8,9},{9,8},{10,11... | collective-permute-start | bytes 2359304 | tf_op jit(solution)/shard_map/ppermute | solution.py:908
  40.1 4.1 %collective-permute-start.3 = (f32[16,512]{1,0:T(8,128)S(1)}, f32[16,512]{1,0:T(8,128)S(1)}, u32[]{:S(2)}, u32[]{:S(2)}) collective-permute-start(f32[16,512]{1,0:T(8,128)S(1)} %get-tuple-element.147.here_ref.here_a.here_b), channel_id=1, source_target_pairs={{0,1},{1,0},{2,3},{3,2},{4,5},{5,4},{6,7},{7,6},{8,9},{9,8},{10,11... | collective-permute-start | bytes 98312 | tf_op jit(solution)/shard_map/ppermute | solution.py:909
  50.1 4.5 %collective-permute-start.4 = (bf16[384,1536]{1,0:T(8,128)(2,1)S(1)}, bf16[384,1536]{1,0:T(8,128)(2,1)S(1)}, u32[]{:S(2)}, u32[]{:S(2)}) collective-permute-start(bf16[384,1536]{1,0:T(8,128)(2,1)S(1)} %get-tuple-element.170), channel_id=1, source_target_pairs={{0,2},{2,0},{4,6},{6,4},{8,10},{10,8},{12,14},{14,12},{16,18},{18,... | collective-permute-start | bytes 3538952 | tf_op jit(solution)/shard_map/ppermute | solution.py:920
  50.1 25.9 %collective-permute-start.1 = (bf16[512,768]{1,0:T(8,128)(2,1)S(1)}, bf16[512,768]{1,0:T(8,128)(2,1)S(1)}, u32[]{:S(2)}, u32[]{:S(2)}) collective-permute-start(bf16[512,768]{1,0:T(8,128)(2,1)S(1)} %get-tuple-element.144), channel_id=1, source_target_pairs={{0,1},{1,0},{2,3},{3,2},{4,5},{5,4},{6,7},{7,6},{8,9},{9,8},{10,11... | collective-permute-start | bytes 2359304 | tf_op jit(solution)/shard_map/ppermute | solution.py:1099
  55.4 15.5 %collective-permute-start.5 = (bf16[192,1536]{1,0:T(8,128)(2,1)S(1)}, bf16[192,1536]{1,0:T(8,128)(2,1)S(1)}, u32[]{:S(2)}, u32[]{:S(2)}) collective-permute-start(bf16[192,1536]{1,0:T(8,128)(2,1)S(1)} %get-tuple-element.178), channel_id=1, source_target_pairs={{0,4},{2,6},{4,0},{6,2},{8,12},{10,14},{12,8},{14,10},{16,20},{18,... | collective-permute-start | bytes 1769480 | tf_op jit(solution)/shard_map/ppermute | solution.py:920
  71.5 14.6 %collective-permute-start.7 = (bf16[48,1536]{1,0:T(8,128)(2,1)S(1)}, bf16[48,1536]{1,0:T(8,128)(2,1)S(1)}, u32[]{:S(2)}, u32[]{:S(2)}) collective-permute-start(bf16[48,1536]{1,0:T(8,128)(2,1)S(1)} %get-tuple-element.197), channel_id=1, source_target_pairs={{0,8},{2,10},{4,12},{6,14},{8,0},{10,2},{12,4},{14,6},{16,24},{18,... | collective-permute-start | bytes 442376 | tf_op jit(solution)/shard_map/ppermute | solution.py:920
  73.2 13.7 %collective-permute-start.8 = (bf16[48,1536]{1,0:T(8,128)(2,1)S(1)}, bf16[48,1536]{1,0:T(8,128)(2,1)S(1)}, u32[]{:S(2)}, u32[]{:S(2)}) collective-permute-start(bf16[48,1536]{1,0:T(8,128)(2,1)S(1)} %get-tuple-element.198), channel_id=1, source_target_pairs={{0,16},{2,18},{4,20},{6,22},{8,24},{10,26},{12,28},{14,30},{16,0},... | collective-permute-start | bytes 442376 | tf_op jit(solution)/shard_map/ppermute | solution.py:920
  75.8 11.1 %collective-permute-start.9 = (bf16[48,1536]{1,0:T(8,128)(2,1)S(1)}, bf16[48,1536]{1,0:T(8,128)(2,1)S(1)}, u32[]{:S(2)}, u32[]{:S(2)}) collective-permute-start(bf16[48,1536]{1,0:T(8,128)(2,1)S(1)} %get-tuple-element.199), channel_id=1, source_target_pairs={{0,24},{2,26},{4,28},{6,30},{8,16},{10,18},{12,20},{14,22},{16,8},... | collective-permute-start | bytes 442376 | tf_op jit(solution)/shard_map/ppermute | solution.py:920
  89.8 18.8 %collective-permute-start.17 = (bf16[48,1536]{1,0:T(8,128)(2,1)S(1)}, bf16[48,1536]{1,0:T(8,128)(2,1)S(1)}, u32[]{:S(2)}, u32[]{:S(2)}) collective-permute-start(bf16[48,1536]{1,0:T(8,128)(2,1)S(1)} %get-tuple-element.208.refs_4_), channel_id=1, source_target_pairs={{0,24},{2,26},{4,28},{6,30},{8,16},{10,18},{12,20},{14,22},{16,8},... | collective-permute-start | bytes 442376 | tf_op jit(solution)/shard_map/ppermute | solution.py:920
  92.7 17.8 %collective-permute-start.16 = (bf16[48,1536]{1,0:T(8,128)(2,1)S(1)}, bf16[48,1536]{1,0:T(8,128)(2,1)S(1)}, u32[]{:S(2)}, u32[]{:S(2)}) collective-permute-start(bf16[48,1536]{1,0:T(8,128)(2,1)S(1)} %get-tuple-element.208.refs_4_), channel_id=1, source_target_pairs={{0,16},{2,18},{4,20},{6,22},{8,24},{10,26},{12,28},{14,30},{16,0},... | collective-permute-start | bytes 442376 | tf_op jit(solution)/shard_map/ppermute | solution.py:920
  94.6 12.0 %collective-permute-start.11 = (bf16[192,1152]{1,0:T(8,128)(2,1)S(1)}, bf16[192,1152]{1,0:T(8,128)(2,1)S(1)}, u32[]{:S(2)}, u32[]{:S(2)}) collective-permute-start(bf16[192,1152]{1,0:T(8,128)(2,1)S(1)} %get-tuple-element.203), channel_id=1, source_target_pairs={{0,4},{2,6},{4,0},{6,2},{8,12},{10,14},{12,8},{14,10},{16,20},{18,... | collective-permute-start | bytes 1327112 | tf_op jit(solution)/shard_map/ppermute | solution.py:920
  99.7 30.8 %collective-permute-start.6 = (bf16[512,768]{1,0:T(8,128)(2,1)S(1)}, bf16[512,768]{1,0:T(8,128)(2,1)S(1)}, u32[]{:S(2)}, u32[]{:S(2)}) collective-permute-start(bf16[512,768]{1,0:T(8,128)(2,1)S(1)} %get-tuple-element.188), channel_id=1, source_target_pairs={{0,1},{1,0},{2,3},{3,2},{4,5},{5,4},{6,7},{7,6},{8,9},{9,8},{10,11... | collective-permute-start | bytes 2359304 | tf_op jit(solution)/shard_map/ppermute | solution.py:1099
  100.4 13.6 %collective-permute-start.15 = (bf16[48,1536]{1,0:T(8,128)(2,1)S(1)}, bf16[48,1536]{1,0:T(8,128)(2,1)S(1)}, u32[]{:S(2)}, u32[]{:S(2)}) collective-permute-start(bf16[48,1536]{1,0:T(8,128)(2,1)S(1)} %get-tuple-element.208.refs_4_), channel_id=1, source_target_pairs={{0,8},{2,10},{4,12},{6,14},{8,0},{10,2},{12,4},{14,6},{16,24},{18,... | collective-permute-start | bytes 442376 | tf_op jit(solution)/shard_map/ppermute | solution.py:920
  107.4 6.5 %collective-permute-start.12 = (bf16[48,1152]{1,0:T(8,128)(2,1)S(1)}, bf16[48,1152]{1,0:T(8,128)(2,1)S(1)}, u32[]{:S(2)}, u32[]{:S(2)}) collective-permute-start(bf16[48,1152]{1,0:T(8,128)(2,1)S(1)} %get-tuple-element.205), channel_id=1, source_target_pairs={{0,8},{2,10},{4,12},{6,14},{8,0},{10,2},{12,4},{14,6},{16,24},{18,... | collective-permute-start | bytes 331784 | tf_op jit(solution)/shard_map/ppermute | solution.py:920
  108.6 10.6 %collective-permute-start.13 = (bf16[48,1152]{1,0:T(8,128)(2,1)S(1)}, bf16[48,1152]{1,0:T(8,128)(2,1)S(1)}, u32[]{:S(2)}, u32[]{:S(2)}) collective-permute-start(bf16[48,1152]{1,0:T(8,128)(2,1)S(1)} %get-tuple-element.206), channel_id=1, source_target_pairs={{0,16},{2,18},{4,20},{6,22},{8,24},{10,26},{12,28},{14,30},{16,0},... | collective-permute-start | bytes 331784 | tf_op jit(solution)/shard_map/ppermute | solution.py:920
  110.5 8.7 %collective-permute-start.14 = (bf16[48,1152]{1,0:T(8,128)(2,1)S(1)}, bf16[48,1152]{1,0:T(8,128)(2,1)S(1)}, u32[]{:S(2)}, u32[]{:S(2)}) collective-permute-start(bf16[48,1152]{1,0:T(8,128)(2,1)S(1)} %get-tuple-element.207), channel_id=1, source_target_pairs={{0,24},{2,26},{4,28},{6,30},{8,16},{10,18},{12,20},{14,22},{16,8},... | collective-permute-start | bytes 331784 | tf_op jit(solution)/shard_map/ppermute | solution.py:920
  119.9 16.2 %collective-permute-start.22 = (bf16[192,1536]{1,0:T(8,128)(2,1)S(1)}, bf16[192,1536]{1,0:T(8,128)(2,1)S(1)}, u32[]{:S(2)}, u32[]{:S(2)}) collective-permute-start(bf16[192,1536]{1,0:T(8,128)(2,1)S(1)} %get-tuple-element.212.refs_4_), channel_id=1, source_target_pairs={{0,4},{2,6},{4,0},{6,2},{8,12},{10,14},{12,8},{14,10},{16,20},{18,... | collective-permute-start | bytes 1769480 | tf_op jit(solution)/shard_map/ppermute | solution.py:920
  121.5 4.0 %collective-permute-start.18 = (bf16[48,384]{1,0:T(8,128)(2,1)S(1)}, bf16[48,384]{1,0:T(8,128)(2,1)S(1)}, u32[]{:S(2)}, u32[]{:S(2)}) collective-permute-start(bf16[48,384]{1,0:T(8,128)(2,1)S(1)} %get-tuple-element.211.own_ref), channel_id=1, source_target_pairs={{0,1},{1,0},{2,3},{3,2},{4,5},{5,4},{6,7},{7,6},{8,9},{9,8},{10,11... | collective-permute-start | bytes 110600 | tf_op jit(solution)/shard_map/ppermute | solution.py:1327
  126.1 7.1 %collective-permute-start.21 = (bf16[48,1152]{1,0:T(8,128)(2,1)S(1)}, bf16[48,1152]{1,0:T(8,128)(2,1)S(1)}, u32[]{:S(2)}, u32[]{:S(2)}) collective-permute-start(bf16[48,1152]{1,0:T(8,128)(2,1)S(1)} %heads_kernel.1.refs_0_), channel_id=1, source_target_pairs={{0,24},{2,26},{4,28},{6,30},{8,16},{10,18},{12,20},{14,22},{16,8},... | collective-permute-start | bytes 331784 | tf_op jit(solution)/shard_map/ppermute | solution.py:920
  128.5 7.6 %collective-permute-start.20 = (bf16[48,1152]{1,0:T(8,128)(2,1)S(1)}, bf16[48,1152]{1,0:T(8,128)(2,1)S(1)}, u32[]{:S(2)}, u32[]{:S(2)}) collective-permute-start(bf16[48,1152]{1,0:T(8,128)(2,1)S(1)} %heads_kernel.1.refs_0_), channel_id=1, source_target_pairs={{0,16},{2,18},{4,20},{6,22},{8,24},{10,26},{12,28},{14,30},{16,0},... | collective-permute-start | bytes 331784 | tf_op jit(solution)/shard_map/ppermute | solution.py:920
  129.5 6.6 %collective-permute-start.19 = (bf16[48,1152]{1,0:T(8,128)(2,1)S(1)}, bf16[48,1152]{1,0:T(8,128)(2,1)S(1)}, u32[]{:S(2)}, u32[]{:S(2)}) collective-permute-start(bf16[48,1152]{1,0:T(8,128)(2,1)S(1)} %heads_kernel.1.refs_0_), channel_id=1, source_target_pairs={{0,8},{2,10},{4,12},{6,14},{8,0},{10,2},{12,4},{14,6},{16,24},{18,... | collective-permute-start | bytes 331784 | tf_op jit(solution)/shard_map/ppermute | solution.py:920
  136.8 5.0 %collective-permute-start.24 = (bf16[384,1536]{1,0:T(8,128)(2,1)S(1)}, bf16[384,1536]{1,0:T(8,128)(2,1)S(1)}, u32[]{:S(2)}, u32[]{:S(2)}) collective-permute-start(bf16[384,1536]{1,0:T(8,128)(2,1)S(1)} %get-tuple-element.215.own_ref), channel_id=1, source_target_pairs={{0,2},{2,0},{4,6},{6,4},{8,10},{10,8},{12,14},{14,12},{16,18},{18,... | collective-permute-start | bytes 3538952 | tf_op jit(solution)/shard_map/ppermute | solution.py:920
  137.3 12.2 %collective-permute-start.23 = (bf16[192,1152]{1,0:T(8,128)(2,1)S(1)}, bf16[192,1152]{1,0:T(8,128)(2,1)S(1)}, u32[]{:S(2)}, u32[]{:S(2)}) collective-permute-start(bf16[192,1152]{1,0:T(8,128)(2,1)S(1)} %get-tuple-element.214.piece_ref.refs_0_), channel_id=1, source_target_pairs={{0,4},{2,6},{4,0},{6,2},{8,12},{10,14},{12,8},{14,10},{16,20},{18,... | collective-permute-start | bytes 1327112 | tf_op jit(solution)/shard_map/ppermute | solution.py:920
  (11 other events, 56.2 us)

commit v7 on v6

--- a/solution.py
+++ b/solution.py
@@ -30,7 +30,7 @@
 
 
 def sigmoid(v):
-    return 0.5 * jnp.tanh(0.5 * v) + 0.5
+    return 1.0 / (1.0 + jnp.exp(-v))
 
 
 def silu(v):

time: 154 us -> 154 us (level)
  no operation moved by 1% of the time
where the time goes in v7:
time: 154 us
  Pallas kernels  76.5 us (50%)
  waiting for transfers between devices  34.2 us (22%)
  starting transfers between devices  31.5 us (20%)
  local copies, waits for them, and re-layouts  10 us (6%)
    pallas_call x28, Pallas kernels, call(): pl.pallas_call(kernel, name=title, grid_spec=pltpu.PrefetchScalarGridSpec...  76.5 us
    ppermute x21, starting transfers between devices, hop(): return lax.ppermute(a, 'batch', [(i, i ^ mask) for i in range(batch)])  23.8 us
    ppermute x21, waiting for transfers between devices, hop(): return lax.ppermute(a, 'batch', [(i, i ^ mask) for i in range(batch)])  23.7 us
    ppermute x2, waiting for transfers between devices, per_device(): pair_of = lambda a: (a, lax.ppermute(a, 'heads', swap))  7.12 us
    unnamed x17, local copies, waits for them, and re-layouts  4.13 us
    ppermute x1, waiting for transfers between devices, per_device(): theirs = lax.ppermute(rest, 'heads', swap)  3.42 us
    ppermute x2, starting transfers between devices, per_device(): pair_of = lambda a: (a, lax.ppermute(a, 'heads', swap))  3.08 us
  transfers between devices with their start and end apart: 27, of which 12 were waited for; matrix products, arithmetic and copies ran while one was open for 5% of the time, Pallas kernels for 41%

profile of v7, /device:TPU:0, one launch (start us, length us, event | category | flops | bytes accessed | tf_op | source)
XLA Modules:
  0.0 153.8 jit_solution(6322566329185487420)
XLA Ops:
  0.7 3.0 %collective-permute-start = (bf16[512,768]{1,0:T(8,128)(2,1)}, bf16[512,768]{1,0:T(8,128)(2,1)S(1)}, u32[]{:S(2)}, u32[]{:S(2)}) collective-permute-start(bf16[512,768]{1,0:T(8,128)(2,1)} %bitcast.14), channel_id=1, source_target_pairs={{0,1},{1,0},{2,3},{3,2},{4,5},{5,4},{6,7},{7,6},{8,9},{9,8},{10,11... | collective-permute-start | bytes 2359304 | tf_op jit(solution)/shard_map/ppermute | solution.py:908
  15.8 6.5 %collective-permute-done.other_ref = bf16[512,768]{1,0:T(8,128)(2,1)S(1)} collective-permute-done((bf16[512,768]{1,0:T(8,128)(2,1)}, bf16[512,768]{1,0:T(8,128)(2,1)S(1)}, u32[]{:S(2)}, u32[]{:S(2)}) %collective-permute-start) | collective-permute-done | bytes 786464 | tf_op jit(solution)/shard_map/ppermute | solution.py:908
  22.3 13.6 %forward_kernel.1 = (bf16[1024,768]{1,0:T(8,128)(2,1)S(1)}, f32[1024,768]{1,0:T(8,128)S(1)}, f32[1024,768]{1,0:T(8,128)S(1)}, bf16[1024,768]{1,0:T(8,128)(2,1)S(...) custom-call(s32[5]{0:T(128)S(1)} %stack.23.at_ref, ...), custom_call_target="tpu_custom_call" | custom-call | flops 17999998976 | tf_op jit(solution)/shard_map/forward_kernel/pallas_call | solution.py:832
  35.8 1.8 %stats_kernel.2 = (f32[512,768]{1,0:T(8,128)S(1)}, f32[8,512]{1,0:T(8,128)S(1)}) custom-call(s32[5]{0:T(128)S(1)} %stack.23.at_ref, bf16[512,768]{1,0:T(8,128)(2,1)S(1)} %bitcast.19, bf16[1024,768]{1,0:T(8,128)(2,1)S(1)} %get-tuple-element.141.gg_ref, f32[8,1024]{1,0:T(8,128)S(1)} %get-tuple-element.145.sq_ref, bf16[768,768]{1,0:T(8,128)(2,1)S(1)} %get-tuple-element.142.out_w), custom_call_target="tpu_custom_call" | custom-call | flops 1000000000 | tf_op jit(solution)/shard_map/stats_kernel/pallas_call | solution.py:832
  41.8 2.3 %branch_kernel.1 = (bf16[512,768]{1,0:T(8,128)(2,1)S(1)}, bf16[512,768]{1,0:T(8,128)(2,1)S(1)}) custom-call(s32[5]{0:T(128)S(1)} %stack.23.at_ref, bf16[1024,768]{1,0:T(8,128)(2,1)S(1)} %get-tuple-element.141.gg_ref, bf16[768,768]{1,0:T(8,128)(2,1)S(1)} %get-tuple-element.142.out_w), custom_call_target="tpu_custom_call" | custom-call | flops 1200000000 | tf_op jit(solution)/shard_map/branch_kernel/pallas_call | solution.py:832
  44.1 6.0 %gate_kernel.1 = (bf16[1024,768]{1,0:T(8,128)(2,1)S(1)}, bf16[1024,768]{1,0:T(8,128)(2,1)S(1)}, bf16[384,1536]{1,0:T(8,128)(2,1)S(1)}, bf16[384,1536]{1,0:T(8,12...) custom-call(s32[5]{0:T(128)S(1)} %stack.23.at_ref, bf16[512,768]{1,0:T(8,128)(2,1)S(1)} %bitcast.20, ...), custom_call_target="tpu_custom_call" | custom-call | flops 4800000000 | tf_op jit(solution)/shard_map/gate_kernel/pallas_call | solution.py:832
  51.8 2.8 %gate_back_kernel.1.refs_2_.from_gate = f32[1024,768]{1,0:T(8,128)S(1)} custom-call(s32[5]{0:T(128)S(1)} %stack.23.at_ref, bf16[1024,768]{1,0:T(8,128)(2,1)S(1)} %get-tuple-element.154.dg_ref, bf16[768,768]{1,0:T(8,128)(2,1)S(1)} %get-tuple-element.128.gate_w), custom_call_target="tpu_custom_call" | custom-call | flops 4000000000 | tf_op jit(solution)/shard_map/gate_back_kernel/pallas_call | solution.py:832
  57.0 9.2 %backward_kernel.2 = (bf16[512,768]{1,0:T(8,128)(2,1)S(1)}, bf16[512,256]{1,0:T(8,128)(2,1)S(1)}, bf16[512,128]{1,0:T(8,128)(2,1)S(1)}, f32[128,768]{1,0:T(8,128...) custom-call(s32[5]{0:T(128)S(1)} %stack.23.at_ref, ...), custom_call_target="tpu_custom_call" | custom-call | flops 7000000000 | tf_op jit(solution)/shard_map/backward_kernel/pallas_call | solution.py:832
  68.0 2.9 %collective-permute-done.5.refs_1_ = bf16[192,1536]{1,0:T(8,128)(2,1)S(1)} collective-permute-done((bf16[192,1536]{1,0:T(8,128)(2,1)S(1)}, bf16[192,1536]{1,0:T(8,128)(2,1)S(1)}, u32[]{:S(2)}, u32[]{:S(2)}) %collective-permute-start.5) | collective-permute-done | bytes 589856 | tf_op jit(solution)/shard_map/ppermute | solution.py:920
  73.2 2.6 %collective-permute-start.8 = (bf16[48,1536]{1,0:T(8,128)(2,1)S(1)}, bf16[48,1536]{1,0:T(8,128)(2,1)S(1)}, u32[]{:S(2)}, u32[]{:S(2)}) collective-permute-start(bf16[48,1536]{1,0:T(8,128)(2,1)S(1)} %get-tuple-element.198), channel_id=1, source_target_pairs={{0,16},{2,18},{4,20},{6,22},{8,24},{10,26},{12,28},{14,30},{16,0},... | collective-permute-start | bytes 442376 | tf_op jit(solution)/shard_map/ppermute | solution.py:920
  76.0 10.1 %backward_kernel.3 = (bf16[512,768]{1,0:T(8,128)(2,1)S(1)}, bf16[512,256]{1,0:T(8,128)(2,1)S(1)}, bf16[512,128]{1,0:T(8,128)(2,1)S(1)}, f32[128,768]{1,0:T(8,128...) custom-call(s32[5]{0:T(128)S(1)} %stack.23.at_ref, ...), custom_call_target="tpu_custom_call" | custom-call | flops 7000000000 | tf_op jit(solution)/shard_map/backward_kernel/pallas_call | solution.py:832
  86.9 2.8 %weights_kernel.1 = (bf16[384,1152]{1,0:T(8,128)(2,1)S(1)}, bf16[384,1152]{1,0:T(8,128)(2,1)S(1)}, bf16[48,1536]{1,0:T(8,128)(2,1)S(1)}) custom-call(s32[5]{0:T(128)S(1)} %stack.23.at_ref, bf16[1024,768]{1,0:T(8,128)(2,1)S(1)} %get-tuple-element.149.normed_ref, bf16[512,768]{1,0:T(8,128)(2,1)S(1)} %get-tuple-element.184.refs_0_, ...), custom_call_target="tpu_custom_call" | custom-call | flops 1200000000 | tf_op jit(solution)/shard_map/weights_kernel/pallas_call | solution.py:832
  89.8 2.9 %collective-permute-start.17 = (bf16[48,1536]{1,0:T(8,128)(2,1)S(1)}, bf16[48,1536]{1,0:T(8,128)(2,1)S(1)}, u32[]{:S(2)}, u32[]{:S(2)}) collective-permute-start(bf16[48,1536]{1,0:T(8,128)(2,1)S(1)} %get-tuple-element.208.refs_4_), channel_id=1, source_target_pairs={{0,24},{2,26},{4,28},{6,30},{8,16},{10,18},{12,20},{14,22},{16,8},... | collective-permute-start | bytes 442376 | tf_op jit(solution)/shard_map/ppermute | solution.py:920
  96.1 3.6 %normed_grad_kernel.1 = (bf16[512,768]{1,0:T(8,128)(2,1)S(1)}, bf16[512,768]{1,0:T(8,128)(2,1)S(1)}) custom-call(s32[5]{0:T(128)S(1)} %stack.23.at_ref, f32[1024,768]{1,0:T(8,128)S(1)} %gate_back_kernel.1.refs_2_.from_gate, bf16[512,768]{1,0:T(8,128)(2,1)S(1)} %get-tuple-element.184.refs_0_, bf16[512,256]{1,0:T(8,128)(2,1)S(1)} %get-tuple-element.185.refs_1_, ...), custom_call_target="tpu_custom_call" | custom-call | flops 4800000000 | tf_op jit(solution)/shard_map/normed_grad_kernel/pallas_call | solution.py:832
  101.2 5.3 %collective-permute-done.11.refs_1_ = bf16[192,1152]{1,0:T(8,128)(2,1)S(1)} collective-permute-done((bf16[192,1152]{1,0:T(8,128)(2,1)S(1)}, bf16[192,1152]{1,0:T(8,128)(2,1)S(1)}, u32[]{:S(2)}, u32[]{:S(2)}) %collective-permute-start.11) | collective-permute-done | bytes 442400 | tf_op jit(solution)/shard_map/ppermute | solution.py:920
  108.6 1.9 %collective-permute-start.13 = (bf16[48,1152]{1,0:T(8,128)(2,1)S(1)}, bf16[48,1152]{1,0:T(8,128)(2,1)S(1)}, u32[]{:S(2)}, u32[]{:S(2)}) collective-permute-start(bf16[48,1152]{1,0:T(8,128)(2,1)S(1)} %get-tuple-element.206), channel_id=1, source_target_pairs={{0,16},{2,18},{4,20},{6,22},{8,24},{10,26},{12,28},{14,30},{16,0},... | collective-permute-start | bytes 331784 | tf_op jit(solution)/shard_map/ppermute | solution.py:920
  111.8 2.1 %mixed_kernel.1 = (f32[512,768]{1,0:T(8,128)}, f32[8,128]{1,0:T(8,128)S(1)}) custom-call(s32[5]{0:T(128)S(1)} %stack.23.at_ref, bf16[512,768]{1,0:T(8,128)(2,1)S(1)} %bitcast.16, bf16[512,768]{1,0:T(8,128)(2,1)S(1)} %get-tuple-element.143.own_ref._, bf16[512,768]{1,0:T(8,128)(2,1)S(1)} %collective-permute-done.1.other_ref.refs_7_, ...), custom_call_target="tpu_custom_call" | custom-call | flops 2000000000 | tf_op jit(solution)/shard_map/mixed_kernel/pallas_call | solution.py:832
  113.9 5.3 %collective-permute-done.13.refs_2_ = bf16[48,1152]{1,0:T(8,128)(2,1)S(1)} collective-permute-done((bf16[48,1152]{1,0:T(8,128)(2,1)S(1)}, bf16[48,1152]{1,0:T(8,128)(2,1)S(1)}, u32[]{:S(2)}, u32[]{:S(2)}) %collective-permute-start.13) | collective-permute-done | bytes 110624 | tf_op jit(solution)/shard_map/ppermute | solution.py:920
  122.0 3.4 %collective-permute-done.18.other_ref = bf16[48,384]{1,0:T(8,128)(2,1)S(1)} collective-permute-done((bf16[48,384]{1,0:T(8,128)(2,1)S(1)}, bf16[48,384]{1,0:T(8,128)(2,1)S(1)}, u32[]{:S(2)}, u32[]{:S(2)}) %collective-permute-start.18) | collective-permute-done | bytes 36896 | tf_op jit(solution)/shard_map/ppermute | solution.py:1327
  126.1 2.4 %collective-permute-start.21 = (bf16[48,1152]{1,0:T(8,128)(2,1)S(1)}, bf16[48,1152]{1,0:T(8,128)(2,1)S(1)}, u32[]{:S(2)}, u32[]{:S(2)}) collective-permute-start(bf16[48,1152]{1,0:T(8,128)(2,1)S(1)} %heads_kernel.1.refs_0_), channel_id=1, source_target_pairs={{0,24},{2,26},{4,28},{6,30},{8,16},{10,18},{12,20},{14,22},{16,8},... | collective-permute-start | bytes 331784 | tf_op jit(solution)/shard_map/ppermute | solution.py:920
  130.5 2.3 %input_kernel.1 = (f32[512,768]{1,0:T(8,128)}, f32[8,128]{1,0:T(8,128)S(1)}) custom-call(s32[5]{0:T(128)S(1)} %stack.23.at_ref, bf16[512,768]{1,0:T(8,128)(2,1)S(1)} %bitcast.17, bf16[512,768]{1,0:T(8,128)(2,1)S(1)} %bitcast.21, bf16[512,768]{1,0:T(8,128)(2,1)S(1)} %get-tuple-element.187.own_ref.refs_2_, ...), custom_call_target="tpu_custom_call" | custom-call | flops 2000000000 | tf_op jit(solution)/shard_map/input_kernel/pallas_call | solution.py:832
  133.3 2.8 %collective-permute-done.20.refs_2_ = bf16[48,1152]{1,0:T(8,128)(2,1)S(1)} collective-permute-done((bf16[48,1152]{1,0:T(8,128)(2,1)S(1)}, bf16[48,1152]{1,0:T(8,128)(2,1)S(1)}, u32[]{:S(2)}, u32[]{:S(2)}) %collective-permute-start.20) | collective-permute-done | bytes 110624 | tf_op jit(solution)/shard_map/ppermute | solution.py:920
  141.8 3.0 %early_kernel.1 = (f32[768,768]{1,0:T(8,128)}, f32[768,768]{1,0:T(8,128)}, f32[8,128]{1,0:T(8,128)S(1)}) custom-call(s32[5]{0:T(128)S(1)} %stack.23.at_ref, bf16[384,1536]{1,0:T(8,128)(2,1)S(1)} %get-tuple-element.215.own_ref, bf16[384,1536]{1,0:T(8,128)(2,1)S(1)} %collective-permute-done.24.other_ref), custom_call_target="tpu_custom_call" | custom-call | flops 3000000000 | tf_op jit(solution)/shard_map/early_kernel/pallas_call | solution.py:832
  144.7 4.8 %collective-permute-done.23.refs_0_ = bf16[192,1152]{1,0:T(8,128)(2,1)S(1)} collective-permute-done((bf16[192,1152]{1,0:T(8,128)(2,1)S(1)}, bf16[192,1152]{1,0:T(8,128)(2,1)S(1)}, u32[]{:S(2)}, u32[]{:S(2)}) %collective-permute-start.23) | collective-permute-done | bytes 442400 | tf_op jit(solution)/shard_map/ppermute | solution.py:920
  (93 shorter events, 49.3 us)
Async XLA Ops:
  0.7 21.6 %collective-permute-start = (bf16[512,768]{1,0:T(8,128)(2,1)}, bf16[512,768]{1,0:T(8,128)(2,1)S(1)}, u32[]{:S(2)}, u32[]{:S(2)}) collective-permute-start(bf16[512,768]{1,0:T(8,128)(2,1)} %bitcast.14), channel_id=1, source_target_pairs={{0,1},{1,0},{2,3},{3,2},{4,5},{5,4},{6,7},{7,6},{8,9},{9,8},{10,11... | collective-permute-start | bytes 2359304 | tf_op jit(solution)/shard_map/ppermute | solution.py:908
  3.7 34.6 %collective-permute-start.2 = (bf16[512,768]{1,0:T(8,128)(2,1)}, bf16[512,768]{1,0:T(8,128)(2,1)S(1)}, u32[]{:S(2)}, u32[]{:S(2)}) collective-permute-start(bf16[512,768]{1,0:T(8,128)(2,1)} %bitcast.18), channel_id=1, source_target_pairs={{0,1},{1,0},{2,3},{3,2},{4,5},{5,4},{6,7},{7,6},{8,9},{9,8},{10,11... | collective-permute-start | bytes 2359304 | tf_op jit(solution)/shard_map/ppermute | solution.py:908
  40.1 4.1 %collective-permute-start.3 = (f32[16,512]{1,0:T(8,128)S(1)}, f32[16,512]{1,0:T(8,128)S(1)}, u32[]{:S(2)}, u32[]{:S(2)}) collective-permute-start(f32[16,512]{1,0:T(8,128)S(1)} %get-tuple-element.147.here_ref.here_a.here_b), channel_id=1, source_target_pairs={{0,1},{1,0},{2,3},{3,2},{4,5},{5,4},{6,7},{7,6},{8,9},{9,8},{10,11... | collective-permute-start | bytes 98312 | tf_op jit(solution)/shard_map/ppermute | solution.py:909
  50.1 4.5 %collective-permute-start.4 = (bf16[384,1536]{1,0:T(8,128)(2,1)S(1)}, bf16[384,1536]{1,0:T(8,128)(2,1)S(1)}, u32[]{:S(2)}, u32[]{:S(2)}) collective-permute-start(bf16[384,1536]{1,0:T(8,128)(2,1)S(1)} %get-tuple-element.170), channel_id=1, source_target_pairs={{0,2},{2,0},{4,6},{6,4},{8,10},{10,8},{12,14},{14,12},{16,18},{18,... | collective-permute-start | bytes 3538952 | tf_op jit(solution)/shard_map/ppermute | solution.py:920
  50.1 25.9 %collective-permute-start.1 = (bf16[512,768]{1,0:T(8,128)(2,1)S(1)}, bf16[512,768]{1,0:T(8,128)(2,1)S(1)}, u32[]{:S(2)}, u32[]{:S(2)}) collective-permute-start(bf16[512,768]{1,0:T(8,128)(2,1)S(1)} %get-tuple-element.144), channel_id=1, source_target_pairs={{0,1},{1,0},{2,3},{3,2},{4,5},{5,4},{6,7},{7,6},{8,9},{9,8},{10,11... | collective-permute-start | bytes 2359304 | tf_op jit(solution)/shard_map/ppermute | solution.py:1099
  55.4 15.5 %collective-permute-start.5 = (bf16[192,1536]{1,0:T(8,128)(2,1)S(1)}, bf16[192,1536]{1,0:T(8,128)(2,1)S(1)}, u32[]{:S(2)}, u32[]{:S(2)}) collective-permute-start(bf16[192,1536]{1,0:T(8,128)(2,1)S(1)} %get-tuple-element.178), channel_id=1, source_target_pairs={{0,4},{2,6},{4,0},{6,2},{8,12},{10,14},{12,8},{14,10},{16,20},{18,... | collective-permute-start | bytes 1769480 | tf_op jit(solution)/shard_map/ppermute | solution.py:920
  71.5 14.6 %collective-permute-start.7 = (bf16[48,1536]{1,0:T(8,128)(2,1)S(1)}, bf16[48,1536]{1,0:T(8,128)(2,1)S(1)}, u32[]{:S(2)}, u32[]{:S(2)}) collective-permute-start(bf16[48,1536]{1,0:T(8,128)(2,1)S(1)} %get-tuple-element.197), channel_id=1, source_target_pairs={{0,8},{2,10},{4,12},{6,14},{8,0},{10,2},{12,4},{14,6},{16,24},{18,... | collective-permute-start | bytes 442376 | tf_op jit(solution)/shard_map/ppermute | solution.py:920
  73.2 13.7 %collective-permute-start.8 = (bf16[48,1536]{1,0:T(8,128)(2,1)S(1)}, bf16[48,1536]{1,0:T(8,128)(2,1)S(1)}, u32[]{:S(2)}, u32[]{:S(2)}) collective-permute-start(bf16[48,1536]{1,0:T(8,128)(2,1)S(1)} %get-tuple-element.198), channel_id=1, source_target_pairs={{0,16},{2,18},{4,20},{6,22},{8,24},{10,26},{12,28},{14,30},{16,0},... | collective-permute-start | bytes 442376 | tf_op jit(solution)/shard_map/ppermute | solution.py:920
  75.8 11.1 %collective-permute-start.9 = (bf16[48,1536]{1,0:T(8,128)(2,1)S(1)}, bf16[48,1536]{1,0:T(8,128)(2,1)S(1)}, u32[]{:S(2)}, u32[]{:S(2)}) collective-permute-start(bf16[48,1536]{1,0:T(8,128)(2,1)S(1)} %get-tuple-element.199), channel_id=1, source_target_pairs={{0,24},{2,26},{4,28},{6,30},{8,16},{10,18},{12,20},{14,22},{16,8},... | collective-permute-start | bytes 442376 | tf_op jit(solution)/shard_map/ppermute | solution.py:920
  89.8 18.8 %collective-permute-start.17 = (bf16[48,1536]{1,0:T(8,128)(2,1)S(1)}, bf16[48,1536]{1,0:T(8,128)(2,1)S(1)}, u32[]{:S(2)}, u32[]{:S(2)}) collective-permute-start(bf16[48,1536]{1,0:T(8,128)(2,1)S(1)} %get-tuple-element.208.refs_4_), channel_id=1, source_target_pairs={{0,24},{2,26},{4,28},{6,30},{8,16},{10,18},{12,20},{14,22},{16,8},... | collective-permute-start | bytes 442376 | tf_op jit(solution)/shard_map/ppermute | solution.py:920
  92.7 17.8 %collective-permute-start.16 = (bf16[48,1536]{1,0:T(8,128)(2,1)S(1)}, bf16[48,1536]{1,0:T(8,128)(2,1)S(1)}, u32[]{:S(2)}, u32[]{:S(2)}) collective-permute-start(bf16[48,1536]{1,0:T(8,128)(2,1)S(1)} %get-tuple-element.208.refs_4_), channel_id=1, source_target_pairs={{0,16},{2,18},{4,20},{6,22},{8,24},{10,26},{12,28},{14,30},{16,0},... | collective-permute-start | bytes 442376 | tf_op jit(solution)/shard_map/ppermute | solution.py:920
  94.6 12.0 %collective-permute-start.11 = (bf16[192,1152]{1,0:T(8,128)(2,1)S(1)}, bf16[192,1152]{1,0:T(8,128)(2,1)S(1)}, u32[]{:S(2)}, u32[]{:S(2)}) collective-permute-start(bf16[192,1152]{1,0:T(8,128)(2,1)S(1)} %get-tuple-element.203), channel_id=1, source_target_pairs={{0,4},{2,6},{4,0},{6,2},{8,12},{10,14},{12,8},{14,10},{16,20},{18,... | collective-permute-start | bytes 1327112 | tf_op jit(solution)/shard_map/ppermute | solution.py:920
  99.7 30.8 %collective-permute-start.6 = (bf16[512,768]{1,0:T(8,128)(2,1)S(1)}, bf16[512,768]{1,0:T(8,128)(2,1)S(1)}, u32[]{:S(2)}, u32[]{:S(2)}) collective-permute-start(bf16[512,768]{1,0:T(8,128)(2,1)S(1)} %get-tuple-element.188), channel_id=1, source_target_pairs={{0,1},{1,0},{2,3},{3,2},{4,5},{5,4},{6,7},{7,6},{8,9},{9,8},{10,11... | collective-permute-start | bytes 2359304 | tf_op jit(solution)/shard_map/ppermute | solution.py:1099
  100.4 13.6 %collective-permute-start.15 = (bf16[48,1536]{1,0:T(8,128)(2,1)S(1)}, bf16[48,1536]{1,0:T(8,128)(2,1)S(1)}, u32[]{:S(2)}, u32[]{:S(2)}) collective-permute-start(bf16[48,1536]{1,0:T(8,128)(2,1)S(1)} %get-tuple-element.208.refs_4_), channel_id=1, source_target_pairs={{0,8},{2,10},{4,12},{6,14},{8,0},{10,2},{12,4},{14,6},{16,24},{18,... | collective-permute-start | bytes 442376 | tf_op jit(solution)/shard_map/ppermute | solution.py:920
  107.4 6.5 %collective-permute-start.12 = (bf16[48,1152]{1,0:T(8,128)(2,1)S(1)}, bf16[48,1152]{1,0:T(8,128)(2,1)S(1)}, u32[]{:S(2)}, u32[]{:S(2)}) collective-permute-start(bf16[48,1152]{1,0:T(8,128)(2,1)S(1)} %get-tuple-element.205), channel_id=1, source_target_pairs={{0,8},{2,10},{4,12},{6,14},{8,0},{10,2},{12,4},{14,6},{16,24},{18,... | collective-permute-start | bytes 331784 | tf_op jit(solution)/shard_map/ppermute | solution.py:920
  108.6 10.6 %collective-permute-start.13 = (bf16[48,1152]{1,0:T(8,128)(2,1)S(1)}, bf16[48,1152]{1,0:T(8,128)(2,1)S(1)}, u32[]{:S(2)}, u32[]{:S(2)}) collective-permute-start(bf16[48,1152]{1,0:T(8,128)(2,1)S(1)} %get-tuple-element.206), channel_id=1, source_target_pairs={{0,16},{2,18},{4,20},{6,22},{8,24},{10,26},{12,28},{14,30},{16,0},... | collective-permute-start | bytes 331784 | tf_op jit(solution)/shard_map/ppermute | solution.py:920
  110.5 8.7 %collective-permute-start.14 = (bf16[48,1152]{1,0:T(8,128)(2,1)S(1)}, bf16[48,1152]{1,0:T(8,128)(2,1)S(1)}, u32[]{:S(2)}, u32[]{:S(2)}) collective-permute-start(bf16[48,1152]{1,0:T(8,128)(2,1)S(1)} %get-tuple-element.207), channel_id=1, source_target_pairs={{0,24},{2,26},{4,28},{6,30},{8,16},{10,18},{12,20},{14,22},{16,8},... | collective-permute-start | bytes 331784 | tf_op jit(solution)/shard_map/ppermute | solution.py:920
  119.9 16.2 %collective-permute-start.22 = (bf16[192,1536]{1,0:T(8,128)(2,1)S(1)}, bf16[192,1536]{1,0:T(8,128)(2,1)S(1)}, u32[]{:S(2)}, u32[]{:S(2)}) collective-permute-start(bf16[192,1536]{1,0:T(8,128)(2,1)S(1)} %get-tuple-element.212.refs_4_), channel_id=1, source_target_pairs={{0,4},{2,6},{4,0},{6,2},{8,12},{10,14},{12,8},{14,10},{16,20},{18,... | collective-permute-start | bytes 1769480 | tf_op jit(solution)/shard_map/ppermute | solution.py:920
  121.5 4.0 %collective-permute-start.18 = (bf16[48,384]{1,0:T(8,128)(2,1)S(1)}, bf16[48,384]{1,0:T(8,128)(2,1)S(1)}, u32[]{:S(2)}, u32[]{:S(2)}) collective-permute-start(bf16[48,384]{1,0:T(8,128)(2,1)S(1)} %get-tuple-element.211.own_ref), channel_id=1, source_target_pairs={{0,1},{1,0},{2,3},{3,2},{4,5},{5,4},{6,7},{7,6},{8,9},{9,8},{10,11... | collective-permute-start | bytes 110600 | tf_op jit(solution)/shard_map/ppermute | solution.py:1327
  126.1 7.1 %collective-permute-start.21 = (bf16[48,1152]{1,0:T(8,128)(2,1)S(1)}, bf16[48,1152]{1,0:T(8,128)(2,1)S(1)}, u32[]{:S(2)}, u32[]{:S(2)}) collective-permute-start(bf16[48,1152]{1,0:T(8,128)(2,1)S(1)} %heads_kernel.1.refs_0_), channel_id=1, source_target_pairs={{0,24},{2,26},{4,28},{6,30},{8,16},{10,18},{12,20},{14,22},{16,8},... | collective-permute-start | bytes 331784 | tf_op jit(solution)/shard_map/ppermute | solution.py:920
  128.5 7.6 %collective-permute-start.20 = (bf16[48,1152]{1,0:T(8,128)(2,1)S(1)}, bf16[48,1152]{1,0:T(8,128)(2,1)S(1)}, u32[]{:S(2)}, u32[]{:S(2)}) collective-permute-start(bf16[48,1152]{1,0:T(8,128)(2,1)S(1)} %heads_kernel.1.refs_0_), channel_id=1, source_target_pairs={{0,16},{2,18},{4,20},{6,22},{8,24},{10,26},{12,28},{14,30},{16,0},... | collective-permute-start | bytes 331784 | tf_op jit(solution)/shard_map/ppermute | solution.py:920
  129.5 6.6 %collective-permute-start.19 = (bf16[48,1152]{1,0:T(8,128)(2,1)S(1)}, bf16[48,1152]{1,0:T(8,128)(2,1)S(1)}, u32[]{:S(2)}, u32[]{:S(2)}) collective-permute-start(bf16[48,1152]{1,0:T(8,128)(2,1)S(1)} %heads_kernel.1.refs_0_), channel_id=1, source_target_pairs={{0,8},{2,10},{4,12},{6,14},{8,0},{10,2},{12,4},{14,6},{16,24},{18,... | collective-permute-start | bytes 331784 | tf_op jit(solution)/shard_map/ppermute | solution.py:920
  136.8 5.0 %collective-permute-start.24 = (bf16[384,1536]{1,0:T(8,128)(2,1)S(1)}, bf16[384,1536]{1,0:T(8,128)(2,1)S(1)}, u32[]{:S(2)}, u32[]{:S(2)}) collective-permute-start(bf16[384,1536]{1,0:T(8,128)(2,1)S(1)} %get-tuple-element.215.own_ref), channel_id=1, source_target_pairs={{0,2},{2,0},{4,6},{6,4},{8,10},{10,8},{12,14},{14,12},{16,18},{18,... | collective-permute-start | bytes 3538952 | tf_op jit(solution)/shard_map/ppermute | solution.py:920
  137.3 12.2 %collective-permute-start.23 = (bf16[192,1152]{1,0:T(8,128)(2,1)S(1)}, bf16[192,1152]{1,0:T(8,128)(2,1)S(1)}, u32[]{:S(2)}, u32[]{:S(2)}) collective-permute-start(bf16[192,1152]{1,0:T(8,128)(2,1)S(1)} %get-tuple-element.214.piece_ref.refs_0_), channel_id=1, source_target_pairs={{0,4},{2,6},{4,0},{6,2},{8,12},{10,14},{12,8},{14,10},{16,20},{18,... | collective-permute-start | bytes 1327112 | tf_op jit(solution)/shard_map/ppermute | solution.py:920
  (11 other events, 56.2 us)

commit v8 on v7

--- a/solution.py
+++ b/solution.py
@@ -362,14 +362,12 @@
     g_ref,
     gg_ref,
     ggain_ref,
-    gate_w,
     _,
     dg_ref,
     dy_ref,
     first_ref,
     second_ref,
     grad_gain_ref,
-    norm_ref,
     scaled_ref,
     *scratch,
 ):
@@ -406,14 +404,21 @@
     def _():
         grad_out[...] = dot(gg_ref[...], scaled_ref[...], TN)
         grad_gate[...] = dot(normed_ref[...], dg_ref[...], TN)
-        norm_ref[...] = row_sums(grad_gate[...], gate_w[...])
         if fast:
             emit(at_ref, (grad_gate, grad_out), (first_ref, second_ref))
 
 
-def partial_kernel(from_row, at_ref, normed_ref, *refs):
-    for low, out in zip(refs[:3], refs[3:]):
+def partial_kernel(from_row, fast, at_ref, normed_ref, *refs):
+    lows, (gate_w, first_ref, second_ref), outs, norm_ref = refs[:3], refs[3:6], refs[6:9], refs[9]
+    for low, out in zip(lows, outs):
         out[...] = dot(normed_ref[from_row:, :], low[...], TN)
+    if not fast:
+        norm_ref[...] = row_sums(first_ref[...], gate_w[...])
+        return
+    half, width = first_ref.shape[0], gate_w.shape[1]
+    for j, ref in enumerate((first_ref, second_ref)):
+        at = pl.ds(pl.multiple_of((at_ref[1] ^ j) * half, LANES), half)
+        norm_ref[:, at] = row_sums(ref[:, :width].astype(f32), gate_w[at, :])
 
 
 def weights_kernel(fast, at_ref, normed_ref, *refs):
@@ -1111,7 +1116,7 @@
             ((model, width), f32, fixed(model, width)),
             ((width, model), f32, fixed(width, model)),
         ]
-    dg, dy, early_a, early_b, grad_gain, norm = run(
+    dg, dy, early_a, early_b, grad_gain = run(
         functools.partial(gate_kernel, half_units, inner_all, fast),
         units,
         at,
@@ -1129,7 +1134,6 @@
             (g, tall(width)),
             (gg, None),
             (ggain, None),
-            (gate_w, None),
             (branch, pl.BlockSpec(memory_space=pl.ANY)),
         ],
         [
@@ -1137,7 +1141,6 @@
             ((length, width), bf16, tall(width), fast),
             *pieces,
             ((8, width), f32, fixed(8, width)),
-            ((8, model), f32, fixed(8, model)),
         ],
         [low(length, model)] + ([big(model, width), big(width, model)] if fast else []),
     )
@@ -1232,14 +1235,19 @@
         early = [kept, hop(sent, "line")]
         behind = (kept,)
     low_b, carry = backward(cut, blocks - cut, (), behind)
-    partial = run(
-        functools.partial(partial_kernel, cut * BLOCK),
+    *partial, norm = run(
+        functools.partial(partial_kernel, cut * BLOCK, fast),
         1,
         at,
-        [(normed, None), *[(a, None) for a in low_b]],
         [
-            ((model, a.shape[1]), f32, fixed(model, a.shape[1])) for a in low_b
+            (normed, None),
+            *[(a, None) for a in low_b],
+            (gate_w, None),
+            (early_a, None),
+            (early_b, None),
         ],
+        [((model, a.shape[1]), f32, fixed(model, a.shape[1])) for a in low_b]
+        + [((8, model), f32, fixed(8, model))],
         [],
     )
     if fast:

time: 154 us -> 155 us (level)
    unnamed x17 -> x33, local copies, waits for them, and re-layouts: 4.13 us -> 5.34 us
  transfers between devices with their start and end apart: 27 -> 27, of which waited for: 12 -> 11; matrix products, arithmetic and copies ran while one was open for 5% -> 5% of each run, Pallas kernels for 41% -> 41%
where the time goes in v8:
time: 155 us; the launch traced here: 154 us
  Pallas kernels  76.7 us (49%)
  waiting for transfers between devices  32.9 us (21%)
  starting transfers between devices  31.9 us (21%)
  local copies, waits for them, and re-layouts  11.2 us (7%)
    pallas_call x28, Pallas kernels, call(): pl.pallas_call(kernel, name=title, grid_spec=pltpu.PrefetchScalarGridSpec...  76.7 us
    ppermute x21, starting transfers between devices, hop(): return lax.ppermute(a, 'batch', [(i, i ^ mask) for i in range(batch)])  23.9 us
    ppermute x21, waiting for transfers between devices, hop(): return lax.ppermute(a, 'batch', [(i, i ^ mask) for i in range(batch)])  23 us
    ppermute x2, waiting for transfers between devices, per_device(): pair_of = lambda a: (a, lax.ppermute(a, 'heads', swap))  6.5 us
    unnamed x33, local copies, waits for them, and re-layouts  5.34 us
    ppermute x1, waiting for transfers between devices, per_device(): theirs = lax.ppermute(rest, 'heads', swap)  3.42 us
  transfers between devices with their start and end apart: 27, of which 11 were waited for; matrix products, arithmetic and copies ran while one was open for 5% of the time, Pallas kernels for 41%

profile of v8, /device:TPU:0, one launch (start us, length us, event | category | flops | bytes accessed | tf_op | source)
XLA Modules:
  0.0 154.3 jit_solution(15927864957487024203)
XLA Ops:
  0.7 3.0 %collective-permute-start = (bf16[512,768]{1,0:T(8,128)(2,1)}, bf16[512,768]{1,0:T(8,128)(2,1)S(1)}, u32[]{:S(2)}, u32[]{:S(2)}) collective-permute-start(bf16[512,768]{1,0:T(8,128)(2,1)} %bitcast.14), channel_id=1, source_target_pairs={{0,1},{1,0},{2,3},{3,2},{4,5},{5,4},{6,7},{7,6},{8,9},{9,8},{10,11... | collective-permute-start | bytes 2359304 | tf_op jit(solution)/shard_map/ppermute | solution.py:913
  15.8 6.5 %collective-permute-done.other_ref = bf16[512,768]{1,0:T(8,128)(2,1)S(1)} collective-permute-done((bf16[512,768]{1,0:T(8,128)(2,1)}, bf16[512,768]{1,0:T(8,128)(2,1)S(1)}, u32[]{:S(2)}, u32[]{:S(2)}) %collective-permute-start) | collective-permute-done | bytes 786464 | tf_op jit(solution)/shard_map/ppermute | solution.py:913
  22.3 13.6 %forward_kernel.1 = (bf16[1024,768]{1,0:T(8,128)(2,1)S(1)}, f32[1024,768]{1,0:T(8,128)S(1)}, f32[1024,768]{1,0:T(8,128)S(1)}, bf16[1024,768]{1,0:T(8,128)(2,1)S(...) custom-call(s32[5]{0:T(128)S(1)} %stack.23.at_ref, ...), custom_call_target="tpu_custom_call" | custom-call | flops 17999998976 | tf_op jit(solution)/shard_map/forward_kernel/pallas_call | solution.py:837
  40.6 2.1 %collective-permute-start.3 = (f32[16,512]{1,0:T(8,128)S(1)}, f32[16,512]{1,0:T(8,128)S(1)}, u32[]{:S(2)}, u32[]{:S(2)}) collective-permute-start(f32[16,512]{1,0:T(8,128)S(1)} %get-tuple-element.147.here_ref.here_a.here_b), channel_id=1, source_target_pairs={{0,1},{1,0},{2,3},{3,2},{4,5},{5,4},{6,7},{7,6},{8,9},{9,8},{10,11... | collective-permute-start | bytes 98312 | tf_op jit(solution)/shard_map/ppermute | solution.py:914
  42.7 2.3 %branch_kernel.1 = (bf16[512,768]{1,0:T(8,128)(2,1)S(1)}, bf16[512,768]{1,0:T(8,128)(2,1)S(1)}) custom-call(s32[5]{0:T(128)S(1)} %stack.23.at_ref, bf16[1024,768]{1,0:T(8,128)(2,1)S(1)} %get-tuple-element.141.gg_ref, bf16[768,768]{1,0:T(8,128)(2,1)S(1)} %get-tuple-element.142.out_w), custom_call_target="tpu_custom_call" | custom-call | flops 1200000000 | tf_op jit(solution)/shard_map/branch_kernel/pallas_call | solution.py:837
  45.0 5.6 %gate_kernel.1 = (bf16[1024,768]{1,0:T(8,128)(2,1)S(1)}, bf16[1024,768]{1,0:T(8,128)(2,1)S(1)}, bf16[384,1536]{1,0:T(8,128)(2,1)S(1)}, bf16[384,1536]{1,0:T(8,128)(2,1)S(1)}, f32[8,768]{1,0:T(8,128)S(1)}) custom-call(s32[5]{0:T(128)S(1)} %stack.23.at_ref, bf16[512,768]{1,0:T(8,128)(2,1)S(1)} %bitcast.20, ...), custom_call_target="tpu_custom_call" | custom-call | flops 4800000000 | tf_op jit(solution)/shard_map/gate_kernel/pallas_call | solution.py:837
  52.3 2.8 %gate_back_kernel.1.refs_2_.from_gate = f32[1024,768]{1,0:T(8,128)S(1)} custom-call(s32[5]{0:T(128)S(1)} %stack.23.at_ref, bf16[1024,768]{1,0:T(8,128)(2,1)S(1)} %get-tuple-element.154.dg_ref, bf16[768,768]{1,0:T(8,128)(2,1)S(1)} %get-tuple-element.128.gate_w.refs_3_), custom_call_target="tpu_custom_call" | custom-call | flops 4000000000 | tf_op jit(solution)/shard_map/gate_back_kernel/pallas_call | solution.py:837
  57.6 9.3 %backward_kernel.2 = (bf16[512,768]{1,0:T(8,128)(2,1)S(1)}, bf16[512,256]{1,0:T(8,128)(2,1)S(1)}, bf16[512,128]{1,0:T(8,128)(2,1)S(1)}, f32[128,768]{1,0:T(8,128...) custom-call(s32[5]{0:T(128)S(1)} %stack.23.at_ref, ...), custom_call_target="tpu_custom_call" | custom-call | flops 7000000000 | tf_op jit(solution)/shard_map/backward_kernel/pallas_call | solution.py:837
  66.9 2.1 %partial_kernel.1 = (f32[768,768]{1,0:T(8,128)S(1)}, f32[768,256]{1,0:T(8,128)S(1)}, f32[768,128]{1,0:T(8,128)S(1)}, f32[8,768]{1,0:T(8,128)S(1)}) custom-call(s32[5]{0:T(128)S(1)} %stack.23.at_ref, bf16[1024,768]{1,0:T(8,128)(2,1)S(1)} %get-tuple-element.149.normed_ref, bf16[512,768]{1,0:T(8,128)(2,1)S(1)} %get-tuple-element.180.refs_0_.refs_3_, ...), custom_call_target="tpu_custom_call" | custom-call | flops 2000000000 | tf_op jit(solution)/shard_map/partial_kernel/pallas_call | solution.py:837
  69.0 2.5 %collective-permute-done.5.refs_1_ = bf16[192,1536]{1,0:T(8,128)(2,1)S(1)} collective-permute-done((bf16[192,1536]{1,0:T(8,128)(2,1)S(1)}, bf16[192,1536]{1,0:T(8,128)(2,1)S(1)}, u32[]{:S(2)}, u32[]{:S(2)}) %collective-permute-start.5) | collective-permute-done | bytes 589856 | tf_op jit(solution)/shard_map/ppermute | solution.py:925
  73.8 2.6 %collective-permute-start.8 = (bf16[48,1536]{1,0:T(8,128)(2,1)S(1)}, bf16[48,1536]{1,0:T(8,128)(2,1)S(1)}, u32[]{:S(2)}, u32[]{:S(2)}) collective-permute-start(bf16[48,1536]{1,0:T(8,128)(2,1)S(1)} %get-tuple-element.198), channel_id=1, source_target_pairs={{0,16},{2,18},{4,20},{6,22},{8,24},{10,26},{12,28},{14,30},{16,0},... | collective-permute-start | bytes 442376 | tf_op jit(solution)/shard_map/ppermute | solution.py:925
  76.6 10.2 %backward_kernel.3 = (bf16[512,768]{1,0:T(8,128)(2,1)S(1)}, bf16[512,256]{1,0:T(8,128)(2,1)S(1)}, bf16[512,128]{1,0:T(8,128)(2,1)S(1)}, f32[128,768]{1,0:T(8,128...) custom-call(s32[5]{0:T(128)S(1)} %stack.23.at_ref, ...), custom_call_target="tpu_custom_call" | custom-call | flops 7000000000 | tf_op jit(solution)/shard_map/backward_kernel/pallas_call | solution.py:837
  87.4 2.9 %weights_kernel.1 = (bf16[384,1152]{1,0:T(8,128)(2,1)S(1)}, bf16[384,1152]{1,0:T(8,128)(2,1)S(1)}, bf16[48,1536]{1,0:T(8,128)(2,1)S(1)}) custom-call(s32[5]{0:T(128)S(1)} %stack.23.at_ref, bf16[1024,768]{1,0:T(8,128)(2,1)S(1)} %get-tuple-element.149.normed_ref, bf16[512,768]{1,0:T(8,128)(2,1)S(1)} %get-tuple-element.184.refs_0_, ...), custom_call_target="tpu_custom_call" | custom-call | flops 1200000000 | tf_op jit(solution)/shard_map/weights_kernel/pallas_call | solution.py:837
  90.4 3.1 %collective-permute-start.17 = (bf16[48,1536]{1,0:T(8,128)(2,1)S(1)}, bf16[48,1536]{1,0:T(8,128)(2,1)S(1)}, u32[]{:S(2)}, u32[]{:S(2)}) collective-permute-start(bf16[48,1536]{1,0:T(8,128)(2,1)S(1)} %get-tuple-element.208.refs_4_), channel_id=1, source_target_pairs={{0,24},{2,26},{4,28},{6,30},{8,16},{10,18},{12,20},{14,22},{16,8},... | collective-permute-start | bytes 442376 | tf_op jit(solution)/shard_map/ppermute | solution.py:925
  96.7 3.6 %normed_grad_kernel.1 = (bf16[512,768]{1,0:T(8,128)(2,1)S(1)}, bf16[512,768]{1,0:T(8,128)(2,1)S(1)}) custom-call(s32[5]{0:T(128)S(1)} %stack.23.at_ref, f32[1024,768]{1,0:T(8,128)S(1)} %gate_back_kernel.1.refs_2_.from_gate, bf16[512,768]{1,0:T(8,128)(2,1)S(1)} %get-tuple-element.184.refs_0_, bf16[512,256]{1,0:T(8,128)(2,1)S(1)} %get-tuple-element.185.refs_1_, ...), custom_call_target="tpu_custom_call" | custom-call | flops 4800000000 | tf_op jit(solution)/shard_map/normed_grad_kernel/pallas_call | solution.py:837
  101.9 5.3 %collective-permute-done.11.refs_1_ = bf16[192,1152]{1,0:T(8,128)(2,1)S(1)} collective-permute-done((bf16[192,1152]{1,0:T(8,128)(2,1)S(1)}, bf16[192,1152]{1,0:T(8,128)(2,1)S(1)}, u32[]{:S(2)}, u32[]{:S(2)}) %collective-permute-start.11) | collective-permute-done | bytes 442400 | tf_op jit(solution)/shard_map/ppermute | solution.py:925
  112.4 2.1 %mixed_kernel.1 = (f32[512,768]{1,0:T(8,128)}, f32[8,128]{1,0:T(8,128)S(1)}) custom-call(s32[5]{0:T(128)S(1)} %stack.23.at_ref, bf16[512,768]{1,0:T(8,128)(2,1)S(1)} %bitcast.16, bf16[512,768]{1,0:T(8,128)(2,1)S(1)} %get-tuple-element.143.own_ref._, bf16[512,768]{1,0:T(8,128)(2,1)S(1)} %collective-permute-done.1.other_ref.refs_7_, ...), custom_call_target="tpu_custom_call" | custom-call | flops 2000000000 | tf_op jit(solution)/shard_map/mixed_kernel/pallas_call | solution.py:837
  114.5 5.4 %collective-permute-done.13.refs_2_ = bf16[48,1152]{1,0:T(8,128)(2,1)S(1)} collective-permute-done((bf16[48,1152]{1,0:T(8,128)(2,1)S(1)}, bf16[48,1152]{1,0:T(8,128)(2,1)S(1)}, u32[]{:S(2)}, u32[]{:S(2)}) %collective-permute-start.13) | collective-permute-done | bytes 110624 | tf_op jit(solution)/shard_map/ppermute | solution.py:925
  122.7 3.4 %collective-permute-done.18.other_ref = bf16[48,384]{1,0:T(8,128)(2,1)S(1)} collective-permute-done((bf16[48,384]{1,0:T(8,128)(2,1)S(1)}, bf16[48,384]{1,0:T(8,128)(2,1)S(1)}, u32[]{:S(2)}, u32[]{:S(2)}) %collective-permute-start.18) | collective-permute-done | bytes 36896 | tf_op jit(solution)/shard_map/ppermute | solution.py:1335
  126.8 2.4 %collective-permute-start.21 = (bf16[48,1152]{1,0:T(8,128)(2,1)S(1)}, bf16[48,1152]{1,0:T(8,128)(2,1)S(1)}, u32[]{:S(2)}, u32[]{:S(2)}) collective-permute-start(bf16[48,1152]{1,0:T(8,128)(2,1)S(1)} %heads_kernel.1.refs_0_), channel_id=1, source_target_pairs={{0,24},{2,26},{4,28},{6,30},{8,16},{10,18},{12,20},{14,22},{16,8},... | collective-permute-start | bytes 331784 | tf_op jit(solution)/shard_map/ppermute | solution.py:925
  131.2 2.3 %input_kernel.1 = (f32[512,768]{1,0:T(8,128)}, f32[8,128]{1,0:T(8,128)S(1)}) custom-call(s32[5]{0:T(128)S(1)} %stack.23.at_ref, bf16[512,768]{1,0:T(8,128)(2,1)S(1)} %bitcast.17, bf16[512,768]{1,0:T(8,128)(2,1)S(1)} %bitcast.21, bf16[512,768]{1,0:T(8,128)(2,1)S(1)} %get-tuple-element.187.own_ref.refs_2_, ...), custom_call_target="tpu_custom_call" | custom-call | flops 2000000000 | tf_op jit(solution)/shard_map/input_kernel/pallas_call | solution.py:837
  134.1 2.5 %collective-permute-done.20.refs_2_ = bf16[48,1152]{1,0:T(8,128)(2,1)S(1)} collective-permute-done((bf16[48,1152]{1,0:T(8,128)(2,1)S(1)}, bf16[48,1152]{1,0:T(8,128)(2,1)S(1)}, u32[]{:S(2)}, u32[]{:S(2)}) %collective-permute-start.20) | collective-permute-done | bytes 110624 | tf_op jit(solution)/shard_map/ppermute | solution.py:925
  142.3 3.0 %early_kernel.1 = (f32[768,768]{1,0:T(8,128)}, f32[768,768]{1,0:T(8,128)}, f32[8,128]{1,0:T(8,128)S(1)}) custom-call(s32[5]{0:T(128)S(1)} %stack.23.at_ref, bf16[384,1536]{1,0:T(8,128)(2,1)S(1)} %get-tuple-element.215.own_ref, bf16[384,1536]{1,0:T(8,128)(2,1)S(1)} %collective-permute-done.24.other_ref), custom_call_target="tpu_custom_call" | custom-call | flops 3000000000 | tf_op jit(solution)/shard_map/early_kernel/pallas_call | solution.py:837
  145.2 4.8 %collective-permute-done.23.refs_0_ = bf16[192,1152]{1,0:T(8,128)(2,1)S(1)} collective-permute-done((bf16[192,1152]{1,0:T(8,128)(2,1)S(1)}, bf16[192,1152]{1,0:T(8,128)(2,1)S(1)}, u32[]{:S(2)}, u32[]{:S(2)}) %collective-permute-start.23) | collective-permute-done | bytes 442400 | tf_op jit(solution)/shard_map/ppermute | solution.py:925
  (109 shorter events, 50.0 us)
Async XLA Ops:
  0.7 21.6 %collective-permute-start = (bf16[512,768]{1,0:T(8,128)(2,1)}, bf16[512,768]{1,0:T(8,128)(2,1)S(1)}, u32[]{:S(2)}, u32[]{:S(2)}) collective-permute-start(bf16[512,768]{1,0:T(8,128)(2,1)} %bitcast.14), channel_id=1, source_target_pairs={{0,1},{1,0},{2,3},{3,2},{4,5},{5,4},{6,7},{7,6},{8,9},{9,8},{10,11... | collective-permute-start | bytes 2359304 | tf_op jit(solution)/shard_map/ppermute | solution.py:913
  3.7 35.2 %collective-permute-start.2 = (bf16[512,768]{1,0:T(8,128)(2,1)}, bf16[512,768]{1,0:T(8,128)(2,1)S(1)}, u32[]{:S(2)}, u32[]{:S(2)}) collective-permute-start(bf16[512,768]{1,0:T(8,128)(2,1)} %bitcast.18), channel_id=1, source_target_pairs={{0,1},{1,0},{2,3},{3,2},{4,5},{5,4},{6,7},{7,6},{8,9},{9,8},{10,11... | collective-permute-start | bytes 2359304 | tf_op jit(solution)/shard_map/ppermute | solution.py:913
  40.6 4.4 %collective-permute-start.3 = (f32[16,512]{1,0:T(8,128)S(1)}, f32[16,512]{1,0:T(8,128)S(1)}, u32[]{:S(2)}, u32[]{:S(2)}) collective-permute-start(f32[16,512]{1,0:T(8,128)S(1)} %get-tuple-element.147.here_ref.here_a.here_b), channel_id=1, source_target_pairs={{0,1},{1,0},{2,3},{3,2},{4,5},{5,4},{6,7},{7,6},{8,9},{9,8},{10,11... | collective-permute-start | bytes 98312 | tf_op jit(solution)/shard_map/ppermute | solution.py:914
  50.6 4.5 %collective-permute-start.4 = (bf16[384,1536]{1,0:T(8,128)(2,1)S(1)}, bf16[384,1536]{1,0:T(8,128)(2,1)S(1)}, u32[]{:S(2)}, u32[]{:S(2)}) collective-permute-start(bf16[384,1536]{1,0:T(8,128)(2,1)S(1)} %get-tuple-element.170.refs_5_), channel_id=1, source_target_pairs={{0,2},{2,0},{4,6},{6,4},{8,10},{10,8},{12,14},{14,12},{16,18},{18,... | collective-permute-start | bytes 3538952 | tf_op jit(solution)/shard_map/ppermute | solution.py:925
  50.7 25.9 %collective-permute-start.1 = (bf16[512,768]{1,0:T(8,128)(2,1)S(1)}, bf16[512,768]{1,0:T(8,128)(2,1)S(1)}, u32[]{:S(2)}, u32[]{:S(2)}) collective-permute-start(bf16[512,768]{1,0:T(8,128)(2,1)S(1)} %get-tuple-element.144), channel_id=1, source_target_pairs={{0,1},{1,0},{2,3},{3,2},{4,5},{5,4},{6,7},{7,6},{8,9},{9,8},{10,11... | collective-permute-start | bytes 2359304 | tf_op jit(solution)/shard_map/ppermute | solution.py:1104
  56.0 15.5 %collective-permute-start.5 = (bf16[192,1536]{1,0:T(8,128)(2,1)S(1)}, bf16[192,1536]{1,0:T(8,128)(2,1)S(1)}, u32[]{:S(2)}, u32[]{:S(2)}) collective-permute-start(bf16[192,1536]{1,0:T(8,128)(2,1)S(1)} %get-tuple-element.178), channel_id=1, source_target_pairs={{0,4},{2,6},{4,0},{6,2},{8,12},{10,14},{12,8},{14,10},{16,20},{18,... | collective-permute-start | bytes 1769480 | tf_op jit(solution)/shard_map/ppermute | solution.py:925
  72.1 14.7 %collective-permute-start.7 = (bf16[48,1536]{1,0:T(8,128)(2,1)S(1)}, bf16[48,1536]{1,0:T(8,128)(2,1)S(1)}, u32[]{:S(2)}, u32[]{:S(2)}) collective-permute-start(bf16[48,1536]{1,0:T(8,128)(2,1)S(1)} %get-tuple-element.197), channel_id=1, source_target_pairs={{0,8},{2,10},{4,12},{6,14},{8,0},{10,2},{12,4},{14,6},{16,24},{18,... | collective-permute-start | bytes 442376 | tf_op jit(solution)/shard_map/ppermute | solution.py:925
  73.8 13.6 %collective-permute-start.8 = (bf16[48,1536]{1,0:T(8,128)(2,1)S(1)}, bf16[48,1536]{1,0:T(8,128)(2,1)S(1)}, u32[]{:S(2)}, u32[]{:S(2)}) collective-permute-start(bf16[48,1536]{1,0:T(8,128)(2,1)S(1)} %get-tuple-element.198), channel_id=1, source_target_pairs={{0,16},{2,18},{4,20},{6,22},{8,24},{10,26},{12,28},{14,30},{16,0},... | collective-permute-start | bytes 442376 | tf_op jit(solution)/shard_map/ppermute | solution.py:925
  76.4 11.1 %collective-permute-start.9 = (bf16[48,1536]{1,0:T(8,128)(2,1)S(1)}, bf16[48,1536]{1,0:T(8,128)(2,1)S(1)}, u32[]{:S(2)}, u32[]{:S(2)}) collective-permute-start(bf16[48,1536]{1,0:T(8,128)(2,1)S(1)} %get-tuple-element.199), channel_id=1, source_target_pairs={{0,24},{2,26},{4,28},{6,30},{8,16},{10,18},{12,20},{14,22},{16,8},... | collective-permute-start | bytes 442376 | tf_op jit(solution)/shard_map/ppermute | solution.py:925
  90.4 18.8 %collective-permute-start.17 = (bf16[48,1536]{1,0:T(8,128)(2,1)S(1)}, bf16[48,1536]{1,0:T(8,128)(2,1)S(1)}, u32[]{:S(2)}, u32[]{:S(2)}) collective-permute-start(bf16[48,1536]{1,0:T(8,128)(2,1)S(1)} %get-tuple-element.208.refs_4_), channel_id=1, source_target_pairs={{0,24},{2,26},{4,28},{6,30},{8,16},{10,18},{12,20},{14,22},{16,8},... | collective-permute-start | bytes 442376 | tf_op jit(solution)/shard_map/ppermute | solution.py:925
  93.5 17.6 %collective-permute-start.16 = (bf16[48,1536]{1,0:T(8,128)(2,1)S(1)}, bf16[48,1536]{1,0:T(8,128)(2,1)S(1)}, u32[]{:S(2)}, u32[]{:S(2)}) collective-permute-start(bf16[48,1536]{1,0:T(8,128)(2,1)S(1)} %get-tuple-element.208.refs_4_), channel_id=1, source_target_pairs={{0,16},{2,18},{4,20},{6,22},{8,24},{10,26},{12,28},{14,30},{16,0},... | collective-permute-start | bytes 442376 | tf_op jit(solution)/shard_map/ppermute | solution.py:925
  95.2 12.0 %collective-permute-start.11 = (bf16[192,1152]{1,0:T(8,128)(2,1)S(1)}, bf16[192,1152]{1,0:T(8,128)(2,1)S(1)}, u32[]{:S(2)}, u32[]{:S(2)}) collective-permute-start(bf16[192,1152]{1,0:T(8,128)(2,1)S(1)} %get-tuple-element.203), channel_id=1, source_target_pairs={{0,4},{2,6},{4,0},{6,2},{8,12},{10,14},{12,8},{14,10},{16,20},{18,... | collective-permute-start | bytes 1327112 | tf_op jit(solution)/shard_map/ppermute | solution.py:925
  100.4 30.9 %collective-permute-start.6 = (bf16[512,768]{1,0:T(8,128)(2,1)S(1)}, bf16[512,768]{1,0:T(8,128)(2,1)S(1)}, u32[]{:S(2)}, u32[]{:S(2)}) collective-permute-start(bf16[512,768]{1,0:T(8,128)(2,1)S(1)} %get-tuple-element.188), channel_id=1, source_target_pairs={{0,1},{1,0},{2,3},{3,2},{4,5},{5,4},{6,7},{7,6},{8,9},{9,8},{10,11... | collective-permute-start | bytes 2359304 | tf_op jit(solution)/shard_map/ppermute | solution.py:1104
  101.0 13.5 %collective-permute-start.15 = (bf16[48,1536]{1,0:T(8,128)(2,1)S(1)}, bf16[48,1536]{1,0:T(8,128)(2,1)S(1)}, u32[]{:S(2)}, u32[]{:S(2)}) collective-permute-start(bf16[48,1536]{1,0:T(8,128)(2,1)S(1)} %get-tuple-element.208.refs_4_), channel_id=1, source_target_pairs={{0,8},{2,10},{4,12},{6,14},{8,0},{10,2},{12,4},{14,6},{16,24},{18,... | collective-permute-start | bytes 442376 | tf_op jit(solution)/shard_map/ppermute | solution.py:925
  108.0 6.5 %collective-permute-start.12 = (bf16[48,1152]{1,0:T(8,128)(2,1)S(1)}, bf16[48,1152]{1,0:T(8,128)(2,1)S(1)}, u32[]{:S(2)}, u32[]{:S(2)}) collective-permute-start(bf16[48,1152]{1,0:T(8,128)(2,1)S(1)} %get-tuple-element.205), channel_id=1, source_target_pairs={{0,8},{2,10},{4,12},{6,14},{8,0},{10,2},{12,4},{14,6},{16,24},{18,... | collective-permute-start | bytes 331784 | tf_op jit(solution)/shard_map/ppermute | solution.py:925
  109.2 10.7 %collective-permute-start.13 = (bf16[48,1152]{1,0:T(8,128)(2,1)S(1)}, bf16[48,1152]{1,0:T(8,128)(2,1)S(1)}, u32[]{:S(2)}, u32[]{:S(2)}) collective-permute-start(bf16[48,1152]{1,0:T(8,128)(2,1)S(1)} %get-tuple-element.206), channel_id=1, source_target_pairs={{0,16},{2,18},{4,20},{6,22},{8,24},{10,26},{12,28},{14,30},{16,0},... | collective-permute-start | bytes 331784 | tf_op jit(solution)/shard_map/ppermute | solution.py:925
  111.1 8.8 %collective-permute-start.14 = (bf16[48,1152]{1,0:T(8,128)(2,1)S(1)}, bf16[48,1152]{1,0:T(8,128)(2,1)S(1)}, u32[]{:S(2)}, u32[]{:S(2)}) collective-permute-start(bf16[48,1152]{1,0:T(8,128)(2,1)S(1)} %get-tuple-element.207), channel_id=1, source_target_pairs={{0,24},{2,26},{4,28},{6,30},{8,16},{10,18},{12,20},{14,22},{16,8},... | collective-permute-start | bytes 331784 | tf_op jit(solution)/shard_map/ppermute | solution.py:925
  120.6 16.0 %collective-permute-start.22 = (bf16[192,1536]{1,0:T(8,128)(2,1)S(1)}, bf16[192,1536]{1,0:T(8,128)(2,1)S(1)}, u32[]{:S(2)}, u32[]{:S(2)}) collective-permute-start(bf16[192,1536]{1,0:T(8,128)(2,1)S(1)} %get-tuple-element.212.refs_4_), channel_id=1, source_target_pairs={{0,4},{2,6},{4,0},{6,2},{8,12},{10,14},{12,8},{14,10},{16,20},{18,... | collective-permute-start | bytes 1769480 | tf_op jit(solution)/shard_map/ppermute | solution.py:925
  122.2 4.0 %collective-permute-start.18 = (bf16[48,384]{1,0:T(8,128)(2,1)S(1)}, bf16[48,384]{1,0:T(8,128)(2,1)S(1)}, u32[]{:S(2)}, u32[]{:S(2)}) collective-permute-start(bf16[48,384]{1,0:T(8,128)(2,1)S(1)} %get-tuple-element.211.own_ref), channel_id=1, source_target_pairs={{0,1},{1,0},{2,3},{3,2},{4,5},{5,4},{6,7},{7,6},{8,9},{9,8},{10,11... | collective-permute-start | bytes 110600 | tf_op jit(solution)/shard_map/ppermute | solution.py:1335
  126.8 7.3 %collective-permute-start.21 = (bf16[48,1152]{1,0:T(8,128)(2,1)S(1)}, bf16[48,1152]{1,0:T(8,128)(2,1)S(1)}, u32[]{:S(2)}, u32[]{:S(2)}) collective-permute-start(bf16[48,1152]{1,0:T(8,128)(2,1)S(1)} %heads_kernel.1.refs_0_), channel_id=1, source_target_pairs={{0,24},{2,26},{4,28},{6,30},{8,16},{10,18},{12,20},{14,22},{16,8},... | collective-permute-start | bytes 331784 | tf_op jit(solution)/shard_map/ppermute | solution.py:925
  129.2 7.4 %collective-permute-start.20 = (bf16[48,1152]{1,0:T(8,128)(2,1)S(1)}, bf16[48,1152]{1,0:T(8,128)(2,1)S(1)}, u32[]{:S(2)}, u32[]{:S(2)}) collective-permute-start(bf16[48,1152]{1,0:T(8,128)(2,1)S(1)} %heads_kernel.1.refs_0_), channel_id=1, source_target_pairs={{0,16},{2,18},{4,20},{6,22},{8,24},{10,26},{12,28},{14,30},{16,0},... | collective-permute-start | bytes 331784 | tf_op jit(solution)/shard_map/ppermute | solution.py:925
  130.2 6.5 %collective-permute-start.19 = (bf16[48,1152]{1,0:T(8,128)(2,1)S(1)}, bf16[48,1152]{1,0:T(8,128)(2,1)S(1)}, u32[]{:S(2)}, u32[]{:S(2)}) collective-permute-start(bf16[48,1152]{1,0:T(8,128)(2,1)S(1)} %heads_kernel.1.refs_0_), channel_id=1, source_target_pairs={{0,8},{2,10},{4,12},{6,14},{8,0},{10,2},{12,4},{14,6},{16,24},{18,... | collective-permute-start | bytes 331784 | tf_op jit(solution)/shard_map/ppermute | solution.py:925
  137.3 5.0 %collective-permute-start.24 = (bf16[384,1536]{1,0:T(8,128)(2,1)S(1)}, bf16[384,1536]{1,0:T(8,128)(2,1)S(1)}, u32[]{:S(2)}, u32[]{:S(2)}) collective-permute-start(bf16[384,1536]{1,0:T(8,128)(2,1)S(1)} %get-tuple-element.215.own_ref), channel_id=1, source_target_pairs={{0,2},{2,0},{4,6},{6,4},{8,10},{10,8},{12,14},{14,12},{16,18},{18,... | collective-permute-start | bytes 3538952 | tf_op jit(solution)/shard_map/ppermute | solution.py:925
  137.9 12.2 %collective-permute-start.23 = (bf16[192,1152]{1,0:T(8,128)(2,1)S(1)}, bf16[192,1152]{1,0:T(8,128)(2,1)S(1)}, u32[]{:S(2)}, u32[]{:S(2)}) collective-permute-start(bf16[192,1152]{1,0:T(8,128)(2,1)S(1)} %get-tuple-element.214.piece_ref.refs_0_), channel_id=1, source_target_pairs={{0,4},{2,6},{4,0},{6,2},{8,12},{10,14},{12,8},{14,10},{16,20},{18,... | collective-permute-start | bytes 1327112 | tf_op jit(solution)/shard_map/ppermute | solution.py:925
  (19 other events, 121.6 us)
